TPU v7x, 256 devices: a whole 4x4x8 slice. The times are simulated.
256 devices in a mesh: cuts: 2 (over x_hi), fsdp: 128 (over y, x_lo, z, core).
Axes of the slice: x: 4 (x_hi: 2, x_lo: 2; x = x_hi * 2 + x_lo), y: 4, z: 8, core: 2. Of those that a mesh axis runs over, the one named last changes fastest.
Arguments:
- tokens: bfloat16 [98304, 8192], P(('cuts', 'fsdp')), may hold values from -33 to 33
- cotangent: bfloat16 [98304, 512], P(('cuts', 'fsdp')), may hold values from -0.022326078 to 0.022326078
- weight: float32 [8192, 512], P('fsdp'), may hold values from -17 to 17
- row_moment: float32 [8192], P('fsdp'), may hold values from 0.05 to 0.5
- col_moment: float32 [512], replicated, may hold values from 0.05 to 0.5
Outputs:
- new_weight: float32 [8192, 512], P('fsdp')
- delta: float32 [8192, 512], P('fsdp')
- rows_new: float32 [8192], P('fsdp')
- cols_new: float32 [512], replicated
- preact: bfloat16 [98304, 512], P(('cuts', 'fsdp'))
All inputs are finite; a program needn't handle non-finite values.
Results may differ from a plain program's by a relative error of at most 0.0049.
Values may be sent and summed in bfloat16 or wider, within the bound.
No kernel may reach another device: no remote copies, remote signals or barrier semaphores. Data moves between devices by JAX's collectives and lax.ppermute only.
A program may use at most 128 MiB of HBM per device.

v0:
```python
import math

import jax
import jax.numpy as jnp
from jax import lax
from jax.sharding import PartitionSpec as P

decay_rate = 0.9
tiny_square = 1e-30
clip_level = 1.0
weight_floor = 0.001
learn_rate = 0.1


def on_device(tokens, cotangent, weight, row_moment, col_moment):
    tok_rows, width = tokens.shape
    hidden_units = cotangent.shape[1]
    columns = tokens
    partial_grad = lax.psum_scatter(
        lax.dot_general(
            columns, cotangent, (((0,), (0,)), ((), ())), preferred_element_type=jnp.float32
        ),
        "fsdp",
        scatter_dimension=0,
        tiled=True,
    )
    gradient = lax.psum(partial_grad, "cuts")
    squares = gradient * gradient
    rows_new = decay_rate * row_moment + (1.0 - decay_rate) * (
        jnp.mean(squares, axis=1) + tiny_square
    )
    col_part = jnp.sum(squares, axis=0)
    row_part = jnp.sum(rows_new)
    weight_part = jnp.sum(weight * weight)
    inv_rows = lax.rsqrt(rows_new)
    col_total, row_total, weight_total = lax.psum((col_part, row_part, weight_part), "fsdp")
    cols_new = decay_rate * col_moment + (1.0 - decay_rate) * (col_total / width + tiny_square)
    mean_row = row_total / width
    update = gradient * jnp.sqrt(mean_row) * inv_rows[:, None] * lax.rsqrt(cols_new)[None, :]
    update_total = lax.psum(jnp.sum(update * update), "fsdp")
    update_rms = jnp.sqrt(update_total / (width * hidden_units))
    clipped = update / jnp.maximum(1.0, update_rms / clip_level)
    weight_rms = jnp.sqrt(weight_total / (width * hidden_units))
    delta = jnp.maximum(weight_floor, weight_rms) * clipped
    new_weight = weight - learn_rate * delta
    half_weight = new_weight.astype(jnp.bfloat16)
    columns = tokens
    summed = jnp.dot(
        columns,
        lax.all_gather(half_weight, "fsdp", axis=0, tiled=True),
        preferred_element_type=jnp.float32,
    )
    preact = (summed * (1.0 / math.sqrt(width))).astype(jnp.bfloat16)
    return (new_weight, delta, rows_new, cols_new, preact)


def solution(mesh):
    return jax.shard_map(
        on_device,
        mesh=mesh,
        in_specs=(
            P(("cuts", "fsdp"), None),
            P(("cuts", "fsdp"), None),
            P("fsdp", None),
            P("fsdp"),
            P(),
        ),
        out_specs=(P("fsdp", None), P("fsdp", None), P("fsdp"), P(), P(("cuts", "fsdp"), None)),
        check_vma=False,
    )
```

profile of v0, /device:TPU:33, one launch (start us, length us, event | category | flops | bytes accessed | tf_op | source)
XLA Modules:
  0.0 1439.1 jit_solution(12802164813947204050)
XLA Ops:
  7.2 0.0 copy-start
  7.2 0.0 reduce-scatter.2.cloned.1.call-start
  7.2 0.9 copy-done
  8.2 11.1 fusion.5
  19.2 0.0 copy-start.1
  19.3 0.0 copy-start.3
  19.3 0.0 copy-start.2
  19.3 0.0 reduce-scatter.2.cloned.1.call-update
  19.3 0.0 all-reduce.4.cloned.1.call-start
  19.3 581.8 %reduce-scatter.2.cloned.1.call-done = f32[64,512]{1,0:T(8,128)} async-done(((f32[8192,512]{1,0:T(8,128)}), f32[64,512]{1,0:T(8,128)}) %reduce-scatter.2.cloned.1.call-update) | async-done | bytes 131088 | tf_op jit(solution)/shard_map/reduce_scatter | solution.py:19
  601.1 0.0 all-reduce.4.cloned.1.call-update
  601.1 0.0 all-gather.2.cloned.1.call-start
  601.2 0.0 copy-done.1
  601.2 0.6 multiply_reduce_fusion.1
  601.8 41.6 %all-reduce.4.cloned.1.call-done = f32[64,512]{1,0:T(8,128)} async-done(((f32[64,512]{1,0:T(8,128)}), f32[64,512]{1,0:T(8,128)}) %all-reduce.4.cloned.1.call-update) | async-done | bytes 131088 | tf_op jit(solution)/shard_map/psum | solution.py:27
  643.5 1.0 multiply_reduce_fusion.3
  644.5 0.0 copy-done.3
  644.5 0.0 copy-start.4
  644.5 0.6 reduce_sum.47
  645.1 270.7 %all-reduce.1 = (f32[512]{0:T(512)S(1)}, f32[]{:T(128)}) all-reduce(f32[512]{0:T(512)S(1)} %get-tuple-element.11, f32[]{:T(128)} %reduce_sum.47), channel_id=1, replica_groups=mesh['cuts'=2,'fsdp'=128] {'fsdp'}, use_global_device_ids=true, to_apply=%region_8.0 | all-reduce | flops 513 | bytes 4104 | tf_op jit(solution)/shard_map/psum | solution.py:36
  916.5 0.0 copy-done.2
  916.5 0.6 fusion.4
  917.1 1.6 multiply_reduce_fusion
  918.7 280.7 %all-reduce = (f32[]{:T(128)}, f32[]{:T(128)}) all-reduce(f32[]{:T(128)} %multiply_reduce_fusion, f32[]{:T(128)} %multiply_reduce_fusion.1), channel_id=1, replica_groups=mesh['cuts'=2,'fsdp'=128] {'fsdp'}, use_global_device_ids=true, to_apply=%region_10.0 | all-reduce | flops 2 | bytes 16 | tf_op jit(solution)/shard_map/psum | solution.py:40
  1200.7 1.7 fusion.2
  1202.5 0.0 all-gather.2.cloned.1.call-update
  1202.5 219.5 %all-gather.2.cloned.1.call-done = bf16[8192,512]{1,0:T(8,128)(2,1)} async-done(((bf16[64,512]{1,0:T(8,128)(2,1)}), bf16[8192,512]{1,0:T(8,128)(2,1)}) %all-gather.2.cloned.1.call-update) | async-done | bytes 8388624 | tf_op jit(solution)/shard_map/all_gather | solution.py:50
  1421.9 9.7 fusion.1
  1431.6 0.0 copy-done.4
  1431.7 0.9 copy.10
  (1 shorter events, 0.0 us)
Async XLA Ops:
  7.2 1.0 copy-start
  7.2 593.9 %reduce-scatter.2.cloned.1.call-start = ((), (), s32[]{:S(2)}) async-start(), calls=%async_computation.1 | async-start | bytes 16908288 | tf_op jit(solution)/shard_map/reduce_scatter | solution.py:19
  19.2 581.9 %copy-start.1 = (f32[64,512]{1,0:T(8,128)S(1)}, f32[64,512]{1,0:T(8,128)}, u32[]{:S(2)}) copy-start(f32[64,512]{1,0:T(8,128)} %param.7) | copy-start | bytes 393220
  19.3 625.2 %copy-start.3 = (f32[64]{0:T(128)S(1)}, f32[64]{0:T(128)}, u32[]{:S(2)}) copy-start(f32[64]{0:T(128)} %param.8) | copy-start | bytes 772
  19.3 897.2 %copy-start.2 = (f32[512]{0:T(512)S(1)}, f32[512]{0:T(512)}, u32[]{:S(2)}) copy-start(f32[512]{0:T(512)} %param.9) | copy-start | bytes 6148
  19.3 624.2 %all-reduce.4.cloned.1.call-start = ((), (), s32[]{:S(2)}) async-start(), calls=%async_computation.2 | async-start | bytes 262144 | tf_op jit(solution)/shard_map/psum | solution.py:27
  601.1 820.8 %all-gather.2.cloned.1.call-start = ((), (), s32[]{:S(2)}) async-start(), calls=%async_computation.3 | async-start | bytes 8454144 | tf_op jit(solution)/shard_map/all_gather | solution.py:50
  644.5 787.1 %copy-start.4 = (f32[64]{0:T(128)}, f32[64]{0:T(128)S(1)}, u32[]{:S(2)}) copy-start(f32[64]{0:T(128)S(1)} %get-tuple-element.20) | copy-start | bytes 772
Sparse Core Ops, SparseCore 0:
  19.4 581.6 reduce-scatter.1
  603.7 39.7 all-reduce.3
  1202.6 219.2 all-gather.1
where the time goes:
time: 1440 us
  waiting for transfers between devices  843 us (59%)
  blocking collectives  551 us (38%)
  matrix products  20.8 us (1%)
  between operations  15.9 us (1%)
    reduce_scatter x1, waiting for transfers between devices, on_device(): lax.psum_scatter(lax.dot_general(columns, cotangent, (((0,), (0,)), ((),...  582 us
    psum x1, blocking collectives, on_device(): update_total = lax.psum(jnp.sum(update * update), 'fsdp')  281 us
    psum x1, blocking collectives, on_device(): lax.psum((col_part, row_part, weight_part), 'fsdp')  271 us
    all_gather x1, waiting for transfers between devices, on_device(): lax.all_gather(half_weight, 'fsdp', axis=0, tiled=True)  219 us
    psum x1, waiting for transfers between devices, on_device(): gradient = lax.psum(partial_grad, 'cuts')  41.6 us
  transfers between devices with their start and end apart: 3, of which 3 were waited for; matrix products, arithmetic and copies ran while one was open for 0% of the time, Pallas kernels for 0%

commit v1 on v0

v1 whole, which is shorter than its diff:
```python
import functools
import math

import jax
import jax.numpy as jnp
from jax import lax
from jax.experimental import pallas as pl
from jax.experimental.pallas import tpu as pltpu
from jax.sharding import Mesh, PartitionSpec as P

decay_rate = 0.9
tiny_square = 1e-30
clip_level = 1.0
weight_floor = 0.001
learn_rate = 0.1

f32 = jnp.float32
bf16 = jnp.bfloat16

AXES = ("cuts", "y1", "y0", "xlo", "z", "core")
SIZES = (2, 2, 2, 2, 8, 2)
Y = ("y1", "y0")
X = ("cuts", "xlo")
ZN = 8
GR = 16


def grad_kernel(pos, tok, tok2, cot, cot2, *outs):
    a_outs, b_outs = outs[:4], outs[4:]
    i, j = pl.program_id(0), pl.program_id(1)
    y1, cuts = pos[1], pos[4]
    dims = (((0,), (0,)), ((), ()))
    g = lax.dot_general(tok[...], cot[...], dims, preferred_element_type=f32)
    g = g + lax.dot_general(tok2[...], cot2[...], dims, preferred_element_type=f32)
    g = g.reshape(ZN, 2, 2, 2, GR, g.shape[-1])
    for rel in range(2):
        for other in range(2):
            a_val = jnp.where(y1 == 0, g[:, rel, other, 0], g[:, 1 - rel, other, 0])
            b_val = jnp.where(cuts == 0, g[:, other, rel, 1], g[:, other, 1 - rel, 1])
            for step in range(2):

                @pl.when(i == step)
                def _():
                    out = a_outs[rel * 2 + step]
                    out[j, other ^ cuts] = a_val.astype(out.dtype)

                @pl.when(j == step)
                def _():
                    out = b_outs[rel * 2 + step]
                    out[i, other ^ y1] = b_val.astype(out.dtype)


def apply_kernel(pos, tok, tok2, *refs):
    a_ins, b_ins, (own, away, half) = refs[:4], refs[4:8], refs[8:]
    i, j = pl.program_id(0), pl.program_id(1)
    y1, cuts = pos[1], pos[4]
    for step in range(2):
        for c in range(2):
            for r5 in range(2):

                @pl.when(i == step)
                def _():
                    r = r5 ^ cuts
                    half[:, c, r5, 0] = jnp.where(
                        y1 == 0, a_ins[c * 2 + step][j, r], a_ins[(1 - c) * 2 + step][j, r]
                    )

                @pl.when(j == step)
                def _():
                    r = c ^ y1
                    half[:, c, r5, 1] = jnp.where(
                        cuts == 0, b_ins[r5 * 2 + step][i, r], b_ins[(1 - r5) * 2 + step][i, r]
                    )

    h = half[...].reshape(-1, half.shape[-1])

    @pl.when((i == 0) & (j == 0))
    def _():
        own[...] = jnp.zeros_like(own)
        away[...] = jnp.zeros_like(away)

    own[...] += jnp.dot(tok[...], h, preferred_element_type=f32)
    away[...] += jnp.dot(tok2[...], h, preferred_element_type=f32)


def half_block(i, j, pos):
    return ((pos[2] ^ i) * 2) + (pos[3] ^ j)


def piece_spec(shape):
    return pl.BlockSpec(shape, lambda i, j, pos: (0,) * len(shape))


def xor_perm(n, k):
    return [(d, d ^ k) for d in range(n)]


SWAP = [(0, 1), (1, 0)]
TURN = [(0, 0), (1, 2), (2, 1), (3, 3)]


def exchange(pieces, axes):
    return [lax.ppermute(pieces[k], axes, xor_perm(4, k)) for k in (1, 2, 3)]


def four_sum(own, got):
    return (own + got[1]) + (got[0] + got[2])


def on_device(tokens, cotangent, weight, row_moment, col_moment):
    tok_rows, width = tokens.shape
    hidden = cotangent.shape[1]
    half_width = width // 2
    step_cols = half_width // 4
    cuts, y1, y0, xlo, _, core = [lax.axis_index(a) for a in AXES]
    pos = jnp.stack([core, y1, y0, xlo, cuts]).astype(jnp.int32)

    away_cols = lax.dynamic_slice_in_dim(tokens, (1 - core) * half_width, half_width, axis=1)
    tokens2 = lax.ppermute(away_cols, "core", SWAP)
    cotangent2 = lax.ppermute(cotangent, "core", SWAP)

    my_weight = lax.dynamic_slice_in_dim(weight, cuts * 32, 32, axis=0)
    my_moment = lax.dynamic_slice_in_dim(row_moment, cuts * 32, 32, axis=0)
    packed = jnp.concatenate(
        [my_weight, jnp.broadcast_to(my_moment[:, None], (32, 128))], axis=1
    )
    packed = lax.ppermute(packed, ("y1", "core"), TURN)
    w32 = packed[:, :hidden]
    moment32 = packed[:, hidden : hidden + 1]

    tok_specs = [
        pl.BlockSpec((tok_rows, step_cols), lambda i, j, pos: (0, pos[0] * 4 + half_block(i, j, pos))),
        pl.BlockSpec((tok_rows, step_cols), lambda i, j, pos: (0, half_block(i, j, pos))),
    ]
    piece = (2, 2, ZN, GR, hidden)
    kept, sent = jax.ShapeDtypeStruct(piece, f32), jax.ShapeDtypeStruct(piece, bf16)
    flops = 2 * 2 * tok_rows * half_width * hidden
    params = pltpu.CompilerParams(vmem_limit_bytes=48 * 2**20)
    cost = pl.CostEstimate(flops=flops, bytes_accessed=12 * 2**20, transcendentals=0)
    parts = pl.pallas_call(
        grad_kernel,
        out_shape=[kept, sent, sent, sent] * 2,
        grid_spec=pltpu.PrefetchScalarGridSpec(
            num_scalar_prefetch=1,
            grid=(2, 2),
            in_specs=tok_specs
            + [pl.BlockSpec((tok_rows, hidden), lambda i, j, pos: (0, 0))] * 2,
            out_specs=[piece_spec(piece)] * 8,
        ),
        compiler_params=params,
        cost_estimate=cost,
    )(pos, tokens, tokens2, cotangent, cotangent2)
    a_parts, b_parts = parts[:4], parts[4:]

    a_got, b_got = exchange(a_parts, Y), exchange(b_parts, X)
    a_sum = a_parts[0] + sum(p.astype(f32) for p in a_got)
    b_sum = b_parts[0] + sum(p.astype(f32) for p in b_got)

    a_parts = [a_sum[k % 2, k // 2] for k in range(4)]
    b_parts = [b_sum[k % 2, k // 2] for k in range(4)]
    a_got = exchange([p.astype(bf16) for p in a_parts], X)
    b_got = exchange([p.astype(bf16) for p in b_parts], Y)
    a_sum = a_parts[0] + sum(p.astype(f32) for p in a_got)
    b_sum = b_parts[0] + sum(p.astype(f32) for p in b_got)

    both = jnp.stack([a_sum, b_sum], axis=1).astype(bf16)
    g32 = jnp.sum(
        lax.all_to_all(both, "z", 0, 0, tiled=True).astype(f32), axis=0
    ).reshape(32, hidden)

    squares = g32 * g32
    rows32 = decay_rate * moment32 + (1.0 - decay_rate) * (
        jnp.mean(squares, axis=1, keepdims=True) + tiny_square
    )
    scaled = squares / rows32
    lane = lax.broadcasted_iota(jnp.int32, (1, hidden), 1)
    scalars = jnp.where(lane == 0, jnp.sum(rows32), 0.0) + jnp.where(
        lane == 1, jnp.sum(w32 * w32), 0.0
    )
    stats = jnp.concatenate(
        [jnp.sum(squares, axis=0, keepdims=True), jnp.sum(scaled, axis=0, keepdims=True), scalars],
        axis=0,
    )
    stats = stats + lax.ppermute(stats, "core", SWAP)
    stats = four_sum(stats, exchange([stats] * 4, Y))
    stats = four_sum(stats, exchange([stats] * 4, X))
    stats = four_sum(stats, [lax.ppermute(stats, "z", xor_perm(8, k)) for k in (1, 2, 3)])
    stats = stats + lax.ppermute(stats, "z", xor_perm(8, 4))
    col_total, scaled_total, row_total, weight_total = stats[0], stats[1], stats[2, 0], stats[2, 1]

    cols_new = decay_rate * col_moment + (1.0 - decay_rate) * (col_total / width + tiny_square)
    mean_row = row_total / width
    update_total = mean_row * jnp.sum(scaled_total / cols_new)
    update_rms = jnp.sqrt(update_total / (width * hidden))
    weight_rms = jnp.sqrt(weight_total / (width * hidden))
    factor = (
        jnp.sqrt(mean_row)
        * jnp.maximum(weight_floor, weight_rms)
        / jnp.maximum(1.0, update_rms / clip_level)
    )
    inv_cols = factor * lax.rsqrt(cols_new)[None, :]
    half32 = (w32 - learn_rate * (g32 * lax.rsqrt(rows32) * inv_cols)).astype(bf16)

    half_z = lax.all_to_all(
        jnp.broadcast_to(half32[None], (ZN, 32, hidden)), "z", 0, 0, tiled=True
    ).reshape(ZN, 2, GR, hidden)
    a_half, b_half = half_z[:, 0], half_z[:, 1]
    a_all = [a_half] + exchange([a_half] * 4, X)
    b_all = [b_half] + exchange([b_half] * 4, Y)
    a_half = jnp.stack([a_all[0], a_all[2], a_all[1], a_all[3]]).reshape(piece)
    b_half = jnp.stack([b_all[0], b_all[2], b_all[1], b_all[3]]).reshape(piece)
    a_all = [a_half] + exchange([a_half] * 4, Y)
    b_all = [b_half] + exchange([b_half] * 4, X)

    result = jax.ShapeDtypeStruct((tok_rows, hidden), f32)
    own, away = pl.pallas_call(
        apply_kernel,
        out_shape=[result, result],
        grid_spec=pltpu.PrefetchScalarGridSpec(
            num_scalar_prefetch=1,
            grid=(2, 2),
            in_specs=tok_specs + [piece_spec(piece)] * 8,
            out_specs=[pl.BlockSpec((tok_rows, hidden), lambda i, j, pos: (0, 0))] * 2,
            scratch_shapes=[pltpu.VMEM((ZN, 2, 2, 2, GR, hidden), bf16)],
        ),
        compiler_params=params,
        cost_estimate=cost,
    )(pos, tokens, tokens2, *a_all, *b_all)
    summed = own + lax.ppermute(away, "core", SWAP)
    preact = (summed * (1.0 / math.sqrt(width))).astype(bf16)

    near = lax.ppermute(g32, ("y1", "core"), TURN)
    far = lax.ppermute(near, "cuts", SWAP)
    g64 = jnp.where(
        cuts == 0, jnp.concatenate([near, far], axis=0), jnp.concatenate([far, near], axis=0)
    )
    rows_new = decay_rate * row_moment + (1.0 - decay_rate) * (
        jnp.mean(g64 * g64, axis=1) + tiny_square
    )
    delta = g64 * lax.rsqrt(rows_new)[:, None] * inv_cols
    new_weight = weight - learn_rate * delta
    return (new_weight, delta, rows_new, cols_new, preact)


def solution(mesh):
    fine = Mesh(mesh.devices.reshape(SIZES), AXES)
    fsdp = ("y1", "y0", "xlo", "z", "core")
    rows = P(("cuts",) + fsdp, None)
    return jax.shard_map(
        on_device,
        mesh=fine,
        in_specs=(rows, rows, P(fsdp, None), P(fsdp), P()),
        out_specs=(P(fsdp, None), P(fsdp, None), P(fsdp), P(), rows),
        check_vma=False,
    )
```

time: 1440 us -> 206 us (0.14)
  waiting for transfers between devices: 843 us -> 77.3 us
  blocking collectives: 551 us -> 14.7 us
  starting transfers between devices: 0.12 us -> 80.1 us
  matrix products: 20.8 us -> 0 us
  Pallas kernels: 0 us -> 15.6 us
    reduce_scatter x1 -> x0, waiting for transfers between devices: 582 us -> none  [on_device(): lax.psum_scatter(lax.dot_general(columns, cotangent, (((0,), (0,)), ((),...]
    psum x2 -> x0, blocking collectives: 551 us -> none  [the longest x1 281 us: on_device(): update_total = lax.psum(jnp.sum(update * update), 'fsdp')]
    all_gather x1 -> x0, waiting for transfers between devices: 219 us -> none  [on_device(): lax.all_gather(half_weight, 'fsdp', axis=0, tiled=True)]
    ppermute x0 -> x41, waiting for transfers between devices: none -> 77.3 us  [the longest x30 53.7 us: exchange(): return [lax.ppermute(pieces[k], axes, xor_perm(4, k)) for k in (1, 2, 3)]]
    ppermute x0 -> x41, starting transfers between devices: none -> 72.1 us  [the longest x30 38.8 us: exchange(): return [lax.ppermute(pieces[k], axes, xor_perm(4, k)) for k in (1, 2, 3)]]
    psum x1 -> x0, waiting for transfers between devices: 41.6 us -> none  [on_device(): gradient = lax.psum(partial_grad, 'cuts')]
    dot_general x2 -> x0, matrix products: 20.8 us -> none  [the longest x1 11.1 us: on_device(): lax.dot_general(columns, cotangent, (((0,), (0,)), ((), ())), preferred_e...]
    pallas_call x0 -> x2, Pallas kernels: none -> 15.6 us  [the longest x1 8.4 us: on_device(): pl.pallas_call(grad_kernel, out_shape=[kept, sent, sent, sent] * 2, grid_...]
  transfers between devices with their start and end apart: 3 -> 42, of which waited for: 3 -> 26; matrix products, arithmetic and copies ran while one was open for 0% -> 2% of each run, Pallas kernels for 0% -> 0%
where the time goes in v1:
time: 206 us; the launch traced here: 203 us
  starting transfers between devices  80.1 us (39%)
  waiting for transfers between devices  77.3 us (38%)
  Pallas kernels  15.6 us (8%)
  blocking collectives  14.7 us (7%)
  other arithmetic  6.97 us (3%)
  local copies, waits for them, and re-layouts  5.78 us (3%)
  between operations  3.05 us (1%)
    ppermute x30, waiting for transfers between devices, exchange(): return [lax.ppermute(pieces[k], axes, xor_perm(4, k)) for k in (1, 2, 3)]  53.7 us
    ppermute x30, starting transfers between devices, exchange(): return [lax.ppermute(pieces[k], axes, xor_perm(4, k)) for k in (1, 2, 3)]  38.8 us
    all_to_all x1, blocking collectives, on_device(): lax.all_to_all(jnp.broadcast_to(half32[None], (ZN, 32, hidden)), 'z', 0,...  14.7 us
    ppermute x1, starting transfers between devices, on_device(): summed = own + lax.ppermute(away, 'core', SWAP)  14.6 us
    pallas_call x1, Pallas kernels, on_device(): pl.pallas_call(grad_kernel, out_shape=[kept, sent, sent, sent] * 2, grid_...  8.4 us
    all_to_all x1, starting transfers between devices, on_device(): lax.all_to_all(both, 'z', 0, 0, tiled=True).astype(f32)  8.01 us
    ppermute x1, starting transfers between devices, on_device(): packed = lax.ppermute(packed, ('y1', 'core'), TURN)  7.26 us
    pallas_call x1, Pallas kernels, on_device(): pl.pallas_call(apply_kernel, out_shape=[result, result], grid_spec=pltpu....  7.19 us
  transfers between devices with their start and end apart: 42, of which 26 were waited for; matrix products, arithmetic and copies ran while one was open for 2% of the time, Pallas kernels for 0%

profile of v1, /device:TPU:33, one launch (start us, length us, event | category | flops | bytes accessed | tf_op | source)
XLA Modules:
  0.0 203.5 jit_solution(9583055937357253488)
XLA Ops:
  0.6 3.9 %constant_dynamic-slice_fusion.1 = bf16[384,4096]{1,0:T(8,128)(2,1)} fusion(bf16[384,8192]{1,0:T(8,128)(2,1)} %tok.3, s32[]{:T(128)S(6)} %select_n.39), kind=kLoop, calls=%fused_computation.54 | loop fusion | bytes 6291460 | tf_op jit(solution)/shard_map/dynamic_slice | solution.py:118
  5.3 5.6 %collective-permute-done.1.cot2 = bf16[384,512]{1,0:T(8,128)(2,1)S(1)} collective-permute-done((bf16[384,512]{1,0:T(8,128)(2,1)S(1)}, bf16[384,512]{1,0:T(8,128)(2,1)S(1)}, u32[]{:S(2)}, u32[]{:S(2)}) %collective-permute-start.1) | collective-permute-done | bytes 393248 | tf_op jit(solution)/shard_map/ppermute | solution.py:120
  11.4 8.4 %shard_map.92 = (f32[2,2,8,16,512]{4,3,2,1,0:T(8,128)S(1)}, bf16[2,2,8,16,512]{4,3,2,1,0:T(8,128)(2,1)S(1)}, bf16[2,2,8,16,512]{4,3,2,1,0:T(8,128)(2,1)S(1)}, bf...) custom-call(s32[5]{0:T(128)S(1)} %stack.59.pos, ...), custom_call_target="tpu_custom_call" | custom-call | flops 3221225472 | bytes 12582912 | tf_op jit(solution)/shard_map/pallas_call | solution.py:140
  21.2 2.6 %collective-permute-start.3 = (bf16[2,2,8,16,512]{4,3,2,1,0:T(8,128)(2,1)S(1)}, bf16[2,2,8,16,512]{4,3,2,1,0:T(8,128)(2,1)S(1)}, u32[]{:S(2)}, u32[]{:S(2)}) collective-permute-start(bf16[2,2,8,16,512]{4,3,2,1,0:T(8,128)(2,1)S(1)} %get-tuple-element.17), channel_id=1, source_target_pairs={{0,64},{32,96},{64,0},{96,32},{1,65},{33,97},{65,1},{97,33},{2,66}... | collective-permute-start | bytes 1572872 | tf_op jit(solution)/shard_map/ppermute | solution.py:103
  23.9 2.5 %collective-permute-start.10 = (bf16[2,2,8,16,512]{4,3,2,1,0:T(8,128)(2,1)S(1)}, bf16[2,2,8,16,512]{4,3,2,1,0:T(8,128)(2,1)S(1)}, u32[]{:S(2)}, u32[]{:S(2)}) collective-permute-start(bf16[2,2,8,16,512]{4,3,2,1,0:T(8,128)(2,1)S(1)} %get-tuple-element.22), channel_id=1, source_target_pairs={{0,144},{16,128},{128,16},{144,0},{1,145},{17,129},{129,17},{145,1... | collective-permute-start | bytes 1572872 | tf_op jit(solution)/shard_map/ppermute | solution.py:103
  26.3 6.7 %collective-permute-done.2 = bf16[2,2,8,16,512]{4,3,2,1,0:T(8,128)(2,1)S(1)} collective-permute-done((bf16[2,2,8,16,512]{4,3,2,1,0:T(8,128)(2,1)S(1)}, bf16[2,2,8,16,512]{4,3,2,1,0:T(8,128)(2,1)S(1)}, u32[]{:S(2)}, u32[]{:S(2)}) %collective-permute-start.2) | collective-permute-done | bytes 524320 | tf_op jit(solution)/shard_map/ppermute | solution.py:103
  33.1 2.7 %collective-permute-start.9 = (bf16[2,2,8,16,512]{4,3,2,1,0:T(8,128)(2,1)S(1)}, bf16[2,2,8,16,512]{4,3,2,1,0:T(8,128)(2,1)S(1)}, u32[]{:S(2)}, u32[]{:S(2)}) collective-permute-start(bf16[2,2,8,16,512]{4,3,2,1,0:T(8,128)(2,1)S(1)} %get-tuple-element.21), channel_id=1, source_target_pairs={{0,128},{16,144},{128,0},{144,16},{1,129},{17,145},{129,1},{145,17... | collective-permute-start | bytes 1572872 | tf_op jit(solution)/shard_map/ppermute | solution.py:103
  35.8 11.0 %collective-permute-done.3 = bf16[2,2,8,16,512]{4,3,2,1,0:T(8,128)(2,1)S(1)} collective-permute-done((bf16[2,2,8,16,512]{4,3,2,1,0:T(8,128)(2,1)S(1)}, bf16[2,2,8,16,512]{4,3,2,1,0:T(8,128)(2,1)S(1)}, u32[]{:S(2)}, u32[]{:S(2)}) %collective-permute-start.3) | collective-permute-done | bytes 524320 | tf_op jit(solution)/shard_map/ppermute | solution.py:103
  50.5 2.4 %collective-permute-start.6 = (bf16[8,16,512]{2,1,0:T(8,128)(2,1)S(1)}, bf16[8,16,512]{2,1,0:T(8,128)(2,1)S(1)}, u32[]{:S(2)}, u32[]{:S(2)}) collective-permute-start(bf16[8,16,512]{2,1,0:T(8,128)(2,1)S(1)} %get-tuple-element.47), channel_id=1, source_target_pairs={{0,128},{16,144},{128,0},{144,16},{1,129},{17,145},{129,1},{145,17... | collective-permute-start | bytes 393224 | tf_op jit(solution)/shard_map/ppermute | solution.py:103
  55.0 2.6 %collective-permute-start.13 = (bf16[8,16,512]{2,1,0:T(8,128)(2,1)S(1)}, bf16[8,16,512]{2,1,0:T(8,128)(2,1)S(1)}, u32[]{:S(2)}, u32[]{:S(2)}) collective-permute-start(bf16[8,16,512]{2,1,0:T(8,128)(2,1)S(1)} %get-tuple-element.49), channel_id=1, source_target_pairs={{0,96},{32,64},{64,32},{96,0},{1,97},{33,65},{65,33},{97,1},{2,98}... | collective-permute-start | bytes 393224 | tf_op jit(solution)/shard_map/ppermute | solution.py:103
  57.6 2.3 %collective-permute-done.7 = bf16[8,16,512]{2,1,0:T(8,128)(2,1)S(1)} collective-permute-done((bf16[8,16,512]{2,1,0:T(8,128)(2,1)S(1)}, bf16[8,16,512]{2,1,0:T(8,128)(2,1)S(1)}, u32[]{:S(2)}, u32[]{:S(2)}) %collective-permute-start.7) | collective-permute-done | bytes 131104 | tf_op jit(solution)/shard_map/ppermute | solution.py:103
  61.6 8.0 %all-to-all-start = ((bf16[8,2,16,512]{3,2,1,0:T(8,128)(2,1)}), bf16[8,2,16,512]{3,2,1,0:T(8,128)(2,1)S(1)}, u32[]{:S(2)}, u32[]{:S(2)}) async-start(bf16[8,2,16,512]{3,2,1,0:T(8,128)(2,1)} %copy.17), calls=%async_computation | async-start | bytes 524288 | tf_op jit(solution)/shard_map/all_to_all | solution.py:168
  69.8 7.3 %collective-permute-start.16 = (f32[32,640]{1,0:T(8,128)S(1)}, f32[32,640]{1,0:T(8,128)S(1)}, u32[]{:S(2)}, u32[]{:S(2)}) collective-permute-start(f32[32,640]{1,0:T(8,128)S(1)} %pad_maximum_fusion.3), channel_id=1, source_target_pairs={{0,0},{1,64},{64,1},{65,65},{2,2},{3,66},{66,3},{67,67},{4,4},{5,6... | collective-permute-start | bytes 245768 | tf_op jit(solution)/shard_map/ppermute | solution.py:127
  77.1 2.2 %collective-permute-done.16 = f32[32,640]{1,0:T(8,128)S(1)} collective-permute-done((f32[32,640]{1,0:T(8,128)S(1)}, f32[32,640]{1,0:T(8,128)S(1)}, u32[]{:S(2)}, u32[]{:S(2)}) %collective-permute-start.16) | collective-permute-done | bytes 81952 | tf_op jit(solution)/shard_map/ppermute | solution.py:127
  82.3 2.6 %collective-permute-start.17 = (f32[3,512]{1,0:T(4,128)S(1)}, f32[3,512]{1,0:T(4,128)S(1)}, u32[]{:S(2)}, u32[]{:S(2)}) collective-permute-start(f32[3,512]{1,0:T(4,128)S(1)} %pad_maximum_fusion.4), channel_id=1, source_target_pairs={{0,1},{1,0},{2,3},{3,2},{4,5},{5,4},{6,7},{7,6},{8,9},{9,8},{10,11... | collective-permute-start | bytes 18440 | tf_op jit(solution)/shard_map/ppermute | solution.py:184
  90.4 2.3 %collective-permute-done.20 = f32[3,512]{1,0:T(4,128)S(1)} collective-permute-done((f32[3,512]{1,0:T(4,128)S(1)}, f32[3,512]{1,0:T(4,128)S(1)}, u32[]{:S(2)}, u32[]{:S(2)}) %collective-permute-start.20) | collective-permute-done | bytes 6176 | tf_op jit(solution)/shard_map/ppermute | solution.py:103
  97.0 2.6 %collective-permute-done.23 = f32[3,512]{1,0:T(4,128)S(1)} collective-permute-done((f32[3,512]{1,0:T(4,128)S(1)}, f32[3,512]{1,0:T(4,128)S(1)}, u32[]{:S(2)}, u32[]{:S(2)}) %collective-permute-start.23) | collective-permute-done | bytes 6176 | tf_op jit(solution)/shard_map/ppermute | solution.py:103
  104.0 3.4 %collective-permute-start.27 = (f32[3,512]{1,0:T(4,128)S(1)}, f32[3,512]{1,0:T(4,128)S(1)}, u32[]{:S(2)}, u32[]{:S(2)}) collective-permute-start(f32[3,512]{1,0:T(4,128)S(1)} %add_add_fusion.2), channel_id=1, source_target_pairs={{0,8},{2,10},{4,12},{6,14},{8,0},{10,2},{12,4},{14,6},{1,9},{3,11}... | collective-permute-start | bytes 18440 | tf_op jit(solution)/shard_map/ppermute | solution.py:188
  107.4 3.1 %collective-permute-done.27 = f32[3,512]{1,0:T(4,128)S(1)} collective-permute-done((f32[3,512]{1,0:T(4,128)S(1)}, f32[3,512]{1,0:T(4,128)S(1)}, u32[]{:S(2)}, u32[]{:S(2)}) %collective-permute-start.27) | collective-permute-done | bytes 6176 | tf_op jit(solution)/shard_map/ppermute | solution.py:188
  114.0 14.7 %all_to_all.10 = bf16[8,32,512]{2,1,0:T(8,128)(2,1)S(1)} all-to-all(bf16[8,32,512]{2,1,0:T(8,128)(2,1)S(1)} %broadcast_in_dim.39), channel_id=1, replica_groups=mesh['cuts'=2,'y1'=2,'y0'=2,'xlo'=2,'z'=8,'core'=2] {'z'}, dimensions={0} | all-to-all | bytes 524288 | tf_op jit(solution)/shard_map/all_to_all | solution.py:204
  129.8 2.2 %collective-permute-start.36 = (bf16[8,16,512]{2,1,0:T(8,128)(2,1)S(1)}, bf16[8,16,512]{2,1,0:T(8,128)(2,1)S(1)}, u32[]{:S(2)}, u32[]{:S(2)}) collective-permute-start(bf16[8,16,512]{2,1,0:T(8,128)(2,1)S(1)} %get-tuple-element.53), channel_id=1, source_target_pairs={{0,96},{32,64},{64,32},{96,0},{1,97},{33,65},{65,33},{97,1},{2,98}... | collective-permute-start | bytes 393224 | tf_op jit(solution)/shard_map/ppermute | solution.py:103
  132.1 2.1 %collective-permute-done.34 = bf16[8,16,512]{2,1,0:T(8,128)(2,1)S(1)} collective-permute-done((bf16[8,16,512]{2,1,0:T(8,128)(2,1)S(1)}, bf16[8,16,512]{2,1,0:T(8,128)(2,1)S(1)}, u32[]{:S(2)}, u32[]{:S(2)}) %collective-permute-start.34) | collective-permute-done | bytes 131104 | tf_op jit(solution)/shard_map/ppermute | solution.py:103
  137.5 2.4 %collective-permute-start.30 = (bf16[8,16,512]{2,1,0:T(8,128)(2,1)S(1)}, bf16[8,16,512]{2,1,0:T(8,128)(2,1)S(1)}, u32[]{:S(2)}, u32[]{:S(2)}) collective-permute-start(bf16[8,16,512]{2,1,0:T(8,128)(2,1)S(1)} %get-tuple-element.52), channel_id=1, source_target_pairs={{0,144},{16,128},{128,16},{144,0},{1,145},{17,129},{129,17},{145,1... | collective-permute-start | bytes 393224 | tf_op jit(solution)/shard_map/ppermute | solution.py:103
  141.0 4.2 %collective-permute-done.28 = bf16[8,16,512]{2,1,0:T(8,128)(2,1)S(1)} collective-permute-done((bf16[8,16,512]{2,1,0:T(8,128)(2,1)S(1)}, bf16[8,16,512]{2,1,0:T(8,128)(2,1)S(1)}, u32[]{:S(2)}, u32[]{:S(2)}) %collective-permute-start.28) | collective-permute-done | bytes 131104 | tf_op jit(solution)/shard_map/ppermute | solution.py:103
  145.2 2.6 %collective-permute-start.39 = (bf16[2,2,8,16,512]{4,3,2,1,0:T(8,128)(2,1)S(1)}, bf16[2,2,8,16,512]{4,3,2,1,0:T(8,128)(2,1)S(1)}, u32[]{:S(2)}, u32[]{:S(2)}) collective-permute-start(bf16[2,2,8,16,512]{4,3,2,1,0:T(8,128)(2,1)S(1)} %bitcast.64), channel_id=1, source_target_pairs={{0,144},{16,128},{128,16},{144,0},{1,145},{17,129},{129,17},{145,1... | collective-permute-start | bytes 1572872 | tf_op jit(solution)/shard_map/ppermute | solution.py:103
  148.0 2.4 %collective-permute-start.32 = (bf16[2,2,8,16,512]{4,3,2,1,0:T(8,128)(2,1)S(1)}, bf16[2,2,8,16,512]{4,3,2,1,0:T(8,128)(2,1)S(1)}, u32[]{:S(2)}, u32[]{:S(2)}) collective-permute-start(bf16[2,2,8,16,512]{4,3,2,1,0:T(8,128)(2,1)S(1)} %bitcast.67), channel_id=1, source_target_pairs={{0,64},{32,96},{64,0},{96,32},{1,65},{33,97},{65,1},{97,33},{2,66}... | collective-permute-start | bytes 1572872 | tf_op jit(solution)/shard_map/ppermute | solution.py:103
  151.9 5.0 %collective-permute-done.38.refs_6_ = bf16[2,2,8,16,512]{4,3,2,1,0:T(8,128)(2,1)S(1)} collective-permute-done((bf16[2,2,8,16,512]{4,3,2,1,0:T(8,128)(2,1)S(1)}, bf16[2,2,8,16,512]{4,3,2,1,0:T(8,128)(2,1)S(1)}, u32[]{:S(2)}, u32[]{:S(2)}) %collective-permute-start.38) | collective-permute-done | bytes 524320 | tf_op jit(solution)/shard_map/ppermute | solution.py:103
  156.8 10.7 %collective-permute-done.39.refs_7_ = bf16[2,2,8,16,512]{4,3,2,1,0:T(8,128)(2,1)S(1)} collective-permute-done((bf16[2,2,8,16,512]{4,3,2,1,0:T(8,128)(2,1)S(1)}, bf16[2,2,8,16,512]{4,3,2,1,0:T(8,128)(2,1)S(1)}, u32[]{:S(2)}, u32[]{:S(2)}) %collective-permute-start.39) | collective-permute-done | bytes 524320 | tf_op jit(solution)/shard_map/ppermute | solution.py:103
  167.6 7.2 %shard_map.93 = (f32[384,512]{1,0:T(8,128)S(1)}, f32[384,512]{1,0:T(8,128)S(1)}) custom-call(s32[5]{0:T(128)S(1)} %stack.59.pos, bf16[384,8192]{1,0:T(8,128)(2,1)} %tok.3, bf16[384,4096]{1,0:T(8,128)(2,1)} %collective-permute-done.tok2, bf16[2,2,8,16,512]{4,3,2,1,0:T(8,128)(2,1)S(1)} %bitcast.69, ...), custom_call_target="tpu_custom_call" | custom-call | flops 3221225472 | bytes 12582912 | tf_op jit(solution)/shard_map/pallas_call | solution.py:216
  174.8 14.6 %collective-permute-start.40 = (f32[384,512]{1,0:T(8,128)S(1)}, f32[384,512]{1,0:T(8,128)S(1)}, u32[]{:S(2)}, u32[]{:S(2)}) collective-permute-start(f32[384,512]{1,0:T(8,128)S(1)} %get-tuple-element.24), channel_id=1, source_target_pairs={{0,1},{1,0},{2,3},{3,2},{4,5},{5,4},{6,7},{7,6},{8,9},{9,8},{10,11... | collective-permute-start | bytes 2359304 | tf_op jit(solution)/shard_map/ppermute | solution.py:229
  191.3 5.2 %collective-permute-done.14 = f32[32,512]{1,0:T(8,128)S(1)} collective-permute-done((f32[32,512]{1,0:T(8,128)S(1)}, f32[32,512]{1,0:T(8,128)S(1)}, u32[]{:S(2)}, u32[]{:S(2)}) %collective-permute-start.14) | collective-permute-done | bytes 65568 | tf_op jit(solution)/shard_map/ppermute | solution.py:232
  196.5 4.6 %collective-permute-done.15 = f32[32,512]{1,0:T(8,128)S(1)} collective-permute-done((f32[32,512]{1,0:T(8,128)S(1)}, f32[32,512]{1,0:T(8,128)S(1)}, u32[]{:S(2)}, u32[]{:S(2)}) %collective-permute-start.15) | collective-permute-done | bytes 65568 | tf_op jit(solution)/shard_map/ppermute | solution.py:233
  (107 shorter events, 40.1 us)
Async XLA Ops:
  4.6 6.9 %collective-permute-start = (bf16[384,4096]{1,0:T(8,128)(2,1)}, bf16[384,4096]{1,0:T(8,128)(2,1)}, u32[]{:S(2)}, u32[]{:S(2)}) collective-permute-start(bf16[384,4096]{1,0:T(8,128)(2,1)} %constant_dynamic-slice_fusion.1), channel_id=1, source_target_pairs={{0,1},{1,0},{2,3},{3,2},{4,5},{5,4},{6,7},{7,6},{8,9},{9,8},{10,11... | collective-permute-start | bytes 9437192 | tf_op jit(solution)/shard_map/ppermute | solution.py:119
  5.3 5.7 %collective-permute-start.1 = (bf16[384,512]{1,0:T(8,128)(2,1)S(1)}, bf16[384,512]{1,0:T(8,128)(2,1)S(1)}, u32[]{:S(2)}, u32[]{:S(2)}) collective-permute-start(bf16[384,512]{1,0:T(8,128)(2,1)S(1)} %copy-done), channel_id=1, source_target_pairs={{0,1},{1,0},{2,3},{3,2},{4,5},{5,4},{6,7},{7,6},{8,9},{9,8},{10,11... | collective-permute-start | bytes 1179656 | tf_op jit(solution)/shard_map/ppermute | solution.py:120
  19.9 13.2 %collective-permute-start.2 = (bf16[2,2,8,16,512]{4,3,2,1,0:T(8,128)(2,1)S(1)}, bf16[2,2,8,16,512]{4,3,2,1,0:T(8,128)(2,1)S(1)}, u32[]{:S(2)}, u32[]{:S(2)}) collective-permute-start(bf16[2,2,8,16,512]{4,3,2,1,0:T(8,128)(2,1)S(1)} %get-tuple-element.16), channel_id=1, source_target_pairs={{0,32},{32,0},{64,96},{96,64},{1,33},{33,1},{65,97},{97,65},{2,34}... | collective-permute-start | bytes 1572872 | tf_op jit(solution)/shard_map/ppermute | solution.py:103
  21.2 25.6 %collective-permute-start.3 = (bf16[2,2,8,16,512]{4,3,2,1,0:T(8,128)(2,1)S(1)}, bf16[2,2,8,16,512]{4,3,2,1,0:T(8,128)(2,1)S(1)}, u32[]{:S(2)}, u32[]{:S(2)}) collective-permute-start(bf16[2,2,8,16,512]{4,3,2,1,0:T(8,128)(2,1)S(1)} %get-tuple-element.17), channel_id=1, source_target_pairs={{0,64},{32,96},{64,0},{96,32},{1,65},{33,97},{65,1},{97,33},{2,66}... | collective-permute-start | bytes 1572872 | tf_op jit(solution)/shard_map/ppermute | solution.py:103
  23.9 24.9 %collective-permute-start.4 = (bf16[2,2,8,16,512]{4,3,2,1,0:T(8,128)(2,1)S(1)}, bf16[2,2,8,16,512]{4,3,2,1,0:T(8,128)(2,1)S(1)}, u32[]{:S(2)}, u32[]{:S(2)}) collective-permute-start(bf16[2,2,8,16,512]{4,3,2,1,0:T(8,128)(2,1)S(1)} %get-tuple-element.18), channel_id=1, source_target_pairs={{0,96},{32,64},{64,32},{96,0},{1,97},{33,65},{65,33},{97,1},{2,98}... | collective-permute-start | bytes 1572872 | tf_op jit(solution)/shard_map/ppermute | solution.py:103
  23.9 29.1 %collective-permute-start.10 = (bf16[2,2,8,16,512]{4,3,2,1,0:T(8,128)(2,1)S(1)}, bf16[2,2,8,16,512]{4,3,2,1,0:T(8,128)(2,1)S(1)}, u32[]{:S(2)}, u32[]{:S(2)}) collective-permute-start(bf16[2,2,8,16,512]{4,3,2,1,0:T(8,128)(2,1)S(1)} %get-tuple-element.22), channel_id=1, source_target_pairs={{0,144},{16,128},{128,16},{144,0},{1,145},{17,129},{129,17},{145,1... | collective-permute-start | bytes 1572872 | tf_op jit(solution)/shard_map/ppermute | solution.py:103
  26.3 26.8 %collective-permute-start.8 = (bf16[2,2,8,16,512]{4,3,2,1,0:T(8,128)(2,1)S(1)}, bf16[2,2,8,16,512]{4,3,2,1,0:T(8,128)(2,1)S(1)}, u32[]{:S(2)}, u32[]{:S(2)}) collective-permute-start(bf16[2,2,8,16,512]{4,3,2,1,0:T(8,128)(2,1)S(1)} %get-tuple-element.20), channel_id=1, source_target_pairs={{0,16},{16,0},{128,144},{144,128},{1,17},{17,1},{129,145},{145,129... | collective-permute-start | bytes 1572872 | tf_op jit(solution)/shard_map/ppermute | solution.py:103
  33.1 20.1 %collective-permute-start.9 = (bf16[2,2,8,16,512]{4,3,2,1,0:T(8,128)(2,1)S(1)}, bf16[2,2,8,16,512]{4,3,2,1,0:T(8,128)(2,1)S(1)}, u32[]{:S(2)}, u32[]{:S(2)}) collective-permute-start(bf16[2,2,8,16,512]{4,3,2,1,0:T(8,128)(2,1)S(1)} %get-tuple-element.21), channel_id=1, source_target_pairs={{0,128},{16,144},{128,0},{144,16},{1,129},{17,145},{129,1},{145,17... | collective-permute-start | bytes 1572872 | tf_op jit(solution)/shard_map/ppermute | solution.py:103
  49.2 5.8 %collective-permute-start.5 = (bf16[8,16,512]{2,1,0:T(8,128)(2,1)S(1)}, bf16[8,16,512]{2,1,0:T(8,128)(2,1)S(1)}, u32[]{:S(2)}, u32[]{:S(2)}) collective-permute-start(bf16[8,16,512]{2,1,0:T(8,128)(2,1)S(1)} %get-tuple-element.45), channel_id=1, source_target_pairs={{0,16},{16,0},{128,144},{144,128},{1,17},{17,1},{129,145},{145,129... | collective-permute-start | bytes 393224 | tf_op jit(solution)/shard_map/ppermute | solution.py:103
  50.5 7.0 %collective-permute-start.6 = (bf16[8,16,512]{2,1,0:T(8,128)(2,1)S(1)}, bf16[8,16,512]{2,1,0:T(8,128)(2,1)S(1)}, u32[]{:S(2)}, u32[]{:S(2)}) collective-permute-start(bf16[8,16,512]{2,1,0:T(8,128)(2,1)S(1)} %get-tuple-element.47), channel_id=1, source_target_pairs={{0,128},{16,144},{128,0},{144,16},{1,129},{17,145},{129,1},{145,17... | collective-permute-start | bytes 393224 | tf_op jit(solution)/shard_map/ppermute | solution.py:103
  53.0 6.9 %collective-permute-start.7 = (bf16[8,16,512]{2,1,0:T(8,128)(2,1)S(1)}, bf16[8,16,512]{2,1,0:T(8,128)(2,1)S(1)}, u32[]{:S(2)}, u32[]{:S(2)}) collective-permute-start(bf16[8,16,512]{2,1,0:T(8,128)(2,1)S(1)} %get-tuple-element.46), channel_id=1, source_target_pairs={{0,144},{16,128},{128,16},{144,0},{1,145},{17,129},{129,17},{145,1... | collective-permute-start | bytes 393224 | tf_op jit(solution)/shard_map/ppermute | solution.py:103
  53.6 6.3 %collective-permute-start.11 = (bf16[8,16,512]{2,1,0:T(8,128)(2,1)S(1)}, bf16[8,16,512]{2,1,0:T(8,128)(2,1)S(1)}, u32[]{:S(2)}, u32[]{:S(2)}) collective-permute-start(bf16[8,16,512]{2,1,0:T(8,128)(2,1)S(1)} %get-tuple-element.48), channel_id=1, source_target_pairs={{0,32},{32,0},{64,96},{96,64},{1,33},{33,1},{65,97},{97,65},{2,34}... | collective-permute-start | bytes 393224 | tf_op jit(solution)/shard_map/ppermute | solution.py:103
  53.7 6.2 %collective-permute-start.12 = (bf16[8,16,512]{2,1,0:T(8,128)(2,1)S(1)}, bf16[8,16,512]{2,1,0:T(8,128)(2,1)S(1)}, u32[]{:S(2)}, u32[]{:S(2)}) collective-permute-start(bf16[8,16,512]{2,1,0:T(8,128)(2,1)S(1)} %get-tuple-element.50), channel_id=1, source_target_pairs={{0,64},{32,96},{64,0},{96,32},{1,65},{33,97},{65,1},{97,33},{2,66}... | collective-permute-start | bytes 393224 | tf_op jit(solution)/shard_map/ppermute | solution.py:103
  55.0 5.8 %collective-permute-start.13 = (bf16[8,16,512]{2,1,0:T(8,128)(2,1)S(1)}, bf16[8,16,512]{2,1,0:T(8,128)(2,1)S(1)}, u32[]{:S(2)}, u32[]{:S(2)}) collective-permute-start(bf16[8,16,512]{2,1,0:T(8,128)(2,1)S(1)} %get-tuple-element.49), channel_id=1, source_target_pairs={{0,96},{32,64},{64,32},{96,0},{1,97},{33,65},{65,33},{97,1},{2,98}... | collective-permute-start | bytes 393224 | tf_op jit(solution)/shard_map/ppermute | solution.py:103
  61.6 18.2 %all-to-all-start = ((bf16[8,2,16,512]{3,2,1,0:T(8,128)(2,1)}), bf16[8,2,16,512]{3,2,1,0:T(8,128)(2,1)S(1)}, u32[]{:S(2)}, u32[]{:S(2)}) async-start(bf16[8,2,16,512]{3,2,1,0:T(8,128)(2,1)} %copy.17), calls=%async_computation | async-start | bytes 524288 | tf_op jit(solution)/shard_map/all_to_all | solution.py:168
  69.8 9.4 %collective-permute-start.16 = (f32[32,640]{1,0:T(8,128)S(1)}, f32[32,640]{1,0:T(8,128)S(1)}, u32[]{:S(2)}, u32[]{:S(2)}) collective-permute-start(f32[32,640]{1,0:T(8,128)S(1)} %pad_maximum_fusion.3), channel_id=1, source_target_pairs={{0,0},{1,64},{64,1},{65,65},{2,2},{3,66},{66,3},{67,67},{4,4},{5,6... | collective-permute-start | bytes 245768 | tf_op jit(solution)/shard_map/ppermute | solution.py:127
  104.0 6.5 %collective-permute-start.27 = (f32[3,512]{1,0:T(4,128)S(1)}, f32[3,512]{1,0:T(4,128)S(1)}, u32[]{:S(2)}, u32[]{:S(2)}) collective-permute-start(f32[3,512]{1,0:T(4,128)S(1)} %add_add_fusion.2), channel_id=1, source_target_pairs={{0,8},{2,10},{4,12},{6,14},{8,0},{10,2},{12,4},{14,6},{1,9},{3,11}... | collective-permute-start | bytes 18440 | tf_op jit(solution)/shard_map/ppermute | solution.py:188
  128.7 5.5 %collective-permute-start.34 = (bf16[8,16,512]{2,1,0:T(8,128)(2,1)S(1)}, bf16[8,16,512]{2,1,0:T(8,128)(2,1)S(1)}, u32[]{:S(2)}, u32[]{:S(2)}) collective-permute-start(bf16[8,16,512]{2,1,0:T(8,128)(2,1)S(1)} %get-tuple-element.53), channel_id=1, source_target_pairs={{0,64},{32,96},{64,0},{96,32},{1,65},{33,97},{65,1},{97,33},{2,66}... | collective-permute-start | bytes 393224 | tf_op jit(solution)/shard_map/ppermute | solution.py:103
  128.8 5.4 %collective-permute-start.35 = (bf16[8,16,512]{2,1,0:T(8,128)(2,1)S(1)}, bf16[8,16,512]{2,1,0:T(8,128)(2,1)S(1)}, u32[]{:S(2)}, u32[]{:S(2)}) collective-permute-start(bf16[8,16,512]{2,1,0:T(8,128)(2,1)S(1)} %get-tuple-element.53), channel_id=1, source_target_pairs={{0,32},{32,0},{64,96},{96,64},{1,33},{33,1},{65,97},{97,65},{2,34}... | collective-permute-start | bytes 393224 | tf_op jit(solution)/shard_map/ppermute | solution.py:103
  129.8 6.0 %collective-permute-start.36 = (bf16[8,16,512]{2,1,0:T(8,128)(2,1)S(1)}, bf16[8,16,512]{2,1,0:T(8,128)(2,1)S(1)}, u32[]{:S(2)}, u32[]{:S(2)}) collective-permute-start(bf16[8,16,512]{2,1,0:T(8,128)(2,1)S(1)} %get-tuple-element.53), channel_id=1, source_target_pairs={{0,96},{32,64},{64,32},{96,0},{1,97},{33,65},{65,33},{97,1},{2,98}... | collective-permute-start | bytes 393224 | tf_op jit(solution)/shard_map/ppermute | solution.py:103
  135.9 14.5 %collective-permute-start.37 = (bf16[2,2,8,16,512]{4,3,2,1,0:T(8,128)(2,1)S(1)}, bf16[2,2,8,16,512]{4,3,2,1,0:T(8,128)(2,1)S(1)}, u32[]{:S(2)}, u32[]{:S(2)}) collective-permute-start(bf16[2,2,8,16,512]{4,3,2,1,0:T(8,128)(2,1)S(1)} %bitcast.62), channel_id=1, source_target_pairs={{0,16},{16,0},{128,144},{144,128},{1,17},{17,1},{129,145},{145,129... | collective-permute-start | bytes 1572872 | tf_op jit(solution)/shard_map/ppermute | solution.py:103
  136.0 9.2 %collective-permute-start.28 = (bf16[8,16,512]{2,1,0:T(8,128)(2,1)S(1)}, bf16[8,16,512]{2,1,0:T(8,128)(2,1)S(1)}, u32[]{:S(2)}, u32[]{:S(2)}) collective-permute-start(bf16[8,16,512]{2,1,0:T(8,128)(2,1)S(1)} %get-tuple-element.52), channel_id=1, source_target_pairs={{0,128},{16,144},{128,0},{144,16},{1,129},{17,145},{129,1},{145,17... | collective-permute-start | bytes 393224 | tf_op jit(solution)/shard_map/ppermute | solution.py:103
  137.2 10.6 %collective-permute-start.29 = (bf16[8,16,512]{2,1,0:T(8,128)(2,1)S(1)}, bf16[8,16,512]{2,1,0:T(8,128)(2,1)S(1)}, u32[]{:S(2)}, u32[]{:S(2)}) collective-permute-start(bf16[8,16,512]{2,1,0:T(8,128)(2,1)S(1)} %get-tuple-element.52), channel_id=1, source_target_pairs={{0,16},{16,0},{128,144},{144,128},{1,17},{17,1},{129,145},{145,129... | collective-permute-start | bytes 393224 | tf_op jit(solution)/shard_map/ppermute | solution.py:103
  137.5 10.4 %collective-permute-start.30 = (bf16[8,16,512]{2,1,0:T(8,128)(2,1)S(1)}, bf16[8,16,512]{2,1,0:T(8,128)(2,1)S(1)}, u32[]{:S(2)}, u32[]{:S(2)}) collective-permute-start(bf16[8,16,512]{2,1,0:T(8,128)(2,1)S(1)} %get-tuple-element.52), channel_id=1, source_target_pairs={{0,144},{16,128},{128,16},{144,0},{1,145},{17,129},{129,17},{145,1... | collective-permute-start | bytes 393224 | tf_op jit(solution)/shard_map/ppermute | solution.py:103
  139.9 17.0 %collective-permute-start.38 = (bf16[2,2,8,16,512]{4,3,2,1,0:T(8,128)(2,1)S(1)}, bf16[2,2,8,16,512]{4,3,2,1,0:T(8,128)(2,1)S(1)}, u32[]{:S(2)}, u32[]{:S(2)}) collective-permute-start(bf16[2,2,8,16,512]{4,3,2,1,0:T(8,128)(2,1)S(1)} %bitcast.63), channel_id=1, source_target_pairs={{0,128},{16,144},{128,0},{144,16},{1,129},{17,145},{129,1},{145,17... | collective-permute-start | bytes 1572872 | tf_op jit(solution)/shard_map/ppermute | solution.py:103
  145.2 22.4 %collective-permute-start.39 = (bf16[2,2,8,16,512]{4,3,2,1,0:T(8,128)(2,1)S(1)}, bf16[2,2,8,16,512]{4,3,2,1,0:T(8,128)(2,1)S(1)}, u32[]{:S(2)}, u32[]{:S(2)}) collective-permute-start(bf16[2,2,8,16,512]{4,3,2,1,0:T(8,128)(2,1)S(1)} %bitcast.64), channel_id=1, source_target_pairs={{0,144},{16,128},{128,16},{144,0},{1,145},{17,129},{129,17},{145,1... | collective-permute-start | bytes 1572872 | tf_op jit(solution)/shard_map/ppermute | solution.py:103
  147.9 19.7 %collective-permute-start.31 = (bf16[2,2,8,16,512]{4,3,2,1,0:T(8,128)(2,1)S(1)}, bf16[2,2,8,16,512]{4,3,2,1,0:T(8,128)(2,1)S(1)}, u32[]{:S(2)}, u32[]{:S(2)}) collective-permute-start(bf16[2,2,8,16,512]{4,3,2,1,0:T(8,128)(2,1)S(1)} %bitcast.66), channel_id=1, source_target_pairs={{0,32},{32,0},{64,96},{96,64},{1,33},{33,1},{65,97},{97,65},{2,34}... | collective-permute-start | bytes 1572872 | tf_op jit(solution)/shard_map/ppermute | solution.py:103
  148.0 19.6 %collective-permute-start.32 = (bf16[2,2,8,16,512]{4,3,2,1,0:T(8,128)(2,1)S(1)}, bf16[2,2,8,16,512]{4,3,2,1,0:T(8,128)(2,1)S(1)}, u32[]{:S(2)}, u32[]{:S(2)}) collective-permute-start(bf16[2,2,8,16,512]{4,3,2,1,0:T(8,128)(2,1)S(1)} %bitcast.67), channel_id=1, source_target_pairs={{0,64},{32,96},{64,0},{96,32},{1,65},{33,97},{65,1},{97,33},{2,66}... | collective-permute-start | bytes 1572872 | tf_op jit(solution)/shard_map/ppermute | solution.py:103
  150.4 17.1 %collective-permute-start.33 = (bf16[2,2,8,16,512]{4,3,2,1,0:T(8,128)(2,1)S(1)}, bf16[2,2,8,16,512]{4,3,2,1,0:T(8,128)(2,1)S(1)}, u32[]{:S(2)}, u32[]{:S(2)}) collective-permute-start(bf16[2,2,8,16,512]{4,3,2,1,0:T(8,128)(2,1)S(1)} %bitcast.68), channel_id=1, source_target_pairs={{0,96},{32,64},{64,32},{96,0},{1,97},{33,65},{65,33},{97,1},{2,98}... | collective-permute-start | bytes 1572872 | tf_op jit(solution)/shard_map/ppermute | solution.py:103
  174.8 27.7 %collective-permute-start.40 = (f32[384,512]{1,0:T(8,128)S(1)}, f32[384,512]{1,0:T(8,128)S(1)}, u32[]{:S(2)}, u32[]{:S(2)}) collective-permute-start(f32[384,512]{1,0:T(8,128)S(1)} %get-tuple-element.24), channel_id=1, source_target_pairs={{0,1},{1,0},{2,3},{3,2},{4,5},{5,4},{6,7},{7,6},{8,9},{9,8},{10,11... | collective-permute-start | bytes 2359304 | tf_op jit(solution)/shard_map/ppermute | solution.py:229
  189.4 7.1 %collective-permute-start.14 = (f32[32,512]{1,0:T(8,128)S(1)}, f32[32,512]{1,0:T(8,128)S(1)}, u32[]{:S(2)}, u32[]{:S(2)}) collective-permute-start(f32[32,512]{1,0:T(8,128)S(1)} %bitcast.71), channel_id=1, source_target_pairs={{0,0},{1,64},{64,1},{65,65},{2,2},{3,66},{66,3},{67,67},{4,4},{5,6... | collective-permute-start | bytes 196616 | tf_op jit(solution)/shard_map/ppermute | solution.py:232
  196.5 4.6 %collective-permute-start.15 = (f32[32,512]{1,0:T(8,128)S(1)}, f32[32,512]{1,0:T(8,128)S(1)}, u32[]{:S(2)}, u32[]{:S(2)}) collective-permute-start(f32[32,512]{1,0:T(8,128)S(1)} %collective-permute-done.14), channel_id=1, source_target_pairs={{0,128},{128,0},{1,129},{129,1},{2,130},{130,2},{3,131},{131,3},{4... | collective-permute-start | bytes 196616 | tf_op jit(solution)/shard_map/ppermute | solution.py:233
  (15 other events, 191.8 us)

commit v2 on v1

v2 whole, which is shorter than its diff:
```python
import functools
import math

import jax
import jax.numpy as jnp
from jax import lax
from jax.experimental import pallas as pl
from jax.experimental.pallas import tpu as pltpu
from jax.sharding import Mesh, PartitionSpec as P

decay_rate = 0.9
tiny_square = 1e-30
clip_level = 1.0
weight_floor = 0.001
learn_rate = 0.1

f32 = jnp.float32
bf16 = jnp.bfloat16

AXES = ("cuts", "y1", "y0", "xlo", "z", "core")
SIZES = (2, 2, 2, 2, 8, 2)
Y = ("y1", "y0")
X = ("cuts", "xlo")
ZN = 8
ZH = 4
GR = 32
SWAP = [(0, 1), (1, 0)]
TURN = [(0, 0), (1, 2), (2, 1), (3, 3)]
FAR_TURN = [(d + 4 * q, e + 4 * (1 - q)) for q in range(2) for d, e in TURN]


def cols_at(part, step):
    def index(g, pos):
        row_bit, x_bit = (step, g) if part == 0 else (g, step)
        return (pos[2] ^ row_bit) * 4 + (pos[3] ^ x_bit) * 2 + part

    return index


def chosen(pos, part):
    return (pos[1], pos[4]) if part == 0 else (pos[4], pos[1])


def copy_kernel(pos, src, dst):
    dst[...] = src[...]


def grad_kernel(part, pos, tok, tok2, cot, cot2, out0, out1):
    pick, inner = chosen(pos, part)
    dims = (((0,), (0,)), ((), ()))
    g = lax.dot_general(tok[...], cot[...], dims, preferred_element_type=f32)
    g = g + lax.dot_general(tok2[...], cot2[...], dims, preferred_element_type=f32)
    g = g.reshape(ZH, 2, 2, GR, g.shape[-1])
    for k in range(2):
        first, second = (g[:, 0, k], g[:, 1, k]) if part == 0 else (g[:, k, 0], g[:, k, 1])
        out0[0, k ^ inner] = jnp.where(pick == 0, first, second).astype(out0.dtype)
        out1[0, k ^ inner] = jnp.where(pick == 0, second, first).astype(out1.dtype)


def apply_kernel(part, n_after, pos, tok, tok2, piece0, piece1, *refs):
    refs = refs[n_after:]
    sums, (own, away, half) = refs[:-3], refs[-3:]
    pick, inner = chosen(pos, part)
    for k in range(2):
        zero, one = piece0[0, k ^ inner], piece1[0, k ^ inner]
        first, second = jnp.where(pick == 0, zero, one), jnp.where(pick == 0, one, zero)
        if part == 0:
            half[:, 0, k], half[:, 1, k] = first, second
        else:
            half[:, k, 0], half[:, k, 1] = first, second
    h = half[...].reshape(-1, half.shape[-1])

    @pl.when(pl.program_id(0) == 0)
    def _():
        for out, begin in zip((own, away), sums or (None, None)):
            out[...] = jnp.zeros_like(out) if begin is None else begin[...]

    own[...] += jnp.dot(tok[...], h, preferred_element_type=f32)
    away[...] += jnp.dot(tok2[...], h, preferred_element_type=f32)


def xor_perm(n, k):
    return [(d, d ^ k) for d in range(n)]


def exchange(pieces, axes):
    return [lax.ppermute(pieces[k], axes, xor_perm(4, k)) for k in (1, 2, 3)]


def four_sum(own, got):
    return (own + got[1]) + (got[0] + got[2])


def on_device(tokens, cotangent, weight, row_moment, col_moment):
    tok_rows, width = tokens.shape
    hidden = cotangent.shape[1]
    seg = width // 16
    cuts, y1, y0, xlo, _, core = [lax.axis_index(a) for a in AXES]
    pos = jnp.stack([core, y1, y0, xlo, cuts]).astype(jnp.int32)
    params = pltpu.CompilerParams(vmem_limit_bytes=32 * 2**20)
    cost = pl.CostEstimate(
        flops=4 * tok_rows * 2 * seg * hidden, bytes_accessed=4 * 2**20, transcendentals=0
    )
    piece = (2, 2, ZH, GR, hidden)
    whole = pl.BlockSpec((tok_rows, hidden), lambda g, pos: (0, 0))
    piece_spec = pl.BlockSpec((1,) + piece[1:], lambda g, pos: (g, 0, 0, 0, 0))

    def tok_specs(part, step):
        index = cols_at(part, step)
        return [
            pl.BlockSpec((tok_rows, seg), lambda g, pos: (0, pos[0] * 8 + index(g, pos))),
            pl.BlockSpec((tok_rows, seg), lambda g, pos: (0, g)),
        ]

    order = [(0, 1), (1, 1), (0, 0), (1, 0)]
    cotangent2 = lax.ppermute(cotangent, "core", SWAP)
    tokens2 = {}
    for part, step in order:
        index = cols_at(part, step)
        away_cols = pl.pallas_call(
            copy_kernel,
            out_shape=jax.ShapeDtypeStruct((tok_rows, 2 * seg), tokens.dtype),
            grid_spec=pltpu.PrefetchScalarGridSpec(
                num_scalar_prefetch=1,
                grid=(2,),
                in_specs=[
                    pl.BlockSpec(
                        (tok_rows, seg),
                        lambda g, pos, index=index: (0, (1 - pos[0]) * 8 + index(g, pos)),
                    )
                ],
                out_specs=pl.BlockSpec((tok_rows, seg), lambda g, pos: (0, g)),
            ),
            compiler_params=params,
        )(pos, tokens)
        tokens2[part, step] = lax.ppermute(away_cols, "core", SWAP)

    my_weight = lax.dynamic_slice_in_dim(weight, cuts * 32, 32, axis=0)
    my_moment = lax.dynamic_slice_in_dim(row_moment, cuts * 32, 32, axis=0)
    packed = jnp.concatenate(
        [my_weight, jnp.broadcast_to(my_moment[:, None], (32, 128))], axis=1
    )
    packed = lax.ppermute(packed, ("y1", "core"), TURN)
    packed = lax.all_gather(packed, "z", axis=0, tiled=True)

    parts = {}
    for part, step in order:
        kept = jax.ShapeDtypeStruct(piece, bf16 if step else f32)
        parts[part, step], parts[part, 2 + step] = pl.pallas_call(
            functools.partial(grad_kernel, part),
            out_shape=[kept, jax.ShapeDtypeStruct(piece, bf16)],
            grid_spec=pltpu.PrefetchScalarGridSpec(
                num_scalar_prefetch=1,
                grid=(2,),
                in_specs=tok_specs(part, step) + [whole] * 2,
                out_specs=[piece_spec] * 2,
            ),
            compiler_params=params,
            cost_estimate=cost,
        )(pos, tokens, tokens2[part, step], cotangent, cotangent2)

    a_parts, b_parts = [[parts[p, k] for k in range(4)] for p in range(2)]
    a_got, b_got = exchange(a_parts, Y), exchange(b_parts, X)
    a_sum = a_parts[0] + sum(p.astype(f32) for p in a_got)
    b_sum = b_parts[0] + sum(p.astype(f32) for p in b_got)

    a_parts = [a_sum[k % 2, k // 2] for k in range(4)]
    b_parts = [b_sum[k % 2, k // 2] for k in range(4)]
    a_got = exchange([p.astype(bf16) for p in a_parts], X)
    b_got = exchange([p.astype(bf16) for p in b_parts], Y)
    a_sum = a_parts[0] + sum(p.astype(f32) for p in a_got)
    b_sum = b_parts[0] + sum(p.astype(f32) for p in b_got)

    both = jnp.concatenate([a_sum, b_sum], axis=0).astype(bf16)
    g32 = jnp.sum(lax.all_to_all(both, "z", 0, 0, tiled=True).astype(f32), axis=0)

    near = lax.ppermute(g32, ("y1", "core"), TURN)
    far = lax.ppermute(g32, ("cuts", "y1", "core"), FAR_TURN)

    gz = lax.all_to_all(
        jnp.broadcast_to(g32.astype(bf16)[None], (ZN, GR, hidden)), "z", 0, 0, tiled=True
    )
    gz, packed, near, far = lax.optimization_barrier((gz, packed, near, far))
    gz = gz.reshape(ZN * GR, hidden).astype(f32)
    wz = packed[:, :hidden]
    moment_z = packed[:, hidden : hidden + 1]

    squares = gz * gz
    rows_z = decay_rate * moment_z + (1.0 - decay_rate) * (
        jnp.mean(squares, axis=1, keepdims=True) + tiny_square
    )
    lane = lax.broadcasted_iota(jnp.int32, (1, hidden), 1)
    scalars = jnp.where(lane == 0, jnp.sum(rows_z), 0.0) + jnp.where(
        lane == 1, jnp.sum(wz * wz), 0.0
    )
    stats = jnp.concatenate(
        [
            jnp.sum(squares, axis=0, keepdims=True),
            jnp.sum(squares / rows_z, axis=0, keepdims=True),
            scalars,
        ],
        axis=0,
    )
    stats = stats + lax.ppermute(stats, "core", SWAP)
    stats = four_sum(stats, exchange([stats] * 4, Y))
    stats = four_sum(stats, exchange([stats] * 4, X))
    col_total, scaled_total, row_total, weight_total = stats[0], stats[1], stats[2, 0], stats[2, 1]

    cols_new = decay_rate * col_moment + (1.0 - decay_rate) * (col_total / width + tiny_square)
    mean_row = row_total / width
    update_total = mean_row * jnp.sum(scaled_total / cols_new)
    update_rms = jnp.sqrt(update_total / (width * hidden))
    weight_rms = jnp.sqrt(weight_total / (width * hidden))
    factor = (
        jnp.sqrt(mean_row)
        * jnp.maximum(weight_floor, weight_rms)
        / jnp.maximum(1.0, update_rms / clip_level)
    )
    inv_cols = factor * lax.rsqrt(cols_new)[None, :]
    half_z = (wz - learn_rate * (gz * lax.rsqrt(rows_z) * inv_cols)).astype(bf16)
    half_z = half_z.reshape(2, ZH, GR, hidden)

    a_half, b_half = half_z[0], half_z[1]
    a_all = [a_half] + exchange([a_half] * 4, X)
    b_all = [b_half] + exchange([b_half] * 4, Y)
    a_half = jnp.stack([a_all[0], a_all[2], a_all[1], a_all[3]]).reshape(piece)
    b_half = jnp.stack([b_all[0], b_all[2], b_all[1], b_all[3]]).reshape(piece)
    a_half, b_half = lax.optimization_barrier((a_half, b_half))
    a_all = [a_half] + exchange([a_half] * 4, Y)
    b_all = [b_half] + exchange([b_half] * 4, X)

    g64 = jnp.where(
        cuts == 0, jnp.concatenate([near, far], axis=0), jnp.concatenate([far, near], axis=0)
    )
    rows_new = decay_rate * row_moment + (1.0 - decay_rate) * (
        jnp.mean(g64 * g64, axis=1) + tiny_square
    )
    delta = g64 * lax.rsqrt(rows_new)[:, None] * inv_cols
    new_weight = weight - learn_rate * delta

    result = jax.ShapeDtypeStruct((tok_rows, hidden), f32)
    sums = []
    for part, step in [(0, 0), (1, 0), (0, 1), (1, 1)]:
        halves = (a_all, b_all)[part]
        after = [new_weight] if (part, step) == (1, 0) else []
        sums = pl.pallas_call(
            functools.partial(apply_kernel, part, len(after)),
            out_shape=[result, result],
            grid_spec=pltpu.PrefetchScalarGridSpec(
                num_scalar_prefetch=1,
                grid=(2,),
                in_specs=tok_specs(part, step)
                + [piece_spec] * 2
                + [pl.BlockSpec(memory_space=pl.ANY)] * len(after)
                + [whole] * len(sums),
                out_specs=[whole] * 2,
                scratch_shapes=[pltpu.VMEM((ZH, 2, 2, GR, hidden), bf16)],
            ),
            compiler_params=params,
            cost_estimate=cost,
        )(pos, tokens, tokens2[part, step], halves[step], halves[2 + step], *after, *sums)
    own, away = sums
    summed = own + lax.ppermute(away, "core", SWAP)
    preact = (summed * (1.0 / math.sqrt(width))).astype(bf16)
    return (new_weight, delta, rows_new, cols_new, preact)


def solution(mesh):
    fine = Mesh(mesh.devices.reshape(SIZES), AXES)
    fsdp = ("y1", "y0", "xlo", "z", "core")
    rows = P(("cuts",) + fsdp, None)
    return jax.shard_map(
        on_device,
        mesh=fine,
        in_specs=(rows, rows, P(fsdp, None), P(fsdp), P()),
        out_specs=(P(fsdp, None), P(fsdp, None), P(fsdp), P(), rows),
        check_vma=False,
    )
```

time: 206 us -> 206 us (level)
  waiting for transfers between devices: 77.3 us -> 42.1 us
  other arithmetic: 6.97 us -> 17.5 us
  blocking collectives: 14.7 us -> 22.9 us
  local copies, waits for them, and re-layouts: 5.78 us -> 12 us
  Pallas kernels: 15.6 us -> 21.4 us
  starting transfers between devices: 80.1 us -> 83.8 us
    all_gather x0 -> x1, blocking collectives: none -> 22.9 us  [on_device(): packed = lax.all_gather(packed, 'z', axis=0, tiled=True)]
    ppermute x30, waiting for transfers between devices: 53.7 us -> 31.7 us  [exchange(): return [lax.ppermute(pieces[k], axes, xor_perm(4, k)) for k in (1, 2, 3)]]
    all_to_all x1 -> x0, blocking collectives: 14.7 us -> none  [on_device(): lax.all_to_all(jnp.broadcast_to(half32[None], (ZN, 32, hidden)), 'z', 0,...]
    ppermute x6 -> x5, waiting for transfers between devices: 9.73 us -> 0.01 us  [the longest x4 0.01 us: on_device(): tokens2[part, step] = lax.ppermute(away_cols, 'core', SWAP)]
    all_to_all x1, waiting for transfers between devices: 0.01 us -> 7.55 us  [on_device(): lax.all_to_all(both, 'z', 0, 0, tiled=True).astype(f32)]
    unnamed x10 -> x20, local copies, waits for them, and re-layouts: 0.02 us -> 6.85 us
    pallas_call x2 -> x12, Pallas kernels: 15.6 us -> 21.4 us  [the longest x4 9.24 us: on_device(): pl.pallas_call(functools.partial(apply_kernel, part, len(after)), out_sha...]
    ppermute x1, waiting for transfers between devices: 5.62 us -> 0.04 us  [on_device(): cotangent2 = lax.ppermute(cotangent, 'core', SWAP)]
  transfers between devices with their start and end apart: 42 -> 42, of which waited for: 26 -> 19; matrix products, arithmetic and copies ran while one was open for 2% -> 4% of each run, Pallas kernels for 0% -> 9%
where the time goes in v2:
time: 206 us; the launch traced here: 203 us
  starting transfers between devices  83.8 us (41%)
  waiting for transfers between devices  42.1 us (20%)
  blocking collectives  22.9 us (11%)
  Pallas kernels  21.4 us (10%)
  other arithmetic  17.5 us (8%)
  local copies, waits for them, and re-layouts  12 us (6%)
  between operations  3.1 us (2%)
    ppermute x30, starting transfers between devices, exchange(): return [lax.ppermute(pieces[k], axes, xor_perm(4, k)) for k in (1, 2, 3)]  42.7 us
    ppermute x30, waiting for transfers between devices, exchange(): return [lax.ppermute(pieces[k], axes, xor_perm(4, k)) for k in (1, 2, 3)]  31.7 us
    all_gather x1, blocking collectives, on_device(): packed = lax.all_gather(packed, 'z', axis=0, tiled=True)  22.9 us
    ppermute x1, starting transfers between devices, on_device(): summed = own + lax.ppermute(away, 'core', SWAP)  10.1 us
    pallas_call x4, Pallas kernels, on_device(): pl.pallas_call(functools.partial(apply_kernel, part, len(after)), out_sha...  9.24 us
    pallas_call x4, Pallas kernels, on_device(): pl.pallas_call(functools.partial(grad_kernel, part), out_shape=[kept, jax...  9 us
    ppermute x1, starting transfers between devices, on_device(): packed = lax.ppermute(packed, ('y1', 'core'), TURN)  8.27 us
    all_to_all x1, starting transfers between devices, on_device(): lax.all_to_all(both, 'z', 0, 0, tiled=True).astype(f32)  8.01 us
  transfers between devices with their start and end apart: 42, of which 19 were waited for; matrix products, arithmetic and copies ran while one was open for 4% of the time, Pallas kernels for 9%

profile of v2, /device:TPU:33, one launch (start us, length us, event | category | flops | bytes accessed | tf_op | source)
XLA Modules:
  0.0 202.8 jit_solution(10813302699306991130)
XLA Ops:
  0.7 2.8 %copy-done = bf16[384,8192]{1,0:T(8,128)(2,1)S(1)} copy-done((bf16[384,8192]{1,0:T(8,128)(2,1)S(1)}, bf16[384,8192]{1,0:T(8,128)(2,1)}, u32[]{:S(2)}) %copy-start) | copy-done | bytes 6291480
  8.8 2.3 %shard_map.93 = (f32[2,2,4,32,512]{4,3,2,1,0:T(8,128)S(1)}, bf16[2,2,4,32,512]{4,3,2,1,0:T(8,128)(2,1)S(1)}) custom-call(s32[5]{0:T(128)S(1)} %stack.47.pos, bf16[384,8192]{1,0:T(8,128)(2,1)S(1)} %copy-done, bf16[384,1024]{1,0:T(8,128)(2,1)S(1)} %collective-permute-done.tok2, bf16[384,512]{1,0:T(8,128)(2,1)S(1)} %copy-done.2, ...), custom_call_target="tpu_custom_call" | custom-call | flops 805306368 | bytes 4194304 | tf_op jit(solution)/shard_map/pallas_call | solution.py:149
  11.1 3.0 %collective-permute-start.4 = (bf16[2,2,4,32,512]{4,3,2,1,0:T(8,128)(2,1)S(1)}, bf16[2,2,4,32,512]{4,3,2,1,0:T(8,128)(2,1)S(1)}, u32[]{:S(2)}, u32[]{:S(2)}) collective-permute-start(bf16[2,2,4,32,512]{4,3,2,1,0:T(8,128)(2,1)S(1)} %get-tuple-element.29), channel_id=1, source_target_pairs={{0,64},{32,96},{64,0},{96,32},{1,65},{33,97},{65,1},{97,33},{2,66}... | collective-permute-start | bytes 1572872 | tf_op jit(solution)/shard_map/ppermute | solution.py:87
  14.1 2.3 %shard_map.95 = (bf16[2,2,4,32,512]{4,3,2,1,0:T(8,128)(2,1)S(1)}, bf16[2,2,4,32,512]{4,3,2,1,0:T(8,128)(2,1)S(1)}) custom-call(s32[5]{0:T(128)S(1)} %stack.47.pos, bf16[384,8192]{1,0:T(8,128)(2,1)S(1)} %copy-done, bf16[384,1024]{1,0:T(8,128)(2,1)S(1)} %collective-permute-done.2.tok2, bf16[384,512]{1,0:T(8,128)(2,1)S(1)} %copy-done.2, ...), custom_call_target="tpu_custom_call" | custom-call | flops 805306368 | bytes 4194304 | tf_op jit(solution)/shard_map/pallas_call | solution.py:149
  17.3 2.2 %shard_map.97 = (f32[2,2,4,32,512]{4,3,2,1,0:T(8,128)S(1)}, bf16[2,2,4,32,512]{4,3,2,1,0:T(8,128)(2,1)S(1)}) custom-call(s32[5]{0:T(128)S(1)} %stack.47.pos, bf16[384,8192]{1,0:T(8,128)(2,1)S(1)} %copy-done, bf16[384,1024]{1,0:T(8,128)(2,1)S(1)} %collective-permute-done.9.tok2, bf16[384,512]{1,0:T(8,128)(2,1)S(1)} %copy-done.2, ...), custom_call_target="tpu_custom_call" | custom-call | flops 805306368 | bytes 4194304 | tf_op jit(solution)/shard_map/pallas_call | solution.py:149
  19.6 2.8 %collective-permute-start.12 = (bf16[2,2,4,32,512]{4,3,2,1,0:T(8,128)(2,1)S(1)}, bf16[2,2,4,32,512]{4,3,2,1,0:T(8,128)(2,1)S(1)}, u32[]{:S(2)}, u32[]{:S(2)}) collective-permute-start(bf16[2,2,4,32,512]{4,3,2,1,0:T(8,128)(2,1)S(1)} %get-tuple-element.33), channel_id=1, source_target_pairs={{0,128},{16,144},{128,0},{144,16},{1,129},{17,145},{129,1},{145,17... | collective-permute-start | bytes 1572872 | tf_op jit(solution)/shard_map/ppermute | solution.py:87
  22.4 2.2 %shard_map.99 = (bf16[2,2,4,32,512]{4,3,2,1,0:T(8,128)(2,1)S(1)}, bf16[2,2,4,32,512]{4,3,2,1,0:T(8,128)(2,1)S(1)}) custom-call(s32[5]{0:T(128)S(1)} %stack.47.pos, bf16[384,8192]{1,0:T(8,128)(2,1)S(1)} %copy-done, bf16[384,1024]{1,0:T(8,128)(2,1)S(1)} %collective-permute-done.10.tok2, bf16[384,512]{1,0:T(8,128)(2,1)S(1)} %copy-done.2, ...), custom_call_target="tpu_custom_call" | custom-call | flops 805306368 | bytes 4194304 | tf_op jit(solution)/shard_map/pallas_call | solution.py:149
  26.0 2.5 %collective-permute-start.13 = (bf16[2,2,4,32,512]{4,3,2,1,0:T(8,128)(2,1)S(1)}, bf16[2,2,4,32,512]{4,3,2,1,0:T(8,128)(2,1)S(1)}, u32[]{:S(2)}, u32[]{:S(2)}) collective-permute-start(bf16[2,2,4,32,512]{4,3,2,1,0:T(8,128)(2,1)S(1)} %get-tuple-element.34), channel_id=1, source_target_pairs={{0,144},{16,128},{128,16},{144,0},{1,145},{17,129},{129,17},{145,1... | collective-permute-start | bytes 1572872 | tf_op jit(solution)/shard_map/ppermute | solution.py:87
  28.5 9.1 %collective-permute-done.3 = bf16[2,2,4,32,512]{4,3,2,1,0:T(8,128)(2,1)S(1)} collective-permute-done((bf16[2,2,4,32,512]{4,3,2,1,0:T(8,128)(2,1)S(1)}, bf16[2,2,4,32,512]{4,3,2,1,0:T(8,128)(2,1)S(1)}, u32[]{:S(2)}, u32[]{:S(2)}) %collective-permute-start.3) | collective-permute-done | bytes 524320 | tf_op jit(solution)/shard_map/ppermute | solution.py:87
  39.4 2.5 %collective-permute-start.7 = (bf16[4,32,512]{2,1,0:T(8,128)(2,1)S(1)}, bf16[4,32,512]{2,1,0:T(8,128)(2,1)S(1)}, u32[]{:S(2)}, u32[]{:S(2)}) collective-permute-start(bf16[4,32,512]{2,1,0:T(8,128)(2,1)S(1)} %get-tuple-element.67), channel_id=1, source_target_pairs={{0,128},{16,144},{128,0},{144,16},{1,129},{17,145},{129,1},{145,17... | collective-permute-start | bytes 393224 | tf_op jit(solution)/shard_map/ppermute | solution.py:87
  42.1 3.1 %collective-permute-done.11 = bf16[2,2,4,32,512]{4,3,2,1,0:T(8,128)(2,1)S(1)} collective-permute-done((bf16[2,2,4,32,512]{4,3,2,1,0:T(8,128)(2,1)S(1)}, bf16[2,2,4,32,512]{4,3,2,1,0:T(8,128)(2,1)S(1)}, u32[]{:S(2)}, u32[]{:S(2)}) %collective-permute-start.11) | collective-permute-done | bytes 524320 | tf_op jit(solution)/shard_map/ppermute | solution.py:87
  47.5 2.6 %collective-permute-start.15 = (bf16[4,32,512]{2,1,0:T(8,128)(2,1)S(1)}, bf16[4,32,512]{2,1,0:T(8,128)(2,1)S(1)}, u32[]{:S(2)}, u32[]{:S(2)}) collective-permute-start(bf16[4,32,512]{2,1,0:T(8,128)(2,1)S(1)} %get-tuple-element.70), channel_id=1, source_target_pairs={{0,64},{32,96},{64,0},{96,32},{1,65},{33,97},{65,1},{97,33},{2,66}... | collective-permute-start | bytes 393224 | tf_op jit(solution)/shard_map/ppermute | solution.py:87
  50.8 3.1 %collective-permute-done.15 = bf16[4,32,512]{2,1,0:T(8,128)(2,1)S(1)} collective-permute-done((bf16[4,32,512]{2,1,0:T(8,128)(2,1)S(1)}, bf16[4,32,512]{2,1,0:T(8,128)(2,1)S(1)}, u32[]{:S(2)}, u32[]{:S(2)}) %collective-permute-start.15) | collective-permute-done | bytes 131104 | tf_op jit(solution)/shard_map/ppermute | solution.py:87
  56.1 8.0 %all-to-all-start = ((bf16[8,32,512]{2,1,0:T(8,128)(2,1)}), bf16[8,32,512]{2,1,0:T(8,128)(2,1)S(1)}, u32[]{:S(2)}, u32[]{:S(2)}) async-start(bf16[8,32,512]{2,1,0:T(8,128)(2,1)} %pad_maximum_fusion.2), calls=%async_computation | async-start | bytes 524288 | tf_op jit(solution)/shard_map/all_to_all | solution.py:175
  64.8 7.5 %all-to-all-done = bf16[8,32,512]{2,1,0:T(8,128)(2,1)S(1)} async-done(((bf16[8,32,512]{2,1,0:T(8,128)(2,1)}), bf16[8,32,512]{2,1,0:T(8,128)(2,1)S(1)}, u32[]{:S(2)}, u32[]{:S(2)}) %all-to-all-start) | async-done | bytes 262176 | tf_op jit(solution)/shard_map/all_to_all | solution.py:175
  73.7 4.4 %all-to-all-start.1 = ((bf16[8,32,512]{2,1,0:T(8,128)(2,1)}), bf16[8,32,512]{2,1,0:T(8,128)(2,1)S(1)}, u32[]{:S(2)}, u32[]{:S(2)}) async-start(bf16[8,32,512]{2,1,0:T(8,128)(2,1)} %broadcast_in_dim.33), calls=%async_computation.1 | async-start | bytes 524288 | tf_op jit(solution)/shard_map/all_to_all | solution.py:180
  79.1 8.3 %collective-permute-start.17 = (f32[32,640]{1,0:T(8,128)S(1)}, f32[32,640]{1,0:T(8,128)S(1)}, u32[]{:S(2)}, u32[]{:S(2)}) collective-permute-start(f32[32,640]{1,0:T(8,128)S(1)} %pad_maximum_fusion.3), channel_id=1, source_target_pairs={{0,0},{1,64},{64,1},{65,65},{2,2},{3,66},{66,3},{67,67},{4,4},{5,6... | collective-permute-start | bytes 245768 | tf_op jit(solution)/shard_map/ppermute | solution.py:143
  89.3 5.1 %collective-permute-start.19 = (f32[32,512]{1,0:T(8,128)}, f32[32,512]{1,0:T(8,128)}, u32[]{:S(2)}, u32[]{:S(2)}) collective-permute-start(f32[32,512]{1,0:T(8,128)} %copy-done.6), channel_id=1, source_target_pairs={{0,128},{1,192},{64,129},{65,193},{128,0},{129,64},{192,1},{193,65... | collective-permute-start | bytes 196616 | tf_op jit(solution)/shard_map/ppermute | solution.py:178
  94.4 22.9 %all_gather.3 = f32[256,640]{1,0:T(8,128)} all-gather(f32[32,640]{1,0:T(8,128)S(1)} %collective-permute-done.17), channel_id=1, replica_groups=mesh['cuts'=2,'y1'=2,'y0'=2,'xlo'=2,'z'=8,'core'=2] {'z'}, dimensions={0}, use_global_device_ids=true | all-gather | bytes 737280 | tf_op jit(solution)/shard_map/all_gather | solution.py:144
  117.9 2.2 %copy.26 = f32[256,640]{0,1:T(8,128)} copy(f32[256,640]{1,0:T(8,128)} %all_gather.3) | data formatting | bytes 1310720 | tf_op jit(solution)/shard_map/optimization_barrier | solution.py:183
  128.7 4.1 %collective-permute-start.21 = (f32[3,512]{1,0:T(4,128)S(1)}, f32[3,512]{1,0:T(4,128)S(1)}, u32[]{:S(2)}, u32[]{:S(2)}) collective-permute-start(f32[3,512]{1,0:T(4,128)S(1)} %fusion.12), channel_id=1, source_target_pairs={{0,64},{32,96},{64,0},{96,32},{1,65},{33,97},{65,1},{97,33},{2,66}... | collective-permute-start | bytes 18440 | tf_op jit(solution)/shard_map/ppermute | solution.py:87
  135.9 2.6 %collective-permute-done.23 = f32[3,512]{1,0:T(4,128)S(1)} collective-permute-done((f32[3,512]{1,0:T(4,128)S(1)}, f32[3,512]{1,0:T(4,128)S(1)}, u32[]{:S(2)}, u32[]{:S(2)}) %collective-permute-start.23) | collective-permute-done | bytes 6176 | tf_op jit(solution)/shard_map/ppermute | solution.py:87
  139.4 2.5 %collective-permute-start.26 = (f32[3,512]{1,0:T(4,128)S(1)}, f32[3,512]{1,0:T(4,128)S(1)}, u32[]{:S(2)}, u32[]{:S(2)}) collective-permute-start(f32[3,512]{1,0:T(4,128)S(1)} %add_add_fusion.3), channel_id=1, source_target_pairs={{0,144},{16,128},{128,16},{144,0},{1,145},{17,129},{129,17},{145,1... | collective-permute-start | bytes 18440 | tf_op jit(solution)/shard_map/ppermute | solution.py:87
  149.1 2.7 %collective-permute-start.32 = (bf16[4,32,512]{2,1,0:T(8,128)(2,1)S(1)}, bf16[4,32,512]{2,1,0:T(8,128)(2,1)S(1)}, u32[]{:S(2)}, u32[]{:S(2)}) collective-permute-start(bf16[4,32,512]{2,1,0:T(8,128)(2,1)S(1)} %bitcast.69), channel_id=1, source_target_pairs={{0,96},{32,64},{64,32},{96,0},{1,97},{33,65},{65,33},{97,1},{2,98}... | collective-permute-start | bytes 393224 | tf_op jit(solution)/shard_map/ppermute | solution.py:87
  162.6 2.7 %collective-permute-start.36 = (bf16[2,2,4,32,512]{4,3,2,1,0:T(8,128)(2,1)}, bf16[2,2,4,32,512]{4,3,2,1,0:T(8,128)(2,1)S(1)}, u32[]{:S(2)}, u32[]{:S(2)}) collective-permute-start(bf16[2,2,4,32,512]{4,3,2,1,0:T(8,128)(2,1)} %bitcast.26.piece0), channel_id=1, source_target_pairs={{0,96},{32,64},{64,32},{96,0},{1,97},{33,65},{65,33},{97,1},{2,98}... | collective-permute-start | bytes 1572872 | tf_op jit(solution)/shard_map/ppermute | solution.py:87
  167.7 3.0 %collective-permute-done.38.piece1 = bf16[2,2,4,32,512]{4,3,2,1,0:T(8,128)(2,1)} collective-permute-done((bf16[2,2,4,32,512]{4,3,2,1,0:T(8,128)(2,1)}, bf16[2,2,4,32,512]{4,3,2,1,0:T(8,128)(2,1)}, u32[]{:S(2)}, u32[]{:S(2)}) %collective-permute-start.38) | collective-permute-done | bytes 524320 | tf_op jit(solution)/shard_map/ppermute | solution.py:87
  175.5 2.8 %copy-done.1 = bf16[384,8192]{1,0:T(8,128)(2,1)S(1)} copy-done((bf16[384,8192]{1,0:T(8,128)(2,1)S(1)}, bf16[384,8192]{1,0:T(8,128)(2,1)}, u32[]{:S(2)}) %copy-start.1) | copy-done | bytes 6291480
  178.3 3.0 %shard_map.100 = (f32[384,512]{1,0:T(8,128)S(1)}, f32[384,512]{1,0:T(8,128)S(1)}) custom-call(s32[5]{0:T(128)S(1)} %stack.47.pos, bf16[384,8192]{1,0:T(8,128)(2,1)S(1)} %copy-done.1, bf16[384,1024]{1,0:T(8,128)(2,1)S(1)} %collective-permute-done.tok2, bf16[2,2,4,32,512]{4,3,2,1,0:T(8,128)(2,1)} %bitcast.26.piece0, ...), custom_call_target="tpu_custom_call" | custom-call | flops 805306368 | bytes 4194304 | tf_op jit(solution)/shard_map/pallas_call | solution.py:246
  181.3 2.1 %shard_map.101 = (f32[384,512]{1,0:T(8,128)S(1)}, f32[384,512]{1,0:T(8,128)S(1)}) custom-call(s32[5]{0:T(128)S(1)} %stack.47.pos, bf16[384,8192]{1,0:T(8,128)(2,1)S(1)} %copy-done.1, bf16[384,1024]{1,0:T(8,128)(2,1)S(1)} %collective-permute-done.9.tok2, bf16[2,2,4,32,512]{4,3,2,1,0:T(8,128)(2,1)S(1)} %bitcast.62, ...), custom_call_target="tpu_custom_call" | custom-call | flops 805306368 | bytes 4194304 | tf_op jit(solution)/shard_map/pallas_call | solution.py:246
  183.5 2.2 %collective-permute-done.36.piece1 = bf16[2,2,4,32,512]{4,3,2,1,0:T(8,128)(2,1)S(1)} collective-permute-done((bf16[2,2,4,32,512]{4,3,2,1,0:T(8,128)(2,1)}, bf16[2,2,4,32,512]{4,3,2,1,0:T(8,128)(2,1)S(1)}, u32[]{:S(2)}, u32[]{:S(2)}) %collective-permute-start.36) | collective-permute-done | bytes 524320 | tf_op jit(solution)/shard_map/ppermute | solution.py:87
  187.7 2.1 %shard_map.103 = (f32[384,512]{1,0:T(8,128)S(1)}, f32[384,512]{1,0:T(8,128)S(1)}) custom-call(s32[5]{0:T(128)S(1)} %stack.47.pos, bf16[384,8192]{1,0:T(8,128)(2,1)S(1)} %copy-done.1, bf16[384,1024]{1,0:T(8,128)(2,1)S(1)} %collective-permute-done.10.tok2, bf16[2,2,4,32,512]{4,3,2,1,0:T(8,128)(2,1)S(1)} %collective-permute-done.33.piece0, ...), custom_call_target="tpu_custom_call" | custom-call | flops 805306368 | bytes 4194304 | tf_op jit(solution)/shard_map/pallas_call | solution.py:246
  189.8 10.1 %collective-permute-start.39 = (f32[384,512]{1,0:T(8,128)S(1)}, f32[384,512]{1,0:T(8,128)S(1)}, u32[]{:S(2)}, u32[]{:S(2)}) collective-permute-start(f32[384,512]{1,0:T(8,128)S(1)} %get-tuple-element.48), channel_id=1, source_target_pairs={{0,1},{1,0},{2,3},{3,2},{4,5},{5,4},{6,7},{7,6},{8,9},{9,8},{10,11... | collective-permute-start | bytes 2359304 | tf_op jit(solution)/shard_map/ppermute | solution.py:263
  (127 shorter events, 61.0 us)
Async XLA Ops:
  5.9 8.2 %collective-permute-start.2 = (bf16[384,1024]{1,0:T(8,128)(2,1)S(1)}, bf16[384,1024]{1,0:T(8,128)(2,1)S(1)}, u32[]{:S(2)}, u32[]{:S(2)}) collective-permute-start(bf16[384,1024]{1,0:T(8,128)(2,1)S(1)} %shard_map.94), channel_id=1, source_target_pairs={{0,1},{1,0},{2,3},{3,2},{4,5},{5,4},{6,7},{7,6},{8,9},{9,8},{10,11... | collective-permute-start | bytes 2359304 | tf_op jit(solution)/shard_map/ppermute | solution.py:136
  7.3 10.0 %collective-permute-start.9 = (bf16[384,1024]{1,0:T(8,128)(2,1)S(1)}, bf16[384,1024]{1,0:T(8,128)(2,1)S(1)}, u32[]{:S(2)}, u32[]{:S(2)}) collective-permute-start(bf16[384,1024]{1,0:T(8,128)(2,1)S(1)} %shard_map.96), channel_id=1, source_target_pairs={{0,1},{1,0},{2,3},{3,2},{4,5},{5,4},{6,7},{7,6},{8,9},{9,8},{10,11... | collective-permute-start | bytes 2359304 | tf_op jit(solution)/shard_map/ppermute | solution.py:136
  8.3 14.1 %collective-permute-start.10 = (bf16[384,1024]{1,0:T(8,128)(2,1)S(1)}, bf16[384,1024]{1,0:T(8,128)(2,1)S(1)}, u32[]{:S(2)}, u32[]{:S(2)}) collective-permute-start(bf16[384,1024]{1,0:T(8,128)(2,1)S(1)} %shard_map.98), channel_id=1, source_target_pairs={{0,1},{1,0},{2,3},{3,2},{4,5},{5,4},{6,7},{7,6},{8,9},{9,8},{10,11... | collective-permute-start | bytes 2359304 | tf_op jit(solution)/shard_map/ppermute | solution.py:136
  11.1 14.9 %collective-permute-start.4 = (bf16[2,2,4,32,512]{4,3,2,1,0:T(8,128)(2,1)S(1)}, bf16[2,2,4,32,512]{4,3,2,1,0:T(8,128)(2,1)S(1)}, u32[]{:S(2)}, u32[]{:S(2)}) collective-permute-start(bf16[2,2,4,32,512]{4,3,2,1,0:T(8,128)(2,1)S(1)} %get-tuple-element.29), channel_id=1, source_target_pairs={{0,64},{32,96},{64,0},{96,32},{1,65},{33,97},{65,1},{97,33},{2,66}... | collective-permute-start | bytes 1572872 | tf_op jit(solution)/shard_map/ppermute | solution.py:87
  16.4 21.2 %collective-permute-start.3 = (bf16[2,2,4,32,512]{4,3,2,1,0:T(8,128)(2,1)S(1)}, bf16[2,2,4,32,512]{4,3,2,1,0:T(8,128)(2,1)S(1)}, u32[]{:S(2)}, u32[]{:S(2)}) collective-permute-start(bf16[2,2,4,32,512]{4,3,2,1,0:T(8,128)(2,1)S(1)} %get-tuple-element.28), channel_id=1, source_target_pairs={{0,32},{32,0},{64,96},{96,64},{1,33},{33,1},{65,97},{97,65},{2,34}... | collective-permute-start | bytes 1572872 | tf_op jit(solution)/shard_map/ppermute | solution.py:87
  16.8 20.9 %collective-permute-start.5 = (bf16[2,2,4,32,512]{4,3,2,1,0:T(8,128)(2,1)S(1)}, bf16[2,2,4,32,512]{4,3,2,1,0:T(8,128)(2,1)S(1)}, u32[]{:S(2)}, u32[]{:S(2)}) collective-permute-start(bf16[2,2,4,32,512]{4,3,2,1,0:T(8,128)(2,1)S(1)} %get-tuple-element.30), channel_id=1, source_target_pairs={{0,96},{32,64},{64,32},{96,0},{1,97},{33,65},{65,33},{97,1},{2,98}... | collective-permute-start | bytes 1572872 | tf_op jit(solution)/shard_map/ppermute | solution.py:87
  19.6 22.3 %collective-permute-start.12 = (bf16[2,2,4,32,512]{4,3,2,1,0:T(8,128)(2,1)S(1)}, bf16[2,2,4,32,512]{4,3,2,1,0:T(8,128)(2,1)S(1)}, u32[]{:S(2)}, u32[]{:S(2)}) collective-permute-start(bf16[2,2,4,32,512]{4,3,2,1,0:T(8,128)(2,1)S(1)} %get-tuple-element.33), channel_id=1, source_target_pairs={{0,128},{16,144},{128,0},{144,16},{1,129},{17,145},{129,1},{145,17... | collective-permute-start | bytes 1572872 | tf_op jit(solution)/shard_map/ppermute | solution.py:87
  24.7 20.5 %collective-permute-start.11 = (bf16[2,2,4,32,512]{4,3,2,1,0:T(8,128)(2,1)S(1)}, bf16[2,2,4,32,512]{4,3,2,1,0:T(8,128)(2,1)S(1)}, u32[]{:S(2)}, u32[]{:S(2)}) collective-permute-start(bf16[2,2,4,32,512]{4,3,2,1,0:T(8,128)(2,1)S(1)} %get-tuple-element.32), channel_id=1, source_target_pairs={{0,16},{16,0},{128,144},{144,128},{1,17},{17,1},{129,145},{145,129... | collective-permute-start | bytes 1572872 | tf_op jit(solution)/shard_map/ppermute | solution.py:87
  26.0 20.2 %collective-permute-start.13 = (bf16[2,2,4,32,512]{4,3,2,1,0:T(8,128)(2,1)S(1)}, bf16[2,2,4,32,512]{4,3,2,1,0:T(8,128)(2,1)S(1)}, u32[]{:S(2)}, u32[]{:S(2)}) collective-permute-start(bf16[2,2,4,32,512]{4,3,2,1,0:T(8,128)(2,1)S(1)} %get-tuple-element.34), channel_id=1, source_target_pairs={{0,144},{16,128},{128,16},{144,0},{1,145},{17,129},{129,17},{145,1... | collective-permute-start | bytes 1572872 | tf_op jit(solution)/shard_map/ppermute | solution.py:87
  38.1 12.0 %collective-permute-start.6 = (bf16[4,32,512]{2,1,0:T(8,128)(2,1)S(1)}, bf16[4,32,512]{2,1,0:T(8,128)(2,1)S(1)}, u32[]{:S(2)}, u32[]{:S(2)}) collective-permute-start(bf16[4,32,512]{2,1,0:T(8,128)(2,1)S(1)} %get-tuple-element.65), channel_id=1, source_target_pairs={{0,16},{16,0},{128,144},{144,128},{1,17},{17,1},{129,145},{145,129... | collective-permute-start | bytes 393224 | tf_op jit(solution)/shard_map/ppermute | solution.py:87
  39.4 11.3 %collective-permute-start.7 = (bf16[4,32,512]{2,1,0:T(8,128)(2,1)S(1)}, bf16[4,32,512]{2,1,0:T(8,128)(2,1)S(1)}, u32[]{:S(2)}, u32[]{:S(2)}) collective-permute-start(bf16[4,32,512]{2,1,0:T(8,128)(2,1)S(1)} %get-tuple-element.67), channel_id=1, source_target_pairs={{0,128},{16,144},{128,0},{144,16},{1,129},{17,145},{129,1},{145,17... | collective-permute-start | bytes 393224 | tf_op jit(solution)/shard_map/ppermute | solution.py:87
  41.9 8.8 %collective-permute-start.8 = (bf16[4,32,512]{2,1,0:T(8,128)(2,1)S(1)}, bf16[4,32,512]{2,1,0:T(8,128)(2,1)S(1)}, u32[]{:S(2)}, u32[]{:S(2)}) collective-permute-start(bf16[4,32,512]{2,1,0:T(8,128)(2,1)S(1)} %get-tuple-element.66), channel_id=1, source_target_pairs={{0,144},{16,128},{128,16},{144,0},{1,145},{17,129},{129,17},{145,1... | collective-permute-start | bytes 393224 | tf_op jit(solution)/shard_map/ppermute | solution.py:87
  47.5 6.4 %collective-permute-start.15 = (bf16[4,32,512]{2,1,0:T(8,128)(2,1)S(1)}, bf16[4,32,512]{2,1,0:T(8,128)(2,1)S(1)}, u32[]{:S(2)}, u32[]{:S(2)}) collective-permute-start(bf16[4,32,512]{2,1,0:T(8,128)(2,1)S(1)} %get-tuple-element.70), channel_id=1, source_target_pairs={{0,64},{32,96},{64,0},{96,32},{1,65},{33,97},{65,1},{97,33},{2,66}... | collective-permute-start | bytes 393224 | tf_op jit(solution)/shard_map/ppermute | solution.py:87
  50.1 5.2 %collective-permute-start.16 = (bf16[4,32,512]{2,1,0:T(8,128)(2,1)S(1)}, bf16[4,32,512]{2,1,0:T(8,128)(2,1)S(1)}, u32[]{:S(2)}, u32[]{:S(2)}) collective-permute-start(bf16[4,32,512]{2,1,0:T(8,128)(2,1)S(1)} %get-tuple-element.69), channel_id=1, source_target_pairs={{0,96},{32,64},{64,32},{96,0},{1,97},{33,65},{65,33},{97,1},{2,98}... | collective-permute-start | bytes 393224 | tf_op jit(solution)/shard_map/ppermute | solution.py:87
  56.1 16.3 %all-to-all-start = ((bf16[8,32,512]{2,1,0:T(8,128)(2,1)}), bf16[8,32,512]{2,1,0:T(8,128)(2,1)S(1)}, u32[]{:S(2)}, u32[]{:S(2)}) async-start(bf16[8,32,512]{2,1,0:T(8,128)(2,1)} %pad_maximum_fusion.2), calls=%async_computation | async-start | bytes 524288 | tf_op jit(solution)/shard_map/all_to_all | solution.py:175
  73.7 44.2 %all-to-all-start.1 = ((bf16[8,32,512]{2,1,0:T(8,128)(2,1)}), bf16[8,32,512]{2,1,0:T(8,128)(2,1)S(1)}, u32[]{:S(2)}, u32[]{:S(2)}) async-start(bf16[8,32,512]{2,1,0:T(8,128)(2,1)} %broadcast_in_dim.33), calls=%async_computation.1 | async-start | bytes 524288 | tf_op jit(solution)/shard_map/all_to_all | solution.py:180
  79.1 15.3 %collective-permute-start.17 = (f32[32,640]{1,0:T(8,128)S(1)}, f32[32,640]{1,0:T(8,128)S(1)}, u32[]{:S(2)}, u32[]{:S(2)}) collective-permute-start(f32[32,640]{1,0:T(8,128)S(1)} %pad_maximum_fusion.3), channel_id=1, source_target_pairs={{0,0},{1,64},{64,1},{65,65},{2,2},{3,66},{66,3},{67,67},{4,4},{5,6... | collective-permute-start | bytes 245768 | tf_op jit(solution)/shard_map/ppermute | solution.py:143
  87.3 29.9 %collective-permute-start.18 = (f32[32,512]{1,0:T(8,128)}, f32[32,512]{1,0:T(8,128)S(1)}, u32[]{:S(2)}, u32[]{:S(2)}) collective-permute-start(f32[32,512]{1,0:T(8,128)} %copy-done.6), channel_id=1, source_target_pairs={{0,0},{1,64},{64,1},{65,65},{2,2},{3,66},{66,3},{67,67},{4,4},{5,6... | collective-permute-start | bytes 196616 | tf_op jit(solution)/shard_map/ppermute | solution.py:177
  89.3 28.6 %collective-permute-start.19 = (f32[32,512]{1,0:T(8,128)}, f32[32,512]{1,0:T(8,128)}, u32[]{:S(2)}, u32[]{:S(2)}) collective-permute-start(f32[32,512]{1,0:T(8,128)} %copy-done.6), channel_id=1, source_target_pairs={{0,128},{1,192},{64,129},{65,193},{128,0},{129,64},{192,1},{193,65... | collective-permute-start | bytes 196616 | tf_op jit(solution)/shard_map/ppermute | solution.py:178
  128.7 6.1 %collective-permute-start.21 = (f32[3,512]{1,0:T(4,128)S(1)}, f32[3,512]{1,0:T(4,128)S(1)}, u32[]{:S(2)}, u32[]{:S(2)}) collective-permute-start(f32[3,512]{1,0:T(4,128)S(1)} %fusion.12), channel_id=1, source_target_pairs={{0,64},{32,96},{64,0},{96,32},{1,65},{33,97},{65,1},{97,33},{2,66}... | collective-permute-start | bytes 18440 | tf_op jit(solution)/shard_map/ppermute | solution.py:87
  148.4 6.4 %collective-permute-start.30 = (bf16[4,32,512]{2,1,0:T(8,128)(2,1)S(1)}, bf16[4,32,512]{2,1,0:T(8,128)(2,1)S(1)}, u32[]{:S(2)}, u32[]{:S(2)}) collective-permute-start(bf16[4,32,512]{2,1,0:T(8,128)(2,1)S(1)} %bitcast.67), channel_id=1, source_target_pairs={{0,64},{32,96},{64,0},{96,32},{1,65},{33,97},{65,1},{97,33},{2,66}... | collective-permute-start | bytes 393224 | tf_op jit(solution)/shard_map/ppermute | solution.py:87
  148.5 7.9 %collective-permute-start.31 = (bf16[4,32,512]{2,1,0:T(8,128)(2,1)S(1)}, bf16[4,32,512]{2,1,0:T(8,128)(2,1)S(1)}, u32[]{:S(2)}, u32[]{:S(2)}) collective-permute-start(bf16[4,32,512]{2,1,0:T(8,128)(2,1)S(1)} %bitcast.68), channel_id=1, source_target_pairs={{0,32},{32,0},{64,96},{96,64},{1,33},{33,1},{65,97},{97,65},{2,34}... | collective-permute-start | bytes 393224 | tf_op jit(solution)/shard_map/ppermute | solution.py:87
  149.1 7.4 %collective-permute-start.32 = (bf16[4,32,512]{2,1,0:T(8,128)(2,1)S(1)}, bf16[4,32,512]{2,1,0:T(8,128)(2,1)S(1)}, u32[]{:S(2)}, u32[]{:S(2)}) collective-permute-start(bf16[4,32,512]{2,1,0:T(8,128)(2,1)S(1)} %bitcast.69), channel_id=1, source_target_pairs={{0,96},{32,64},{64,32},{96,0},{1,97},{33,65},{65,33},{97,1},{2,98}... | collective-permute-start | bytes 393224 | tf_op jit(solution)/shard_map/ppermute | solution.py:87
  151.8 5.6 %collective-permute-start.27 = (bf16[4,32,512]{2,1,0:T(8,128)(2,1)S(1)}, bf16[4,32,512]{2,1,0:T(8,128)(2,1)S(1)}, u32[]{:S(2)}, u32[]{:S(2)}) collective-permute-start(bf16[4,32,512]{2,1,0:T(8,128)(2,1)S(1)} %bitcast.63), channel_id=1, source_target_pairs={{0,128},{16,144},{128,0},{144,16},{1,129},{17,145},{129,1},{145,17... | collective-permute-start | bytes 393224 | tf_op jit(solution)/shard_map/ppermute | solution.py:87
  153.7 5.2 %collective-permute-start.28 = (bf16[4,32,512]{2,1,0:T(8,128)(2,1)S(1)}, bf16[4,32,512]{2,1,0:T(8,128)(2,1)S(1)}, u32[]{:S(2)}, u32[]{:S(2)}) collective-permute-start(bf16[4,32,512]{2,1,0:T(8,128)(2,1)S(1)} %bitcast.64), channel_id=1, source_target_pairs={{0,16},{16,0},{128,144},{144,128},{1,17},{17,1},{129,145},{145,129... | collective-permute-start | bytes 393224 | tf_op jit(solution)/shard_map/ppermute | solution.py:87
  160.8 10.0 %collective-permute-start.38 = (bf16[2,2,4,32,512]{4,3,2,1,0:T(8,128)(2,1)}, bf16[2,2,4,32,512]{4,3,2,1,0:T(8,128)(2,1)}, u32[]{:S(2)}, u32[]{:S(2)}) collective-permute-start(bf16[2,2,4,32,512]{4,3,2,1,0:T(8,128)(2,1)} %bitcast.26.piece0), channel_id=1, source_target_pairs={{0,64},{32,96},{64,0},{96,32},{1,65},{33,97},{65,1},{97,33},{2,66}... | collective-permute-start | bytes 1572872 | tf_op jit(solution)/shard_map/ppermute | solution.py:87
  162.0 21.4 %collective-permute-start.35 = (bf16[2,2,4,32,512]{4,3,2,1,0:T(8,128)(2,1)}, bf16[2,2,4,32,512]{4,3,2,1,0:T(8,128)(2,1)S(1)}, u32[]{:S(2)}, u32[]{:S(2)}) collective-permute-start(bf16[2,2,4,32,512]{4,3,2,1,0:T(8,128)(2,1)} %bitcast.26.piece0), channel_id=1, source_target_pairs={{0,32},{32,0},{64,96},{96,64},{1,33},{33,1},{65,97},{97,65},{2,34}... | collective-permute-start | bytes 1572872 | tf_op jit(solution)/shard_map/ppermute | solution.py:87
  162.6 23.0 %collective-permute-start.36 = (bf16[2,2,4,32,512]{4,3,2,1,0:T(8,128)(2,1)}, bf16[2,2,4,32,512]{4,3,2,1,0:T(8,128)(2,1)S(1)}, u32[]{:S(2)}, u32[]{:S(2)}) collective-permute-start(bf16[2,2,4,32,512]{4,3,2,1,0:T(8,128)(2,1)} %bitcast.26.piece0), channel_id=1, source_target_pairs={{0,96},{32,64},{64,32},{96,0},{1,97},{33,65},{65,33},{97,1},{2,98}... | collective-permute-start | bytes 1572872 | tf_op jit(solution)/shard_map/ppermute | solution.py:87
  165.3 16.0 %collective-permute-start.37 = (bf16[2,2,4,32,512]{4,3,2,1,0:T(8,128)(2,1)}, bf16[2,2,4,32,512]{4,3,2,1,0:T(8,128)(2,1)S(1)}, u32[]{:S(2)}, u32[]{:S(2)}) collective-permute-start(bf16[2,2,4,32,512]{4,3,2,1,0:T(8,128)(2,1)} %bitcast.59), channel_id=1, source_target_pairs={{0,128},{16,144},{128,0},{144,16},{1,129},{17,145},{129,1},{145,17... | collective-permute-start | bytes 1572872 | tf_op jit(solution)/shard_map/ppermute | solution.py:87
  166.1 21.6 %collective-permute-start.33 = (bf16[2,2,4,32,512]{4,3,2,1,0:T(8,128)(2,1)}, bf16[2,2,4,32,512]{4,3,2,1,0:T(8,128)(2,1)S(1)}, u32[]{:S(2)}, u32[]{:S(2)}) collective-permute-start(bf16[2,2,4,32,512]{4,3,2,1,0:T(8,128)(2,1)} %bitcast.60), channel_id=1, source_target_pairs={{0,16},{16,0},{128,144},{144,128},{1,17},{17,1},{129,145},{145,129... | collective-permute-start | bytes 1572872 | tf_op jit(solution)/shard_map/ppermute | solution.py:87
  170.8 16.9 %collective-permute-start.34 = (bf16[2,2,4,32,512]{4,3,2,1,0:T(8,128)(2,1)}, bf16[2,2,4,32,512]{4,3,2,1,0:T(8,128)(2,1)S(1)}, u32[]{:S(2)}, u32[]{:S(2)}) collective-permute-start(bf16[2,2,4,32,512]{4,3,2,1,0:T(8,128)(2,1)} %bitcast.61), channel_id=1, source_target_pairs={{0,144},{16,128},{128,16},{144,0},{1,145},{17,129},{129,17},{145,1... | collective-permute-start | bytes 1572872 | tf_op jit(solution)/shard_map/ppermute | solution.py:87
  189.8 12.1 %collective-permute-start.39 = (f32[384,512]{1,0:T(8,128)S(1)}, f32[384,512]{1,0:T(8,128)S(1)}, u32[]{:S(2)}, u32[]{:S(2)}) collective-permute-start(f32[384,512]{1,0:T(8,128)S(1)} %get-tuple-element.48), channel_id=1, source_target_pairs={{0,1},{1,0},{2,3},{3,2},{4,5},{5,4},{6,7},{7,6},{8,9},{9,8},{10,11... | collective-permute-start | bytes 2359304 | tf_op jit(solution)/shard_map/ppermute | solution.py:263
  (20 other events, 162.0 us)

commit v3 on v2

--- a/solution.py
+++ b/solution.py
@@ -57,8 +57,7 @@
         out1[0, k ^ inner] = jnp.where(pick == 0, second, first).astype(out1.dtype)
 
 
-def apply_kernel(part, n_after, pos, tok, tok2, piece0, piece1, *refs):
-    refs = refs[n_after:]
+def apply_kernel(part, pos, tok, tok2, piece0, piece1, *refs):
     sums, (own, away, half) = refs[:-3], refs[-3:]
     pick, inner = chosen(pos, part)
     for k in range(2):
@@ -79,6 +78,77 @@
     away[...] += jnp.dot(tok2[...], h, preferred_element_type=f32)
 
 
+def second_sum_kernel(*refs):
+    out = refs[-1]
+    for part in range(2):
+        own, first, second, third = refs[4 * part : 4 * part + 4]
+        total = own[...] + first[...].astype(f32) + second[...].astype(f32)
+        out[ZH * part : ZH * part + ZH] = (total + third[...].astype(f32)).astype(out.dtype)
+
+
+def row_moment_of(moment, squares):
+    mean = jnp.sum(squares, axis=1, keepdims=True) * (1.0 / squares.shape[1])
+    return decay_rate * moment + (1.0 - decay_rate) * (mean + tiny_square)
+
+
+def stats_kernel(gz, packed, stats, scaled):
+    hidden = gz.shape[-1]
+    cols = jnp.zeros((GR, hidden), f32)
+    scaled_cols = jnp.zeros((GR, hidden), f32)
+    weights = jnp.zeros((GR, hidden), f32)
+    row_total = jnp.zeros((GR, 1), f32)
+    for z in range(ZN):
+        g = gz[z].astype(f32)
+        squares = g * g
+        rows = row_moment_of(packed[z, :, hidden : hidden + 1], squares)
+        u = g * lax.rsqrt(rows)
+        scaled[z] = u
+        w = packed[z, :, :hidden]
+        cols, scaled_cols, weights = cols + squares, scaled_cols + u * u, weights + w * w
+        row_total = row_total + rows
+    lane = lax.broadcasted_iota(jnp.int32, (1, hidden), 1)
+    total = lambda v: jnp.sum(v, axis=0, keepdims=True)
+    scalars = jnp.where(lane == 0, total(row_total), 0.0) + jnp.where(
+        lane == 1, jnp.sum(total(weights), axis=1, keepdims=True), 0.0
+    )
+    stats[...] = jnp.zeros_like(stats)
+    stats[0:1], stats[1:2], stats[2:3] = total(cols), total(scaled_cols), scalars
+
+
+def rows_kernel(width, stats, col_moment, packed, scaled, a_half, b_half, cols_new, inv_cols):
+    hidden = scaled.shape[-1]
+    lane = lax.broadcasted_iota(jnp.int32, (1, hidden), 1)
+    pick = lambda k: jnp.sum(jnp.where(lane == k, stats[2:3], 0.0), axis=1, keepdims=True)
+    cols = decay_rate * col_moment[...] + (1.0 - decay_rate) * (
+        stats[0:1] * (1.0 / width) + tiny_square
+    )
+    mean_row = pick(0) * (1.0 / width)
+    update_total = mean_row * jnp.sum(stats[1:2] / cols, axis=1, keepdims=True)
+    update_rms = jnp.sqrt(update_total * (1.0 / (width * hidden)))
+    weight_rms = jnp.sqrt(pick(1) * (1.0 / (width * hidden)))
+    factor = (
+        jnp.sqrt(mean_row)
+        * jnp.maximum(weight_floor, weight_rms)
+        / jnp.maximum(1.0, update_rms / clip_level)
+    )
+    inv = factor * lax.rsqrt(cols)
+    cols_new[...], inv_cols[...] = cols, inv
+    for z in range(ZN):
+        new = packed[z, :, :hidden] - learn_rate * (scaled[z] * inv)
+        (a_half, b_half)[z // ZH][z % ZH] = new.astype(bf16)
+
+
+def return_kernel(pos, near, far, weight, moment, inv_cols, new_weight, delta, rows_new):
+    for k, source in enumerate((near, far)):
+        rows = pl.ds(pl.multiple_of(GR * (k ^ pos[4]), GR), GR)
+        g = source[...]
+        moments = row_moment_of(moment[rows], g * g)
+        change = g * lax.rsqrt(moments) * inv_cols[...]
+        rows_new[rows] = moments
+        delta[rows] = change
+        new_weight[rows] = weight[rows] - learn_rate * change
+
+
 def xor_perm(n, k):
     return [(d, d ^ k) for d in range(n)]
 
@@ -112,7 +182,7 @@
             pl.BlockSpec((tok_rows, seg), lambda g, pos: (0, g)),
         ]
 
-    order = [(0, 1), (1, 1), (0, 0), (1, 0)]
+    order = [(0, 0), (1, 0), (0, 1), (1, 1)]
     cotangent2 = lax.ppermute(cotangent, "core", SWAP)
     tokens2 = {}
     for part, step in order:
@@ -141,9 +211,9 @@
         [my_weight, jnp.broadcast_to(my_moment[:, None], (32, 128))], axis=1
     )
     packed = lax.ppermute(packed, ("y1", "core"), TURN)
-    packed = lax.all_gather(packed, "z", axis=0, tiled=True)
-
-    parts = {}
+
+    tokens2, cotangent2 = lax.optimization_barrier((tokens2, cotangent2))
+    parts, chain = {}, pos
     for part, step in order:
         kept = jax.ShapeDtypeStruct(piece, bf16 if step else f32)
         parts[part, step], parts[part, 2 + step] = pl.pallas_call(
@@ -157,7 +227,12 @@
             ),
             compiler_params=params,
             cost_estimate=cost,
-        )(pos, tokens, tokens2[part, step], cotangent, cotangent2)
+        )(chain, tokens, tokens2[part, step], cotangent, cotangent2)
+        chain, _ = lax.optimization_barrier((pos, parts[part, 2 + step]))
+    packed, parts[1, 3] = lax.optimization_barrier((packed, parts[1, 3]))
+    packed = lax.all_to_all(
+        jnp.broadcast_to(packed[None], (ZN,) + packed.shape), "z", 0, 0, tiled=True
+    )
 
     a_parts, b_parts = [[parts[p, k] for k in range(4)] for p in range(2)]
     a_got, b_got = exchange(a_parts, Y), exchange(b_parts, X)
@@ -168,101 +243,81 @@
     b_parts = [b_sum[k % 2, k // 2] for k in range(4)]
     a_got = exchange([p.astype(bf16) for p in a_parts], X)
     b_got = exchange([p.astype(bf16) for p in b_parts], Y)
-    a_sum = a_parts[0] + sum(p.astype(f32) for p in a_got)
-    b_sum = b_parts[0] + sum(p.astype(f32) for p in b_got)
-
-    both = jnp.concatenate([a_sum, b_sum], axis=0).astype(bf16)
+    b_got, packed = lax.optimization_barrier((b_got, packed))
+    line = (ZN, GR, hidden)
+    both = pl.pallas_call(
+        second_sum_kernel, out_shape=jax.ShapeDtypeStruct(line, bf16), compiler_params=params
+    )(a_parts[0], *a_got, b_parts[0], *b_got)
+
     g32 = jnp.sum(lax.all_to_all(both, "z", 0, 0, tiled=True).astype(f32), axis=0)
 
     near = lax.ppermute(g32, ("y1", "core"), TURN)
     far = lax.ppermute(g32, ("cuts", "y1", "core"), FAR_TURN)
 
-    gz = lax.all_to_all(
-        jnp.broadcast_to(g32.astype(bf16)[None], (ZN, GR, hidden)), "z", 0, 0, tiled=True
-    )
-    gz, packed, near, far = lax.optimization_barrier((gz, packed, near, far))
-    gz = gz.reshape(ZN * GR, hidden).astype(f32)
-    wz = packed[:, :hidden]
-    moment_z = packed[:, hidden : hidden + 1]
-
-    squares = gz * gz
-    rows_z = decay_rate * moment_z + (1.0 - decay_rate) * (
-        jnp.mean(squares, axis=1, keepdims=True) + tiny_square
-    )
-    lane = lax.broadcasted_iota(jnp.int32, (1, hidden), 1)
-    scalars = jnp.where(lane == 0, jnp.sum(rows_z), 0.0) + jnp.where(
-        lane == 1, jnp.sum(wz * wz), 0.0
-    )
-    stats = jnp.concatenate(
-        [
-            jnp.sum(squares, axis=0, keepdims=True),
-            jnp.sum(squares / rows_z, axis=0, keepdims=True),
-            scalars,
-        ],
-        axis=0,
-    )
+    gz = lax.all_to_all(jnp.broadcast_to(g32.astype(bf16)[None], line), "z", 0, 0, tiled=True)
+    gz, near, far = lax.optimization_barrier((gz, near, far))
+
+    stats, scaled = pl.pallas_call(
+        stats_kernel,
+        out_shape=[jax.ShapeDtypeStruct((8, hidden), f32), jax.ShapeDtypeStruct(line, f32)],
+        compiler_params=params,
+    )(gz, packed)
     stats = stats + lax.ppermute(stats, "core", SWAP)
     stats = four_sum(stats, exchange([stats] * 4, Y))
     stats = four_sum(stats, exchange([stats] * 4, X))
-    col_total, scaled_total, row_total, weight_total = stats[0], stats[1], stats[2, 0], stats[2, 1]
-
-    cols_new = decay_rate * col_moment + (1.0 - decay_rate) * (col_total / width + tiny_square)
-    mean_row = row_total / width
-    update_total = mean_row * jnp.sum(scaled_total / cols_new)
-    update_rms = jnp.sqrt(update_total / (width * hidden))
-    weight_rms = jnp.sqrt(weight_total / (width * hidden))
-    factor = (
-        jnp.sqrt(mean_row)
-        * jnp.maximum(weight_floor, weight_rms)
-        / jnp.maximum(1.0, update_rms / clip_level)
-    )
-    inv_cols = factor * lax.rsqrt(cols_new)[None, :]
-    half_z = (wz - learn_rate * (gz * lax.rsqrt(rows_z) * inv_cols)).astype(bf16)
-    half_z = half_z.reshape(2, ZH, GR, hidden)
-
-    a_half, b_half = half_z[0], half_z[1]
+
+    row_vector = jax.ShapeDtypeStruct((1, hidden), f32)
+    a_half, b_half, cols_new, inv_cols = pl.pallas_call(
+        functools.partial(rows_kernel, width),
+        out_shape=[jax.ShapeDtypeStruct((ZH, GR, hidden), bf16)] * 2 + [row_vector] * 2,
+        compiler_params=params,
+    )(stats, col_moment.reshape(1, hidden), packed, scaled)
     a_all = [a_half] + exchange([a_half] * 4, X)
     b_all = [b_half] + exchange([b_half] * 4, Y)
     a_half = jnp.stack([a_all[0], a_all[2], a_all[1], a_all[3]]).reshape(piece)
     b_half = jnp.stack([b_all[0], b_all[2], b_all[1], b_all[3]]).reshape(piece)
     a_half, b_half = lax.optimization_barrier((a_half, b_half))
-    a_all = [a_half] + exchange([a_half] * 4, Y)
-    b_all = [b_half] + exchange([b_half] * 4, X)
-
-    g64 = jnp.where(
-        cuts == 0, jnp.concatenate([near, far], axis=0), jnp.concatenate([far, near], axis=0)
-    )
-    rows_new = decay_rate * row_moment + (1.0 - decay_rate) * (
-        jnp.mean(g64 * g64, axis=1) + tiny_square
-    )
-    delta = g64 * lax.rsqrt(rows_new)[:, None] * inv_cols
-    new_weight = weight - learn_rate * delta
+    a_all, b_all = [a_half], [b_half]
+    got = {}
+    for k in (2, 1, 3):
+        got[0, k] = lax.ppermute(a_half, Y, xor_perm(4, k))
+        got[1, k] = lax.ppermute(b_half, X, xor_perm(4, k))
+    a_all += [got[0, k] for k in (1, 2, 3)]
+    b_all += [got[1, k] for k in (1, 2, 3)]
+
+    slab = jax.ShapeDtypeStruct(weight.shape, f32)
+    new_weight, delta, rows_new = pl.pallas_call(
+        return_kernel,
+        out_shape=[slab, slab, jax.ShapeDtypeStruct((weight.shape[0], 1), f32)],
+        in_specs=[pl.BlockSpec(memory_space=pltpu.SMEM)]
+        + [pl.BlockSpec(memory_space=pltpu.VMEM)] * 5,
+        compiler_params=params,
+    )(pos, near, far, weight, row_moment[:, None], inv_cols)
+    a_all[2], _ = lax.optimization_barrier((a_all[2], rows_new))
 
     result = jax.ShapeDtypeStruct((tok_rows, hidden), f32)
     sums = []
     for part, step in [(0, 0), (1, 0), (0, 1), (1, 1)]:
         halves = (a_all, b_all)[part]
-        after = [new_weight] if (part, step) == (1, 0) else []
         sums = pl.pallas_call(
-            functools.partial(apply_kernel, part, len(after)),
+            functools.partial(apply_kernel, part),
             out_shape=[result, result],
             grid_spec=pltpu.PrefetchScalarGridSpec(
                 num_scalar_prefetch=1,
                 grid=(2,),
                 in_specs=tok_specs(part, step)
                 + [piece_spec] * 2
-                + [pl.BlockSpec(memory_space=pl.ANY)] * len(after)
                 + [whole] * len(sums),
                 out_specs=[whole] * 2,
                 scratch_shapes=[pltpu.VMEM((ZH, 2, 2, GR, hidden), bf16)],
             ),
             compiler_params=params,
             cost_estimate=cost,
-        )(pos, tokens, tokens2[part, step], halves[step], halves[2 + step], *after, *sums)
+        )(pos, tokens, tokens2[part, step], halves[step], halves[2 + step], *sums)
     own, away = sums
     summed = own + lax.ppermute(away, "core", SWAP)
     preact = (summed * (1.0 / math.sqrt(width))).astype(bf16)
-    return (new_weight, delta, rows_new, cols_new, preact)
+    return (new_weight, delta, rows_new[:, 0], cols_new[0], preact)
 
 
 def solution(mesh):

time: 206 us -> 192 us (0.932)
  local copies, waits for them, and re-layouts: 12 us -> 21.4 us
  other arithmetic: 17.5 us -> 8.71 us
  blocking collectives: 22.9 us -> 14.5 us
  Pallas kernels: 21.4 us -> 29.7 us
  starting transfers between devices: 83.8 us -> 77.5 us
  waiting for transfers between devices: 42.1 us -> 36.3 us
  between operations: 3.1 us -> 0.97 us
    all_gather x1 -> x0, blocking collectives: 22.9 us -> none  [on_device(): packed = lax.all_gather(packed, 'z', axis=0, tiled=True)]
    all_to_all x0 -> x1, blocking collectives: none -> 14.5 us  [on_device(): lax.all_to_all(both, 'z', 0, 0, tiled=True).astype(f32)]
    ppermute x30 -> x24, waiting for transfers between devices: 31.7 us -> 17.9 us  [exchange(): return [lax.ppermute(pieces[k], axes, xor_perm(4, k)) for k in (1, 2, 3)]]
    ppermute x30 -> x24, starting transfers between devices: 42.7 us -> 31 us  [exchange(): return [lax.ppermute(pieces[k], axes, xor_perm(4, k)) for k in (1, 2, 3)]]
    unnamed x20 -> x44, local copies, waits for them, and re-layouts: 6.85 us -> 17.9 us
    all_to_all x2, waiting for transfers between devices: 7.55 us -> 0.01 us  [the longest x1 0.01 us: on_device(): lax.all_to_all(jnp.broadcast_to(packed[None], (ZN,) + packed.shape), 'z',...]
    ppermute x0 -> x6, starting transfers between devices: none -> 6.78 us  [the longest x3 3.59 us: on_device(): got[0, k] = lax.ppermute(a_half, Y, xor_perm(4, k))]
    pallas_call x4 -> x8, Pallas kernels: 9.24 us -> 15.4 us  [the longest x4 12 us: on_device(): pl.pallas_call(functools.partial(apply_kernel, part), out_shape=[result,...]
  transfers between devices with their start and end apart: 42 -> 42, of which waited for: 19 -> 17; matrix products, arithmetic and copies ran while one was open for 4% -> 4% of each run, Pallas kernels for 9% -> 11%
where the time goes in v3:
time: 192 us; the launch traced here: 189 us
  starting transfers between devices  77.5 us (40%)
  waiting for transfers between devices  36.3 us (19%)
  Pallas kernels  29.7 us (15%)
  local copies, waits for them, and re-layouts  21.4 us (11%)
  blocking collectives  14.5 us (8%)
  other arithmetic  8.71 us (5%)
    ppermute x24, starting transfers between devices, exchange(): return [lax.ppermute(pieces[k], axes, xor_perm(4, k)) for k in (1, 2, 3)]  31 us
    unnamed x44, local copies, waits for them, and re-layouts  17.9 us
    ppermute x24, waiting for transfers between devices, exchange(): return [lax.ppermute(pieces[k], axes, xor_perm(4, k)) for k in (1, 2, 3)]  17.9 us
    all_to_all x1, blocking collectives, on_device(): lax.all_to_all(both, 'z', 0, 0, tiled=True).astype(f32)  14.5 us
    pallas_call x4, Pallas kernels, on_device(): pl.pallas_call(functools.partial(apply_kernel, part), out_shape=[result,...  12 us
    pallas_call x4, Pallas kernels, on_device(): pl.pallas_call(functools.partial(grad_kernel, part), out_shape=[kept, jax...  11.1 us
    ppermute x1, starting transfers between devices, on_device(): summed = own + lax.ppermute(away, 'core', SWAP)  10.6 us
    all_to_all x1, starting transfers between devices, on_device(): lax.all_to_all(jnp.broadcast_to(packed[None], (ZN,) + packed.shape), 'z',...  8.01 us
  transfers between devices with their start and end apart: 42, of which 17 were waited for; matrix products, arithmetic and copies ran while one was open for 4% of the time, Pallas kernels for 11%

profile of v3, /device:TPU:33, one launch (start us, length us, event | category | flops | bytes accessed | tf_op | source)
XLA Modules:
  0.0 189.1 jit_solution(3749336305744926019)
XLA Ops:
  0.7 2.8 %copy-done = bf16[384,8192]{1,0:T(8,128)(2,1)S(1)} copy-done((bf16[384,8192]{1,0:T(8,128)(2,1)S(1)}, bf16[384,8192]{1,0:T(8,128)(2,1)}, u32[]{:S(2)}) %copy-start) | copy-done | bytes 6291480
  8.8 2.3 %collective-permute-done.4.cot2 = bf16[384,512]{1,0:T(8,128)(2,1)S(1)} collective-permute-done((bf16[384,512]{1,0:T(8,128)(2,1)S(1)}, bf16[384,512]{1,0:T(8,128)(2,1)S(1)}, u32[]{:S(2)}, u32[]{:S(2)}) %collective-permute-start.4) | collective-permute-done | bytes 393248 | tf_op jit(solution)/shard_map/ppermute | solution.py:186
  11.2 3.0 %shard_map.96 = (f32[2,2,4,32,512]{4,3,2,1,0:T(8,128)S(1)}, bf16[2,2,4,32,512]{4,3,2,1,0:T(8,128)(2,1)}) custom-call(s32[5]{0:T(128)S(1)} %stack.53.pos, bf16[384,8192]{1,0:T(8,128)(2,1)S(1)} %copy-done, bf16[384,1024]{1,0:T(8,128)(2,1)S(1)} %collective-permute-done.tok2, bf16[384,512]{1,0:T(8,128)(2,1)S(1)} %copy-done.3, ...), custom_call_target="tpu_custom_call" | custom-call | flops 805306368 | bytes 4194304 | tf_op jit(solution)/shard_map/pallas_call | solution.py:219
  15.1 2.9 %collective-permute-start.6 = (bf16[2,2,4,32,512]{4,3,2,1,0:T(8,128)(2,1)}, bf16[2,2,4,32,512]{4,3,2,1,0:T(8,128)(2,1)}, u32[]{:S(2)}, u32[]{:S(2)}) collective-permute-start(bf16[2,2,4,32,512]{4,3,2,1,0:T(8,128)(2,1)} %get-tuple-element.53), channel_id=1, source_target_pairs={{0,64},{32,96},{64,0},{96,32},{1,65},{33,97},{65,1},{97,33},{2,66}... | collective-permute-start | bytes 1572872 | tf_op jit(solution)/shard_map/ppermute | solution.py:157
  18.0 2.2 %shard_map.97 = (f32[2,2,4,32,512]{4,3,2,1,0:T(8,128)S(1)}, bf16[2,2,4,32,512]{4,3,2,1,0:T(8,128)(2,1)S(1)}) custom-call(s32[5]{0:T(128)S(1)} %stack.53.pos, bf16[384,8192]{1,0:T(8,128)(2,1)S(1)} %copy-done, bf16[384,1024]{1,0:T(8,128)(2,1)S(1)} %collective-permute-done.2.tok2, bf16[384,512]{1,0:T(8,128)(2,1)S(1)} %copy-done.3, ...), custom_call_target="tpu_custom_call" | custom-call | flops 805306368 | bytes 4194304 | tf_op jit(solution)/shard_map/pallas_call | solution.py:219
  21.3 3.0 %shard_map.98 = (bf16[2,2,4,32,512]{4,3,2,1,0:T(8,128)(2,1)}, bf16[2,2,4,32,512]{4,3,2,1,0:T(8,128)(2,1)}) custom-call(s32[5]{0:T(128)S(1)} %stack.53.pos, bf16[384,8192]{1,0:T(8,128)(2,1)S(1)} %copy-done, bf16[384,1024]{1,0:T(8,128)(2,1)S(1)} %collective-permute-done.1.tok2, bf16[384,512]{1,0:T(8,128)(2,1)S(1)} %copy-done.3, ...), custom_call_target="tpu_custom_call" | custom-call | flops 805306368 | bytes 4194304 | tf_op jit(solution)/shard_map/pallas_call | solution.py:219
  25.3 5.3 %collective-permute-start.13 = (f32[32,640]{1,0:T(8,128)S(1)}, f32[32,640]{1,0:T(8,128)S(1)}, u32[]{:S(2)}, u32[]{:S(2)}) collective-permute-start(f32[32,640]{1,0:T(8,128)S(1)} %pad_maximum_fusion.2), channel_id=1, source_target_pairs={{0,0},{1,64},{64,1},{65,65},{2,2},{3,66},{66,3},{67,67},{4,4},{5,6... | collective-permute-start | bytes 245768 | tf_op jit(solution)/shard_map/ppermute | solution.py:213
  30.6 2.8 %collective-permute-start.12 = (bf16[2,2,4,32,512]{4,3,2,1,0:T(8,128)(2,1)}, bf16[2,2,4,32,512]{4,3,2,1,0:T(8,128)(2,1)}, u32[]{:S(2)}, u32[]{:S(2)}) collective-permute-start(bf16[2,2,4,32,512]{4,3,2,1,0:T(8,128)(2,1)} %copy-done.19), channel_id=1, source_target_pairs={{0,128},{16,144},{128,0},{144,16},{1,129},{17,145},{129,1},{145,17... | collective-permute-start | bytes 1572872 | tf_op jit(solution)/shard_map/ppermute | solution.py:157
  33.4 2.8 %copy-done.1 = bf16[384,8192]{1,0:T(8,128)(2,1)S(1)} copy-done((bf16[384,8192]{1,0:T(8,128)(2,1)S(1)}, bf16[384,8192]{1,0:T(8,128)(2,1)}, u32[]{:S(2)}) %copy-start.1) | copy-done | bytes 6291480
  36.2 2.9 %shard_map.99 = (bf16[2,2,4,32,512]{4,3,2,1,0:T(8,128)(2,1)S(1)}, bf16[2,2,4,32,512]{4,3,2,1,0:T(8,128)(2,1)}) custom-call(s32[5]{0:T(128)S(1)} %stack.53.pos, bf16[384,8192]{1,0:T(8,128)(2,1)S(1)} %copy-done.1, bf16[384,1024]{1,0:T(8,128)(2,1)S(1)} %collective-permute-done.3.tok2, bf16[384,512]{1,0:T(8,128)(2,1)S(1)} %copy-done.3, ...), custom_call_target="tpu_custom_call" | custom-call | flops 805306368 | bytes 4194304 | tf_op jit(solution)/shard_map/pallas_call | solution.py:219
  39.9 2.7 %collective-permute-done.13 = f32[32,640]{1,0:T(8,128)S(1)} collective-permute-done((f32[32,640]{1,0:T(8,128)S(1)}, f32[32,640]{1,0:T(8,128)S(1)}, u32[]{:S(2)}, u32[]{:S(2)}) %collective-permute-start.13) | collective-permute-done | bytes 81952 | tf_op jit(solution)/shard_map/ppermute | solution.py:213
  42.6 2.5 %collective-permute-start.14 = (bf16[2,2,4,32,512]{4,3,2,1,0:T(8,128)(2,1)}, bf16[2,2,4,32,512]{4,3,2,1,0:T(8,128)(2,1)}, u32[]{:S(2)}, u32[]{:S(2)}) collective-permute-start(bf16[2,2,4,32,512]{4,3,2,1,0:T(8,128)(2,1)} %get-tuple-element.66), channel_id=1, source_target_pairs={{0,144},{16,128},{128,16},{144,0},{1,145},{17,129},{129,17},{145,1... | collective-permute-start | bytes 1572872 | tf_op jit(solution)/shard_map/ppermute | solution.py:157
  46.0 8.0 %all-to-all-start = ((f32[8,32,640]{2,1,0:T(8,128)}), f32[8,32,640]{2,1,0:T(8,128)S(1)}, u32[]{:S(2)}, u32[]{:S(2)}) async-start(f32[8,32,640]{2,1,0:T(8,128)} %broadcast_in_dim.9), calls=%async_computation | async-start | bytes 1310720 | tf_op jit(solution)/shard_map/all_to_all | solution.py:233
  57.6 2.4 %collective-permute-start.9 = (bf16[4,32,512]{2,1,0:T(8,128)(2,1)}, bf16[4,32,512]{2,1,0:T(8,128)(2,1)}, u32[]{:S(2)}, u32[]{:S(2)}) collective-permute-start(bf16[4,32,512]{2,1,0:T(8,128)(2,1)} %get-tuple-element.103), channel_id=1, source_target_pairs={{0,128},{16,144},{128,0},{144,16},{1,129},{17,145},{129,1},{145,17... | collective-permute-start | bytes 393224 | tf_op jit(solution)/shard_map/ppermute | solution.py:157
  60.1 4.0 %collective-permute-done.11 = bf16[2,2,4,32,512]{4,3,2,1,0:T(8,128)(2,1)S(1)} collective-permute-done((bf16[2,2,4,32,512]{4,3,2,1,0:T(8,128)(2,1)}, bf16[2,2,4,32,512]{4,3,2,1,0:T(8,128)(2,1)S(1)}, u32[]{:S(2)}, u32[]{:S(2)}) %collective-permute-start.11) | collective-permute-done | bytes 524320 | tf_op jit(solution)/shard_map/ppermute | solution.py:157
  66.3 2.9 %collective-permute-start.16 = (bf16[4,32,512]{2,1,0:T(8,128)(2,1)S(1)}, bf16[4,32,512]{2,1,0:T(8,128)(2,1)S(1)}, u32[]{:S(2)}, u32[]{:S(2)}) collective-permute-start(bf16[4,32,512]{2,1,0:T(8,128)(2,1)S(1)} %get-tuple-element.100), channel_id=1, source_target_pairs={{0,64},{32,96},{64,0},{96,32},{1,65},{33,97},{65,1},{97,33},{2,66}... | collective-permute-start | bytes 393224 | tf_op jit(solution)/shard_map/ppermute | solution.py:157
  69.1 4.7 %collective-permute-done.17.refs_7_ = bf16[4,32,512]{2,1,0:T(8,128)(2,1)S(1)} collective-permute-done((bf16[4,32,512]{2,1,0:T(8,128)(2,1)S(1)}, bf16[4,32,512]{2,1,0:T(8,128)(2,1)S(1)}, u32[]{:S(2)}, u32[]{:S(2)}) %collective-permute-start.17) | collective-permute-done | bytes 131104 | tf_op jit(solution)/shard_map/ppermute | solution.py:157
  75.3 2.4 %collective-permute-done.15.refs_5_ = bf16[4,32,512]{2,1,0:T(8,128)(2,1)S(1)} collective-permute-done((bf16[4,32,512]{2,1,0:T(8,128)(2,1)S(1)}, bf16[4,32,512]{2,1,0:T(8,128)(2,1)S(1)}, u32[]{:S(2)}, u32[]{:S(2)}) %collective-permute-start.15) | collective-permute-done | bytes 131104 | tf_op jit(solution)/shard_map/ppermute | solution.py:157
  83.1 14.5 %all_to_all.15 = bf16[8,32,512]{2,1,0:T(8,128)(2,1)S(1)} all-to-all(bf16[8,32,512]{2,1,0:T(8,128)(2,1)S(1)} %shard_map.100), channel_id=1, replica_groups=mesh['cuts'=2,'y1'=2,'y0'=2,'xlo'=2,'z'=8,'core'=2] {'z'}, dimensions={0} | all-to-all | bytes 524288 | tf_op jit(solution)/shard_map/all_to_all | solution.py:252
  99.9 4.7 %all-to-all-start.2 = ((bf16[8,32,512]{2,1,0:T(8,128)(2,1)}), bf16[8,32,512]{2,1,0:T(8,128)(2,1)S(1)}, u32[]{:S(2)}, u32[]{:S(2)}) async-start(bf16[8,32,512]{2,1,0:T(8,128)(2,1)} %broadcast_in_dim.10), calls=%async_computation.2 | async-start | bytes 524288 | tf_op jit(solution)/shard_map/all_to_all | solution.py:257
  104.6 7.1 %collective-permute-start.19 = (f32[32,512]{1,0:T(8,128)}, f32[32,512]{1,0:T(8,128)S(1)}, u32[]{:S(2)}, u32[]{:S(2)}) collective-permute-start(f32[32,512]{1,0:T(8,128)} %convert_reduce_fusion), channel_id=1, source_target_pairs={{0,128},{1,192},{64,129},{65,193},{128,0},{129,64},{192,1},{193,65... | collective-permute-start | bytes 196616 | tf_op jit(solution)/shard_map/ppermute | solution.py:255
  113.8 5.1 %collective-permute-done.18.near = f32[32,512]{1,0:T(8,128)S(1)} collective-permute-done((f32[32,512]{1,0:T(8,128)}, f32[32,512]{1,0:T(8,128)S(1)}, u32[]{:S(2)}, u32[]{:S(2)}) %collective-permute-start.18) | collective-permute-done | bytes 65568 | tf_op jit(solution)/shard_map/ppermute | solution.py:254
  121.8 2.6 %collective-permute-start.21 = (f32[8,512]{1,0:T(8,128)S(1)}, f32[8,512]{1,0:T(8,128)S(1)}, u32[]{:S(2)}, u32[]{:S(2)}) collective-permute-start(f32[8,512]{1,0:T(8,128)S(1)} %add.53), channel_id=1, source_target_pairs={{0,64},{32,96},{64,0},{96,32},{1,65},{33,97},{65,1},{97,33},{2,66}... | collective-permute-start | bytes 49160 | tf_op jit(solution)/shard_map/ppermute | solution.py:157
  134.3 2.2 %collective-permute-start.27 = (bf16[4,32,512]{2,1,0:T(8,128)(2,1)S(1)}, bf16[4,32,512]{2,1,0:T(8,128)(2,1)S(1)}, u32[]{:S(2)}, u32[]{:S(2)}) collective-permute-start(bf16[4,32,512]{2,1,0:T(8,128)(2,1)S(1)} %get-tuple-element.82), channel_id=1, source_target_pairs={{0,128},{16,144},{128,0},{144,16},{1,129},{17,145},{129,1},{145,17... | collective-permute-start | bytes 393224 | tf_op jit(solution)/shard_map/ppermute | solution.py:157
  147.3 2.2 %collective-permute-start.36 = (bf16[2,2,4,32,512]{4,3,2,1,0:T(8,128)(2,1)}, bf16[2,2,4,32,512]{4,3,2,1,0:T(8,128)(2,1)}, u32[]{:S(2)}, u32[]{:S(2)}) collective-permute-start(bf16[2,2,4,32,512]{4,3,2,1,0:T(8,128)(2,1)} %bitcast.20.piece0), channel_id=1, source_target_pairs={{0,96},{32,64},{64,32},{96,0},{1,97},{33,65},{65,33},{97,1},{2,98}... | collective-permute-start | bytes 1572872 | tf_op jit(solution)/shard_map/ppermute | solution.py:283
  151.4 3.7 %collective-permute-done.38.piece1 = bf16[2,2,4,32,512]{4,3,2,1,0:T(8,128)(2,1)S(1)} collective-permute-done((bf16[2,2,4,32,512]{4,3,2,1,0:T(8,128)(2,1)}, bf16[2,2,4,32,512]{4,3,2,1,0:T(8,128)(2,1)S(1)}, u32[]{:S(2)}, u32[]{:S(2)}) %collective-permute-start.38) | collective-permute-done | bytes 524320 | tf_op jit(solution)/shard_map/ppermute | solution.py:283
  158.0 2.8 %copy-done.2 = bf16[384,8192]{1,0:T(8,128)(2,1)S(1)} copy-done((bf16[384,8192]{1,0:T(8,128)(2,1)S(1)}, bf16[384,8192]{1,0:T(8,128)(2,1)}, u32[]{:S(2)}) %copy-start.2) | copy-done | bytes 6291480
  161.8 2.9 %shard_map.104 = (f32[384,512]{1,0:T(8,128)S(1)}, f32[384,512]{1,0:T(8,128)S(1)}) custom-call(s32[5]{0:T(128)S(1)} %stack.53.pos, bf16[384,8192]{1,0:T(8,128)(2,1)S(1)} %copy-done.2, bf16[384,1024]{1,0:T(8,128)(2,1)S(1)} %collective-permute-done.tok2, bf16[2,2,4,32,512]{4,3,2,1,0:T(8,128)(2,1)} %bitcast.20.piece0, bf16[2,2,4,32,512]{4,3,2,1,0:T(8,128)(2,1)S(1)} %copy-done.10), custom_call_target="tpu_custom_call" | custom-call | flops 805306368 | bytes 4194304 | tf_op jit(solution)/shard_map/pallas_call | solution.py:302
  164.8 3.0 %shard_map.105 = (f32[384,512]{1,0:T(8,128)S(1)}, f32[384,512]{1,0:T(8,128)S(1)}) custom-call(s32[5]{0:T(128)S(1)} %stack.53.pos, bf16[384,8192]{1,0:T(8,128)(2,1)S(1)} %copy-done.2, bf16[384,1024]{1,0:T(8,128)(2,1)S(1)} %copy-done.5, bf16[2,2,4,32,512]{4,3,2,1,0:T(8,128)(2,1)} %bitcast.25.piece0, ...), custom_call_target="tpu_custom_call" | custom-call | flops 805306368 | bytes 4194304 | tf_op jit(solution)/shard_map/pallas_call | solution.py:302
  169.6 3.0 %shard_map.106 = (f32[384,512]{1,0:T(8,128)S(1)}, f32[384,512]{1,0:T(8,128)S(1)}) custom-call(s32[5]{0:T(128)S(1)} %stack.53.pos, bf16[384,8192]{1,0:T(8,128)(2,1)S(1)} %copy-done.2, bf16[384,1024]{1,0:T(8,128)(2,1)S(1)} %collective-permute-done.1.tok2, bf16[2,2,4,32,512]{4,3,2,1,0:T(8,128)(2,1)} %collective-permute-done.35.piece0, ...), custom_call_target="tpu_custom_call" | custom-call | flops 805306368 | bytes 4194304 | tf_op jit(solution)/shard_map/pallas_call | solution.py:302
  172.6 3.0 %shard_map.107 = (f32[384,512]{1,0:T(8,128)S(1)}, f32[384,512]{1,0:T(8,128)S(1)}) custom-call(s32[5]{0:T(128)S(1)} %stack.53.pos, bf16[384,8192]{1,0:T(8,128)(2,1)S(1)} %copy-done.2, bf16[384,1024]{1,0:T(8,128)(2,1)S(1)} %collective-permute-done.3.tok2, bf16[2,2,4,32,512]{4,3,2,1,0:T(8,128)(2,1)} %collective-permute-done.33.piece0, ...), custom_call_target="tpu_custom_call" | custom-call | flops 805306368 | bytes 4194304 | tf_op jit(solution)/shard_map/pallas_call | solution.py:302
  175.6 10.6 %collective-permute-start.39 = (f32[384,512]{1,0:T(8,128)S(1)}, f32[384,512]{1,0:T(8,128)S(1)}, u32[]{:S(2)}, u32[]{:S(2)}) collective-permute-start(f32[384,512]{1,0:T(8,128)S(1)} %get-tuple-element.94), channel_id=1, source_target_pairs={{0,1},{1,0},{2,3},{3,2},{4,5},{5,4},{6,7},{7,6},{8,9},{9,8},{10,11... | collective-permute-start | bytes 2359304 | tf_op jit(solution)/shard_map/ppermute | solution.py:318
  (136 shorter events, 60.8 us)
Async XLA Ops:
  4.3 6.8 %collective-permute-start = (bf16[384,1024]{1,0:T(8,128)(2,1)S(1)}, bf16[384,1024]{1,0:T(8,128)(2,1)S(1)}, u32[]{:S(2)}, u32[]{:S(2)}) collective-permute-start(bf16[384,1024]{1,0:T(8,128)(2,1)S(1)} %shard_map.92), channel_id=1, source_target_pairs={{0,1},{1,0},{2,3},{3,2},{4,5},{5,4},{6,7},{7,6},{8,9},{9,8},{10,11... | collective-permute-start | bytes 2359304 | tf_op jit(solution)/shard_map/ppermute | solution.py:206
  5.9 5.2 %collective-permute-start.1 = (bf16[384,1024]{1,0:T(8,128)(2,1)S(1)}, bf16[384,1024]{1,0:T(8,128)(2,1)S(1)}, u32[]{:S(2)}, u32[]{:S(2)}) collective-permute-start(bf16[384,1024]{1,0:T(8,128)(2,1)S(1)} %shard_map.93), channel_id=1, source_target_pairs={{0,1},{1,0},{2,3},{3,2},{4,5},{5,4},{6,7},{7,6},{8,9},{9,8},{10,11... | collective-permute-start | bytes 2359304 | tf_op jit(solution)/shard_map/ppermute | solution.py:206
  6.8 4.3 %collective-permute-start.2 = (bf16[384,1024]{1,0:T(8,128)(2,1)S(1)}, bf16[384,1024]{1,0:T(8,128)(2,1)S(1)}, u32[]{:S(2)}, u32[]{:S(2)}) collective-permute-start(bf16[384,1024]{1,0:T(8,128)(2,1)S(1)} %shard_map.94), channel_id=1, source_target_pairs={{0,1},{1,0},{2,3},{3,2},{4,5},{5,4},{6,7},{7,6},{8,9},{9,8},{10,11... | collective-permute-start | bytes 2359304 | tf_op jit(solution)/shard_map/ppermute | solution.py:206
  15.1 38.9 %collective-permute-start.6 = (bf16[2,2,4,32,512]{4,3,2,1,0:T(8,128)(2,1)}, bf16[2,2,4,32,512]{4,3,2,1,0:T(8,128)(2,1)}, u32[]{:S(2)}, u32[]{:S(2)}) collective-permute-start(bf16[2,2,4,32,512]{4,3,2,1,0:T(8,128)(2,1)} %get-tuple-element.53), channel_id=1, source_target_pairs={{0,64},{32,96},{64,0},{96,32},{1,65},{33,97},{65,1},{97,33},{2,66}... | collective-permute-start | bytes 1572872 | tf_op jit(solution)/shard_map/ppermute | solution.py:157
  24.3 29.7 %collective-permute-start.5 = (bf16[2,2,4,32,512]{4,3,2,1,0:T(8,128)(2,1)}, bf16[2,2,4,32,512]{4,3,2,1,0:T(8,128)(2,1)}, u32[]{:S(2)}, u32[]{:S(2)}) collective-permute-start(bf16[2,2,4,32,512]{4,3,2,1,0:T(8,128)(2,1)} %get-tuple-element.59), channel_id=1, source_target_pairs={{0,32},{32,0},{64,96},{96,64},{1,33},{33,1},{65,97},{97,65},{2,34}... | collective-permute-start | bytes 1572872 | tf_op jit(solution)/shard_map/ppermute | solution.py:157
  24.7 29.3 %collective-permute-start.7 = (bf16[2,2,4,32,512]{4,3,2,1,0:T(8,128)(2,1)}, bf16[2,2,4,32,512]{4,3,2,1,0:T(8,128)(2,1)}, u32[]{:S(2)}, u32[]{:S(2)}) collective-permute-start(bf16[2,2,4,32,512]{4,3,2,1,0:T(8,128)(2,1)} %get-tuple-element.60), channel_id=1, source_target_pairs={{0,96},{32,64},{64,32},{96,0},{1,97},{33,65},{65,33},{97,1},{2,98}... | collective-permute-start | bytes 1572872 | tf_op jit(solution)/shard_map/ppermute | solution.py:157
  25.3 17.3 %collective-permute-start.13 = (f32[32,640]{1,0:T(8,128)S(1)}, f32[32,640]{1,0:T(8,128)S(1)}, u32[]{:S(2)}, u32[]{:S(2)}) collective-permute-start(f32[32,640]{1,0:T(8,128)S(1)} %pad_maximum_fusion.2), channel_id=1, source_target_pairs={{0,0},{1,64},{64,1},{65,65},{2,2},{3,66},{66,3},{67,67},{4,4},{5,6... | collective-permute-start | bytes 245768 | tf_op jit(solution)/shard_map/ppermute | solution.py:213
  30.6 29.5 %collective-permute-start.12 = (bf16[2,2,4,32,512]{4,3,2,1,0:T(8,128)(2,1)}, bf16[2,2,4,32,512]{4,3,2,1,0:T(8,128)(2,1)}, u32[]{:S(2)}, u32[]{:S(2)}) collective-permute-start(bf16[2,2,4,32,512]{4,3,2,1,0:T(8,128)(2,1)} %copy-done.19), channel_id=1, source_target_pairs={{0,128},{16,144},{128,0},{144,16},{1,129},{17,145},{129,1},{145,17... | collective-permute-start | bytes 1572872 | tf_op jit(solution)/shard_map/ppermute | solution.py:157
  42.6 17.5 %collective-permute-start.14 = (bf16[2,2,4,32,512]{4,3,2,1,0:T(8,128)(2,1)}, bf16[2,2,4,32,512]{4,3,2,1,0:T(8,128)(2,1)}, u32[]{:S(2)}, u32[]{:S(2)}) collective-permute-start(bf16[2,2,4,32,512]{4,3,2,1,0:T(8,128)(2,1)} %get-tuple-element.66), channel_id=1, source_target_pairs={{0,144},{16,128},{128,16},{144,0},{1,145},{17,129},{129,17},{145,1... | collective-permute-start | bytes 1572872 | tf_op jit(solution)/shard_map/ppermute | solution.py:157
  46.0 32.4 %all-to-all-start = ((f32[8,32,640]{2,1,0:T(8,128)}), f32[8,32,640]{2,1,0:T(8,128)S(1)}, u32[]{:S(2)}, u32[]{:S(2)}) async-start(f32[8,32,640]{2,1,0:T(8,128)} %broadcast_in_dim.9), calls=%async_computation | async-start | bytes 1310720 | tf_op jit(solution)/shard_map/all_to_all | solution.py:233
  54.0 10.1 %collective-permute-start.11 = (bf16[2,2,4,32,512]{4,3,2,1,0:T(8,128)(2,1)}, bf16[2,2,4,32,512]{4,3,2,1,0:T(8,128)(2,1)S(1)}, u32[]{:S(2)}, u32[]{:S(2)}) collective-permute-start(bf16[2,2,4,32,512]{4,3,2,1,0:T(8,128)(2,1)} %copy-done.20), channel_id=1, source_target_pairs={{0,16},{16,0},{128,144},{144,128},{1,17},{17,1},{129,145},{145,129... | collective-permute-start | bytes 1572872 | tf_op jit(solution)/shard_map/ppermute | solution.py:157
  56.8 21.5 %collective-permute-start.10 = (bf16[4,32,512]{2,1,0:T(8,128)(2,1)}, bf16[4,32,512]{2,1,0:T(8,128)(2,1)S(1)}, u32[]{:S(2)}, u32[]{:S(2)}) collective-permute-start(bf16[4,32,512]{2,1,0:T(8,128)(2,1)} %get-tuple-element.102), channel_id=1, source_target_pairs={{0,144},{16,128},{128,16},{144,0},{1,145},{17,129},{129,17},{145,1... | collective-permute-start | bytes 393224 | tf_op jit(solution)/shard_map/ppermute | solution.py:157
  57.6 20.8 %collective-permute-start.9 = (bf16[4,32,512]{2,1,0:T(8,128)(2,1)}, bf16[4,32,512]{2,1,0:T(8,128)(2,1)}, u32[]{:S(2)}, u32[]{:S(2)}) collective-permute-start(bf16[4,32,512]{2,1,0:T(8,128)(2,1)} %get-tuple-element.103), channel_id=1, source_target_pairs={{0,128},{16,144},{128,0},{144,16},{1,129},{17,145},{129,1},{145,17... | collective-permute-start | bytes 393224 | tf_op jit(solution)/shard_map/ppermute | solution.py:157
  60.0 18.3 %collective-permute-start.8 = (bf16[4,32,512]{2,1,0:T(8,128)(2,1)}, bf16[4,32,512]{2,1,0:T(8,128)(2,1)}, u32[]{:S(2)}, u32[]{:S(2)}) collective-permute-start(bf16[4,32,512]{2,1,0:T(8,128)(2,1)} %get-tuple-element.104), channel_id=1, source_target_pairs={{0,16},{16,0},{128,144},{144,128},{1,17},{17,1},{129,145},{145,129... | collective-permute-start | bytes 393224 | tf_op jit(solution)/shard_map/ppermute | solution.py:157
  66.0 7.9 %collective-permute-start.17 = (bf16[4,32,512]{2,1,0:T(8,128)(2,1)S(1)}, bf16[4,32,512]{2,1,0:T(8,128)(2,1)S(1)}, u32[]{:S(2)}, u32[]{:S(2)}) collective-permute-start(bf16[4,32,512]{2,1,0:T(8,128)(2,1)S(1)} %get-tuple-element.99), channel_id=1, source_target_pairs={{0,96},{32,64},{64,32},{96,0},{1,97},{33,65},{65,33},{97,1},{2,98}... | collective-permute-start | bytes 393224 | tf_op jit(solution)/shard_map/ppermute | solution.py:157
  66.3 8.4 %collective-permute-start.16 = (bf16[4,32,512]{2,1,0:T(8,128)(2,1)S(1)}, bf16[4,32,512]{2,1,0:T(8,128)(2,1)S(1)}, u32[]{:S(2)}, u32[]{:S(2)}) collective-permute-start(bf16[4,32,512]{2,1,0:T(8,128)(2,1)S(1)} %get-tuple-element.100), channel_id=1, source_target_pairs={{0,64},{32,96},{64,0},{96,32},{1,65},{33,97},{65,1},{97,33},{2,66}... | collective-permute-start | bytes 393224 | tf_op jit(solution)/shard_map/ppermute | solution.py:157
  99.9 19.1 %all-to-all-start.2 = ((bf16[8,32,512]{2,1,0:T(8,128)(2,1)}), bf16[8,32,512]{2,1,0:T(8,128)(2,1)S(1)}, u32[]{:S(2)}, u32[]{:S(2)}) async-start(bf16[8,32,512]{2,1,0:T(8,128)(2,1)} %broadcast_in_dim.10), calls=%async_computation.2 | async-start | bytes 524288 | tf_op jit(solution)/shard_map/all_to_all | solution.py:257
  104.6 9.2 %collective-permute-start.19 = (f32[32,512]{1,0:T(8,128)}, f32[32,512]{1,0:T(8,128)S(1)}, u32[]{:S(2)}, u32[]{:S(2)}) collective-permute-start(f32[32,512]{1,0:T(8,128)} %convert_reduce_fusion), channel_id=1, source_target_pairs={{0,128},{1,192},{64,129},{65,193},{128,0},{129,64},{192,1},{193,65... | collective-permute-start | bytes 196616 | tf_op jit(solution)/shard_map/ppermute | solution.py:255
  111.7 7.3 %collective-permute-start.18 = (f32[32,512]{1,0:T(8,128)}, f32[32,512]{1,0:T(8,128)S(1)}, u32[]{:S(2)}, u32[]{:S(2)}) collective-permute-start(f32[32,512]{1,0:T(8,128)} %convert_reduce_fusion), channel_id=1, source_target_pairs={{0,0},{1,64},{64,1},{65,65},{2,2},{3,66},{66,3},{67,67},{4,4},{5,6... | collective-permute-start | bytes 196616 | tf_op jit(solution)/shard_map/ppermute | solution.py:254
  127.8 4.1 %collective-permute-start.24 = (f32[8,512]{1,0:T(8,128)S(1)}, f32[8,512]{1,0:T(8,128)S(1)}, u32[]{:S(2)}, u32[]{:S(2)}) collective-permute-start(f32[8,512]{1,0:T(8,128)S(1)} %add_add_fusion.3), channel_id=1, source_target_pairs={{0,128},{16,144},{128,0},{144,16},{1,129},{17,145},{129,1},{145,17... | collective-permute-start | bytes 49160 | tf_op jit(solution)/shard_map/ppermute | solution.py:157
  132.6 6.2 %collective-permute-start.29 = (bf16[4,32,512]{2,1,0:T(8,128)(2,1)S(1)}, bf16[4,32,512]{2,1,0:T(8,128)(2,1)S(1)}, u32[]{:S(2)}, u32[]{:S(2)}) collective-permute-start(bf16[4,32,512]{2,1,0:T(8,128)(2,1)S(1)} %get-tuple-element.82), channel_id=1, source_target_pairs={{0,144},{16,128},{128,16},{144,0},{1,145},{17,129},{129,17},{145,1... | collective-permute-start | bytes 393224 | tf_op jit(solution)/shard_map/ppermute | solution.py:157
  134.0 6.3 %collective-permute-start.28 = (bf16[4,32,512]{2,1,0:T(8,128)(2,1)S(1)}, bf16[4,32,512]{2,1,0:T(8,128)(2,1)S(1)}, u32[]{:S(2)}, u32[]{:S(2)}) collective-permute-start(bf16[4,32,512]{2,1,0:T(8,128)(2,1)S(1)} %get-tuple-element.82), channel_id=1, source_target_pairs={{0,16},{16,0},{128,144},{144,128},{1,17},{17,1},{129,145},{145,129... | collective-permute-start | bytes 393224 | tf_op jit(solution)/shard_map/ppermute | solution.py:157
  134.3 6.1 %collective-permute-start.27 = (bf16[4,32,512]{2,1,0:T(8,128)(2,1)S(1)}, bf16[4,32,512]{2,1,0:T(8,128)(2,1)S(1)}, u32[]{:S(2)}, u32[]{:S(2)}) collective-permute-start(bf16[4,32,512]{2,1,0:T(8,128)(2,1)S(1)} %get-tuple-element.82), channel_id=1, source_target_pairs={{0,128},{16,144},{128,0},{144,16},{1,129},{17,145},{129,1},{145,17... | collective-permute-start | bytes 393224 | tf_op jit(solution)/shard_map/ppermute | solution.py:157
  136.4 5.3 %collective-permute-start.32 = (bf16[4,32,512]{2,1,0:T(8,128)(2,1)S(1)}, bf16[4,32,512]{2,1,0:T(8,128)(2,1)S(1)}, u32[]{:S(2)}, u32[]{:S(2)}) collective-permute-start(bf16[4,32,512]{2,1,0:T(8,128)(2,1)S(1)} %get-tuple-element.83), channel_id=1, source_target_pairs={{0,96},{32,64},{64,32},{96,0},{1,97},{33,65},{65,33},{97,1},{2,98}... | collective-permute-start | bytes 393224 | tf_op jit(solution)/shard_map/ppermute | solution.py:157
  138.7 5.5 %collective-permute-start.30 = (bf16[4,32,512]{2,1,0:T(8,128)(2,1)S(1)}, bf16[4,32,512]{2,1,0:T(8,128)(2,1)S(1)}, u32[]{:S(2)}, u32[]{:S(2)}) collective-permute-start(bf16[4,32,512]{2,1,0:T(8,128)(2,1)S(1)} %get-tuple-element.83), channel_id=1, source_target_pairs={{0,64},{32,96},{64,0},{96,32},{1,65},{33,97},{65,1},{97,33},{2,66}... | collective-permute-start | bytes 393224 | tf_op jit(solution)/shard_map/ppermute | solution.py:157
  145.1 10.0 %collective-permute-start.38 = (bf16[2,2,4,32,512]{4,3,2,1,0:T(8,128)(2,1)}, bf16[2,2,4,32,512]{4,3,2,1,0:T(8,128)(2,1)S(1)}, u32[]{:S(2)}, u32[]{:S(2)}) collective-permute-start(bf16[2,2,4,32,512]{4,3,2,1,0:T(8,128)(2,1)} %bitcast.20.piece0), channel_id=1, source_target_pairs={{0,64},{32,96},{64,0},{96,32},{1,65},{33,97},{65,1},{97,33},{2,66}... | collective-permute-start | bytes 1572872 | tf_op jit(solution)/shard_map/ppermute | solution.py:283
  146.5 18.3 %collective-permute-start.37 = (bf16[2,2,4,32,512]{4,3,2,1,0:T(8,128)(2,1)}, bf16[2,2,4,32,512]{4,3,2,1,0:T(8,128)(2,1)}, u32[]{:S(2)}, u32[]{:S(2)}) collective-permute-start(bf16[2,2,4,32,512]{4,3,2,1,0:T(8,128)(2,1)} %bitcast.25.piece0), channel_id=1, source_target_pairs={{0,128},{16,144},{128,0},{144,16},{1,129},{17,145},{129,1},{145,17... | collective-permute-start | bytes 1572872 | tf_op jit(solution)/shard_map/ppermute | solution.py:284
  147.3 22.3 %collective-permute-start.36 = (bf16[2,2,4,32,512]{4,3,2,1,0:T(8,128)(2,1)}, bf16[2,2,4,32,512]{4,3,2,1,0:T(8,128)(2,1)}, u32[]{:S(2)}, u32[]{:S(2)}) collective-permute-start(bf16[2,2,4,32,512]{4,3,2,1,0:T(8,128)(2,1)} %bitcast.20.piece0), channel_id=1, source_target_pairs={{0,96},{32,64},{64,32},{96,0},{1,97},{33,65},{65,33},{97,1},{2,98}... | collective-permute-start | bytes 1572872 | tf_op jit(solution)/shard_map/ppermute | solution.py:283
  149.5 20.1 %collective-permute-start.35 = (bf16[2,2,4,32,512]{4,3,2,1,0:T(8,128)(2,1)}, bf16[2,2,4,32,512]{4,3,2,1,0:T(8,128)(2,1)}, u32[]{:S(2)}, u32[]{:S(2)}) collective-permute-start(bf16[2,2,4,32,512]{4,3,2,1,0:T(8,128)(2,1)} %bitcast.20.piece0), channel_id=1, source_target_pairs={{0,32},{32,0},{64,96},{96,64},{1,33},{33,1},{65,97},{97,65},{2,34}... | collective-permute-start | bytes 1572872 | tf_op jit(solution)/shard_map/ppermute | solution.py:283
  149.5 23.1 %collective-permute-start.34 = (bf16[2,2,4,32,512]{4,3,2,1,0:T(8,128)(2,1)}, bf16[2,2,4,32,512]{4,3,2,1,0:T(8,128)(2,1)}, u32[]{:S(2)}, u32[]{:S(2)}) collective-permute-start(bf16[2,2,4,32,512]{4,3,2,1,0:T(8,128)(2,1)} %bitcast.25.piece0), channel_id=1, source_target_pairs={{0,144},{16,128},{128,16},{144,0},{1,145},{17,129},{129,17},{145,1... | collective-permute-start | bytes 1572872 | tf_op jit(solution)/shard_map/ppermute | solution.py:284
  155.9 16.7 %collective-permute-start.33 = (bf16[2,2,4,32,512]{4,3,2,1,0:T(8,128)(2,1)}, bf16[2,2,4,32,512]{4,3,2,1,0:T(8,128)(2,1)}, u32[]{:S(2)}, u32[]{:S(2)}) collective-permute-start(bf16[2,2,4,32,512]{4,3,2,1,0:T(8,128)(2,1)} %bitcast.25.piece0), channel_id=1, source_target_pairs={{0,16},{16,0},{128,144},{144,128},{1,17},{17,1},{129,145},{145,129... | collective-permute-start | bytes 1572872 | tf_op jit(solution)/shard_map/ppermute | solution.py:284
  175.6 12.5 %collective-permute-start.39 = (f32[384,512]{1,0:T(8,128)S(1)}, f32[384,512]{1,0:T(8,128)S(1)}, u32[]{:S(2)}, u32[]{:S(2)}) collective-permute-start(f32[384,512]{1,0:T(8,128)S(1)} %get-tuple-element.94), channel_id=1, source_target_pairs={{0,1},{1,0},{2,3},{3,2},{4,5},{5,4},{6,7},{7,6},{8,9},{9,8},{10,11... | collective-permute-start | bytes 2359304 | tf_op jit(solution)/shard_map/ppermute | solution.py:318
  (32 other events, 193.7 us)

commit v4 on v3

--- a/solution.py
+++ b/solution.py
@@ -25,8 +25,21 @@
 ZH = 4
 GR = 32
 SWAP = [(0, 1), (1, 0)]
-TURN = [(0, 0), (1, 2), (2, 1), (3, 3)]
-FAR_TURN = [(d + 4 * q, e + 4 * (1 - q)) for q in range(2) for d, e in TURN]
+
+
+def reverse_bits(z):
+    return (z & 1) * 4 + (z & 2) + (z // 4)
+
+
+TURN = [
+    ((y * ZN + z) * 2 + c, (c * ZN + reverse_bits(z)) * 2 + y)
+    for y in range(2)
+    for z in range(ZN)
+    for c in range(2)
+]
+FAR_TURN = [(d + 32 * q, e + 32 * (1 - q)) for q in range(2) for d, e in TURN]
+TURNED = ("y1", "z", "core")
+LINE_STEP = {1: 4, 2: 2, 3: 6}
 
 
 def cols_at(part, step):
@@ -78,12 +91,25 @@
     away[...] += jnp.dot(tok2[...], h, preferred_element_type=f32)
 
 
-def second_sum_kernel(*refs):
-    out = refs[-1]
-    for part in range(2):
-        own, first, second, third = refs[4 * part : 4 * part + 4]
-        total = own[...] + first[...].astype(f32) + second[...].astype(f32)
-        out[ZH * part : ZH * part + ZH] = (total + third[...].astype(f32)).astype(out.dtype)
+def second_sum_kernel(pos, *refs):
+    ins, (keep, send) = refs[:8], refs[8:]
+    a_sum, b_sum = [
+        ins[n][...] + sum(ins[n + k][...].astype(f32) for k in (1, 2, 3)) for n in (0, 4)
+    ]
+    upper = pos[5] >= ZH
+    keep[...] = jnp.where(upper, b_sum, a_sum)
+    send[...] = jnp.where(upper, a_sum, b_sum).astype(bf16)
+
+
+def third_sum_kernel(pos, keep, got, *outs):
+    for k in range(4):
+        block = (pos[5] % ZH) ^ k
+        outs[k][...] = (keep[block] + got[block].astype(f32)).astype(outs[k].dtype)
+
+
+def line_kernel(pos, *refs):
+    for k in range(4):
+        refs[4][(pos[5] % ZH) ^ k] = refs[k][...]
 
 
 def row_moment_of(moment, squares):
@@ -91,14 +117,16 @@
     return decay_rate * moment + (1.0 - decay_rate) * (mean + tiny_square)
 
 
-def stats_kernel(gz, packed, stats, scaled):
-    hidden = gz.shape[-1]
+def stats_kernel(pos, near_half, far_half, packed, stats, scaled):
+    hidden = near_half.shape[-1]
+    upper = pos[5] >= ZH
     cols = jnp.zeros((GR, hidden), f32)
     scaled_cols = jnp.zeros((GR, hidden), f32)
     weights = jnp.zeros((GR, hidden), f32)
     row_total = jnp.zeros((GR, 1), f32)
     for z in range(ZN):
-        g = gz[z].astype(f32)
+        near, far = near_half[z % ZH].astype(f32), far_half[z % ZH].astype(f32)
+        g = jnp.where(upper, far, near) if z < ZH else jnp.where(upper, near, far)
         squares = g * g
         rows = row_moment_of(packed[z, :, hidden : hidden + 1], squares)
         u = g * lax.rsqrt(rows)
@@ -165,11 +193,12 @@
     tok_rows, width = tokens.shape
     hidden = cotangent.shape[1]
     seg = width // 16
-    cuts, y1, y0, xlo, _, core = [lax.axis_index(a) for a in AXES]
-    pos = jnp.stack([core, y1, y0, xlo, cuts]).astype(jnp.int32)
-    params = pltpu.CompilerParams(vmem_limit_bytes=32 * 2**20)
+    cuts, y1, y0, xlo, z, core = [lax.axis_index(a) for a in AXES]
+    pos = jnp.stack([core, y1, y0, xlo, cuts, reverse_bits(z)]).astype(jnp.int32)
+    params = pltpu.CompilerParams(vmem_limit_bytes=12 * 2**20)
+    small = pltpu.CompilerParams(vmem_limit_bytes=6 * 2**20)
     cost = pl.CostEstimate(
-        flops=4 * tok_rows * 2 * seg * hidden, bytes_accessed=4 * 2**20, transcendentals=0
+        flops=64 * tok_rows * seg * hidden, bytes_accessed=16 * 2**20, transcendentals=0
     )
     piece = (2, 2, ZH, GR, hidden)
     whole = pl.BlockSpec((tok_rows, hidden), lambda g, pos: (0, 0))
@@ -201,7 +230,7 @@
                 ],
                 out_specs=pl.BlockSpec((tok_rows, seg), lambda g, pos: (0, g)),
             ),
-            compiler_params=params,
+            compiler_params=small,
         )(pos, tokens)
         tokens2[part, step] = lax.ppermute(away_cols, "core", SWAP)
 
@@ -210,9 +239,9 @@
     packed = jnp.concatenate(
         [my_weight, jnp.broadcast_to(my_moment[:, None], (32, 128))], axis=1
     )
-    packed = lax.ppermute(packed, ("y1", "core"), TURN)
-
+    packed = lax.ppermute(packed, TURNED, TURN)
     tokens2, cotangent2 = lax.optimization_barrier((tokens2, cotangent2))
+
     parts, chain = {}, pos
     for part, step in order:
         kept = jax.ShapeDtypeStruct(piece, bf16 if step else f32)
@@ -229,13 +258,15 @@
             cost_estimate=cost,
         )(chain, tokens, tokens2[part, step], cotangent, cotangent2)
         chain, _ = lax.optimization_barrier((pos, parts[part, 2 + step]))
-    packed, parts[1, 3] = lax.optimization_barrier((packed, parts[1, 3]))
-    packed = lax.all_to_all(
-        jnp.broadcast_to(packed[None], (ZN,) + packed.shape), "z", 0, 0, tiled=True
-    )
-
     a_parts, b_parts = [[parts[p, k] for k in range(4)] for p in range(2)]
     a_got, b_got = exchange(a_parts, Y), exchange(b_parts, X)
+    a_got, packed = lax.optimization_barrier((a_got, packed))
+    packed = lax.psum(
+        lax.dynamic_update_slice_in_dim(
+            jnp.zeros((ZN,) + packed.shape, f32), packed[None], pos[5], axis=0
+        ),
+        "z",
+    )
     a_sum = a_parts[0] + sum(p.astype(f32) for p in a_got)
     b_sum = b_parts[0] + sum(p.astype(f32) for p in b_got)
 
@@ -243,25 +274,47 @@
     b_parts = [b_sum[k % 2, k // 2] for k in range(4)]
     a_got = exchange([p.astype(bf16) for p in a_parts], X)
     b_got = exchange([p.astype(bf16) for p in b_parts], Y)
-    b_got, packed = lax.optimization_barrier((b_got, packed))
-    line = (ZN, GR, hidden)
-    both = pl.pallas_call(
-        second_sum_kernel, out_shape=jax.ShapeDtypeStruct(line, bf16), compiler_params=params
-    )(a_parts[0], *a_got, b_parts[0], *b_got)
-
-    g32 = jnp.sum(lax.all_to_all(both, "z", 0, 0, tiled=True).astype(f32), axis=0)
-
-    near = lax.ppermute(g32, ("y1", "core"), TURN)
-    far = lax.ppermute(g32, ("cuts", "y1", "core"), FAR_TURN)
-
-    gz = lax.all_to_all(jnp.broadcast_to(g32.astype(bf16)[None], line), "z", 0, 0, tiled=True)
-    gz, near, far = lax.optimization_barrier((gz, near, far))
+    line, part_line, block = (ZN, GR, hidden), (ZH, GR, hidden), (GR, hidden)
+    in_specs = lambda n: [pl.BlockSpec(memory_space=pltpu.SMEM)] + [
+        pl.BlockSpec(memory_space=pltpu.VMEM)
+    ] * n
+    keep, send = pl.pallas_call(
+        second_sum_kernel,
+        out_shape=[jax.ShapeDtypeStruct(part_line, f32), jax.ShapeDtypeStruct(part_line, bf16)],
+        in_specs=in_specs(8),
+        compiler_params=small,
+    )(pos, a_parts[0], *a_got, b_parts[0], *b_got)
+
+    got = lax.ppermute(send, "z", xor_perm(ZN, 1))
+    blocks = pl.pallas_call(
+        third_sum_kernel,
+        out_shape=[jax.ShapeDtypeStruct(block, f32)] + [jax.ShapeDtypeStruct(block, bf16)] * 3,
+        in_specs=in_specs(2),
+        compiler_params=small,
+    )(pos, keep, got)
+    got = [lax.ppermute(blocks[k], "z", xor_perm(ZN, LINE_STEP[k])) for k in (1, 2, 3)]
+    g32 = blocks[0] + sum(p.astype(f32) for p in got)
+
+    near = lax.ppermute(g32, TURNED, TURN)
+    far = lax.ppermute(g32, ("cuts",) + TURNED, FAR_TURN)
+
+    g16 = g32.astype(bf16)
+    got = [lax.ppermute(g16, "z", xor_perm(ZN, LINE_STEP[k])) for k in (1, 2, 3)]
+    near_half = pl.pallas_call(
+        line_kernel,
+        out_shape=jax.ShapeDtypeStruct(part_line, bf16),
+        in_specs=in_specs(4),
+        compiler_params=small,
+    )(pos, g16, *got)
+    far_half = lax.ppermute(near_half, "z", xor_perm(ZN, 1))
+    far_half, near, far, packed = lax.optimization_barrier((far_half, near, far, packed))
 
     stats, scaled = pl.pallas_call(
         stats_kernel,
         out_shape=[jax.ShapeDtypeStruct((8, hidden), f32), jax.ShapeDtypeStruct(line, f32)],
-        compiler_params=params,
-    )(gz, packed)
+        in_specs=in_specs(3),
+        compiler_params=small,
+    )(pos, near_half, far_half, packed)
     stats = stats + lax.ppermute(stats, "core", SWAP)
     stats = four_sum(stats, exchange([stats] * 4, Y))
     stats = four_sum(stats, exchange([stats] * 4, X))
@@ -270,7 +323,7 @@
     a_half, b_half, cols_new, inv_cols = pl.pallas_call(
         functools.partial(rows_kernel, width),
         out_shape=[jax.ShapeDtypeStruct((ZH, GR, hidden), bf16)] * 2 + [row_vector] * 2,
-        compiler_params=params,
+        compiler_params=small,
     )(stats, col_moment.reshape(1, hidden), packed, scaled)
     a_all = [a_half] + exchange([a_half] * 4, X)
     b_all = [b_half] + exchange([b_half] * 4, Y)
@@ -289,9 +342,8 @@
     new_weight, delta, rows_new = pl.pallas_call(
         return_kernel,
         out_shape=[slab, slab, jax.ShapeDtypeStruct((weight.shape[0], 1), f32)],
-        in_specs=[pl.BlockSpec(memory_space=pltpu.SMEM)]
-        + [pl.BlockSpec(memory_space=pltpu.VMEM)] * 5,
-        compiler_params=params,
+        in_specs=in_specs(5),
+        compiler_params=small,
     )(pos, near, far, weight, row_moment[:, None], inv_cols)
     a_all[2], _ = lax.optimization_barrier((a_all[2], rows_new))
 

time: 192 us -> 237 us (1.23)
  waiting for transfers between devices: 36.3 us -> 85.3 us
  blocking collectives: 14.5 us -> 0 us
  between operations: 0.97 us -> 14.4 us
  starting transfers between devices: 77.5 us -> 84.5 us
  other arithmetic: 8.71 us -> 2.38 us
  local copies, waits for them, and re-layouts: 21.4 us -> 15.2 us
  Pallas kernels: 29.7 us -> 33.2 us
    ppermute x3 -> x11, starting transfers between devices: 14.3 us -> 35.9 us  [the longest x1 10.2 us: on_device(): packed = lax.ppermute(packed, TURNED, TURN)]
    ppermute x24, waiting for transfers between devices: 17.9 us -> 39.2 us  [exchange(): return [lax.ppermute(pieces[k], axes, xor_perm(4, k)) for k in (1, 2, 3)]]
    psum x0 -> x1, waiting for transfers between devices: none -> 14.9 us  [on_device(): lax.psum(lax.dynamic_update_slice_in_dim(jnp.zeros((ZN,) + packed.shape,...]
    all_to_all x1 -> x0, blocking collectives: 14.5 us -> none  [on_device(): lax.all_to_all(both, 'z', 0, 0, tiled=True).astype(f32)]
    all_to_all x2 -> x0, starting transfers between devices: 12.7 us -> none  [the longest x1 8.01 us: on_device(): lax.all_to_all(jnp.broadcast_to(packed[None], (ZN,) + packed.shape), 'z',...]
    ppermute x3 -> x11, waiting for transfers between devices: 8.07 us -> 19.4 us  [the longest x1 8.94 us: on_device(): far = lax.ppermute(g32, ('cuts',) + TURNED, FAR_TURN)]
    ppermute x1, starting transfers between devices: 0.09 us -> 5.64 us  [on_device(): stats = stats + lax.ppermute(stats, 'core', SWAP)]
    unnamed x44 -> x22, local copies, waits for them, and re-layouts: 17.9 us -> 13.2 us
  transfers between devices with their start and end apart: 42 -> 49, of which waited for: 17 -> 28; matrix products, arithmetic and copies ran while one was open for 4% -> 1% of each run, Pallas kernels for 11% -> 12%
where the time goes in v4:
time: 237 us; the launch traced here: 235 us
  waiting for transfers between devices  85.3 us (36%)
  starting transfers between devices  84.5 us (36%)
  Pallas kernels  33.2 us (14%)
  local copies, waits for them, and re-layouts  15.2 us (6%)
  between operations  14.4 us (6%)
  other arithmetic  2.38 us (1%)
    ppermute x24, waiting for transfers between devices, exchange(): return [lax.ppermute(pieces[k], axes, xor_perm(4, k)) for k in (1, 2, 3)]  39.2 us
    ppermute x24, starting transfers between devices, exchange(): return [lax.ppermute(pieces[k], axes, xor_perm(4, k)) for k in (1, 2, 3)]  26.6 us
    psum x1, waiting for transfers between devices, on_device(): lax.psum(lax.dynamic_update_slice_in_dim(jnp.zeros((ZN,) + packed.shape,...  14.9 us
    pallas_call x4, Pallas kernels, on_device(): pl.pallas_call(functools.partial(grad_kernel, part), out_shape=[kept, jax...  13.5 us
    unnamed x22, local copies, waits for them, and re-layouts  13.2 us
    pallas_call x4, Pallas kernels, on_device(): pl.pallas_call(functools.partial(apply_kernel, part), out_shape=[result,...  11.8 us
    ppermute x1, starting transfers between devices, on_device(): packed = lax.ppermute(packed, TURNED, TURN)  10.2 us
    ppermute x1, starting transfers between devices, on_device(): near = lax.ppermute(g32, TURNED, TURN)  9.46 us
  transfers between devices with their start and end apart: 49, of which 28 were waited for; matrix products, arithmetic and copies ran while one was open for 1% of the time, Pallas kernels for 12%

profile of v4, /device:TPU:33, one launch (start us, length us, event | category | flops | bytes accessed | tf_op | source)
XLA Modules:
  0.0 235.0 jit_solution(365740581042209058)
XLA Ops:
  7.3 2.8 %copy-done = bf16[384,8192]{1,0:T(8,128)(2,1)S(1)} copy-done((bf16[384,8192]{1,0:T(8,128)(2,1)S(1)}, bf16[384,8192]{1,0:T(8,128)(2,1)}, u32[]{:S(2)}) %copy-start) | copy-done | bytes 6291480
  18.1 10.2 %collective-permute-start.8 = (f32[32,640]{1,0:T(8,128)S(1)}, f32[32,640]{1,0:T(8,128)S(1)}, u32[]{:S(2)}, u32[]{:S(2)}) collective-permute-start(f32[32,640]{1,0:T(8,128)S(1)} %pad_maximum_fusion.2), channel_id=1, source_target_pairs={{0,0},{1,64},{2,8},{3,72},{4,4},{5,68},{6,12},{7,76},{8,2},{9,66},... | collective-permute-start | bytes 245768 | tf_op jit(solution)/shard_map/ppermute | solution.py:242
  28.3 2.8 %copy-done.1 = bf16[384,8192]{1,0:T(8,128)(2,1)S(1)} copy-done((bf16[384,8192]{1,0:T(8,128)(2,1)S(1)}, bf16[384,8192]{1,0:T(8,128)(2,1)}, u32[]{:S(2)}) %copy-start.1) | copy-done | bytes 6291480
  31.1 3.4 %shard_map.96 = (f32[2,2,4,32,512]{4,3,2,1,0:T(8,128)S(1)}, bf16[2,2,4,32,512]{4,3,2,1,0:T(8,128)(2,1)S(1)}) custom-call(s32[6]{0:T(128)S(1)} %stack.57.pos, bf16[384,8192]{1,0:T(8,128)(2,1)S(1)} %copy-done.1, bf16[384,1024]{1,0:T(8,128)(2,1)} %collective-permute-done.tok2, bf16[384,512]{1,0:T(8,128)(2,1)} %cot.7, bf16[384,512]{1,0:T(8,128)(2,1)} %collective-permute-done.4.cot2), custom_call_target="tpu_custom_call" | custom-call | flops 6442450944 | bytes 16777216 | tf_op jit(solution)/shard_map/pallas_call | solution.py:248
  34.8 3.4 %shard_map.97 = (f32[2,2,4,32,512]{4,3,2,1,0:T(8,128)S(1)}, bf16[2,2,4,32,512]{4,3,2,1,0:T(8,128)(2,1)S(1)}) custom-call(s32[6]{0:T(128)S(1)} %stack.57.pos, bf16[384,8192]{1,0:T(8,128)(2,1)S(1)} %copy-done.1, bf16[384,1024]{1,0:T(8,128)(2,1)} %collective-permute-done.2.tok2, bf16[384,512]{1,0:T(8,128)(2,1)} %cot.7, bf16[384,512]{1,0:T(8,128)(2,1)} %collective-permute-done.4.cot2), custom_call_target="tpu_custom_call" | custom-call | flops 6442450944 | bytes 16777216 | tf_op jit(solution)/shard_map/pallas_call | solution.py:248
  38.1 3.4 %shard_map.98 = (bf16[2,2,4,32,512]{4,3,2,1,0:T(8,128)(2,1)S(1)}, bf16[2,2,4,32,512]{4,3,2,1,0:T(8,128)(2,1)S(1)}) custom-call(s32[6]{0:T(128)S(1)} %stack.57.pos, bf16[384,8192]{1,0:T(8,128)(2,1)S(1)} %copy-done.1, bf16[384,1024]{1,0:T(8,128)(2,1)} %collective-permute-done.1.tok2, bf16[384,512]{1,0:T(8,128)(2,1)} %cot.7, ...), custom_call_target="tpu_custom_call" | custom-call | flops 6442450944 | bytes 16777216 | tf_op jit(solution)/shard_map/pallas_call | solution.py:248
  41.5 2.7 %collective-permute-start.7 = (bf16[2,2,4,32,512]{4,3,2,1,0:T(8,128)(2,1)S(1)}, bf16[2,2,4,32,512]{4,3,2,1,0:T(8,128)(2,1)S(1)}, u32[]{:S(2)}, u32[]{:S(2)}) collective-permute-start(bf16[2,2,4,32,512]{4,3,2,1,0:T(8,128)(2,1)S(1)} %get-tuple-element.65), channel_id=1, source_target_pairs={{0,96},{32,64},{64,32},{96,0},{1,97},{33,65},{65,33},{97,1},{2,98}... | collective-permute-start | bytes 1572872 | tf_op jit(solution)/shard_map/ppermute | solution.py:185
  44.2 2.7 %collective-permute-start.13 = (bf16[2,2,4,32,512]{4,3,2,1,0:T(8,128)(2,1)S(1)}, bf16[2,2,4,32,512]{4,3,2,1,0:T(8,128)(2,1)S(1)}, u32[]{:S(2)}, u32[]{:S(2)}) collective-permute-start(bf16[2,2,4,32,512]{4,3,2,1,0:T(8,128)(2,1)S(1)} %get-tuple-element.61), channel_id=1, source_target_pairs={{0,128},{16,144},{128,0},{144,16},{1,129},{17,145},{129,1},{145,17... | collective-permute-start | bytes 1572872 | tf_op jit(solution)/shard_map/ppermute | solution.py:185
  47.0 3.4 %shard_map.99 = (bf16[2,2,4,32,512]{4,3,2,1,0:T(8,128)(2,1)S(1)}, bf16[2,2,4,32,512]{4,3,2,1,0:T(8,128)(2,1)S(1)}) custom-call(s32[6]{0:T(128)S(1)} %stack.57.pos, bf16[384,8192]{1,0:T(8,128)(2,1)S(1)} %copy-done.1, bf16[384,1024]{1,0:T(8,128)(2,1)} %collective-permute-done.3.tok2, bf16[384,512]{1,0:T(8,128)(2,1)} %cot.7, ...), custom_call_target="tpu_custom_call" | custom-call | flops 6442450944 | bytes 16777216 | tf_op jit(solution)/shard_map/pallas_call | solution.py:248
  50.8 10.1 %collective-permute-done.5 = bf16[2,2,4,32,512]{4,3,2,1,0:T(8,128)(2,1)S(1)} collective-permute-done((bf16[2,2,4,32,512]{4,3,2,1,0:T(8,128)(2,1)S(1)}, bf16[2,2,4,32,512]{4,3,2,1,0:T(8,128)(2,1)S(1)}, u32[]{:S(2)}, u32[]{:S(2)}) %collective-permute-start.5) | collective-permute-done | bytes 524320 | tf_op jit(solution)/shard_map/ppermute | solution.py:185
  64.7 6.3 %collective-permute-done.12 = bf16[2,2,4,32,512]{4,3,2,1,0:T(8,128)(2,1)S(1)} collective-permute-done((bf16[2,2,4,32,512]{4,3,2,1,0:T(8,128)(2,1)S(1)}, bf16[2,2,4,32,512]{4,3,2,1,0:T(8,128)(2,1)S(1)}, u32[]{:S(2)}, u32[]{:S(2)}) %collective-permute-start.12) | collective-permute-done | bytes 524320 | tf_op jit(solution)/shard_map/ppermute | solution.py:185
  72.2 5.9 %collective-permute-done.14 = bf16[2,2,4,32,512]{4,3,2,1,0:T(8,128)(2,1)S(1)} collective-permute-done((bf16[2,2,4,32,512]{4,3,2,1,0:T(8,128)(2,1)S(1)}, bf16[2,2,4,32,512]{4,3,2,1,0:T(8,128)(2,1)S(1)}, u32[]{:S(2)}, u32[]{:S(2)}) %collective-permute-start.14) | collective-permute-done | bytes 524320 | tf_op jit(solution)/shard_map/ppermute | solution.py:185
  80.2 3.8 %collective-permute-start.17 = (bf16[4,32,512]{2,1,0:T(8,128)(2,1)}, bf16[4,32,512]{2,1,0:T(8,128)(2,1)S(1)}, u32[]{:S(2)}, u32[]{:S(2)}) collective-permute-start(bf16[4,32,512]{2,1,0:T(8,128)(2,1)} %get-tuple-element.111), channel_id=1, source_target_pairs={{0,96},{32,64},{64,32},{96,0},{1,97},{33,65},{65,33},{97,1},{2,98}... | collective-permute-start | bytes 393224 | tf_op jit(solution)/shard_map/ppermute | solution.py:185
  86.1 3.1 %collective-permute-done.17.refs_7_ = bf16[4,32,512]{2,1,0:T(8,128)(2,1)S(1)} collective-permute-done((bf16[4,32,512]{2,1,0:T(8,128)(2,1)}, bf16[4,32,512]{2,1,0:T(8,128)(2,1)S(1)}, u32[]{:S(2)}, u32[]{:S(2)}) %collective-permute-start.17) | collective-permute-done | bytes 131104 | tf_op jit(solution)/shard_map/ppermute | solution.py:185
  90.0 3.8 %collective-permute-done.18.got = bf16[4,32,512]{2,1,0:T(8,128)(2,1)S(1)} collective-permute-done((bf16[4,32,512]{2,1,0:T(8,128)(2,1)S(1)}, bf16[4,32,512]{2,1,0:T(8,128)(2,1)S(1)}, u32[]{:S(2)}, u32[]{:S(2)}) %collective-permute-start.18) | collective-permute-done | bytes 131104 | tf_op jit(solution)/shard_map/ppermute | solution.py:288
  97.2 3.0 %collective-permute-start.21 = (bf16[32,512]{1,0:T(8,128)(2,1)S(1)}, bf16[32,512]{1,0:T(8,128)(2,1)S(1)}, u32[]{:S(2)}, u32[]{:S(2)}) collective-permute-start(bf16[32,512]{1,0:T(8,128)(2,1)S(1)} %get-tuple-element.79), channel_id=1, source_target_pairs={{0,12},{2,14},{4,8},{6,10},{8,4},{10,6},{12,0},{14,2},{1,13},{3,15... | collective-permute-start | bytes 98312 | tf_op jit(solution)/shard_map/ppermute | solution.py:295
  103.0 3.8 %collective-permute-start.22 = (bf16[32,512]{1,0:T(8,128)(2,1)S(1)}, bf16[32,512]{1,0:T(8,128)(2,1)S(1)}, u32[]{:S(2)}, u32[]{:S(2)}) collective-permute-start(bf16[32,512]{1,0:T(8,128)(2,1)S(1)} %get-tuple-element.105.refs_0_), channel_id=1, source_target_pairs={{0,8},{2,10},{4,12},{6,14},{8,0},{10,2},{12,4},{14,6},{1,9},{3,11}... | collective-permute-start | bytes 98312 | tf_op jit(solution)/shard_map/ppermute | solution.py:302
  115.2 9.5 %collective-permute-start.26 = (f32[32,512]{1,0:T(8,128)S(1)}, f32[32,512]{1,0:T(8,128)S(1)}, u32[]{:S(2)}, u32[]{:S(2)}) collective-permute-start(f32[32,512]{1,0:T(8,128)S(1)} %get-tuple-element.106), channel_id=1, source_target_pairs={{0,0},{1,64},{2,8},{3,72},{4,4},{5,68},{6,12},{7,76},{8,2},{9,66},... | collective-permute-start | bytes 196616 | tf_op jit(solution)/shard_map/ppermute | solution.py:298
  124.7 2.6 %collective-permute-start.27 = (f32[32,512]{1,0:T(8,128)S(1)}, f32[32,512]{1,0:T(8,128)S(1)}, u32[]{:S(2)}, u32[]{:S(2)}) collective-permute-start(f32[32,512]{1,0:T(8,128)S(1)} %get-tuple-element.106), channel_id=1, source_target_pairs={{0,128},{1,192},{2,136},{3,200},{4,132},{5,196},{6,140},{7,204},{8... | collective-permute-start | bytes 196616 | tf_op jit(solution)/shard_map/ppermute | solution.py:299
  127.3 8.9 %collective-permute-done.27.far = f32[32,512]{1,0:T(8,128)S(1)} collective-permute-done((f32[32,512]{1,0:T(8,128)S(1)}, f32[32,512]{1,0:T(8,128)S(1)}, u32[]{:S(2)}, u32[]{:S(2)}) %collective-permute-start.27) | collective-permute-done | bytes 65568 | tf_op jit(solution)/shard_map/ppermute | solution.py:299
  136.3 14.9 %all-reduce.2.cloned.1.call-done.packed = f32[8,32,640]{2,1,0:T(8,128)} async-done(((f32[8,32,640]{2,1,0:T(8,128)}), f32[8,32,640]{2,1,0:T(8,128)}) %all-reduce.2.cloned.1.call-update) | async-done | bytes 655376 | tf_op jit(solution)/shard_map/psum | solution.py:264
  153.2 5.6 %collective-permute-start.28 = (f32[8,512]{1,0:T(8,128)S(1)}, f32[8,512]{1,0:T(8,128)S(1)}, u32[]{:S(2)}, u32[]{:S(2)}) collective-permute-start(f32[8,512]{1,0:T(8,128)S(1)} %get-tuple-element.85), channel_id=1, source_target_pairs={{0,1},{1,0},{2,3},{3,2},{4,5},{5,4},{6,7},{7,6},{8,9},{9,8},{10,11... | collective-permute-start | bytes 49160 | tf_op jit(solution)/shard_map/ppermute | solution.py:318
  159.6 2.7 %collective-permute-start.29 = (f32[8,512]{1,0:T(8,128)S(1)}, f32[8,512]{1,0:T(8,128)S(1)}, u32[]{:S(2)}, u32[]{:S(2)}) collective-permute-start(f32[8,512]{1,0:T(8,128)S(1)} %add.80), channel_id=1, source_target_pairs={{0,64},{32,96},{64,0},{96,32},{1,65},{33,97},{65,1},{97,33},{2,66}... | collective-permute-start | bytes 49160 | tf_op jit(solution)/shard_map/ppermute | solution.py:185
  166.5 2.8 %collective-permute-start.32 = (f32[8,512]{1,0:T(8,128)S(1)}, f32[8,512]{1,0:T(8,128)S(1)}, u32[]{:S(2)}, u32[]{:S(2)}) collective-permute-start(f32[8,512]{1,0:T(8,128)S(1)} %add_add_fusion.4), channel_id=1, source_target_pairs={{0,128},{16,144},{128,0},{144,16},{1,129},{17,145},{129,1},{145,17... | collective-permute-start | bytes 49160 | tf_op jit(solution)/shard_map/ppermute | solution.py:185
  192.2 3.4 %collective-permute-done.46.piece1 = bf16[2,2,4,32,512]{4,3,2,1,0:T(8,128)(2,1)S(1)} collective-permute-done((bf16[2,2,4,32,512]{4,3,2,1,0:T(8,128)(2,1)S(1)}, bf16[2,2,4,32,512]{4,3,2,1,0:T(8,128)(2,1)S(1)}, u32[]{:S(2)}, u32[]{:S(2)}) %collective-permute-start.46) | collective-permute-done | bytes 524320 | tf_op jit(solution)/shard_map/ppermute | solution.py:336
  197.3 2.8 %copy-done.2 = bf16[384,8192]{1,0:T(8,128)(2,1)S(1)} copy-done((bf16[384,8192]{1,0:T(8,128)(2,1)S(1)}, bf16[384,8192]{1,0:T(8,128)(2,1)}, u32[]{:S(2)}) %copy-start.2) | copy-done | bytes 6291480
  201.1 3.0 %shard_map.106 = (f32[384,512]{1,0:T(8,128)S(1)}, f32[384,512]{1,0:T(8,128)S(1)}) custom-call(s32[6]{0:T(128)S(1)} %stack.57.pos, bf16[384,8192]{1,0:T(8,128)(2,1)S(1)} %copy-done.2, bf16[384,1024]{1,0:T(8,128)(2,1)} %collective-permute-done.tok2, bf16[2,2,4,32,512]{4,3,2,1,0:T(8,128)(2,1)S(1)} %bitcast.44, bf16[2,2,4,32,512]{4,3,2,1,0:T(8,128)(2,1)S(1)} %copy-done.8), custom_call_target="tpu_custom_call" | custom-call | flops 6442450944 | bytes 16777216 | tf_op jit(solution)/shard_map/pallas_call | solution.py:354
  204.1 3.0 %shard_map.107 = (f32[384,512]{1,0:T(8,128)S(1)}, f32[384,512]{1,0:T(8,128)S(1)}) custom-call(s32[6]{0:T(128)S(1)} %stack.57.pos, bf16[384,8192]{1,0:T(8,128)(2,1)S(1)} %copy-done.2, bf16[384,1024]{1,0:T(8,128)(2,1)} %collective-permute-done.2.tok2, bf16[2,2,4,32,512]{4,3,2,1,0:T(8,128)(2,1)S(1)} %bitcast.40, ...), custom_call_target="tpu_custom_call" | custom-call | flops 6442450944 | bytes 16777216 | tf_op jit(solution)/shard_map/pallas_call | solution.py:354
  207.1 3.7 %collective-permute-done.44.piece1 = bf16[2,2,4,32,512]{4,3,2,1,0:T(8,128)(2,1)S(1)} collective-permute-done((bf16[2,2,4,32,512]{4,3,2,1,0:T(8,128)(2,1)S(1)}, bf16[2,2,4,32,512]{4,3,2,1,0:T(8,128)(2,1)S(1)}, u32[]{:S(2)}, u32[]{:S(2)}) %collective-permute-start.44) | collective-permute-done | bytes 524320 | tf_op jit(solution)/shard_map/ppermute | solution.py:336
  210.8 3.0 %shard_map.108 = (f32[384,512]{1,0:T(8,128)S(1)}, f32[384,512]{1,0:T(8,128)S(1)}) custom-call(s32[6]{0:T(128)S(1)} %stack.57.pos, bf16[384,8192]{1,0:T(8,128)(2,1)S(1)} %copy-done.2, bf16[384,1024]{1,0:T(8,128)(2,1)} %collective-permute-done.1.tok2, bf16[2,2,4,32,512]{4,3,2,1,0:T(8,128)(2,1)S(1)} %collective-permute-done.43.piece0, ...), custom_call_target="tpu_custom_call" | custom-call | flops 6442450944 | bytes 16777216 | tf_op jit(solution)/shard_map/pallas_call | solution.py:354
  213.8 3.0 %shard_map.109 = (f32[384,512]{1,0:T(8,128)S(1)}, f32[384,512]{1,0:T(8,128)S(1)}) custom-call(s32[6]{0:T(128)S(1)} %stack.57.pos, bf16[384,8192]{1,0:T(8,128)(2,1)S(1)} %copy-done.2, bf16[384,1024]{1,0:T(8,128)(2,1)} %collective-permute-done.3.tok2, bf16[2,2,4,32,512]{4,3,2,1,0:T(8,128)(2,1)S(1)} %collective-permute-done.41.piece0, ...), custom_call_target="tpu_custom_call" | custom-call | flops 6442450944 | bytes 16777216 | tf_op jit(solution)/shard_map/pallas_call | solution.py:354
  216.7 8.6 %collective-permute-start.47 = (f32[384,512]{1,0:T(8,128)S(1)}, f32[384,512]{1,0:T(8,128)S(1)}, u32[]{:S(2)}, u32[]{:S(2)}) collective-permute-start(f32[384,512]{1,0:T(8,128)S(1)} %get-tuple-element.104), channel_id=1, source_target_pairs={{0,1},{1,0},{2,3},{3,2},{4,5},{5,4},{6,7},{7,6},{8,9},{9,8},{10,11... | collective-permute-start | bytes 2359304 | tf_op jit(solution)/shard_map/ppermute | solution.py:370
  (128 shorter events, 68.5 us)
Async XLA Ops:
  7.2 144.1 %all-reduce.2.cloned.1.call-start = ((), (), s32[]{:S(2)}) async-start(), calls=%async_computation | async-start | bytes 1310720 | tf_op jit(solution)/shard_map/psum | solution.py:264
  10.9 17.4 %collective-permute-start = (bf16[384,1024]{1,0:T(8,128)(2,1)S(1)}, bf16[384,1024]{1,0:T(8,128)(2,1)}, u32[]{:S(2)}, u32[]{:S(2)}) collective-permute-start(bf16[384,1024]{1,0:T(8,128)(2,1)S(1)} %shard_map.92), channel_id=1, source_target_pairs={{0,1},{1,0},{2,3},{3,2},{4,5},{5,4},{6,7},{7,6},{8,9},{9,8},{10,11... | collective-permute-start | bytes 2359304 | tf_op jit(solution)/shard_map/ppermute | solution.py:235
  12.5 15.8 %collective-permute-start.1 = (bf16[384,1024]{1,0:T(8,128)(2,1)S(1)}, bf16[384,1024]{1,0:T(8,128)(2,1)}, u32[]{:S(2)}, u32[]{:S(2)}) collective-permute-start(bf16[384,1024]{1,0:T(8,128)(2,1)S(1)} %shard_map.93), channel_id=1, source_target_pairs={{0,1},{1,0},{2,3},{3,2},{4,5},{5,4},{6,7},{7,6},{8,9},{9,8},{10,11... | collective-permute-start | bytes 2359304 | tf_op jit(solution)/shard_map/ppermute | solution.py:235
  13.4 14.9 %collective-permute-start.2 = (bf16[384,1024]{1,0:T(8,128)(2,1)S(1)}, bf16[384,1024]{1,0:T(8,128)(2,1)}, u32[]{:S(2)}, u32[]{:S(2)}) collective-permute-start(bf16[384,1024]{1,0:T(8,128)(2,1)S(1)} %shard_map.94), channel_id=1, source_target_pairs={{0,1},{1,0},{2,3},{3,2},{4,5},{5,4},{6,7},{7,6},{8,9},{9,8},{10,11... | collective-permute-start | bytes 2359304 | tf_op jit(solution)/shard_map/ppermute | solution.py:235
  14.8 13.5 %collective-permute-start.3 = (bf16[384,1024]{1,0:T(8,128)(2,1)S(1)}, bf16[384,1024]{1,0:T(8,128)(2,1)}, u32[]{:S(2)}, u32[]{:S(2)}) collective-permute-start(bf16[384,1024]{1,0:T(8,128)(2,1)S(1)} %shard_map.95), channel_id=1, source_target_pairs={{0,1},{1,0},{2,3},{3,2},{4,5},{5,4},{6,7},{7,6},{8,9},{9,8},{10,11... | collective-permute-start | bytes 2359304 | tf_op jit(solution)/shard_map/ppermute | solution.py:235
  18.1 32.3 %collective-permute-start.8 = (f32[32,640]{1,0:T(8,128)S(1)}, f32[32,640]{1,0:T(8,128)S(1)}, u32[]{:S(2)}, u32[]{:S(2)}) collective-permute-start(f32[32,640]{1,0:T(8,128)S(1)} %pad_maximum_fusion.2), channel_id=1, source_target_pairs={{0,0},{1,64},{2,8},{3,72},{4,4},{5,68},{6,12},{7,76},{8,2},{9,66},... | collective-permute-start | bytes 245768 | tf_op jit(solution)/shard_map/ppermute | solution.py:242
  34.5 27.3 %collective-permute-start.6 = (bf16[2,2,4,32,512]{4,3,2,1,0:T(8,128)(2,1)S(1)}, bf16[2,2,4,32,512]{4,3,2,1,0:T(8,128)(2,1)S(1)}, u32[]{:S(2)}, u32[]{:S(2)}) collective-permute-start(bf16[2,2,4,32,512]{4,3,2,1,0:T(8,128)(2,1)S(1)} %get-tuple-element.58), channel_id=1, source_target_pairs={{0,64},{32,96},{64,0},{96,32},{1,65},{33,97},{65,1},{97,33},{2,66}... | collective-permute-start | bytes 1572872 | tf_op jit(solution)/shard_map/ppermute | solution.py:185
  41.5 20.2 %collective-permute-start.7 = (bf16[2,2,4,32,512]{4,3,2,1,0:T(8,128)(2,1)S(1)}, bf16[2,2,4,32,512]{4,3,2,1,0:T(8,128)(2,1)S(1)}, u32[]{:S(2)}, u32[]{:S(2)}) collective-permute-start(bf16[2,2,4,32,512]{4,3,2,1,0:T(8,128)(2,1)S(1)} %get-tuple-element.65), channel_id=1, source_target_pairs={{0,96},{32,64},{64,32},{96,0},{1,97},{33,65},{65,33},{97,1},{2,98}... | collective-permute-start | bytes 1572872 | tf_op jit(solution)/shard_map/ppermute | solution.py:185
  44.2 33.8 %collective-permute-start.13 = (bf16[2,2,4,32,512]{4,3,2,1,0:T(8,128)(2,1)S(1)}, bf16[2,2,4,32,512]{4,3,2,1,0:T(8,128)(2,1)S(1)}, u32[]{:S(2)}, u32[]{:S(2)}) collective-permute-start(bf16[2,2,4,32,512]{4,3,2,1,0:T(8,128)(2,1)S(1)} %get-tuple-element.61), channel_id=1, source_target_pairs={{0,128},{16,144},{128,0},{144,16},{1,129},{17,145},{129,1},{145,17... | collective-permute-start | bytes 1572872 | tf_op jit(solution)/shard_map/ppermute | solution.py:185
  47.0 13.9 %collective-permute-start.5 = (bf16[2,2,4,32,512]{4,3,2,1,0:T(8,128)(2,1)S(1)}, bf16[2,2,4,32,512]{4,3,2,1,0:T(8,128)(2,1)S(1)}, u32[]{:S(2)}, u32[]{:S(2)}) collective-permute-start(bf16[2,2,4,32,512]{4,3,2,1,0:T(8,128)(2,1)S(1)} %get-tuple-element.64), channel_id=1, source_target_pairs={{0,32},{32,0},{64,96},{96,64},{1,33},{33,1},{65,97},{97,65},{2,34}... | collective-permute-start | bytes 1572872 | tf_op jit(solution)/shard_map/ppermute | solution.py:185
  50.4 20.6 %collective-permute-start.12 = (bf16[2,2,4,32,512]{4,3,2,1,0:T(8,128)(2,1)S(1)}, bf16[2,2,4,32,512]{4,3,2,1,0:T(8,128)(2,1)S(1)}, u32[]{:S(2)}, u32[]{:S(2)}) collective-permute-start(bf16[2,2,4,32,512]{4,3,2,1,0:T(8,128)(2,1)S(1)} %get-tuple-element.72), channel_id=1, source_target_pairs={{0,16},{16,0},{128,144},{144,128},{1,17},{17,1},{129,145},{145,129... | collective-permute-start | bytes 1572872 | tf_op jit(solution)/shard_map/ppermute | solution.py:185
  60.9 17.2 %collective-permute-start.14 = (bf16[2,2,4,32,512]{4,3,2,1,0:T(8,128)(2,1)S(1)}, bf16[2,2,4,32,512]{4,3,2,1,0:T(8,128)(2,1)S(1)}, u32[]{:S(2)}, u32[]{:S(2)}) collective-permute-start(bf16[2,2,4,32,512]{4,3,2,1,0:T(8,128)(2,1)S(1)} %get-tuple-element.73), channel_id=1, source_target_pairs={{0,144},{16,128},{128,16},{144,0},{1,145},{17,129},{129,17},{145,1... | collective-permute-start | bytes 1572872 | tf_op jit(solution)/shard_map/ppermute | solution.py:185
  62.8 17.4 %collective-permute-start.10 = (bf16[4,32,512]{2,1,0:T(8,128)(2,1)}, bf16[4,32,512]{2,1,0:T(8,128)(2,1)S(1)}, u32[]{:S(2)}, u32[]{:S(2)}) collective-permute-start(bf16[4,32,512]{2,1,0:T(8,128)(2,1)} %get-tuple-element.115), channel_id=1, source_target_pairs={{0,128},{16,144},{128,0},{144,16},{1,129},{17,145},{129,1},{145,17... | collective-permute-start | bytes 393224 | tf_op jit(solution)/shard_map/ppermute | solution.py:185
  64.1 20.0 %collective-permute-start.11 = (bf16[4,32,512]{2,1,0:T(8,128)(2,1)}, bf16[4,32,512]{2,1,0:T(8,128)(2,1)S(1)}, u32[]{:S(2)}, u32[]{:S(2)}) collective-permute-start(bf16[4,32,512]{2,1,0:T(8,128)(2,1)} %get-tuple-element.114), channel_id=1, source_target_pairs={{0,144},{16,128},{128,16},{144,0},{1,145},{17,129},{129,17},{145,1... | collective-permute-start | bytes 393224 | tf_op jit(solution)/shard_map/ppermute | solution.py:185
  71.0 13.1 %collective-permute-start.9 = (bf16[4,32,512]{2,1,0:T(8,128)(2,1)}, bf16[4,32,512]{2,1,0:T(8,128)(2,1)S(1)}, u32[]{:S(2)}, u32[]{:S(2)}) collective-permute-start(bf16[4,32,512]{2,1,0:T(8,128)(2,1)} %get-tuple-element.116), channel_id=1, source_target_pairs={{0,16},{16,0},{128,144},{144,128},{1,17},{17,1},{129,145},{145,129... | collective-permute-start | bytes 393224 | tf_op jit(solution)/shard_map/ppermute | solution.py:185
  79.2 7.0 %collective-permute-start.16 = (bf16[4,32,512]{2,1,0:T(8,128)(2,1)}, bf16[4,32,512]{2,1,0:T(8,128)(2,1)S(1)}, u32[]{:S(2)}, u32[]{:S(2)}) collective-permute-start(bf16[4,32,512]{2,1,0:T(8,128)(2,1)} %get-tuple-element.112), channel_id=1, source_target_pairs={{0,64},{32,96},{64,0},{96,32},{1,65},{33,97},{65,1},{97,33},{2,66}... | collective-permute-start | bytes 393224 | tf_op jit(solution)/shard_map/ppermute | solution.py:185
  80.2 9.0 %collective-permute-start.17 = (bf16[4,32,512]{2,1,0:T(8,128)(2,1)}, bf16[4,32,512]{2,1,0:T(8,128)(2,1)S(1)}, u32[]{:S(2)}, u32[]{:S(2)}) collective-permute-start(bf16[4,32,512]{2,1,0:T(8,128)(2,1)} %get-tuple-element.111), channel_id=1, source_target_pairs={{0,96},{32,64},{64,32},{96,0},{1,97},{33,65},{65,33},{97,1},{2,98}... | collective-permute-start | bytes 393224 | tf_op jit(solution)/shard_map/ppermute | solution.py:185
  94.4 6.9 %collective-permute-start.19 = (bf16[32,512]{1,0:T(8,128)(2,1)S(1)}, bf16[32,512]{1,0:T(8,128)(2,1)S(1)}, u32[]{:S(2)}, u32[]{:S(2)}) collective-permute-start(bf16[32,512]{1,0:T(8,128)(2,1)S(1)} %get-tuple-element.77), channel_id=1, source_target_pairs={{0,8},{2,10},{4,12},{6,14},{8,0},{10,2},{12,4},{14,6},{1,9},{3,11}... | collective-permute-start | bytes 98312 | tf_op jit(solution)/shard_map/ppermute | solution.py:295
  97.2 5.8 %collective-permute-start.21 = (bf16[32,512]{1,0:T(8,128)(2,1)S(1)}, bf16[32,512]{1,0:T(8,128)(2,1)S(1)}, u32[]{:S(2)}, u32[]{:S(2)}) collective-permute-start(bf16[32,512]{1,0:T(8,128)(2,1)S(1)} %get-tuple-element.79), channel_id=1, source_target_pairs={{0,12},{2,14},{4,8},{6,10},{8,4},{10,6},{12,0},{14,2},{1,13},{3,15... | collective-permute-start | bytes 98312 | tf_op jit(solution)/shard_map/ppermute | solution.py:295
  103.0 6.8 %collective-permute-start.22 = (bf16[32,512]{1,0:T(8,128)(2,1)S(1)}, bf16[32,512]{1,0:T(8,128)(2,1)S(1)}, u32[]{:S(2)}, u32[]{:S(2)}) collective-permute-start(bf16[32,512]{1,0:T(8,128)(2,1)S(1)} %get-tuple-element.105.refs_0_), channel_id=1, source_target_pairs={{0,8},{2,10},{4,12},{6,14},{8,0},{10,2},{12,4},{14,6},{1,9},{3,11}... | collective-permute-start | bytes 98312 | tf_op jit(solution)/shard_map/ppermute | solution.py:302
  113.2 23.1 %collective-permute-start.25 = (bf16[4,32,512]{2,1,0:T(8,128)(2,1)S(1)}, bf16[4,32,512]{2,1,0:T(8,128)(2,1)S(1)}, u32[]{:S(2)}, u32[]{:S(2)}) collective-permute-start(bf16[4,32,512]{2,1,0:T(8,128)(2,1)S(1)} %shard_map.102.near_half), channel_id=1, source_target_pairs={{0,2},{2,0},{4,6},{6,4},{8,10},{10,8},{12,14},{14,12},{1,3},{3,1},... | collective-permute-start | bytes 393224 | tf_op jit(solution)/shard_map/ppermute | solution.py:309
  115.2 12.1 %collective-permute-start.26 = (f32[32,512]{1,0:T(8,128)S(1)}, f32[32,512]{1,0:T(8,128)S(1)}, u32[]{:S(2)}, u32[]{:S(2)}) collective-permute-start(f32[32,512]{1,0:T(8,128)S(1)} %get-tuple-element.106), channel_id=1, source_target_pairs={{0,0},{1,64},{2,8},{3,72},{4,4},{5,68},{6,12},{7,76},{8,2},{9,66},... | collective-permute-start | bytes 196616 | tf_op jit(solution)/shard_map/ppermute | solution.py:298
  124.7 11.6 %collective-permute-start.27 = (f32[32,512]{1,0:T(8,128)S(1)}, f32[32,512]{1,0:T(8,128)S(1)}, u32[]{:S(2)}, u32[]{:S(2)}) collective-permute-start(f32[32,512]{1,0:T(8,128)S(1)} %get-tuple-element.106), channel_id=1, source_target_pairs={{0,128},{1,192},{2,136},{3,200},{4,132},{5,196},{6,140},{7,204},{8... | collective-permute-start | bytes 196616 | tf_op jit(solution)/shard_map/ppermute | solution.py:299
  153.2 6.5 %collective-permute-start.28 = (f32[8,512]{1,0:T(8,128)S(1)}, f32[8,512]{1,0:T(8,128)S(1)}, u32[]{:S(2)}, u32[]{:S(2)}) collective-permute-start(f32[8,512]{1,0:T(8,128)S(1)} %get-tuple-element.85), channel_id=1, source_target_pairs={{0,1},{1,0},{2,3},{3,2},{4,5},{5,4},{6,7},{7,6},{8,9},{9,8},{10,11... | collective-permute-start | bytes 49160 | tf_op jit(solution)/shard_map/ppermute | solution.py:318
  175.9 5.8 %collective-permute-start.39 = (bf16[4,32,512]{2,1,0:T(8,128)(2,1)S(1)}, bf16[4,32,512]{2,1,0:T(8,128)(2,1)S(1)}, u32[]{:S(2)}, u32[]{:S(2)}) collective-permute-start(bf16[4,32,512]{2,1,0:T(8,128)(2,1)S(1)} %get-tuple-element.93), channel_id=1, source_target_pairs={{0,32},{32,0},{64,96},{96,64},{1,33},{33,1},{65,97},{97,65},{2,34}... | collective-permute-start | bytes 393224 | tf_op jit(solution)/shard_map/ppermute | solution.py:185
  185.9 9.7 %collective-permute-start.46 = (bf16[2,2,4,32,512]{4,3,2,1,0:T(8,128)(2,1)S(1)}, bf16[2,2,4,32,512]{4,3,2,1,0:T(8,128)(2,1)S(1)}, u32[]{:S(2)}, u32[]{:S(2)}) collective-permute-start(bf16[2,2,4,32,512]{4,3,2,1,0:T(8,128)(2,1)S(1)} %bitcast.41), channel_id=1, source_target_pairs={{0,64},{32,96},{64,0},{96,32},{1,65},{33,97},{65,1},{97,33},{2,66}... | collective-permute-start | bytes 1572872 | tf_op jit(solution)/shard_map/ppermute | solution.py:336
  187.9 19.2 %collective-permute-start.43 = (bf16[2,2,4,32,512]{4,3,2,1,0:T(8,128)(2,1)S(1)}, bf16[2,2,4,32,512]{4,3,2,1,0:T(8,128)(2,1)S(1)}, u32[]{:S(2)}, u32[]{:S(2)}) collective-permute-start(bf16[2,2,4,32,512]{4,3,2,1,0:T(8,128)(2,1)S(1)} %bitcast.42), channel_id=1, source_target_pairs={{0,32},{32,0},{64,96},{96,64},{1,33},{33,1},{65,97},{97,65},{2,34}... | collective-permute-start | bytes 1572872 | tf_op jit(solution)/shard_map/ppermute | solution.py:336
  188.5 22.3 %collective-permute-start.44 = (bf16[2,2,4,32,512]{4,3,2,1,0:T(8,128)(2,1)S(1)}, bf16[2,2,4,32,512]{4,3,2,1,0:T(8,128)(2,1)S(1)}, u32[]{:S(2)}, u32[]{:S(2)}) collective-permute-start(bf16[2,2,4,32,512]{4,3,2,1,0:T(8,128)(2,1)S(1)} %bitcast.43), channel_id=1, source_target_pairs={{0,96},{32,64},{64,32},{96,0},{1,97},{33,65},{65,33},{97,1},{2,98}... | collective-permute-start | bytes 1572872 | tf_op jit(solution)/shard_map/ppermute | solution.py:336
  190.8 13.3 %collective-permute-start.45 = (bf16[2,2,4,32,512]{4,3,2,1,0:T(8,128)(2,1)S(1)}, bf16[2,2,4,32,512]{4,3,2,1,0:T(8,128)(2,1)S(1)}, u32[]{:S(2)}, u32[]{:S(2)}) collective-permute-start(bf16[2,2,4,32,512]{4,3,2,1,0:T(8,128)(2,1)S(1)} %bitcast.37), channel_id=1, source_target_pairs={{0,128},{16,144},{128,0},{144,16},{1,129},{17,145},{129,1},{145,17... | collective-permute-start | bytes 1572872 | tf_op jit(solution)/shard_map/ppermute | solution.py:337
  190.9 22.8 %collective-permute-start.41 = (bf16[2,2,4,32,512]{4,3,2,1,0:T(8,128)(2,1)S(1)}, bf16[2,2,4,32,512]{4,3,2,1,0:T(8,128)(2,1)S(1)}, u32[]{:S(2)}, u32[]{:S(2)}) collective-permute-start(bf16[2,2,4,32,512]{4,3,2,1,0:T(8,128)(2,1)S(1)} %bitcast.38), channel_id=1, source_target_pairs={{0,16},{16,0},{128,144},{144,128},{1,17},{17,1},{129,145},{145,129... | collective-permute-start | bytes 1572872 | tf_op jit(solution)/shard_map/ppermute | solution.py:337
  196.4 17.3 %collective-permute-start.42 = (bf16[2,2,4,32,512]{4,3,2,1,0:T(8,128)(2,1)S(1)}, bf16[2,2,4,32,512]{4,3,2,1,0:T(8,128)(2,1)S(1)}, u32[]{:S(2)}, u32[]{:S(2)}) collective-permute-start(bf16[2,2,4,32,512]{4,3,2,1,0:T(8,128)(2,1)S(1)} %bitcast.39), channel_id=1, source_target_pairs={{0,144},{16,128},{128,16},{144,0},{1,145},{17,129},{129,17},{145,1... | collective-permute-start | bytes 1572872 | tf_op jit(solution)/shard_map/ppermute | solution.py:337
  216.7 10.5 %collective-permute-start.47 = (f32[384,512]{1,0:T(8,128)S(1)}, f32[384,512]{1,0:T(8,128)S(1)}, u32[]{:S(2)}, u32[]{:S(2)}) collective-permute-start(f32[384,512]{1,0:T(8,128)S(1)} %get-tuple-element.104), channel_id=1, source_target_pairs={{0,1},{1,0},{2,3},{3,2},{4,5},{5,4},{6,7},{7,6},{8,9},{9,8},{10,11... | collective-permute-start | bytes 2359304 | tf_op jit(solution)/shard_map/ppermute | solution.py:370
  (28 other events, 205.0 us)
Sparse Core Ops, SparseCore 0:
  80.3 70.8 all-reduce.1

commit v5 on v4

--- a/solution.py
+++ b/solution.py
@@ -128,10 +128,10 @@
         near, far = near_half[z % ZH].astype(f32), far_half[z % ZH].astype(f32)
         g = jnp.where(upper, far, near) if z < ZH else jnp.where(upper, near, far)
         squares = g * g
-        rows = row_moment_of(packed[z, :, hidden : hidden + 1], squares)
+        rows = row_moment_of(packed[reverse_bits(z), :, hidden : hidden + 1], squares)
         u = g * lax.rsqrt(rows)
         scaled[z] = u
-        w = packed[z, :, :hidden]
+        w = packed[reverse_bits(z), :, :hidden]
         cols, scaled_cols, weights = cols + squares, scaled_cols + u * u, weights + w * w
         row_total = row_total + rows
     lane = lax.broadcasted_iota(jnp.int32, (1, hidden), 1)
@@ -162,7 +162,7 @@
     inv = factor * lax.rsqrt(cols)
     cols_new[...], inv_cols[...] = cols, inv
     for z in range(ZN):
-        new = packed[z, :, :hidden] - learn_rate * (scaled[z] * inv)
+        new = packed[reverse_bits(z), :, :hidden] - learn_rate * (scaled[z] * inv)
         (a_half, b_half)[z // ZH][z % ZH] = new.astype(bf16)
 
 
@@ -261,11 +261,8 @@
     a_parts, b_parts = [[parts[p, k] for k in range(4)] for p in range(2)]
     a_got, b_got = exchange(a_parts, Y), exchange(b_parts, X)
     a_got, packed = lax.optimization_barrier((a_got, packed))
-    packed = lax.psum(
-        lax.dynamic_update_slice_in_dim(
-            jnp.zeros((ZN,) + packed.shape, f32), packed[None], pos[5], axis=0
-        ),
-        "z",
+    packed = lax.all_to_all(
+        jnp.broadcast_to(packed[None], (ZN,) + packed.shape), "z", 0, 0, tiled=True
     )
     a_sum = a_parts[0] + sum(p.astype(f32) for p in a_got)
     b_sum = b_parts[0] + sum(p.astype(f32) for p in b_got)
@@ -274,6 +271,7 @@
     b_parts = [b_sum[k % 2, k // 2] for k in range(4)]
     a_got = exchange([p.astype(bf16) for p in a_parts], X)
     b_got = exchange([p.astype(bf16) for p in b_parts], Y)
+    b_got, packed = lax.optimization_barrier((b_got, packed))
     line, part_line, block = (ZN, GR, hidden), (ZH, GR, hidden), (GR, hidden)
     in_specs = lambda n: [pl.BlockSpec(memory_space=pltpu.SMEM)] + [
         pl.BlockSpec(memory_space=pltpu.VMEM)
@@ -307,7 +305,7 @@
         compiler_params=small,
     )(pos, g16, *got)
     far_half = lax.ppermute(near_half, "z", xor_perm(ZN, 1))
-    far_half, near, far, packed = lax.optimization_barrier((far_half, near, far, packed))
+    far_half, near, far = lax.optimization_barrier((far_half, near, far))
 
     stats, scaled = pl.pallas_call(
         stats_kernel,

time: 237 us -> 196 us (0.83)
  waiting for transfers between devices: 85.3 us -> 61.4 us
  between operations: 14.4 us -> 0.99 us
  local copies, waits for them, and re-layouts: 15.2 us -> 11.4 us
  other arithmetic: 2.38 us -> 4.89 us
    psum x1 -> x0, waiting for transfers between devices: 14.9 us -> none  [on_device(): lax.psum(lax.dynamic_update_slice_in_dim(jnp.zeros((ZN,) + packed.shape,...]
    ppermute x24, waiting for transfers between devices: 39.2 us -> 28.4 us  [exchange(): return [lax.ppermute(pieces[k], axes, xor_perm(4, k)) for k in (1, 2, 3)]]
    ppermute x1, starting transfers between devices: 5.64 us -> 0.09 us  [on_device(): stats = stats + lax.ppermute(stats, 'core', SWAP)]
    all_to_all x0 -> x1, starting transfers between devices: none -> 3.64 us  [on_device(): lax.all_to_all(jnp.broadcast_to(packed[None], (ZN,) + packed.shape), 'z',...]
    unnamed x22 -> x18, local copies, waits for them, and re-layouts: 13.2 us -> 10 us
    another operation x2, other arithmetic: 0.64 us -> 3.15 us
  transfers between devices with their start and end apart: 49 -> 49, of which waited for: 28 -> 20; matrix products, arithmetic and copies ran while one was open for 1% -> 3% of each run, Pallas kernels for 12% -> 14%
where the time goes in v5:
time: 196 us
  starting transfers between devices  82.3 us (42%)
  waiting for transfers between devices  61.4 us (31%)
  Pallas kernels  34.8 us (18%)
  local copies, waits for them, and re-layouts  11.4 us (6%)
  other arithmetic  4.89 us (2%)
    ppermute x24, waiting for transfers between devices, exchange(): return [lax.ppermute(pieces[k], axes, xor_perm(4, k)) for k in (1, 2, 3)]  28.4 us
    ppermute x24, starting transfers between devices, exchange(): return [lax.ppermute(pieces[k], axes, xor_perm(4, k)) for k in (1, 2, 3)]  27.5 us
    pallas_call x4, Pallas kernels, on_device(): pl.pallas_call(functools.partial(grad_kernel, part), out_shape=[kept, jax...  15 us
    pallas_call x4, Pallas kernels, on_device(): pl.pallas_call(functools.partial(apply_kernel, part), out_shape=[result,...  11.9 us
    ppermute x1, starting transfers between devices, on_device(): packed = lax.ppermute(packed, TURNED, TURN)  10.2 us
    unnamed x18, local copies, waits for them, and re-layouts  10 us
    ppermute x1, starting transfers between devices, on_device(): near = lax.ppermute(g32, TURNED, TURN)  9.78 us
    ppermute x1, waiting for transfers between devices, on_device(): far = lax.ppermute(g32, ('cuts',) + TURNED, FAR_TURN)  8.54 us
  transfers between devices with their start and end apart: 49, of which 20 were waited for; matrix products, arithmetic and copies ran while one was open for 3% of the time, Pallas kernels for 14%

profile of v5, /device:TPU:33, one launch (start us, length us, event | category | flops | bytes accessed | tf_op | source)
XLA Modules:
  0.0 195.8 jit_solution(5518061132684791059)
XLA Ops:
  0.7 2.8 %copy-done = bf16[384,8192]{1,0:T(8,128)(2,1)S(1)} copy-done((bf16[384,8192]{1,0:T(8,128)(2,1)S(1)}, bf16[384,8192]{1,0:T(8,128)(2,1)}, u32[]{:S(2)}) %copy-start) | copy-done | bytes 6291480
  9.0 2.5 %collective-permute-done.4.cot2 = bf16[384,512]{1,0:T(8,128)(2,1)} collective-permute-done((bf16[384,512]{1,0:T(8,128)(2,1)}, bf16[384,512]{1,0:T(8,128)(2,1)}, u32[]{:S(2)}, u32[]{:S(2)}) %collective-permute-start.4) | collective-permute-done | bytes 393248 | tf_op jit(solution)/shard_map/ppermute | solution.py:215
  11.5 10.2 %collective-permute-start.8 = (f32[32,640]{1,0:T(8,128)S(1)}, f32[32,640]{1,0:T(8,128)S(1)}, u32[]{:S(2)}, u32[]{:S(2)}) collective-permute-start(f32[32,640]{1,0:T(8,128)S(1)} %pad_maximum_fusion.2), channel_id=1, source_target_pairs={{0,0},{1,64},{2,8},{3,72},{4,4},{5,68},{6,12},{7,76},{8,2},{9,66},... | collective-permute-start | bytes 245768 | tf_op jit(solution)/shard_map/ppermute | solution.py:242
  21.8 2.8 %copy-done.1 = bf16[384,8192]{1,0:T(8,128)(2,1)S(1)} copy-done((bf16[384,8192]{1,0:T(8,128)(2,1)S(1)}, bf16[384,8192]{1,0:T(8,128)(2,1)}, u32[]{:S(2)}) %copy-start.1) | copy-done | bytes 6291480
  24.5 3.4 %shard_map.96 = (f32[2,2,4,32,512]{4,3,2,1,0:T(8,128)S(1)}, bf16[2,2,4,32,512]{4,3,2,1,0:T(8,128)(2,1)S(1)}) custom-call(s32[6]{0:T(128)S(1)} %stack.57.pos, bf16[384,8192]{1,0:T(8,128)(2,1)S(1)} %copy-done.1, bf16[384,1024]{1,0:T(8,128)(2,1)} %collective-permute-done.tok2, bf16[384,512]{1,0:T(8,128)(2,1)} %cot.7, bf16[384,512]{1,0:T(8,128)(2,1)} %collective-permute-done.4.cot2), custom_call_target="tpu_custom_call" | custom-call | flops 6442450944 | bytes 16777216 | tf_op jit(solution)/shard_map/pallas_call | solution.py:248
  28.2 4.0 %shard_map.97 = (f32[2,2,4,32,512]{4,3,2,1,0:T(8,128)S(1)}, bf16[2,2,4,32,512]{4,3,2,1,0:T(8,128)(2,1)}) custom-call(s32[6]{0:T(128)S(1)} %stack.57.pos, bf16[384,8192]{1,0:T(8,128)(2,1)S(1)} %copy-done.1, bf16[384,1024]{1,0:T(8,128)(2,1)} %collective-permute-done.2.tok2, bf16[384,512]{1,0:T(8,128)(2,1)} %cot.7, bf16[384,512]{1,0:T(8,128)(2,1)} %collective-permute-done.4.cot2), custom_call_target="tpu_custom_call" | custom-call | flops 6442450944 | bytes 16777216 | tf_op jit(solution)/shard_map/pallas_call | solution.py:248
  32.2 2.7 %collective-permute-start.13 = (bf16[2,2,4,32,512]{4,3,2,1,0:T(8,128)(2,1)}, bf16[2,2,4,32,512]{4,3,2,1,0:T(8,128)(2,1)S(1)}, u32[]{:S(2)}, u32[]{:S(2)}) collective-permute-start(bf16[2,2,4,32,512]{4,3,2,1,0:T(8,128)(2,1)} %get-tuple-element.64), channel_id=1, source_target_pairs={{0,128},{16,144},{128,0},{144,16},{1,129},{17,145},{129,1},{145,17... | collective-permute-start | bytes 1572872 | tf_op jit(solution)/shard_map/ppermute | solution.py:185
  35.0 3.4 %shard_map.98 = (bf16[2,2,4,32,512]{4,3,2,1,0:T(8,128)(2,1)S(1)}, bf16[2,2,4,32,512]{4,3,2,1,0:T(8,128)(2,1)S(1)}) custom-call(s32[6]{0:T(128)S(1)} %stack.57.pos, bf16[384,8192]{1,0:T(8,128)(2,1)S(1)} %copy-done.1, bf16[384,1024]{1,0:T(8,128)(2,1)} %collective-permute-done.1.tok2, bf16[384,512]{1,0:T(8,128)(2,1)} %cot.7, ...), custom_call_target="tpu_custom_call" | custom-call | flops 6442450944 | bytes 16777216 | tf_op jit(solution)/shard_map/pallas_call | solution.py:248
  38.4 2.7 %collective-permute-start.7 = (bf16[2,2,4,32,512]{4,3,2,1,0:T(8,128)(2,1)S(1)}, bf16[2,2,4,32,512]{4,3,2,1,0:T(8,128)(2,1)S(1)}, u32[]{:S(2)}, u32[]{:S(2)}) collective-permute-start(bf16[2,2,4,32,512]{4,3,2,1,0:T(8,128)(2,1)S(1)} %get-tuple-element.68), channel_id=1, source_target_pairs={{0,96},{32,64},{64,32},{96,0},{1,97},{33,65},{65,33},{97,1},{2,98}... | collective-permute-start | bytes 1572872 | tf_op jit(solution)/shard_map/ppermute | solution.py:185
  41.1 4.2 %shard_map.99 = (bf16[2,2,4,32,512]{4,3,2,1,0:T(8,128)(2,1)}, bf16[2,2,4,32,512]{4,3,2,1,0:T(8,128)(2,1)}) custom-call(s32[6]{0:T(128)S(1)} %stack.57.pos, bf16[384,8192]{1,0:T(8,128)(2,1)S(1)} %copy-done.1, bf16[384,1024]{1,0:T(8,128)(2,1)} %collective-permute-done.3.tok2, bf16[384,512]{1,0:T(8,128)(2,1)} %cot.7, bf16[384,512]{1,0:T(8,128)(2,1)} %collective-permute-done.4.cot2), custom_call_target="tpu_custom_call" | custom-call | flops 6442450944 | bytes 16777216 | tf_op jit(solution)/shard_map/pallas_call | solution.py:248
  46.2 8.8 %collective-permute-done.5 = bf16[2,2,4,32,512]{4,3,2,1,0:T(8,128)(2,1)S(1)} collective-permute-done((bf16[2,2,4,32,512]{4,3,2,1,0:T(8,128)(2,1)S(1)}, bf16[2,2,4,32,512]{4,3,2,1,0:T(8,128)(2,1)S(1)}, u32[]{:S(2)}, u32[]{:S(2)}) %collective-permute-start.5) | collective-permute-done | bytes 524320 | tf_op jit(solution)/shard_map/ppermute | solution.py:185
  57.7 3.6 %all-to-all-start = ((f32[8,32,640]{2,1,0:T(8,128)}), f32[8,32,640]{2,1,0:T(8,128)S(1)}, u32[]{:S(2)}, u32[]{:S(2)}) async-start(f32[8,32,640]{2,1,0:T(8,128)} %broadcast_in_dim.7), calls=%async_computation | async-start | bytes 1310720 | tf_op jit(solution)/shard_map/all_to_all | solution.py:264
  69.8 7.0 %collective-permute-done.17.refs_7_ = bf16[4,32,512]{2,1,0:T(8,128)(2,1)S(1)} collective-permute-done((bf16[4,32,512]{2,1,0:T(8,128)(2,1)S(1)}, bf16[4,32,512]{2,1,0:T(8,128)(2,1)S(1)}, u32[]{:S(2)}, u32[]{:S(2)}) %collective-permute-start.17) | collective-permute-done | bytes 131104 | tf_op jit(solution)/shard_map/ppermute | solution.py:185
  76.8 4.1 %collective-permute-done.15.refs_5_ = bf16[4,32,512]{2,1,0:T(8,128)(2,1)S(1)} collective-permute-done((bf16[4,32,512]{2,1,0:T(8,128)(2,1)S(1)}, bf16[4,32,512]{2,1,0:T(8,128)(2,1)S(1)}, u32[]{:S(2)}, u32[]{:S(2)}) %collective-permute-start.15) | collective-permute-done | bytes 131104 | tf_op jit(solution)/shard_map/ppermute | solution.py:185
  82.8 2.6 %collective-permute-done.18.got = bf16[4,32,512]{2,1,0:T(8,128)(2,1)S(1)} collective-permute-done((bf16[4,32,512]{2,1,0:T(8,128)(2,1)S(1)}, bf16[4,32,512]{2,1,0:T(8,128)(2,1)S(1)}, u32[]{:S(2)}, u32[]{:S(2)}) %collective-permute-start.18) | collective-permute-done | bytes 131104 | tf_op jit(solution)/shard_map/ppermute | solution.py:286
  86.0 4.0 %collective-permute-start.19 = (bf16[32,512]{1,0:T(8,128)(2,1)S(1)}, bf16[32,512]{1,0:T(8,128)(2,1)S(1)}, u32[]{:S(2)}, u32[]{:S(2)}) collective-permute-start(bf16[32,512]{1,0:T(8,128)(2,1)S(1)} %get-tuple-element.84), channel_id=1, source_target_pairs={{0,8},{2,10},{4,12},{6,14},{8,0},{10,2},{12,4},{14,6},{1,9},{3,11}... | collective-permute-start | bytes 98312 | tf_op jit(solution)/shard_map/ppermute | solution.py:293
  101.0 4.9 %collective-permute-done.22.refs_1_ = bf16[32,512]{1,0:T(8,128)(2,1)S(1)} collective-permute-done((bf16[32,512]{1,0:T(8,128)(2,1)S(1)}, bf16[32,512]{1,0:T(8,128)(2,1)S(1)}, u32[]{:S(2)}, u32[]{:S(2)}) %collective-permute-start.22) | collective-permute-done | bytes 32800 | tf_op jit(solution)/shard_map/ppermute | solution.py:300
  106.7 9.8 %collective-permute-start.26 = (f32[32,512]{1,0:T(8,128)S(1)}, f32[32,512]{1,0:T(8,128)S(1)}, u32[]{:S(2)}, u32[]{:S(2)}) collective-permute-start(f32[32,512]{1,0:T(8,128)S(1)} %get-tuple-element.112), channel_id=1, source_target_pairs={{0,0},{1,64},{2,8},{3,72},{4,4},{5,68},{6,12},{7,76},{8,2},{9,66},... | collective-permute-start | bytes 196616 | tf_op jit(solution)/shard_map/ppermute | solution.py:296
  116.4 3.1 %collective-permute-start.27 = (f32[32,512]{1,0:T(8,128)S(1)}, f32[32,512]{1,0:T(8,128)S(1)}, u32[]{:S(2)}, u32[]{:S(2)}) collective-permute-start(f32[32,512]{1,0:T(8,128)S(1)} %get-tuple-element.112), channel_id=1, source_target_pairs={{0,128},{1,192},{2,136},{3,200},{4,132},{5,196},{6,140},{7,204},{8... | collective-permute-start | bytes 196616 | tf_op jit(solution)/shard_map/ppermute | solution.py:297
  119.5 8.5 %collective-permute-done.27.far = f32[32,512]{1,0:T(8,128)S(1)} collective-permute-done((f32[32,512]{1,0:T(8,128)S(1)}, f32[32,512]{1,0:T(8,128)S(1)}, u32[]{:S(2)}, u32[]{:S(2)}) %collective-permute-start.27) | collective-permute-done | bytes 65568 | tf_op jit(solution)/shard_map/ppermute | solution.py:297
  131.6 2.4 %collective-permute-start.29 = (f32[8,512]{1,0:T(8,128)S(1)}, f32[8,512]{1,0:T(8,128)S(1)}, u32[]{:S(2)}, u32[]{:S(2)}) collective-permute-start(f32[8,512]{1,0:T(8,128)S(1)} %add.74), channel_id=1, source_target_pairs={{0,64},{32,96},{64,0},{96,32},{1,65},{33,97},{65,1},{97,33},{2,66}... | collective-permute-start | bytes 49160 | tf_op jit(solution)/shard_map/ppermute | solution.py:185
  135.7 2.5 %collective-permute-start.34 = (f32[8,512]{1,0:T(8,128)S(1)}, f32[8,512]{1,0:T(8,128)S(1)}, u32[]{:S(2)}, u32[]{:S(2)}) collective-permute-start(f32[8,512]{1,0:T(8,128)S(1)} %add_add_fusion.4), channel_id=1, source_target_pairs={{0,144},{16,128},{128,16},{144,0},{1,145},{17,129},{129,17},{145,1... | collective-permute-start | bytes 49160 | tf_op jit(solution)/shard_map/ppermute | solution.py:185
  144.4 2.5 %collective-permute-start.35 = (bf16[4,32,512]{2,1,0:T(8,128)(2,1)S(1)}, bf16[4,32,512]{2,1,0:T(8,128)(2,1)S(1)}, u32[]{:S(2)}, u32[]{:S(2)}) collective-permute-start(bf16[4,32,512]{2,1,0:T(8,128)(2,1)S(1)} %get-tuple-element.98), channel_id=1, source_target_pairs={{0,128},{16,144},{128,0},{144,16},{1,129},{17,145},{129,1},{145,17... | collective-permute-start | bytes 393224 | tf_op jit(solution)/shard_map/ppermute | solution.py:185
  152.6 2.4 %collective-permute-done.38 = bf16[4,32,512]{2,1,0:T(8,128)(2,1)S(1)} collective-permute-done((bf16[4,32,512]{2,1,0:T(8,128)(2,1)S(1)}, bf16[4,32,512]{2,1,0:T(8,128)(2,1)S(1)}, u32[]{:S(2)}, u32[]{:S(2)}) %collective-permute-start.38) | collective-permute-done | bytes 131104 | tf_op jit(solution)/shard_map/ppermute | solution.py:185
  162.4 3.6 %collective-permute-done.46.piece1 = bf16[2,2,4,32,512]{4,3,2,1,0:T(8,128)(2,1)} collective-permute-done((bf16[2,2,4,32,512]{4,3,2,1,0:T(8,128)(2,1)S(1)}, bf16[2,2,4,32,512]{4,3,2,1,0:T(8,128)(2,1)}, u32[]{:S(2)}, u32[]{:S(2)}) %collective-permute-start.46) | collective-permute-done | bytes 524320 | tf_op jit(solution)/shard_map/ppermute | solution.py:334
  166.7 2.8 %copy-done.2 = bf16[384,8192]{1,0:T(8,128)(2,1)S(1)} copy-done((bf16[384,8192]{1,0:T(8,128)(2,1)S(1)}, bf16[384,8192]{1,0:T(8,128)(2,1)}, u32[]{:S(2)}) %copy-start.2) | copy-done | bytes 6291480
  169.5 3.0 %shard_map.106 = (f32[384,512]{1,0:T(8,128)S(1)}, f32[384,512]{1,0:T(8,128)S(1)}) custom-call(s32[6]{0:T(128)S(1)} %stack.57.pos, bf16[384,8192]{1,0:T(8,128)(2,1)S(1)} %copy-done.2, bf16[384,1024]{1,0:T(8,128)(2,1)} %collective-permute-done.tok2, bf16[2,2,4,32,512]{4,3,2,1,0:T(8,128)(2,1)S(1)} %bitcast.42, ...), custom_call_target="tpu_custom_call" | custom-call | flops 6442450944 | bytes 16777216 | tf_op jit(solution)/shard_map/pallas_call | solution.py:352
  172.6 3.0 %shard_map.107 = (f32[384,512]{1,0:T(8,128)S(1)}, f32[384,512]{1,0:T(8,128)S(1)}) custom-call(s32[6]{0:T(128)S(1)} %stack.57.pos, bf16[384,8192]{1,0:T(8,128)(2,1)S(1)} %copy-done.2, bf16[384,1024]{1,0:T(8,128)(2,1)} %collective-permute-done.2.tok2, bf16[2,2,4,32,512]{4,3,2,1,0:T(8,128)(2,1)S(1)} %bitcast.38, ...), custom_call_target="tpu_custom_call" | custom-call | flops 6442450944 | bytes 16777216 | tf_op jit(solution)/shard_map/pallas_call | solution.py:352
  175.6 5.0 %collective-permute-done.44.piece1 = bf16[2,2,4,32,512]{4,3,2,1,0:T(8,128)(2,1)S(1)} collective-permute-done((bf16[2,2,4,32,512]{4,3,2,1,0:T(8,128)(2,1)S(1)}, bf16[2,2,4,32,512]{4,3,2,1,0:T(8,128)(2,1)S(1)}, u32[]{:S(2)}, u32[]{:S(2)}) %collective-permute-start.44) | collective-permute-done | bytes 524320 | tf_op jit(solution)/shard_map/ppermute | solution.py:334
  180.5 3.0 %shard_map.108 = (f32[384,512]{1,0:T(8,128)S(1)}, f32[384,512]{1,0:T(8,128)S(1)}) custom-call(s32[6]{0:T(128)S(1)} %stack.57.pos, bf16[384,8192]{1,0:T(8,128)(2,1)S(1)} %copy-done.2, bf16[384,1024]{1,0:T(8,128)(2,1)} %collective-permute-done.1.tok2, bf16[2,2,4,32,512]{4,3,2,1,0:T(8,128)(2,1)S(1)} %collective-permute-done.43.piece0, ...), custom_call_target="tpu_custom_call" | custom-call | flops 6442450944 | bytes 16777216 | tf_op jit(solution)/shard_map/pallas_call | solution.py:352
  183.5 3.0 %shard_map.109 = (f32[384,512]{1,0:T(8,128)S(1)}, f32[384,512]{1,0:T(8,128)S(1)}) custom-call(s32[6]{0:T(128)S(1)} %stack.57.pos, bf16[384,8192]{1,0:T(8,128)(2,1)S(1)} %copy-done.2, bf16[384,1024]{1,0:T(8,128)(2,1)} %collective-permute-done.3.tok2, bf16[2,2,4,32,512]{4,3,2,1,0:T(8,128)(2,1)S(1)} %collective-permute-done.41.piece0, ...), custom_call_target="tpu_custom_call" | custom-call | flops 6442450944 | bytes 16777216 | tf_op jit(solution)/shard_map/pallas_call | solution.py:352
  186.5 6.4 %collective-permute-start.47 = (f32[384,512]{1,0:T(8,128)S(1)}, f32[384,512]{1,0:T(8,128)S(1)}, u32[]{:S(2)}, u32[]{:S(2)}) collective-permute-start(f32[384,512]{1,0:T(8,128)S(1)} %get-tuple-element.110), channel_id=1, source_target_pairs={{0,1},{1,0},{2,3},{3,2},{4,5},{5,4},{6,7},{7,6},{8,9},{9,8},{10,11... | collective-permute-start | bytes 2359304 | tf_op jit(solution)/shard_map/ppermute | solution.py:368
  (123 shorter events, 60.3 us)
Async XLA Ops:
  4.3 17.4 %collective-permute-start = (bf16[384,1024]{1,0:T(8,128)(2,1)S(1)}, bf16[384,1024]{1,0:T(8,128)(2,1)}, u32[]{:S(2)}, u32[]{:S(2)}) collective-permute-start(bf16[384,1024]{1,0:T(8,128)(2,1)S(1)} %shard_map.92), channel_id=1, source_target_pairs={{0,1},{1,0},{2,3},{3,2},{4,5},{5,4},{6,7},{7,6},{8,9},{9,8},{10,11... | collective-permute-start | bytes 2359304 | tf_op jit(solution)/shard_map/ppermute | solution.py:235
  5.9 15.8 %collective-permute-start.1 = (bf16[384,1024]{1,0:T(8,128)(2,1)S(1)}, bf16[384,1024]{1,0:T(8,128)(2,1)}, u32[]{:S(2)}, u32[]{:S(2)}) collective-permute-start(bf16[384,1024]{1,0:T(8,128)(2,1)S(1)} %shard_map.93), channel_id=1, source_target_pairs={{0,1},{1,0},{2,3},{3,2},{4,5},{5,4},{6,7},{7,6},{8,9},{9,8},{10,11... | collective-permute-start | bytes 2359304 | tf_op jit(solution)/shard_map/ppermute | solution.py:235
  6.8 14.9 %collective-permute-start.2 = (bf16[384,1024]{1,0:T(8,128)(2,1)S(1)}, bf16[384,1024]{1,0:T(8,128)(2,1)}, u32[]{:S(2)}, u32[]{:S(2)}) collective-permute-start(bf16[384,1024]{1,0:T(8,128)(2,1)S(1)} %shard_map.94), channel_id=1, source_target_pairs={{0,1},{1,0},{2,3},{3,2},{4,5},{5,4},{6,7},{7,6},{8,9},{9,8},{10,11... | collective-permute-start | bytes 2359304 | tf_op jit(solution)/shard_map/ppermute | solution.py:235
  8.2 13.5 %collective-permute-start.3 = (bf16[384,1024]{1,0:T(8,128)(2,1)S(1)}, bf16[384,1024]{1,0:T(8,128)(2,1)}, u32[]{:S(2)}, u32[]{:S(2)}) collective-permute-start(bf16[384,1024]{1,0:T(8,128)(2,1)S(1)} %shard_map.95), channel_id=1, source_target_pairs={{0,1},{1,0},{2,3},{3,2},{4,5},{5,4},{6,7},{7,6},{8,9},{9,8},{10,11... | collective-permute-start | bytes 2359304 | tf_op jit(solution)/shard_map/ppermute | solution.py:235
  11.5 33.7 %collective-permute-start.8 = (f32[32,640]{1,0:T(8,128)S(1)}, f32[32,640]{1,0:T(8,128)S(1)}, u32[]{:S(2)}, u32[]{:S(2)}) collective-permute-start(f32[32,640]{1,0:T(8,128)S(1)} %pad_maximum_fusion.2), channel_id=1, source_target_pairs={{0,0},{1,64},{2,8},{3,72},{4,4},{5,68},{6,12},{7,76},{8,2},{9,66},... | collective-permute-start | bytes 245768 | tf_op jit(solution)/shard_map/ppermute | solution.py:242
  27.9 17.7 %collective-permute-start.6 = (bf16[2,2,4,32,512]{4,3,2,1,0:T(8,128)(2,1)S(1)}, bf16[2,2,4,32,512]{4,3,2,1,0:T(8,128)(2,1)S(1)}, u32[]{:S(2)}, u32[]{:S(2)}) collective-permute-start(bf16[2,2,4,32,512]{4,3,2,1,0:T(8,128)(2,1)S(1)} %get-tuple-element.61), channel_id=1, source_target_pairs={{0,64},{32,96},{64,0},{96,32},{1,65},{33,97},{65,1},{97,33},{2,66}... | collective-permute-start | bytes 1572872 | tf_op jit(solution)/shard_map/ppermute | solution.py:185
  32.2 33.0 %collective-permute-start.13 = (bf16[2,2,4,32,512]{4,3,2,1,0:T(8,128)(2,1)}, bf16[2,2,4,32,512]{4,3,2,1,0:T(8,128)(2,1)S(1)}, u32[]{:S(2)}, u32[]{:S(2)}) collective-permute-start(bf16[2,2,4,32,512]{4,3,2,1,0:T(8,128)(2,1)} %get-tuple-element.64), channel_id=1, source_target_pairs={{0,128},{16,144},{128,0},{144,16},{1,129},{17,145},{129,1},{145,17... | collective-permute-start | bytes 1572872 | tf_op jit(solution)/shard_map/ppermute | solution.py:185
  38.4 16.7 %collective-permute-start.7 = (bf16[2,2,4,32,512]{4,3,2,1,0:T(8,128)(2,1)S(1)}, bf16[2,2,4,32,512]{4,3,2,1,0:T(8,128)(2,1)S(1)}, u32[]{:S(2)}, u32[]{:S(2)}) collective-permute-start(bf16[2,2,4,32,512]{4,3,2,1,0:T(8,128)(2,1)S(1)} %get-tuple-element.68), channel_id=1, source_target_pairs={{0,96},{32,64},{64,32},{96,0},{1,97},{33,65},{65,33},{97,1},{2,98}... | collective-permute-start | bytes 1572872 | tf_op jit(solution)/shard_map/ppermute | solution.py:185
  41.1 14.0 %collective-permute-start.5 = (bf16[2,2,4,32,512]{4,3,2,1,0:T(8,128)(2,1)S(1)}, bf16[2,2,4,32,512]{4,3,2,1,0:T(8,128)(2,1)S(1)}, u32[]{:S(2)}, u32[]{:S(2)}) collective-permute-start(bf16[2,2,4,32,512]{4,3,2,1,0:T(8,128)(2,1)S(1)} %get-tuple-element.67), channel_id=1, source_target_pairs={{0,32},{32,0},{64,96},{96,64},{1,33},{33,1},{65,97},{97,65},{2,34}... | collective-permute-start | bytes 1572872 | tf_op jit(solution)/shard_map/ppermute | solution.py:185
  45.2 21.1 %collective-permute-start.12 = (bf16[2,2,4,32,512]{4,3,2,1,0:T(8,128)(2,1)}, bf16[2,2,4,32,512]{4,3,2,1,0:T(8,128)(2,1)}, u32[]{:S(2)}, u32[]{:S(2)}) collective-permute-start(bf16[2,2,4,32,512]{4,3,2,1,0:T(8,128)(2,1)} %get-tuple-element.75), channel_id=1, source_target_pairs={{0,16},{16,0},{128,144},{144,128},{1,17},{17,1},{129,145},{145,129... | collective-permute-start | bytes 1572872 | tf_op jit(solution)/shard_map/ppermute | solution.py:185
  45.6 20.8 %collective-permute-start.14 = (bf16[2,2,4,32,512]{4,3,2,1,0:T(8,128)(2,1)}, bf16[2,2,4,32,512]{4,3,2,1,0:T(8,128)(2,1)}, u32[]{:S(2)}, u32[]{:S(2)}) collective-permute-start(bf16[2,2,4,32,512]{4,3,2,1,0:T(8,128)(2,1)} %get-tuple-element.76), channel_id=1, source_target_pairs={{0,144},{16,128},{128,16},{144,0},{1,145},{17,129},{129,17},{145,1... | collective-permute-start | bytes 1572872 | tf_op jit(solution)/shard_map/ppermute | solution.py:185
  57.7 23.2 %all-to-all-start = ((f32[8,32,640]{2,1,0:T(8,128)}), f32[8,32,640]{2,1,0:T(8,128)S(1)}, u32[]{:S(2)}, u32[]{:S(2)}) async-start(f32[8,32,640]{2,1,0:T(8,128)} %broadcast_in_dim.7), calls=%async_computation | async-start | bytes 1310720 | tf_op jit(solution)/shard_map/all_to_all | solution.py:264
  63.0 17.8 %collective-permute-start.11 = (bf16[4,32,512]{2,1,0:T(8,128)(2,1)S(1)}, bf16[4,32,512]{2,1,0:T(8,128)(2,1)S(1)}, u32[]{:S(2)}, u32[]{:S(2)}) collective-permute-start(bf16[4,32,512]{2,1,0:T(8,128)(2,1)S(1)} %get-tuple-element.120), channel_id=1, source_target_pairs={{0,144},{16,128},{128,16},{144,0},{1,145},{17,129},{129,17},{145,1... | collective-permute-start | bytes 393224 | tf_op jit(solution)/shard_map/ppermute | solution.py:185
  64.0 16.9 %collective-permute-start.10 = (bf16[4,32,512]{2,1,0:T(8,128)(2,1)S(1)}, bf16[4,32,512]{2,1,0:T(8,128)(2,1)S(1)}, u32[]{:S(2)}, u32[]{:S(2)}) collective-permute-start(bf16[4,32,512]{2,1,0:T(8,128)(2,1)S(1)} %get-tuple-element.121), channel_id=1, source_target_pairs={{0,128},{16,144},{128,0},{144,16},{1,129},{17,145},{129,1},{145,17... | collective-permute-start | bytes 393224 | tf_op jit(solution)/shard_map/ppermute | solution.py:185
  65.2 15.6 %collective-permute-start.9 = (bf16[4,32,512]{2,1,0:T(8,128)(2,1)S(1)}, bf16[4,32,512]{2,1,0:T(8,128)(2,1)S(1)}, u32[]{:S(2)}, u32[]{:S(2)}) collective-permute-start(bf16[4,32,512]{2,1,0:T(8,128)(2,1)S(1)} %get-tuple-element.122), channel_id=1, source_target_pairs={{0,16},{16,0},{128,144},{144,128},{1,17},{17,1},{129,145},{145,129... | collective-permute-start | bytes 393224 | tf_op jit(solution)/shard_map/ppermute | solution.py:185
  67.9 8.8 %collective-permute-start.17 = (bf16[4,32,512]{2,1,0:T(8,128)(2,1)S(1)}, bf16[4,32,512]{2,1,0:T(8,128)(2,1)S(1)}, u32[]{:S(2)}, u32[]{:S(2)}) collective-permute-start(bf16[4,32,512]{2,1,0:T(8,128)(2,1)S(1)} %get-tuple-element.117), channel_id=1, source_target_pairs={{0,96},{32,64},{64,32},{96,0},{1,97},{33,65},{65,33},{97,1},{2,98}... | collective-permute-start | bytes 393224 | tf_op jit(solution)/shard_map/ppermute | solution.py:185
  68.1 8.7 %collective-permute-start.16 = (bf16[4,32,512]{2,1,0:T(8,128)(2,1)S(1)}, bf16[4,32,512]{2,1,0:T(8,128)(2,1)S(1)}, u32[]{:S(2)}, u32[]{:S(2)}) collective-permute-start(bf16[4,32,512]{2,1,0:T(8,128)(2,1)S(1)} %get-tuple-element.118), channel_id=1, source_target_pairs={{0,64},{32,96},{64,0},{96,32},{1,65},{33,97},{65,1},{97,33},{2,66}... | collective-permute-start | bytes 393224 | tf_op jit(solution)/shard_map/ppermute | solution.py:185
  86.0 6.8 %collective-permute-start.19 = (bf16[32,512]{1,0:T(8,128)(2,1)S(1)}, bf16[32,512]{1,0:T(8,128)(2,1)S(1)}, u32[]{:S(2)}, u32[]{:S(2)}) collective-permute-start(bf16[32,512]{1,0:T(8,128)(2,1)S(1)} %get-tuple-element.84), channel_id=1, source_target_pairs={{0,8},{2,10},{4,12},{6,14},{8,0},{10,2},{12,4},{14,6},{1,9},{3,11}... | collective-permute-start | bytes 98312 | tf_op jit(solution)/shard_map/ppermute | solution.py:293
  99.0 6.8 %collective-permute-start.22 = (bf16[32,512]{1,0:T(8,128)(2,1)S(1)}, bf16[32,512]{1,0:T(8,128)(2,1)S(1)}, u32[]{:S(2)}, u32[]{:S(2)}) collective-permute-start(bf16[32,512]{1,0:T(8,128)(2,1)S(1)} %get-tuple-element.111.refs_0_), channel_id=1, source_target_pairs={{0,8},{2,10},{4,12},{6,14},{8,0},{10,2},{12,4},{14,6},{1,9},{3,11}... | collective-permute-start | bytes 98312 | tf_op jit(solution)/shard_map/ppermute | solution.py:300
  106.5 21.6 %collective-permute-start.25 = (bf16[4,32,512]{2,1,0:T(8,128)(2,1)S(1)}, bf16[4,32,512]{2,1,0:T(8,128)(2,1)S(1)}, u32[]{:S(2)}, u32[]{:S(2)}) collective-permute-start(bf16[4,32,512]{2,1,0:T(8,128)(2,1)S(1)} %shard_map.102.near_half), channel_id=1, source_target_pairs={{0,2},{2,0},{4,6},{6,4},{8,10},{10,8},{12,14},{14,12},{1,3},{3,1},... | collective-permute-start | bytes 393224 | tf_op jit(solution)/shard_map/ppermute | solution.py:307
  106.7 12.8 %collective-permute-start.26 = (f32[32,512]{1,0:T(8,128)S(1)}, f32[32,512]{1,0:T(8,128)S(1)}, u32[]{:S(2)}, u32[]{:S(2)}) collective-permute-start(f32[32,512]{1,0:T(8,128)S(1)} %get-tuple-element.112), channel_id=1, source_target_pairs={{0,0},{1,64},{2,8},{3,72},{4,4},{5,68},{6,12},{7,76},{8,2},{9,66},... | collective-permute-start | bytes 196616 | tf_op jit(solution)/shard_map/ppermute | solution.py:296
  116.4 11.6 %collective-permute-start.27 = (f32[32,512]{1,0:T(8,128)S(1)}, f32[32,512]{1,0:T(8,128)S(1)}, u32[]{:S(2)}, u32[]{:S(2)}) collective-permute-start(f32[32,512]{1,0:T(8,128)S(1)} %get-tuple-element.112), channel_id=1, source_target_pairs={{0,128},{1,192},{2,136},{3,200},{4,132},{5,196},{6,140},{7,204},{8... | collective-permute-start | bytes 196616 | tf_op jit(solution)/shard_map/ppermute | solution.py:297
  143.0 6.3 %collective-permute-start.37 = (bf16[4,32,512]{2,1,0:T(8,128)(2,1)S(1)}, bf16[4,32,512]{2,1,0:T(8,128)(2,1)S(1)}, u32[]{:S(2)}, u32[]{:S(2)}) collective-permute-start(bf16[4,32,512]{2,1,0:T(8,128)(2,1)S(1)} %get-tuple-element.98), channel_id=1, source_target_pairs={{0,144},{16,128},{128,16},{144,0},{1,145},{17,129},{129,17},{145,1... | collective-permute-start | bytes 393224 | tf_op jit(solution)/shard_map/ppermute | solution.py:185
  144.0 6.9 %collective-permute-start.36 = (bf16[4,32,512]{2,1,0:T(8,128)(2,1)S(1)}, bf16[4,32,512]{2,1,0:T(8,128)(2,1)S(1)}, u32[]{:S(2)}, u32[]{:S(2)}) collective-permute-start(bf16[4,32,512]{2,1,0:T(8,128)(2,1)S(1)} %get-tuple-element.98), channel_id=1, source_target_pairs={{0,16},{16,0},{128,144},{144,128},{1,17},{17,1},{129,145},{145,129... | collective-permute-start | bytes 393224 | tf_op jit(solution)/shard_map/ppermute | solution.py:185
  144.4 6.5 %collective-permute-start.35 = (bf16[4,32,512]{2,1,0:T(8,128)(2,1)S(1)}, bf16[4,32,512]{2,1,0:T(8,128)(2,1)S(1)}, u32[]{:S(2)}, u32[]{:S(2)}) collective-permute-start(bf16[4,32,512]{2,1,0:T(8,128)(2,1)S(1)} %get-tuple-element.98), channel_id=1, source_target_pairs={{0,128},{16,144},{128,0},{144,16},{1,129},{17,145},{129,1},{145,17... | collective-permute-start | bytes 393224 | tf_op jit(solution)/shard_map/ppermute | solution.py:185
  155.1 10.9 %collective-permute-start.46 = (bf16[2,2,4,32,512]{4,3,2,1,0:T(8,128)(2,1)S(1)}, bf16[2,2,4,32,512]{4,3,2,1,0:T(8,128)(2,1)}, u32[]{:S(2)}, u32[]{:S(2)}) collective-permute-start(bf16[2,2,4,32,512]{4,3,2,1,0:T(8,128)(2,1)S(1)} %bitcast.39), channel_id=1, source_target_pairs={{0,64},{32,96},{64,0},{96,32},{1,65},{33,97},{65,1},{97,33},{2,66}... | collective-permute-start | bytes 1572872 | tf_op jit(solution)/shard_map/ppermute | solution.py:334
  157.9 14.7 %collective-permute-start.45 = (bf16[2,2,4,32,512]{4,3,2,1,0:T(8,128)(2,1)S(1)}, bf16[2,2,4,32,512]{4,3,2,1,0:T(8,128)(2,1)S(1)}, u32[]{:S(2)}, u32[]{:S(2)}) collective-permute-start(bf16[2,2,4,32,512]{4,3,2,1,0:T(8,128)(2,1)S(1)} %bitcast.35), channel_id=1, source_target_pairs={{0,128},{16,144},{128,0},{144,16},{1,129},{17,145},{129,1},{145,17... | collective-permute-start | bytes 1572872 | tf_op jit(solution)/shard_map/ppermute | solution.py:335
  158.3 25.2 %collective-permute-start.42 = (bf16[2,2,4,32,512]{4,3,2,1,0:T(8,128)(2,1)S(1)}, bf16[2,2,4,32,512]{4,3,2,1,0:T(8,128)(2,1)S(1)}, u32[]{:S(2)}, u32[]{:S(2)}) collective-permute-start(bf16[2,2,4,32,512]{4,3,2,1,0:T(8,128)(2,1)S(1)} %bitcast.36), channel_id=1, source_target_pairs={{0,144},{16,128},{128,16},{144,0},{1,145},{17,129},{129,17},{145,1... | collective-permute-start | bytes 1572872 | tf_op jit(solution)/shard_map/ppermute | solution.py:335
  160.3 23.2 %collective-permute-start.41 = (bf16[2,2,4,32,512]{4,3,2,1,0:T(8,128)(2,1)S(1)}, bf16[2,2,4,32,512]{4,3,2,1,0:T(8,128)(2,1)S(1)}, u32[]{:S(2)}, u32[]{:S(2)}) collective-permute-start(bf16[2,2,4,32,512]{4,3,2,1,0:T(8,128)(2,1)S(1)} %bitcast.37), channel_id=1, source_target_pairs={{0,16},{16,0},{128,144},{144,128},{1,17},{17,1},{129,145},{145,129... | collective-permute-start | bytes 1572872 | tf_op jit(solution)/shard_map/ppermute | solution.py:335
  160.5 20.0 %collective-permute-start.44 = (bf16[2,2,4,32,512]{4,3,2,1,0:T(8,128)(2,1)S(1)}, bf16[2,2,4,32,512]{4,3,2,1,0:T(8,128)(2,1)S(1)}, u32[]{:S(2)}, u32[]{:S(2)}) collective-permute-start(bf16[2,2,4,32,512]{4,3,2,1,0:T(8,128)(2,1)S(1)} %bitcast.40), channel_id=1, source_target_pairs={{0,96},{32,64},{64,32},{96,0},{1,97},{33,65},{65,33},{97,1},{2,98}... | collective-permute-start | bytes 1572872 | tf_op jit(solution)/shard_map/ppermute | solution.py:334
  166.0 14.6 %collective-permute-start.43 = (bf16[2,2,4,32,512]{4,3,2,1,0:T(8,128)(2,1)S(1)}, bf16[2,2,4,32,512]{4,3,2,1,0:T(8,128)(2,1)S(1)}, u32[]{:S(2)}, u32[]{:S(2)}) collective-permute-start(bf16[2,2,4,32,512]{4,3,2,1,0:T(8,128)(2,1)S(1)} %bitcast.41), channel_id=1, source_target_pairs={{0,32},{32,0},{64,96},{96,64},{1,33},{33,1},{65,97},{97,65},{2,34}... | collective-permute-start | bytes 1572872 | tf_op jit(solution)/shard_map/ppermute | solution.py:334
  186.5 8.3 %collective-permute-start.47 = (f32[384,512]{1,0:T(8,128)S(1)}, f32[384,512]{1,0:T(8,128)S(1)}, u32[]{:S(2)}, u32[]{:S(2)}) collective-permute-start(f32[384,512]{1,0:T(8,128)S(1)} %get-tuple-element.110), channel_id=1, source_target_pairs={{0,1},{1,0},{2,3},{3,2},{4,5},{5,4},{6,7},{7,6},{8,9},{9,8},{10,11... | collective-permute-start | bytes 2359304 | tf_op jit(solution)/shard_map/ppermute | solution.py:368
  (26 other events, 174.2 us)

commit v6 on v5

--- a/solution.py
+++ b/solution.py
@@ -117,34 +117,26 @@
     return decay_rate * moment + (1.0 - decay_rate) * (mean + tiny_square)
 
 
-def stats_kernel(pos, near_half, far_half, packed, stats, scaled):
-    hidden = near_half.shape[-1]
-    upper = pos[5] >= ZH
-    cols = jnp.zeros((GR, hidden), f32)
-    scaled_cols = jnp.zeros((GR, hidden), f32)
-    weights = jnp.zeros((GR, hidden), f32)
-    row_total = jnp.zeros((GR, 1), f32)
-    for z in range(ZN):
-        near, far = near_half[z % ZH].astype(f32), far_half[z % ZH].astype(f32)
-        g = jnp.where(upper, far, near) if z < ZH else jnp.where(upper, near, far)
-        squares = g * g
-        rows = row_moment_of(packed[reverse_bits(z), :, hidden : hidden + 1], squares)
-        u = g * lax.rsqrt(rows)
-        scaled[z] = u
-        w = packed[reverse_bits(z), :, :hidden]
-        cols, scaled_cols, weights = cols + squares, scaled_cols + u * u, weights + w * w
-        row_total = row_total + rows
+def stats_kernel(g32, packed, stats, block):
+    hidden = g32.shape[-1]
+    g, w = g32[...], packed[:, :hidden]
+    squares = g * g
+    rows = row_moment_of(packed[:, hidden : hidden + 1], squares)
+    u = g * lax.rsqrt(rows)
+    block[:, :hidden], block[:, hidden:] = w, u
     lane = lax.broadcasted_iota(jnp.int32, (1, hidden), 1)
     total = lambda v: jnp.sum(v, axis=0, keepdims=True)
-    scalars = jnp.where(lane == 0, total(row_total), 0.0) + jnp.where(
-        lane == 1, jnp.sum(total(weights), axis=1, keepdims=True), 0.0
+    scalars = jnp.where(lane == 0, total(rows), 0.0) + jnp.where(
+        lane == 1, jnp.sum(total(w * w), axis=1, keepdims=True), 0.0
     )
     stats[...] = jnp.zeros_like(stats)
-    stats[0:1], stats[1:2], stats[2:3] = total(cols), total(scaled_cols), scalars
-
-
-def rows_kernel(width, stats, col_moment, packed, scaled, a_half, b_half, cols_new, inv_cols):
-    hidden = scaled.shape[-1]
+    stats[0:1], stats[1:2], stats[2:3] = total(squares), total(u * u), scalars
+
+
+def rows_kernel(width, pos, stats, col_moment, near_half, far_half, *outs):
+    a_half, b_half, cols_new, inv_cols = outs
+    hidden = stats.shape[-1]
+    upper = pos[5] >= ZH
     lane = lax.broadcasted_iota(jnp.int32, (1, hidden), 1)
     pick = lambda k: jnp.sum(jnp.where(lane == k, stats[2:3], 0.0), axis=1, keepdims=True)
     cols = decay_rate * col_moment[...] + (1.0 - decay_rate) * (
@@ -161,9 +153,13 @@
     )
     inv = factor * lax.rsqrt(cols)
     cols_new[...], inv_cols[...] = cols, inv
-    for z in range(ZN):
-        new = packed[reverse_bits(z), :, :hidden] - learn_rate * (scaled[z] * inv)
-        (a_half, b_half)[z // ZH][z % ZH] = new.astype(bf16)
+    for z in range(ZH):
+        near, far = [
+            (v[z, :, :hidden] - learn_rate * (v[z, :, hidden:] * inv)).astype(bf16)
+            for v in (near_half, far_half)
+        ]
+        a_half[z] = jnp.where(upper, far, near)
+        b_half[z] = jnp.where(upper, near, far)
 
 
 def return_kernel(pos, near, far, weight, moment, inv_cols, new_weight, delta, rows_new):
@@ -195,7 +191,7 @@
     seg = width // 16
     cuts, y1, y0, xlo, z, core = [lax.axis_index(a) for a in AXES]
     pos = jnp.stack([core, y1, y0, xlo, cuts, reverse_bits(z)]).astype(jnp.int32)
-    params = pltpu.CompilerParams(vmem_limit_bytes=12 * 2**20)
+    params = pltpu.CompilerParams(vmem_limit_bytes=16 * 2**20)
     small = pltpu.CompilerParams(vmem_limit_bytes=6 * 2**20)
     cost = pl.CostEstimate(
         flops=64 * tok_rows * seg * hidden, bytes_accessed=16 * 2**20, transcendentals=0
@@ -211,7 +207,7 @@
             pl.BlockSpec((tok_rows, seg), lambda g, pos: (0, g)),
         ]
 
-    order = [(0, 0), (1, 0), (0, 1), (1, 1)]
+    order = [(0, 1), (1, 1), (0, 0), (1, 0)]
     cotangent2 = lax.ppermute(cotangent, "core", SWAP)
     tokens2 = {}
     for part, step in order:
@@ -240,9 +236,8 @@
         [my_weight, jnp.broadcast_to(my_moment[:, None], (32, 128))], axis=1
     )
     packed = lax.ppermute(packed, TURNED, TURN)
-    tokens2, cotangent2 = lax.optimization_barrier((tokens2, cotangent2))
-
-    parts, chain = {}, pos
+
+    parts = {}
     for part, step in order:
         kept = jax.ShapeDtypeStruct(piece, bf16 if step else f32)
         parts[part, step], parts[part, 2 + step] = pl.pallas_call(
@@ -256,14 +251,9 @@
             ),
             compiler_params=params,
             cost_estimate=cost,
-        )(chain, tokens, tokens2[part, step], cotangent, cotangent2)
-        chain, _ = lax.optimization_barrier((pos, parts[part, 2 + step]))
+        )(pos, tokens, tokens2[part, step], cotangent, cotangent2)
     a_parts, b_parts = [[parts[p, k] for k in range(4)] for p in range(2)]
     a_got, b_got = exchange(a_parts, Y), exchange(b_parts, X)
-    a_got, packed = lax.optimization_barrier((a_got, packed))
-    packed = lax.all_to_all(
-        jnp.broadcast_to(packed[None], (ZN,) + packed.shape), "z", 0, 0, tiled=True
-    )
     a_sum = a_parts[0] + sum(p.astype(f32) for p in a_got)
     b_sum = b_parts[0] + sum(p.astype(f32) for p in b_got)
 
@@ -296,38 +286,48 @@
     near = lax.ppermute(g32, TURNED, TURN)
     far = lax.ppermute(g32, ("cuts",) + TURNED, FAR_TURN)
 
-    g16 = g32.astype(bf16)
-    got = [lax.ppermute(g16, "z", xor_perm(ZN, LINE_STEP[k])) for k in (1, 2, 3)]
+    stats, own = pl.pallas_call(
+        stats_kernel,
+        out_shape=[
+            jax.ShapeDtypeStruct((8, hidden), f32),
+            jax.ShapeDtypeStruct((GR, 2 * hidden), f32),
+        ],
+        compiler_params=small,
+    )(g32, packed)
+    got = [lax.ppermute(own, "z", xor_perm(ZN, LINE_STEP[k])) for k in (1, 2, 3)]
     near_half = pl.pallas_call(
         line_kernel,
-        out_shape=jax.ShapeDtypeStruct(part_line, bf16),
+        out_shape=jax.ShapeDtypeStruct((ZH,) + own.shape, f32),
         in_specs=in_specs(4),
         compiler_params=small,
-    )(pos, g16, *got)
+    )(pos, own, *got)
     far_half = lax.ppermute(near_half, "z", xor_perm(ZN, 1))
-    far_half, near, far = lax.optimization_barrier((far_half, near, far))
-
-    stats, scaled = pl.pallas_call(
-        stats_kernel,
-        out_shape=[jax.ShapeDtypeStruct((8, hidden), f32), jax.ShapeDtypeStruct(line, f32)],
-        in_specs=in_specs(3),
-        compiler_params=small,
-    )(pos, near_half, far_half, packed)
     stats = stats + lax.ppermute(stats, "core", SWAP)
     stats = four_sum(stats, exchange([stats] * 4, Y))
     stats = four_sum(stats, exchange([stats] * 4, X))
+    stats = four_sum(stats, [lax.ppermute(stats, "z", xor_perm(ZN, k)) for k in (1, 2, 3)])
+    stats = stats + lax.ppermute(stats, "z", xor_perm(ZN, 4))
+    stats, near, far = lax.optimization_barrier((stats, near, far))
 
     row_vector = jax.ShapeDtypeStruct((1, hidden), f32)
     a_half, b_half, cols_new, inv_cols = pl.pallas_call(
         functools.partial(rows_kernel, width),
         out_shape=[jax.ShapeDtypeStruct((ZH, GR, hidden), bf16)] * 2 + [row_vector] * 2,
-        compiler_params=small,
-    )(stats, col_moment.reshape(1, hidden), packed, scaled)
+        in_specs=in_specs(4),
+        compiler_params=small,
+    )(pos, stats, col_moment.reshape(1, hidden), near_half, far_half)
     a_all = [a_half] + exchange([a_half] * 4, X)
     b_all = [b_half] + exchange([b_half] * 4, Y)
     a_half = jnp.stack([a_all[0], a_all[2], a_all[1], a_all[3]]).reshape(piece)
     b_half = jnp.stack([b_all[0], b_all[2], b_all[1], b_all[3]]).reshape(piece)
-    a_half, b_half = lax.optimization_barrier((a_half, b_half))
+    slab = jax.ShapeDtypeStruct(weight.shape, f32)
+    new_weight, delta, rows_new = pl.pallas_call(
+        return_kernel,
+        out_shape=[slab, slab, jax.ShapeDtypeStruct((weight.shape[0], 1), f32)],
+        in_specs=in_specs(5),
+        compiler_params=small,
+    )(pos, near, far, weight, row_moment[:, None], inv_cols)
+    a_half, b_half, rows_new = lax.optimization_barrier((a_half, b_half, rows_new))
     a_all, b_all = [a_half], [b_half]
     got = {}
     for k in (2, 1, 3):
@@ -335,15 +335,6 @@
         got[1, k] = lax.ppermute(b_half, X, xor_perm(4, k))
     a_all += [got[0, k] for k in (1, 2, 3)]
     b_all += [got[1, k] for k in (1, 2, 3)]
-
-    slab = jax.ShapeDtypeStruct(weight.shape, f32)
-    new_weight, delta, rows_new = pl.pallas_call(
-        return_kernel,
-        out_shape=[slab, slab, jax.ShapeDtypeStruct((weight.shape[0], 1), f32)],
-        in_specs=in_specs(5),
-        compiler_params=small,
-    )(pos, near, far, weight, row_moment[:, None], inv_cols)
-    a_all[2], _ = lax.optimization_barrier((a_all[2], rows_new))
 
     result = jax.ShapeDtypeStruct((tok_rows, hidden), f32)
     sums = []

time: 196 us -> 196 us (level)
  waiting for transfers between devices: 61.4 us -> 68.8 us
  Pallas kernels: 34.8 us -> 29.3 us
  other arithmetic: 4.89 us -> 2.43 us
    ppermute x24, waiting for transfers between devices: 28.4 us -> 36 us  [exchange(): return [lax.ppermute(pieces[k], axes, xor_perm(4, k)) for k in (1, 2, 3)]]
    ppermute x1, starting transfers between devices: 6.42 us -> 1.57 us  [on_device(): summed = own + lax.ppermute(away, 'core', SWAP)]
    ppermute x1, starting transfers between devices: 0.09 us -> 4.9 us  [on_device(): stats = stats + lax.ppermute(stats, 'core', SWAP)]
    ppermute x3 -> x7, starting transfers between devices: 5.74 us -> 10.3 us  [the longest x3 6.06 us: on_device(): lax.ppermute(own, 'z', xor_perm(ZN, LINE_STEP[k]))]
    ppermute x3, waiting for transfers between devices: 8.53 us -> 13 us  [on_device(): got[0, k] = lax.ppermute(a_half, Y, xor_perm(4, k))]
    ppermute x24, starting transfers between devices: 27.5 us -> 31.5 us  [exchange(): return [lax.ppermute(pieces[k], axes, xor_perm(4, k)) for k in (1, 2, 3)]]
    pallas_call x4, Pallas kernels: 11.9 us -> 8.25 us  [on_device(): pl.pallas_call(functools.partial(apply_kernel, part), out_shape=[result,...]
    all_to_all x1 -> x0, starting transfers between devices: 3.64 us -> none  [on_device(): lax.all_to_all(jnp.broadcast_to(packed[None], (ZN,) + packed.shape), 'z',...]
  transfers between devices with their start and end apart: 49 -> 52, of which waited for: 20 -> 26; matrix products, arithmetic and copies ran while one was open for 3% -> 1% of each run, Pallas kernels for 14% -> 12%
where the time goes in v6:
time: 196 us
  starting transfers between devices  83.8 us (43%)
  waiting for transfers between devices  68.8 us (35%)
  Pallas kernels  29.3 us (15%)
  local copies, waits for them, and re-layouts  10.4 us (5%)
  other arithmetic  2.43 us (1%)
    ppermute x24, waiting for transfers between devices, exchange(): return [lax.ppermute(pieces[k], axes, xor_perm(4, k)) for k in (1, 2, 3)]  36 us
    ppermute x24, starting transfers between devices, exchange(): return [lax.ppermute(pieces[k], axes, xor_perm(4, k)) for k in (1, 2, 3)]  31.5 us
    pallas_call x4, Pallas kernels, on_device(): pl.pallas_call(functools.partial(grad_kernel, part), out_shape=[kept, jax...  13.1 us
    ppermute x3, waiting for transfers between devices, on_device(): got[0, k] = lax.ppermute(a_half, Y, xor_perm(4, k))  13 us
    ppermute x1, starting transfers between devices, on_device(): near = lax.ppermute(g32, TURNED, TURN)  11.3 us
    ppermute x1, starting transfers between devices, on_device(): packed = lax.ppermute(packed, TURNED, TURN)  10.1 us
    unnamed x22, local copies, waits for them, and re-layouts  9.98 us
    pallas_call x4, Pallas kernels, on_device(): pl.pallas_call(functools.partial(apply_kernel, part), out_shape=[result,...  8.25 us
  transfers between devices with their start and end apart: 52, of which 26 were waited for; matrix products, arithmetic and copies ran while one was open for 1% of the time, Pallas kernels for 12%

profile of v6, /device:TPU:33, one launch (start us, length us, event | category | flops | bytes accessed | tf_op | source)
XLA Modules:
  0.0 195.7 jit_solution(17177257826904832861)
XLA Ops:
  0.7 2.8 %copy-done = bf16[384,8192]{1,0:T(8,128)(2,1)S(1)} copy-done((bf16[384,8192]{1,0:T(8,128)(2,1)S(1)}, bf16[384,8192]{1,0:T(8,128)(2,1)}, u32[]{:S(2)}) %copy-start) | copy-done | bytes 6291480
  6.7 10.1 %collective-permute-start.17 = (f32[32,640]{1,0:T(8,128)S(1)}, f32[32,640]{1,0:T(8,128)S(1)}, u32[]{:S(2)}, u32[]{:S(2)}) collective-permute-start(f32[32,640]{1,0:T(8,128)S(1)} %pad_maximum_fusion.2), channel_id=1, source_target_pairs={{0,0},{1,64},{2,8},{3,72},{4,4},{5,68},{6,12},{7,76},{8,2},{9,66},... | collective-permute-start | bytes 245768 | tf_op jit(solution)/shard_map/ppermute | solution.py:238
  16.8 2.8 %copy-done.1 = bf16[384,8192]{1,0:T(8,128)(2,1)S(1)} copy-done((bf16[384,8192]{1,0:T(8,128)(2,1)S(1)}, bf16[384,8192]{1,0:T(8,128)(2,1)}, u32[]{:S(2)}) %copy-start.1) | copy-done | bytes 6291480
  22.3 3.3 %shard_map.97 = (f32[2,2,4,32,512]{4,3,2,1,0:T(8,128)S(1)}, bf16[2,2,4,32,512]{4,3,2,1,0:T(8,128)(2,1)S(1)}) custom-call(s32[6]{0:T(128)S(1)} %stack.57.pos, bf16[384,8192]{1,0:T(8,128)(2,1)S(1)} %copy-done.2, bf16[384,1024]{1,0:T(8,128)(2,1)S(1)} %collective-permute-done.9.tok2, bf16[384,512]{1,0:T(8,128)(2,1)} %cot.7, ...), custom_call_target="tpu_custom_call" | custom-call | flops 6442450944 | bytes 16777216 | tf_op jit(solution)/shard_map/pallas_call | solution.py:243
  25.6 2.8 %collective-permute-start.12 = (bf16[2,2,4,32,512]{4,3,2,1,0:T(8,128)(2,1)S(1)}, bf16[2,2,4,32,512]{4,3,2,1,0:T(8,128)(2,1)S(1)}, u32[]{:S(2)}, u32[]{:S(2)}) collective-permute-start(bf16[2,2,4,32,512]{4,3,2,1,0:T(8,128)(2,1)S(1)} %get-tuple-element.52), channel_id=1, source_target_pairs={{0,128},{16,144},{128,0},{144,16},{1,129},{17,145},{129,1},{145,17... | collective-permute-start | bytes 1572872 | tf_op jit(solution)/shard_map/ppermute | solution.py:181
  28.4 3.3 %shard_map.99 = (bf16[2,2,4,32,512]{4,3,2,1,0:T(8,128)(2,1)S(1)}, bf16[2,2,4,32,512]{4,3,2,1,0:T(8,128)(2,1)S(1)}) custom-call(s32[6]{0:T(128)S(1)} %stack.57.pos, bf16[384,8192]{1,0:T(8,128)(2,1)S(1)} %copy-done.2, bf16[384,1024]{1,0:T(8,128)(2,1)S(1)} %collective-permute-done.10.tok2, bf16[384,512]{1,0:T(8,128)(2,1)} %cot.7, ...), custom_call_target="tpu_custom_call" | custom-call | flops 6442450944 | bytes 16777216 | tf_op jit(solution)/shard_map/pallas_call | solution.py:243
  32.8 3.3 %shard_map.93 = (f32[2,2,4,32,512]{4,3,2,1,0:T(8,128)S(1)}, bf16[2,2,4,32,512]{4,3,2,1,0:T(8,128)(2,1)S(1)}) custom-call(s32[6]{0:T(128)S(1)} %stack.57.pos, bf16[384,8192]{1,0:T(8,128)(2,1)S(1)} %copy-done.2, bf16[384,1024]{1,0:T(8,128)(2,1)S(1)} %collective-permute-done.tok2, bf16[384,512]{1,0:T(8,128)(2,1)} %cot.7, ...), custom_call_target="tpu_custom_call" | custom-call | flops 6442450944 | bytes 16777216 | tf_op jit(solution)/shard_map/pallas_call | solution.py:243
  36.5 3.3 %shard_map.95 = (bf16[2,2,4,32,512]{4,3,2,1,0:T(8,128)(2,1)S(1)}, bf16[2,2,4,32,512]{4,3,2,1,0:T(8,128)(2,1)S(1)}) custom-call(s32[6]{0:T(128)S(1)} %stack.57.pos, bf16[384,8192]{1,0:T(8,128)(2,1)S(1)} %copy-done.2, bf16[384,1024]{1,0:T(8,128)(2,1)S(1)} %collective-permute-done.2.tok2, bf16[384,512]{1,0:T(8,128)(2,1)} %cot.7, ...), custom_call_target="tpu_custom_call" | custom-call | flops 6442450944 | bytes 16777216 | tf_op jit(solution)/shard_map/pallas_call | solution.py:243
  41.6 10.9 %collective-permute-done.11 = bf16[2,2,4,32,512]{4,3,2,1,0:T(8,128)(2,1)S(1)} collective-permute-done((bf16[2,2,4,32,512]{4,3,2,1,0:T(8,128)(2,1)S(1)}, bf16[2,2,4,32,512]{4,3,2,1,0:T(8,128)(2,1)S(1)}, u32[]{:S(2)}, u32[]{:S(2)}) %collective-permute-start.11) | collective-permute-done | bytes 524320 | tf_op jit(solution)/shard_map/ppermute | solution.py:181
  53.4 3.5 %collective-permute-start.15 = (bf16[4,32,512]{2,1,0:T(8,128)(2,1)S(1)}, bf16[4,32,512]{2,1,0:T(8,128)(2,1)S(1)}, u32[]{:S(2)}, u32[]{:S(2)}) collective-permute-start(bf16[4,32,512]{2,1,0:T(8,128)(2,1)S(1)} %get-tuple-element.92), channel_id=1, source_target_pairs={{0,64},{32,96},{64,0},{96,32},{1,65},{33,97},{65,1},{97,33},{2,66}... | collective-permute-start | bytes 393224 | tf_op jit(solution)/shard_map/ppermute | solution.py:181
  56.8 1.9 collective-permute-done.3
  58.7 3.9 %collective-permute-start.16 = (bf16[4,32,512]{2,1,0:T(8,128)(2,1)S(1)}, bf16[4,32,512]{2,1,0:T(8,128)(2,1)S(1)}, u32[]{:S(2)}, u32[]{:S(2)}) collective-permute-start(bf16[4,32,512]{2,1,0:T(8,128)(2,1)S(1)} %get-tuple-element.91), channel_id=1, source_target_pairs={{0,96},{32,64},{64,32},{96,0},{1,97},{33,65},{65,33},{97,1},{2,98}... | collective-permute-start | bytes 393224 | tf_op jit(solution)/shard_map/ppermute | solution.py:181
  62.6 7.0 %collective-permute-done.5 = bf16[2,2,4,32,512]{4,3,2,1,0:T(8,128)(2,1)S(1)} collective-permute-done((bf16[2,2,4,32,512]{4,3,2,1,0:T(8,128)(2,1)S(1)}, bf16[2,2,4,32,512]{4,3,2,1,0:T(8,128)(2,1)S(1)}, u32[]{:S(2)}, u32[]{:S(2)}) %collective-permute-start.5) | collective-permute-done | bytes 524320 | tf_op jit(solution)/shard_map/ppermute | solution.py:181
  74.0 4.0 %collective-permute-done.7.refs_2_ = bf16[4,32,512]{2,1,0:T(8,128)(2,1)S(1)} collective-permute-done((bf16[4,32,512]{2,1,0:T(8,128)(2,1)S(1)}, bf16[4,32,512]{2,1,0:T(8,128)(2,1)S(1)}, u32[]{:S(2)}, u32[]{:S(2)}) %collective-permute-start.7) | collective-permute-done | bytes 131104 | tf_op jit(solution)/shard_map/ppermute | solution.py:181
  78.0 2.1 %collective-permute-done.8.refs_3_ = bf16[4,32,512]{2,1,0:T(8,128)(2,1)S(1)} collective-permute-done((bf16[4,32,512]{2,1,0:T(8,128)(2,1)S(1)}, bf16[4,32,512]{2,1,0:T(8,128)(2,1)S(1)}, u32[]{:S(2)}, u32[]{:S(2)}) %collective-permute-start.8) | collective-permute-done | bytes 131104 | tf_op jit(solution)/shard_map/ppermute | solution.py:181
  80.8 3.8 %collective-permute-done.18.got = bf16[4,32,512]{2,1,0:T(8,128)(2,1)S(1)} collective-permute-done((bf16[4,32,512]{2,1,0:T(8,128)(2,1)S(1)}, bf16[4,32,512]{2,1,0:T(8,128)(2,1)S(1)}, u32[]{:S(2)}, u32[]{:S(2)}) %collective-permute-start.18) | collective-permute-done | bytes 131104 | tf_op jit(solution)/shard_map/ppermute | solution.py:276
  87.3 3.7 %collective-permute-start.21 = (bf16[32,512]{1,0:T(8,128)(2,1)S(1)}, bf16[32,512]{1,0:T(8,128)(2,1)S(1)}, u32[]{:S(2)}, u32[]{:S(2)}) collective-permute-start(bf16[32,512]{1,0:T(8,128)(2,1)S(1)} %get-tuple-element.62), channel_id=1, source_target_pairs={{0,12},{2,14},{4,8},{6,10},{8,4},{10,6},{12,0},{14,2},{1,13},{3,15... | collective-permute-start | bytes 98312 | tf_op jit(solution)/shard_map/ppermute | solution.py:283
  92.5 4.6 %collective-permute-start.35 = (f32[32,1024]{1,0:T(8,128)S(1)}, f32[32,1024]{1,0:T(8,128)S(1)}, u32[]{:S(2)}, u32[]{:S(2)}) collective-permute-start(f32[32,1024]{1,0:T(8,128)S(1)} %get-tuple-element.68.refs_0_), channel_id=1, source_target_pairs={{0,8},{2,10},{4,12},{6,14},{8,0},{10,2},{12,4},{14,6},{1,9},{3,11}... | collective-permute-start | bytes 393224 | tf_op jit(solution)/shard_map/ppermute | solution.py:297
  98.6 4.9 %collective-permute-start.22 = (f32[8,512]{1,0:T(8,128)S(1)}, f32[8,512]{1,0:T(8,128)S(1)}, u32[]{:S(2)}, u32[]{:S(2)}) collective-permute-start(f32[8,512]{1,0:T(8,128)S(1)} %get-tuple-element.64), channel_id=1, source_target_pairs={{0,1},{1,0},{2,3},{3,2},{4,5},{5,4},{6,7},{7,6},{8,9},{9,8},{10,11... | collective-permute-start | bytes 49160 | tf_op jit(solution)/shard_map/ppermute | solution.py:305
  104.3 4.1 %collective-permute-start.24 = (f32[8,512]{1,0:T(8,128)S(1)}, f32[8,512]{1,0:T(8,128)S(1)}, u32[]{:S(2)}, u32[]{:S(2)}) collective-permute-start(f32[8,512]{1,0:T(8,128)S(1)} %add.86), channel_id=1, source_target_pairs={{0,32},{32,0},{64,96},{96,64},{1,33},{33,1},{65,97},{97,65},{2,34}... | collective-permute-start | bytes 49160 | tf_op jit(solution)/shard_map/ppermute | solution.py:181
  118.3 2.1 %collective-permute-start.29 = (f32[8,512]{1,0:T(8,128)S(1)}, f32[8,512]{1,0:T(8,128)S(1)}, u32[]{:S(2)}, u32[]{:S(2)}) collective-permute-start(f32[8,512]{1,0:T(8,128)S(1)} %add_add_fusion.4), channel_id=1, source_target_pairs={{0,4},{2,6},{4,0},{6,2},{8,12},{10,14},{12,8},{14,10},{1,5},{3,7},... | collective-permute-start | bytes 49160 | tf_op jit(solution)/shard_map/ppermute | solution.py:308
  121.5 11.3 %collective-permute-start.33 = (f32[32,512]{1,0:T(8,128)S(1)}, f32[32,512]{1,0:T(8,128)S(1)}, u32[]{:S(2)}, u32[]{:S(2)}) collective-permute-start(f32[32,512]{1,0:T(8,128)S(1)} %add_add_fusion.2.g32), channel_id=1, source_target_pairs={{0,0},{1,64},{2,8},{3,72},{4,4},{5,68},{6,12},{7,76},{8,2},{9,66},... | collective-permute-start | bytes 196616 | tf_op jit(solution)/shard_map/ppermute | solution.py:286
  134.4 5.8 %collective-permute-done.32 = f32[8,512]{1,0:T(8,128)S(1)} collective-permute-done((f32[8,512]{1,0:T(8,128)S(1)}, f32[8,512]{1,0:T(8,128)S(1)}, u32[]{:S(2)}, u32[]{:S(2)}) %collective-permute-start.32) | collective-permute-done | bytes 16416 | tf_op jit(solution)/shard_map/ppermute | solution.py:309
  140.2 5.1 %collective-permute-done.34.far = f32[32,512]{1,0:T(8,128)S(1)} collective-permute-done((f32[32,512]{1,0:T(8,128)S(1)}, f32[32,512]{1,0:T(8,128)S(1)}, u32[]{:S(2)}, u32[]{:S(2)}) %collective-permute-start.34) | collective-permute-done | bytes 65568 | tf_op jit(solution)/shard_map/ppermute | solution.py:287
  146.5 2.3 %collective-permute-start.43 = (bf16[4,32,512]{2,1,0:T(8,128)(2,1)S(1)}, bf16[4,32,512]{2,1,0:T(8,128)(2,1)S(1)}, u32[]{:S(2)}, u32[]{:S(2)}) collective-permute-start(bf16[4,32,512]{2,1,0:T(8,128)(2,1)S(1)} %get-tuple-element.73), channel_id=1, source_target_pairs={{0,32},{32,0},{64,96},{96,64},{1,33},{33,1},{65,97},{97,65},{2,34}... | collective-permute-start | bytes 393224 | tf_op jit(solution)/shard_map/ppermute | solution.py:181
  148.9 2.4 %collective-permute-start.44 = (bf16[4,32,512]{2,1,0:T(8,128)(2,1)S(1)}, bf16[4,32,512]{2,1,0:T(8,128)(2,1)S(1)}, u32[]{:S(2)}, u32[]{:S(2)}) collective-permute-start(bf16[4,32,512]{2,1,0:T(8,128)(2,1)S(1)} %get-tuple-element.73), channel_id=1, source_target_pairs={{0,96},{32,64},{64,32},{96,0},{1,97},{33,65},{65,33},{97,1},{2,98}... | collective-permute-start | bytes 393224 | tf_op jit(solution)/shard_map/ppermute | solution.py:181
  164.2 10.7 %collective-permute-done.50.piece1 = bf16[2,2,4,32,512]{4,3,2,1,0:T(8,128)(2,1)S(1)} collective-permute-done((bf16[2,2,4,32,512]{4,3,2,1,0:T(8,128)(2,1)S(1)}, bf16[2,2,4,32,512]{4,3,2,1,0:T(8,128)(2,1)S(1)}, u32[]{:S(2)}, u32[]{:S(2)}) %collective-permute-start.50) | collective-permute-done | bytes 524320 | tf_op jit(solution)/shard_map/ppermute | solution.py:334
  175.8 2.8 %copy-done.3 = bf16[384,8192]{1,0:T(8,128)(2,1)S(1)} copy-done((bf16[384,8192]{1,0:T(8,128)(2,1)S(1)}, bf16[384,8192]{1,0:T(8,128)(2,1)}, u32[]{:S(2)}) %copy-start.3) | copy-done | bytes 6291480
  179.8 2.1 %shard_map.106 = (f32[384,512]{1,0:T(8,128)S(1)}, f32[384,512]{1,0:T(8,128)S(1)}) custom-call(s32[6]{0:T(128)S(1)} %stack.57.pos, bf16[384,8192]{1,0:T(8,128)(2,1)S(1)} %copy-done.3, bf16[384,1024]{1,0:T(8,128)(2,1)S(1)} %copy-done.9, bf16[2,2,4,32,512]{4,3,2,1,0:T(8,128)(2,1)S(1)} %bitcast.42, bf16[2,2,4,32,512]{4,3,2,1,0:T(8,128)(2,1)S(1)} %collective-permute-done.50.piece1), custom_call_target="tpu_custom_call" | custom-call | flops 6442450944 | bytes 16777216 | tf_op jit(solution)/shard_map/pallas_call | solution.py:343
  181.8 2.1 %shard_map.107 = (f32[384,512]{1,0:T(8,128)S(1)}, f32[384,512]{1,0:T(8,128)S(1)}) custom-call(s32[6]{0:T(128)S(1)} %stack.57.pos, bf16[384,8192]{1,0:T(8,128)(2,1)S(1)} %copy-done.3, bf16[384,1024]{1,0:T(8,128)(2,1)S(1)} %collective-permute-done.9.tok2, bf16[2,2,4,32,512]{4,3,2,1,0:T(8,128)(2,1)S(1)} %bitcast.38, ...), custom_call_target="tpu_custom_call" | custom-call | flops 6442450944 | bytes 16777216 | tf_op jit(solution)/shard_map/pallas_call | solution.py:343
  186.2 2.1 %shard_map.108 = (f32[384,512]{1,0:T(8,128)S(1)}, f32[384,512]{1,0:T(8,128)S(1)}) custom-call(s32[6]{0:T(128)S(1)} %stack.57.pos, bf16[384,8192]{1,0:T(8,128)(2,1)S(1)} %copy-done.3, bf16[384,1024]{1,0:T(8,128)(2,1)S(1)} %copy-done.7, bf16[2,2,4,32,512]{4,3,2,1,0:T(8,128)(2,1)S(1)} %collective-permute-done.47.piece0, ...), custom_call_target="tpu_custom_call" | custom-call | flops 6442450944 | bytes 16777216 | tf_op jit(solution)/shard_map/pallas_call | solution.py:343
  189.3 2.1 %shard_map.109 = (f32[384,512]{1,0:T(8,128)S(1)}, f32[384,512]{1,0:T(8,128)S(1)}) custom-call(s32[6]{0:T(128)S(1)} %stack.57.pos, bf16[384,8192]{1,0:T(8,128)(2,1)S(1)} %copy-done.3, bf16[384,1024]{1,0:T(8,128)(2,1)S(1)} %collective-permute-done.10.tok2, bf16[2,2,4,32,512]{4,3,2,1,0:T(8,128)(2,1)S(1)} %collective-permute-done.45.piece0, ...), custom_call_target="tpu_custom_call" | custom-call | flops 6442450944 | bytes 16777216 | tf_op jit(solution)/shard_map/pallas_call | solution.py:343
  (134 shorter events, 58.1 us)
Async XLA Ops:
  4.3 17.5 %collective-permute-start.9 = (bf16[384,1024]{1,0:T(8,128)(2,1)S(1)}, bf16[384,1024]{1,0:T(8,128)(2,1)S(1)}, u32[]{:S(2)}, u32[]{:S(2)}) collective-permute-start(bf16[384,1024]{1,0:T(8,128)(2,1)S(1)} %shard_map.96), channel_id=1, source_target_pairs={{0,1},{1,0},{2,3},{3,2},{4,5},{5,4},{6,7},{7,6},{8,9},{9,8},{10,11... | collective-permute-start | bytes 2359304 | tf_op jit(solution)/shard_map/ppermute | solution.py:231
  5.1 16.2 %collective-permute-start.1 = (bf16[384,512]{1,0:T(8,128)(2,1)}, bf16[384,512]{1,0:T(8,128)(2,1)}, u32[]{:S(2)}, u32[]{:S(2)}) collective-permute-start(bf16[384,512]{1,0:T(8,128)(2,1)} %cot.7), channel_id=1, source_target_pairs={{0,1},{1,0},{2,3},{3,2},{4,5},{5,4},{6,7},{7,6},{8,9},{9,8},{10,11... | collective-permute-start | bytes 1179656 | tf_op jit(solution)/shard_map/ppermute | solution.py:211
  6.0 22.4 %collective-permute-start.10 = (bf16[384,1024]{1,0:T(8,128)(2,1)S(1)}, bf16[384,1024]{1,0:T(8,128)(2,1)S(1)}, u32[]{:S(2)}, u32[]{:S(2)}) collective-permute-start(bf16[384,1024]{1,0:T(8,128)(2,1)S(1)} %shard_map.98), channel_id=1, source_target_pairs={{0,1},{1,0},{2,3},{3,2},{4,5},{5,4},{6,7},{7,6},{8,9},{9,8},{10,11... | collective-permute-start | bytes 2359304 | tf_op jit(solution)/shard_map/ppermute | solution.py:231
  6.7 64.6 %collective-permute-start.17 = (f32[32,640]{1,0:T(8,128)S(1)}, f32[32,640]{1,0:T(8,128)S(1)}, u32[]{:S(2)}, u32[]{:S(2)}) collective-permute-start(f32[32,640]{1,0:T(8,128)S(1)} %pad_maximum_fusion.2), channel_id=1, source_target_pairs={{0,0},{1,64},{2,8},{3,72},{4,4},{5,68},{6,12},{7,76},{8,2},{9,66},... | collective-permute-start | bytes 245768 | tf_op jit(solution)/shard_map/ppermute | solution.py:238
  20.3 11.8 %collective-permute-start = (bf16[384,1024]{1,0:T(8,128)(2,1)S(1)}, bf16[384,1024]{1,0:T(8,128)(2,1)S(1)}, u32[]{:S(2)}, u32[]{:S(2)}) collective-permute-start(bf16[384,1024]{1,0:T(8,128)(2,1)S(1)} %shard_map.92), channel_id=1, source_target_pairs={{0,1},{1,0},{2,3},{3,2},{4,5},{5,4},{6,7},{7,6},{8,9},{9,8},{10,11... | collective-permute-start | bytes 2359304 | tf_op jit(solution)/shard_map/ppermute | solution.py:231
  21.3 14.8 %collective-permute-start.2 = (bf16[384,1024]{1,0:T(8,128)(2,1)S(1)}, bf16[384,1024]{1,0:T(8,128)(2,1)S(1)}, u32[]{:S(2)}, u32[]{:S(2)}) collective-permute-start(bf16[384,1024]{1,0:T(8,128)(2,1)S(1)} %shard_map.94), channel_id=1, source_target_pairs={{0,1},{1,0},{2,3},{3,2},{4,5},{5,4},{6,7},{7,6},{8,9},{9,8},{10,11... | collective-permute-start | bytes 2359304 | tf_op jit(solution)/shard_map/ppermute | solution.py:231
  25.6 15.6 %collective-permute-start.12 = (bf16[2,2,4,32,512]{4,3,2,1,0:T(8,128)(2,1)S(1)}, bf16[2,2,4,32,512]{4,3,2,1,0:T(8,128)(2,1)S(1)}, u32[]{:S(2)}, u32[]{:S(2)}) collective-permute-start(bf16[2,2,4,32,512]{4,3,2,1,0:T(8,128)(2,1)S(1)} %get-tuple-element.52), channel_id=1, source_target_pairs={{0,128},{16,144},{128,0},{144,16},{1,129},{17,145},{129,1},{145,17... | collective-permute-start | bytes 1572872 | tf_op jit(solution)/shard_map/ppermute | solution.py:181
  31.7 20.8 %collective-permute-start.11 = (bf16[2,2,4,32,512]{4,3,2,1,0:T(8,128)(2,1)S(1)}, bf16[2,2,4,32,512]{4,3,2,1,0:T(8,128)(2,1)S(1)}, u32[]{:S(2)}, u32[]{:S(2)}) collective-permute-start(bf16[2,2,4,32,512]{4,3,2,1,0:T(8,128)(2,1)S(1)} %get-tuple-element.51), channel_id=1, source_target_pairs={{0,16},{16,0},{128,144},{144,128},{1,17},{17,1},{129,145},{145,129... | collective-permute-start | bytes 1572872 | tf_op jit(solution)/shard_map/ppermute | solution.py:181
  32.1 20.4 %collective-permute-start.13 = (bf16[2,2,4,32,512]{4,3,2,1,0:T(8,128)(2,1)S(1)}, bf16[2,2,4,32,512]{4,3,2,1,0:T(8,128)(2,1)S(1)}, u32[]{:S(2)}, u32[]{:S(2)}) collective-permute-start(bf16[2,2,4,32,512]{4,3,2,1,0:T(8,128)(2,1)S(1)} %get-tuple-element.53), channel_id=1, source_target_pairs={{0,144},{16,128},{128,16},{144,0},{1,145},{17,129},{129,17},{145,1... | collective-permute-start | bytes 1572872 | tf_op jit(solution)/shard_map/ppermute | solution.py:181
  36.1 17.3 %collective-permute-start.4 = (bf16[2,2,4,32,512]{4,3,2,1,0:T(8,128)(2,1)S(1)}, bf16[2,2,4,32,512]{4,3,2,1,0:T(8,128)(2,1)S(1)}, u32[]{:S(2)}, u32[]{:S(2)}) collective-permute-start(bf16[2,2,4,32,512]{4,3,2,1,0:T(8,128)(2,1)S(1)} %get-tuple-element.48), channel_id=1, source_target_pairs={{0,64},{32,96},{64,0},{96,32},{1,65},{33,97},{65,1},{97,33},{2,66}... | collective-permute-start | bytes 1572872 | tf_op jit(solution)/shard_map/ppermute | solution.py:181
  41.2 17.5 %collective-permute-start.3 = (bf16[2,2,4,32,512]{4,3,2,1,0:T(8,128)(2,1)S(1)}, bf16[2,2,4,32,512]{4,3,2,1,0:T(8,128)(2,1)S(1)}, u32[]{:S(2)}, u32[]{:S(2)}) collective-permute-start(bf16[2,2,4,32,512]{4,3,2,1,0:T(8,128)(2,1)S(1)} %get-tuple-element.47), channel_id=1, source_target_pairs={{0,32},{32,0},{64,96},{96,64},{1,33},{33,1},{65,97},{97,65},{2,34}... | collective-permute-start | bytes 1572872 | tf_op jit(solution)/shard_map/ppermute | solution.py:181
  52.5 17.1 %collective-permute-start.5 = (bf16[2,2,4,32,512]{4,3,2,1,0:T(8,128)(2,1)S(1)}, bf16[2,2,4,32,512]{4,3,2,1,0:T(8,128)(2,1)S(1)}, u32[]{:S(2)}, u32[]{:S(2)}) collective-permute-start(bf16[2,2,4,32,512]{4,3,2,1,0:T(8,128)(2,1)S(1)} %get-tuple-element.49), channel_id=1, source_target_pairs={{0,96},{32,64},{64,32},{96,0},{1,97},{33,65},{65,33},{97,1},{2,98}... | collective-permute-start | bytes 1572872 | tf_op jit(solution)/shard_map/ppermute | solution.py:181
  52.9 19.2 %collective-permute-start.14 = (bf16[4,32,512]{2,1,0:T(8,128)(2,1)S(1)}, bf16[4,32,512]{2,1,0:T(8,128)(2,1)S(1)}, u32[]{:S(2)}, u32[]{:S(2)}) collective-permute-start(bf16[4,32,512]{2,1,0:T(8,128)(2,1)S(1)} %get-tuple-element.93), channel_id=1, source_target_pairs={{0,32},{32,0},{64,96},{96,64},{1,33},{33,1},{65,97},{97,65},{2,34}... | collective-permute-start | bytes 393224 | tf_op jit(solution)/shard_map/ppermute | solution.py:181
  53.4 20.6 %collective-permute-start.15 = (bf16[4,32,512]{2,1,0:T(8,128)(2,1)S(1)}, bf16[4,32,512]{2,1,0:T(8,128)(2,1)S(1)}, u32[]{:S(2)}, u32[]{:S(2)}) collective-permute-start(bf16[4,32,512]{2,1,0:T(8,128)(2,1)S(1)} %get-tuple-element.92), channel_id=1, source_target_pairs={{0,64},{32,96},{64,0},{96,32},{1,65},{33,97},{65,1},{97,33},{2,66}... | collective-permute-start | bytes 393224 | tf_op jit(solution)/shard_map/ppermute | solution.py:181
  58.7 15.3 %collective-permute-start.16 = (bf16[4,32,512]{2,1,0:T(8,128)(2,1)S(1)}, bf16[4,32,512]{2,1,0:T(8,128)(2,1)S(1)}, u32[]{:S(2)}, u32[]{:S(2)}) collective-permute-start(bf16[4,32,512]{2,1,0:T(8,128)(2,1)S(1)} %get-tuple-element.91), channel_id=1, source_target_pairs={{0,96},{32,64},{64,32},{96,0},{1,97},{33,65},{65,33},{97,1},{2,98}... | collective-permute-start | bytes 393224 | tf_op jit(solution)/shard_map/ppermute | solution.py:181
  72.1 8.0 %collective-permute-start.8 = (bf16[4,32,512]{2,1,0:T(8,128)(2,1)S(1)}, bf16[4,32,512]{2,1,0:T(8,128)(2,1)S(1)}, u32[]{:S(2)}, u32[]{:S(2)}) collective-permute-start(bf16[4,32,512]{2,1,0:T(8,128)(2,1)S(1)} %get-tuple-element.94), channel_id=1, source_target_pairs={{0,144},{16,128},{128,16},{144,0},{1,145},{17,129},{129,17},{145,1... | collective-permute-start | bytes 393224 | tf_op jit(solution)/shard_map/ppermute | solution.py:181
  92.5 15.9 %collective-permute-start.35 = (f32[32,1024]{1,0:T(8,128)S(1)}, f32[32,1024]{1,0:T(8,128)S(1)}, u32[]{:S(2)}, u32[]{:S(2)}) collective-permute-start(f32[32,1024]{1,0:T(8,128)S(1)} %get-tuple-element.68.refs_0_), channel_id=1, source_target_pairs={{0,8},{2,10},{4,12},{6,14},{8,0},{10,2},{12,4},{14,6},{1,9},{3,11}... | collective-permute-start | bytes 393224 | tf_op jit(solution)/shard_map/ppermute | solution.py:297
  97.1 12.2 %collective-permute-start.36 = (f32[32,1024]{1,0:T(8,128)S(1)}, f32[32,1024]{1,0:T(8,128)S(1)}, u32[]{:S(2)}, u32[]{:S(2)}) collective-permute-start(f32[32,1024]{1,0:T(8,128)S(1)} %get-tuple-element.68.refs_0_), channel_id=1, source_target_pairs={{0,4},{2,6},{4,0},{6,2},{8,12},{10,14},{12,8},{14,10},{1,5},{3,7},... | collective-permute-start | bytes 393224 | tf_op jit(solution)/shard_map/ppermute | solution.py:297
  98.6 11.5 %collective-permute-start.37 = (f32[32,1024]{1,0:T(8,128)S(1)}, f32[32,1024]{1,0:T(8,128)S(1)}, u32[]{:S(2)}, u32[]{:S(2)}) collective-permute-start(f32[32,1024]{1,0:T(8,128)S(1)} %get-tuple-element.68.refs_0_), channel_id=1, source_target_pairs={{0,12},{2,14},{4,8},{6,10},{8,4},{10,6},{12,0},{14,2},{1,13},{3,15... | collective-permute-start | bytes 393224 | tf_op jit(solution)/shard_map/ppermute | solution.py:297
  110.7 34.6 %collective-permute-start.38 = (f32[4,32,1024]{2,1,0:T(8,128)S(1)}, f32[4,32,1024]{2,1,0:T(8,128)S(1)}, u32[]{:S(2)}, u32[]{:S(2)}) collective-permute-start(f32[4,32,1024]{2,1,0:T(8,128)S(1)} %shard_map.103.near_half), channel_id=1, source_target_pairs={{0,2},{2,0},{4,6},{6,4},{8,10},{10,8},{12,14},{14,12},{1,3},{3,1},... | collective-permute-start | bytes 1572872 | tf_op jit(solution)/shard_map/ppermute | solution.py:304
  118.3 14.4 %collective-permute-start.29 = (f32[8,512]{1,0:T(8,128)S(1)}, f32[8,512]{1,0:T(8,128)S(1)}, u32[]{:S(2)}, u32[]{:S(2)}) collective-permute-start(f32[8,512]{1,0:T(8,128)S(1)} %add_add_fusion.4), channel_id=1, source_target_pairs={{0,4},{2,6},{4,0},{6,2},{8,12},{10,14},{12,8},{14,10},{1,5},{3,7},... | collective-permute-start | bytes 49160 | tf_op jit(solution)/shard_map/ppermute | solution.py:308
  120.4 12.8 %collective-permute-start.30 = (f32[8,512]{1,0:T(8,128)S(1)}, f32[8,512]{1,0:T(8,128)S(1)}, u32[]{:S(2)}, u32[]{:S(2)}) collective-permute-start(f32[8,512]{1,0:T(8,128)S(1)} %add_add_fusion.4), channel_id=1, source_target_pairs={{0,2},{2,0},{4,6},{6,4},{8,10},{10,8},{12,14},{14,12},{1,3},{3,1},... | collective-permute-start | bytes 49160 | tf_op jit(solution)/shard_map/ppermute | solution.py:308
  121.5 11.8 %collective-permute-start.31 = (f32[8,512]{1,0:T(8,128)S(1)}, f32[8,512]{1,0:T(8,128)S(1)}, u32[]{:S(2)}, u32[]{:S(2)}) collective-permute-start(f32[8,512]{1,0:T(8,128)S(1)} %add_add_fusion.4), channel_id=1, source_target_pairs={{0,6},{2,4},{4,2},{6,0},{8,14},{10,12},{12,10},{14,8},{1,7},{3,5},... | collective-permute-start | bytes 49160 | tf_op jit(solution)/shard_map/ppermute | solution.py:308
  121.5 18.7 %collective-permute-start.33 = (f32[32,512]{1,0:T(8,128)S(1)}, f32[32,512]{1,0:T(8,128)S(1)}, u32[]{:S(2)}, u32[]{:S(2)}) collective-permute-start(f32[32,512]{1,0:T(8,128)S(1)} %add_add_fusion.2.g32), channel_id=1, source_target_pairs={{0,0},{1,64},{2,8},{3,72},{4,4},{5,68},{6,12},{7,76},{8,2},{9,66},... | collective-permute-start | bytes 196616 | tf_op jit(solution)/shard_map/ppermute | solution.py:286
  132.8 12.5 %collective-permute-start.34 = (f32[32,512]{1,0:T(8,128)S(1)}, f32[32,512]{1,0:T(8,128)S(1)}, u32[]{:S(2)}, u32[]{:S(2)}) collective-permute-start(f32[32,512]{1,0:T(8,128)S(1)} %add_add_fusion.2.g32), channel_id=1, source_target_pairs={{0,128},{1,192},{2,136},{3,200},{4,132},{5,196},{6,140},{7,204},{8... | collective-permute-start | bytes 196616 | tf_op jit(solution)/shard_map/ppermute | solution.py:287
  146.5 9.9 %collective-permute-start.43 = (bf16[4,32,512]{2,1,0:T(8,128)(2,1)S(1)}, bf16[4,32,512]{2,1,0:T(8,128)(2,1)S(1)}, u32[]{:S(2)}, u32[]{:S(2)}) collective-permute-start(bf16[4,32,512]{2,1,0:T(8,128)(2,1)S(1)} %get-tuple-element.73), channel_id=1, source_target_pairs={{0,32},{32,0},{64,96},{96,64},{1,33},{33,1},{65,97},{97,65},{2,34}... | collective-permute-start | bytes 393224 | tf_op jit(solution)/shard_map/ppermute | solution.py:181
  159.6 15.3 %collective-permute-start.50 = (bf16[2,2,4,32,512]{4,3,2,1,0:T(8,128)(2,1)S(1)}, bf16[2,2,4,32,512]{4,3,2,1,0:T(8,128)(2,1)S(1)}, u32[]{:S(2)}, u32[]{:S(2)}) collective-permute-start(bf16[2,2,4,32,512]{4,3,2,1,0:T(8,128)(2,1)S(1)} %bitcast.39), channel_id=1, source_target_pairs={{0,64},{32,96},{64,0},{96,32},{1,65},{33,97},{65,1},{97,33},{2,66}... | collective-permute-start | bytes 1572872 | tf_op jit(solution)/shard_map/ppermute | solution.py:334
  160.9 24.0 %collective-permute-start.47 = (bf16[2,2,4,32,512]{4,3,2,1,0:T(8,128)(2,1)S(1)}, bf16[2,2,4,32,512]{4,3,2,1,0:T(8,128)(2,1)S(1)}, u32[]{:S(2)}, u32[]{:S(2)}) collective-permute-start(bf16[2,2,4,32,512]{4,3,2,1,0:T(8,128)(2,1)S(1)} %bitcast.40), channel_id=1, source_target_pairs={{0,32},{32,0},{64,96},{96,64},{1,33},{33,1},{65,97},{97,65},{2,34}... | collective-permute-start | bytes 1572872 | tf_op jit(solution)/shard_map/ppermute | solution.py:334
  161.5 24.7 %collective-permute-start.48 = (bf16[2,2,4,32,512]{4,3,2,1,0:T(8,128)(2,1)S(1)}, bf16[2,2,4,32,512]{4,3,2,1,0:T(8,128)(2,1)S(1)}, u32[]{:S(2)}, u32[]{:S(2)}) collective-permute-start(bf16[2,2,4,32,512]{4,3,2,1,0:T(8,128)(2,1)S(1)} %bitcast.41), channel_id=1, source_target_pairs={{0,96},{32,64},{64,32},{96,0},{1,97},{33,65},{65,33},{97,1},{2,98}... | collective-permute-start | bytes 1572872 | tf_op jit(solution)/shard_map/ppermute | solution.py:334
  162.9 18.9 %collective-permute-start.49 = (bf16[2,2,4,32,512]{4,3,2,1,0:T(8,128)(2,1)S(1)}, bf16[2,2,4,32,512]{4,3,2,1,0:T(8,128)(2,1)S(1)}, u32[]{:S(2)}, u32[]{:S(2)}) collective-permute-start(bf16[2,2,4,32,512]{4,3,2,1,0:T(8,128)(2,1)S(1)} %bitcast.35), channel_id=1, source_target_pairs={{0,128},{16,144},{128,0},{144,16},{1,129},{17,145},{129,1},{145,17... | collective-permute-start | bytes 1572872 | tf_op jit(solution)/shard_map/ppermute | solution.py:335
  164.0 24.3 %collective-permute-start.45 = (bf16[2,2,4,32,512]{4,3,2,1,0:T(8,128)(2,1)S(1)}, bf16[2,2,4,32,512]{4,3,2,1,0:T(8,128)(2,1)S(1)}, u32[]{:S(2)}, u32[]{:S(2)}) collective-permute-start(bf16[2,2,4,32,512]{4,3,2,1,0:T(8,128)(2,1)S(1)} %bitcast.36), channel_id=1, source_target_pairs={{0,16},{16,0},{128,144},{144,128},{1,17},{17,1},{129,145},{145,129... | collective-permute-start | bytes 1572872 | tf_op jit(solution)/shard_map/ppermute | solution.py:335
  174.9 14.4 %collective-permute-start.46 = (bf16[2,2,4,32,512]{4,3,2,1,0:T(8,128)(2,1)S(1)}, bf16[2,2,4,32,512]{4,3,2,1,0:T(8,128)(2,1)S(1)}, u32[]{:S(2)}, u32[]{:S(2)}) collective-permute-start(bf16[2,2,4,32,512]{4,3,2,1,0:T(8,128)(2,1)S(1)} %bitcast.37), channel_id=1, source_target_pairs={{0,144},{16,128},{128,16},{144,0},{1,145},{17,129},{129,17},{145,1... | collective-permute-start | bytes 1572872 | tf_op jit(solution)/shard_map/ppermute | solution.py:335
  (31 other events, 232.6 us)

commit v7 on v6

--- a/solution.py
+++ b/solution.py
@@ -28,7 +28,7 @@
 
 
 def reverse_bits(z):
-    return (z & 1) * 4 + (z & 2) + (z // 4)
+    return (z & 1) * 4 + (z & 2) + ((z >> 2) & 1)
 
 
 TURN = [
@@ -52,6 +52,13 @@
 
 def chosen(pos, part):
     return (pos[1], pos[4]) if part == 0 else (pos[4], pos[1])
+
+
+def pack_kernel(pos, weight, moment, out):
+    rows = pl.ds(pl.multiple_of(GR * pos[4], GR), GR)
+    hidden = weight.shape[-1]
+    out[:, :hidden] = weight[rows]
+    out[:, hidden:] = jnp.broadcast_to(moment[rows], (GR, out.shape[-1] - hidden))
 
 
 def copy_kernel(pos, src, dst):
@@ -230,11 +237,16 @@
         )(pos, tokens)
         tokens2[part, step] = lax.ppermute(away_cols, "core", SWAP)
 
-    my_weight = lax.dynamic_slice_in_dim(weight, cuts * 32, 32, axis=0)
-    my_moment = lax.dynamic_slice_in_dim(row_moment, cuts * 32, 32, axis=0)
-    packed = jnp.concatenate(
-        [my_weight, jnp.broadcast_to(my_moment[:, None], (32, 128))], axis=1
-    )
+    in_specs = lambda n: [pl.BlockSpec(memory_space=pltpu.SMEM)] + [
+        pl.BlockSpec(memory_space=pltpu.VMEM)
+    ] * n
+    moment = row_moment[:, None]
+    packed = pl.pallas_call(
+        pack_kernel,
+        out_shape=jax.ShapeDtypeStruct((GR, hidden + 128), f32),
+        in_specs=in_specs(2),
+        compiler_params=small,
+    )(pos, weight, moment)
     packed = lax.ppermute(packed, TURNED, TURN)
 
     parts = {}
@@ -263,9 +275,6 @@
     b_got = exchange([p.astype(bf16) for p in b_parts], Y)
     b_got, packed = lax.optimization_barrier((b_got, packed))
     line, part_line, block = (ZN, GR, hidden), (ZH, GR, hidden), (GR, hidden)
-    in_specs = lambda n: [pl.BlockSpec(memory_space=pltpu.SMEM)] + [
-        pl.BlockSpec(memory_space=pltpu.VMEM)
-    ] * n
     keep, send = pl.pallas_call(
         second_sum_kernel,
         out_shape=[jax.ShapeDtypeStruct(part_line, f32), jax.ShapeDtypeStruct(part_line, bf16)],
@@ -326,7 +335,7 @@
         out_shape=[slab, slab, jax.ShapeDtypeStruct((weight.shape[0], 1), f32)],
         in_specs=in_specs(5),
         compiler_params=small,
-    )(pos, near, far, weight, row_moment[:, None], inv_cols)
+    )(pos, near, far, weight, moment, inv_cols)
     a_half, b_half, rows_new = lax.optimization_barrier((a_half, b_half, rows_new))
     a_all, b_all = [a_half], [b_half]
     got = {}

time: 196 us -> 197 us (level)
  waiting for transfers between devices: 68.8 us -> 73.1 us
  local copies, waits for them, and re-layouts: 10.4 us -> 6.33 us
    ppermute x3, waiting for transfers between devices: 13 us -> 17 us  [on_device(): got[0, k] = lax.ppermute(a_half, Y, xor_perm(4, k))]
    unnamed x22 -> x12, local copies, waits for them, and re-layouts: 9.98 us -> 6.05 us
where the time goes in v7:
time: 197 us; the launch traced here: 196 us
  starting transfers between devices  83.5 us (42%)
  waiting for transfers between devices  73.1 us (37%)
  Pallas kernels  29.9 us (15%)
  local copies, waits for them, and re-layouts  6.33 us (3%)
  other arithmetic  2.44 us (1%)
    ppermute x24, waiting for transfers between devices, exchange(): return [lax.ppermute(pieces[k], axes, xor_perm(4, k)) for k in (1, 2, 3)]  36.2 us
    ppermute x24, starting transfers between devices, exchange(): return [lax.ppermute(pieces[k], axes, xor_perm(4, k)) for k in (1, 2, 3)]  31.4 us
    ppermute x3, waiting for transfers between devices, on_device(): got[0, k] = lax.ppermute(a_half, Y, xor_perm(4, k))  17 us
    pallas_call x4, Pallas kernels, on_device(): pl.pallas_call(functools.partial(grad_kernel, part), out_shape=[kept, jax...  13.1 us
    ppermute x1, starting transfers between devices, on_device(): near = lax.ppermute(g32, TURNED, TURN)  11.3 us
    ppermute x1, starting transfers between devices, on_device(): packed = lax.ppermute(packed, TURNED, TURN)  10.1 us
    pallas_call x4, Pallas kernels, on_device(): pl.pallas_call(functools.partial(apply_kernel, part), out_shape=[result,...  8.25 us
    ppermute x3, starting transfers between devices, on_device(): lax.ppermute(own, 'z', xor_perm(ZN, LINE_STEP[k]))  6.06 us
  transfers between devices with their start and end apart: 52, of which 26 were waited for; matrix products, arithmetic and copies ran while one was open for 1% of the time, Pallas kernels for 12%

profile of v7, /device:TPU:33, one launch (start us, length us, event | category | flops | bytes accessed | tf_op | source)
XLA Modules:
  0.0 196.3 jit_solution(5647621763235281975)
XLA Ops:
  0.7 2.8 %copy-done = bf16[384,8192]{1,0:T(8,128)(2,1)S(1)} copy-done((bf16[384,8192]{1,0:T(8,128)(2,1)S(1)}, bf16[384,8192]{1,0:T(8,128)(2,1)}, u32[]{:S(2)}) %copy-start) | copy-done | bytes 6291480
  7.2 10.1 %collective-permute-start.17 = (f32[32,640]{1,0:T(8,128)S(1)}, f32[32,640]{1,0:T(8,128)S(1)}, u32[]{:S(2)}, u32[]{:S(2)}) collective-permute-start(f32[32,640]{1,0:T(8,128)S(1)} %shard_map.100), channel_id=1, source_target_pairs={{0,0},{1,64},{2,8},{3,72},{4,4},{5,68},{6,12},{7,76},{8,2},{9,66},... | collective-permute-start | bytes 245768 | tf_op jit(solution)/shard_map/ppermute | solution.py:250
  17.3 2.8 %copy-done.1 = bf16[384,8192]{1,0:T(8,128)(2,1)S(1)} copy-done((bf16[384,8192]{1,0:T(8,128)(2,1)S(1)}, bf16[384,8192]{1,0:T(8,128)(2,1)}, u32[]{:S(2)}) %copy-start.1) | copy-done | bytes 6291480
  22.9 3.3 %shard_map.97 = (f32[2,2,4,32,512]{4,3,2,1,0:T(8,128)S(1)}, bf16[2,2,4,32,512]{4,3,2,1,0:T(8,128)(2,1)S(1)}) custom-call(s32[6]{0:T(128)S(1)} %stack.57.pos, bf16[384,8192]{1,0:T(8,128)(2,1)S(1)} %copy-done.2, bf16[384,1024]{1,0:T(8,128)(2,1)S(1)} %collective-permute-done.9.tok2, bf16[384,512]{1,0:T(8,128)(2,1)} %cot.7, ...), custom_call_target="tpu_custom_call" | custom-call | flops 6442450944 | bytes 16777216 | tf_op jit(solution)/shard_map/pallas_call | solution.py:255
  26.1 2.8 %collective-permute-start.12 = (bf16[2,2,4,32,512]{4,3,2,1,0:T(8,128)(2,1)S(1)}, bf16[2,2,4,32,512]{4,3,2,1,0:T(8,128)(2,1)S(1)}, u32[]{:S(2)}, u32[]{:S(2)}) collective-permute-start(bf16[2,2,4,32,512]{4,3,2,1,0:T(8,128)(2,1)S(1)} %get-tuple-element.52), channel_id=1, source_target_pairs={{0,128},{16,144},{128,0},{144,16},{1,129},{17,145},{129,1},{145,17... | collective-permute-start | bytes 1572872 | tf_op jit(solution)/shard_map/ppermute | solution.py:188
  29.0 3.3 %shard_map.99 = (bf16[2,2,4,32,512]{4,3,2,1,0:T(8,128)(2,1)S(1)}, bf16[2,2,4,32,512]{4,3,2,1,0:T(8,128)(2,1)S(1)}) custom-call(s32[6]{0:T(128)S(1)} %stack.57.pos, bf16[384,8192]{1,0:T(8,128)(2,1)S(1)} %copy-done.2, bf16[384,1024]{1,0:T(8,128)(2,1)S(1)} %collective-permute-done.10.tok2, bf16[384,512]{1,0:T(8,128)(2,1)} %cot.7, ...), custom_call_target="tpu_custom_call" | custom-call | flops 6442450944 | bytes 16777216 | tf_op jit(solution)/shard_map/pallas_call | solution.py:255
  33.3 3.3 %shard_map.93 = (f32[2,2,4,32,512]{4,3,2,1,0:T(8,128)S(1)}, bf16[2,2,4,32,512]{4,3,2,1,0:T(8,128)(2,1)S(1)}) custom-call(s32[6]{0:T(128)S(1)} %stack.57.pos, bf16[384,8192]{1,0:T(8,128)(2,1)S(1)} %copy-done.2, bf16[384,1024]{1,0:T(8,128)(2,1)S(1)} %collective-permute-done.tok2, bf16[384,512]{1,0:T(8,128)(2,1)} %cot.7, ...), custom_call_target="tpu_custom_call" | custom-call | flops 6442450944 | bytes 16777216 | tf_op jit(solution)/shard_map/pallas_call | solution.py:255
  37.0 3.3 %shard_map.95 = (bf16[2,2,4,32,512]{4,3,2,1,0:T(8,128)(2,1)S(1)}, bf16[2,2,4,32,512]{4,3,2,1,0:T(8,128)(2,1)S(1)}) custom-call(s32[6]{0:T(128)S(1)} %stack.57.pos, bf16[384,8192]{1,0:T(8,128)(2,1)S(1)} %copy-done.2, bf16[384,1024]{1,0:T(8,128)(2,1)S(1)} %collective-permute-done.2.tok2, bf16[384,512]{1,0:T(8,128)(2,1)} %cot.7, ...), custom_call_target="tpu_custom_call" | custom-call | flops 6442450944 | bytes 16777216 | tf_op jit(solution)/shard_map/pallas_call | solution.py:255
  42.1 10.9 %collective-permute-done.11 = bf16[2,2,4,32,512]{4,3,2,1,0:T(8,128)(2,1)S(1)} collective-permute-done((bf16[2,2,4,32,512]{4,3,2,1,0:T(8,128)(2,1)S(1)}, bf16[2,2,4,32,512]{4,3,2,1,0:T(8,128)(2,1)S(1)}, u32[]{:S(2)}, u32[]{:S(2)}) %collective-permute-start.11) | collective-permute-done | bytes 524320 | tf_op jit(solution)/shard_map/ppermute | solution.py:188
  53.9 3.5 %collective-permute-start.15 = (bf16[4,32,512]{2,1,0:T(8,128)(2,1)S(1)}, bf16[4,32,512]{2,1,0:T(8,128)(2,1)S(1)}, u32[]{:S(2)}, u32[]{:S(2)}) collective-permute-start(bf16[4,32,512]{2,1,0:T(8,128)(2,1)S(1)} %get-tuple-element.92), channel_id=1, source_target_pairs={{0,64},{32,96},{64,0},{96,32},{1,65},{33,97},{65,1},{97,33},{2,66}... | collective-permute-start | bytes 393224 | tf_op jit(solution)/shard_map/ppermute | solution.py:188
  59.2 3.9 %collective-permute-start.16 = (bf16[4,32,512]{2,1,0:T(8,128)(2,1)S(1)}, bf16[4,32,512]{2,1,0:T(8,128)(2,1)S(1)}, u32[]{:S(2)}, u32[]{:S(2)}) collective-permute-start(bf16[4,32,512]{2,1,0:T(8,128)(2,1)S(1)} %get-tuple-element.91), channel_id=1, source_target_pairs={{0,96},{32,64},{64,32},{96,0},{1,97},{33,65},{65,33},{97,1},{2,98}... | collective-permute-start | bytes 393224 | tf_op jit(solution)/shard_map/ppermute | solution.py:188
  63.1 7.0 %collective-permute-done.5 = bf16[2,2,4,32,512]{4,3,2,1,0:T(8,128)(2,1)S(1)} collective-permute-done((bf16[2,2,4,32,512]{4,3,2,1,0:T(8,128)(2,1)S(1)}, bf16[2,2,4,32,512]{4,3,2,1,0:T(8,128)(2,1)S(1)}, u32[]{:S(2)}, u32[]{:S(2)}) %collective-permute-start.5) | collective-permute-done | bytes 524320 | tf_op jit(solution)/shard_map/ppermute | solution.py:188
  72.6 1.8 collective-permute-start.8
  74.5 4.0 %collective-permute-done.7.refs_2_ = bf16[4,32,512]{2,1,0:T(8,128)(2,1)S(1)} collective-permute-done((bf16[4,32,512]{2,1,0:T(8,128)(2,1)S(1)}, bf16[4,32,512]{2,1,0:T(8,128)(2,1)S(1)}, u32[]{:S(2)}, u32[]{:S(2)}) %collective-permute-start.7) | collective-permute-done | bytes 131104 | tf_op jit(solution)/shard_map/ppermute | solution.py:188
  78.5 2.1 %collective-permute-done.8.refs_3_ = bf16[4,32,512]{2,1,0:T(8,128)(2,1)S(1)} collective-permute-done((bf16[4,32,512]{2,1,0:T(8,128)(2,1)S(1)}, bf16[4,32,512]{2,1,0:T(8,128)(2,1)S(1)}, u32[]{:S(2)}, u32[]{:S(2)}) %collective-permute-start.8) | collective-permute-done | bytes 131104 | tf_op jit(solution)/shard_map/ppermute | solution.py:188
  81.4 3.8 %collective-permute-done.18.got = bf16[4,32,512]{2,1,0:T(8,128)(2,1)S(1)} collective-permute-done((bf16[4,32,512]{2,1,0:T(8,128)(2,1)S(1)}, bf16[4,32,512]{2,1,0:T(8,128)(2,1)S(1)}, u32[]{:S(2)}, u32[]{:S(2)}) %collective-permute-start.18) | collective-permute-done | bytes 131104 | tf_op jit(solution)/shard_map/ppermute | solution.py:285
  87.8 3.7 %collective-permute-start.21 = (bf16[32,512]{1,0:T(8,128)(2,1)S(1)}, bf16[32,512]{1,0:T(8,128)(2,1)S(1)}, u32[]{:S(2)}, u32[]{:S(2)}) collective-permute-start(bf16[32,512]{1,0:T(8,128)(2,1)S(1)} %get-tuple-element.62), channel_id=1, source_target_pairs={{0,12},{2,14},{4,8},{6,10},{8,4},{10,6},{12,0},{14,2},{1,13},{3,15... | collective-permute-start | bytes 98312 | tf_op jit(solution)/shard_map/ppermute | solution.py:292
  93.0 4.6 %collective-permute-start.35 = (f32[32,1024]{1,0:T(8,128)S(1)}, f32[32,1024]{1,0:T(8,128)S(1)}, u32[]{:S(2)}, u32[]{:S(2)}) collective-permute-start(f32[32,1024]{1,0:T(8,128)S(1)} %get-tuple-element.68.refs_0_), channel_id=1, source_target_pairs={{0,8},{2,10},{4,12},{6,14},{8,0},{10,2},{12,4},{14,6},{1,9},{3,11}... | collective-permute-start | bytes 393224 | tf_op jit(solution)/shard_map/ppermute | solution.py:306
  99.1 4.9 %collective-permute-start.22 = (f32[8,512]{1,0:T(8,128)S(1)}, f32[8,512]{1,0:T(8,128)S(1)}, u32[]{:S(2)}, u32[]{:S(2)}) collective-permute-start(f32[8,512]{1,0:T(8,128)S(1)} %get-tuple-element.64), channel_id=1, source_target_pairs={{0,1},{1,0},{2,3},{3,2},{4,5},{5,4},{6,7},{7,6},{8,9},{9,8},{10,11... | collective-permute-start | bytes 49160 | tf_op jit(solution)/shard_map/ppermute | solution.py:314
  104.9 4.1 %collective-permute-start.24 = (f32[8,512]{1,0:T(8,128)S(1)}, f32[8,512]{1,0:T(8,128)S(1)}, u32[]{:S(2)}, u32[]{:S(2)}) collective-permute-start(f32[8,512]{1,0:T(8,128)S(1)} %add.80), channel_id=1, source_target_pairs={{0,32},{32,0},{64,96},{96,64},{1,33},{33,1},{65,97},{97,65},{2,34}... | collective-permute-start | bytes 49160 | tf_op jit(solution)/shard_map/ppermute | solution.py:188
  118.9 2.1 %collective-permute-start.29 = (f32[8,512]{1,0:T(8,128)S(1)}, f32[8,512]{1,0:T(8,128)S(1)}, u32[]{:S(2)}, u32[]{:S(2)}) collective-permute-start(f32[8,512]{1,0:T(8,128)S(1)} %add_add_fusion.4), channel_id=1, source_target_pairs={{0,4},{2,6},{4,0},{6,2},{8,12},{10,14},{12,8},{14,10},{1,5},{3,7},... | collective-permute-start | bytes 49160 | tf_op jit(solution)/shard_map/ppermute | solution.py:317
  122.0 11.3 %collective-permute-start.33 = (f32[32,512]{1,0:T(8,128)S(1)}, f32[32,512]{1,0:T(8,128)S(1)}, u32[]{:S(2)}, u32[]{:S(2)}) collective-permute-start(f32[32,512]{1,0:T(8,128)S(1)} %add_add_fusion.2.g32), channel_id=1, source_target_pairs={{0,0},{1,64},{2,8},{3,72},{4,4},{5,68},{6,12},{7,76},{8,2},{9,66},... | collective-permute-start | bytes 196616 | tf_op jit(solution)/shard_map/ppermute | solution.py:295
  134.9 5.8 %collective-permute-done.32 = f32[8,512]{1,0:T(8,128)S(1)} collective-permute-done((f32[8,512]{1,0:T(8,128)S(1)}, f32[8,512]{1,0:T(8,128)S(1)}, u32[]{:S(2)}, u32[]{:S(2)}) %collective-permute-start.32) | collective-permute-done | bytes 16416 | tf_op jit(solution)/shard_map/ppermute | solution.py:318
  140.7 5.1 %collective-permute-done.34.far = f32[32,512]{1,0:T(8,128)S(1)} collective-permute-done((f32[32,512]{1,0:T(8,128)S(1)}, f32[32,512]{1,0:T(8,128)S(1)}, u32[]{:S(2)}, u32[]{:S(2)}) %collective-permute-start.34) | collective-permute-done | bytes 65568 | tf_op jit(solution)/shard_map/ppermute | solution.py:296
  147.0 2.3 %collective-permute-start.43 = (bf16[4,32,512]{2,1,0:T(8,128)(2,1)S(1)}, bf16[4,32,512]{2,1,0:T(8,128)(2,1)S(1)}, u32[]{:S(2)}, u32[]{:S(2)}) collective-permute-start(bf16[4,32,512]{2,1,0:T(8,128)(2,1)S(1)} %get-tuple-element.73), channel_id=1, source_target_pairs={{0,32},{32,0},{64,96},{96,64},{1,33},{33,1},{65,97},{97,65},{2,34}... | collective-permute-start | bytes 393224 | tf_op jit(solution)/shard_map/ppermute | solution.py:188
  149.4 2.4 %collective-permute-start.44 = (bf16[4,32,512]{2,1,0:T(8,128)(2,1)S(1)}, bf16[4,32,512]{2,1,0:T(8,128)(2,1)S(1)}, u32[]{:S(2)}, u32[]{:S(2)}) collective-permute-start(bf16[4,32,512]{2,1,0:T(8,128)(2,1)S(1)} %get-tuple-element.73), channel_id=1, source_target_pairs={{0,96},{32,64},{64,32},{96,0},{1,97},{33,65},{65,33},{97,1},{2,98}... | collective-permute-start | bytes 393224 | tf_op jit(solution)/shard_map/ppermute | solution.py:188
  164.7 10.7 %collective-permute-done.50.piece1 = bf16[2,2,4,32,512]{4,3,2,1,0:T(8,128)(2,1)S(1)} collective-permute-done((bf16[2,2,4,32,512]{4,3,2,1,0:T(8,128)(2,1)S(1)}, bf16[2,2,4,32,512]{4,3,2,1,0:T(8,128)(2,1)S(1)}, u32[]{:S(2)}, u32[]{:S(2)}) %collective-permute-start.50) | collective-permute-done | bytes 524320 | tf_op jit(solution)/shard_map/ppermute | solution.py:343
  176.3 2.1 %shard_map.107 = (f32[384,512]{1,0:T(8,128)S(1)}, f32[384,512]{1,0:T(8,128)S(1)}) custom-call(s32[6]{0:T(128)S(1)} %stack.57.pos, bf16[384,8192]{1,0:T(8,128)(2,1)S(1)} %copy-done.2, bf16[384,1024]{1,0:T(8,128)(2,1)S(1)} %collective-permute-done.tok2, bf16[2,2,4,32,512]{4,3,2,1,0:T(8,128)(2,1)S(1)} %bitcast.42, ...), custom_call_target="tpu_custom_call" | custom-call | flops 6442450944 | bytes 16777216 | tf_op jit(solution)/shard_map/pallas_call | solution.py:352
  178.4 2.1 %shard_map.108 = (f32[384,512]{1,0:T(8,128)S(1)}, f32[384,512]{1,0:T(8,128)S(1)}) custom-call(s32[6]{0:T(128)S(1)} %stack.57.pos, bf16[384,8192]{1,0:T(8,128)(2,1)S(1)} %copy-done.2, bf16[384,1024]{1,0:T(8,128)(2,1)S(1)} %collective-permute-done.9.tok2, bf16[2,2,4,32,512]{4,3,2,1,0:T(8,128)(2,1)S(1)} %bitcast.38, ...), custom_call_target="tpu_custom_call" | custom-call | flops 6442450944 | bytes 16777216 | tf_op jit(solution)/shard_map/pallas_call | solution.py:352
  180.5 4.9 %collective-permute-done.47.piece0 = bf16[2,2,4,32,512]{4,3,2,1,0:T(8,128)(2,1)S(1)} collective-permute-done((bf16[2,2,4,32,512]{4,3,2,1,0:T(8,128)(2,1)S(1)}, bf16[2,2,4,32,512]{4,3,2,1,0:T(8,128)(2,1)S(1)}, u32[]{:S(2)}, u32[]{:S(2)}) %collective-permute-start.47) | collective-permute-done | bytes 524320 | tf_op jit(solution)/shard_map/ppermute | solution.py:343
  186.7 2.1 %shard_map.109 = (f32[384,512]{1,0:T(8,128)S(1)}, f32[384,512]{1,0:T(8,128)S(1)}) custom-call(s32[6]{0:T(128)S(1)} %stack.57.pos, bf16[384,8192]{1,0:T(8,128)(2,1)S(1)} %copy-done.2, bf16[384,1024]{1,0:T(8,128)(2,1)S(1)} %collective-permute-done.2.tok2, bf16[2,2,4,32,512]{4,3,2,1,0:T(8,128)(2,1)S(1)} %collective-permute-done.47.piece0, ...), custom_call_target="tpu_custom_call" | custom-call | flops 6442450944 | bytes 16777216 | tf_op jit(solution)/shard_map/pallas_call | solution.py:352
  189.8 2.1 %shard_map.110 = (f32[384,512]{1,0:T(8,128)S(1)}, f32[384,512]{1,0:T(8,128)S(1)}) custom-call(s32[6]{0:T(128)S(1)} %stack.57.pos, bf16[384,8192]{1,0:T(8,128)(2,1)S(1)} %copy-done.2, bf16[384,1024]{1,0:T(8,128)(2,1)S(1)} %collective-permute-done.10.tok2, bf16[2,2,4,32,512]{4,3,2,1,0:T(8,128)(2,1)S(1)} %collective-permute-done.45.piece0, ...), custom_call_target="tpu_custom_call" | custom-call | flops 6442450944 | bytes 16777216 | tf_op jit(solution)/shard_map/pallas_call | solution.py:352
  (121 shorter events, 56.5 us)
Async XLA Ops:
  4.3 18.1 %collective-permute-start.9 = (bf16[384,1024]{1,0:T(8,128)(2,1)S(1)}, bf16[384,1024]{1,0:T(8,128)(2,1)S(1)}, u32[]{:S(2)}, u32[]{:S(2)}) collective-permute-start(bf16[384,1024]{1,0:T(8,128)(2,1)S(1)} %shard_map.96), channel_id=1, source_target_pairs={{0,1},{1,0},{2,3},{3,2},{4,5},{5,4},{6,7},{7,6},{8,9},{9,8},{10,11... | collective-permute-start | bytes 2359304 | tf_op jit(solution)/shard_map/ppermute | solution.py:238
  5.1 16.7 %collective-permute-start.1 = (bf16[384,512]{1,0:T(8,128)(2,1)}, bf16[384,512]{1,0:T(8,128)(2,1)}, u32[]{:S(2)}, u32[]{:S(2)}) collective-permute-start(bf16[384,512]{1,0:T(8,128)(2,1)} %cot.7), channel_id=1, source_target_pairs={{0,1},{1,0},{2,3},{3,2},{4,5},{5,4},{6,7},{7,6},{8,9},{9,8},{10,11... | collective-permute-start | bytes 1179656 | tf_op jit(solution)/shard_map/ppermute | solution.py:218
  6.0 23.0 %collective-permute-start.10 = (bf16[384,1024]{1,0:T(8,128)(2,1)S(1)}, bf16[384,1024]{1,0:T(8,128)(2,1)S(1)}, u32[]{:S(2)}, u32[]{:S(2)}) collective-permute-start(bf16[384,1024]{1,0:T(8,128)(2,1)S(1)} %shard_map.98), channel_id=1, source_target_pairs={{0,1},{1,0},{2,3},{3,2},{4,5},{5,4},{6,7},{7,6},{8,9},{9,8},{10,11... | collective-permute-start | bytes 2359304 | tf_op jit(solution)/shard_map/ppermute | solution.py:238
  7.2 64.5 %collective-permute-start.17 = (f32[32,640]{1,0:T(8,128)S(1)}, f32[32,640]{1,0:T(8,128)S(1)}, u32[]{:S(2)}, u32[]{:S(2)}) collective-permute-start(f32[32,640]{1,0:T(8,128)S(1)} %shard_map.100), channel_id=1, source_target_pairs={{0,0},{1,64},{2,8},{3,72},{4,4},{5,68},{6,12},{7,76},{8,2},{9,66},... | collective-permute-start | bytes 245768 | tf_op jit(solution)/shard_map/ppermute | solution.py:250
  20.9 11.8 %collective-permute-start = (bf16[384,1024]{1,0:T(8,128)(2,1)S(1)}, bf16[384,1024]{1,0:T(8,128)(2,1)S(1)}, u32[]{:S(2)}, u32[]{:S(2)}) collective-permute-start(bf16[384,1024]{1,0:T(8,128)(2,1)S(1)} %shard_map.92), channel_id=1, source_target_pairs={{0,1},{1,0},{2,3},{3,2},{4,5},{5,4},{6,7},{7,6},{8,9},{9,8},{10,11... | collective-permute-start | bytes 2359304 | tf_op jit(solution)/shard_map/ppermute | solution.py:238
  21.8 14.8 %collective-permute-start.2 = (bf16[384,1024]{1,0:T(8,128)(2,1)S(1)}, bf16[384,1024]{1,0:T(8,128)(2,1)S(1)}, u32[]{:S(2)}, u32[]{:S(2)}) collective-permute-start(bf16[384,1024]{1,0:T(8,128)(2,1)S(1)} %shard_map.94), channel_id=1, source_target_pairs={{0,1},{1,0},{2,3},{3,2},{4,5},{5,4},{6,7},{7,6},{8,9},{9,8},{10,11... | collective-permute-start | bytes 2359304 | tf_op jit(solution)/shard_map/ppermute | solution.py:238
  26.1 15.6 %collective-permute-start.12 = (bf16[2,2,4,32,512]{4,3,2,1,0:T(8,128)(2,1)S(1)}, bf16[2,2,4,32,512]{4,3,2,1,0:T(8,128)(2,1)S(1)}, u32[]{:S(2)}, u32[]{:S(2)}) collective-permute-start(bf16[2,2,4,32,512]{4,3,2,1,0:T(8,128)(2,1)S(1)} %get-tuple-element.52), channel_id=1, source_target_pairs={{0,128},{16,144},{128,0},{144,16},{1,129},{17,145},{129,1},{145,17... | collective-permute-start | bytes 1572872 | tf_op jit(solution)/shard_map/ppermute | solution.py:188
  32.3 20.8 %collective-permute-start.11 = (bf16[2,2,4,32,512]{4,3,2,1,0:T(8,128)(2,1)S(1)}, bf16[2,2,4,32,512]{4,3,2,1,0:T(8,128)(2,1)S(1)}, u32[]{:S(2)}, u32[]{:S(2)}) collective-permute-start(bf16[2,2,4,32,512]{4,3,2,1,0:T(8,128)(2,1)S(1)} %get-tuple-element.51), channel_id=1, source_target_pairs={{0,16},{16,0},{128,144},{144,128},{1,17},{17,1},{129,145},{145,129... | collective-permute-start | bytes 1572872 | tf_op jit(solution)/shard_map/ppermute | solution.py:188
  32.7 20.4 %collective-permute-start.13 = (bf16[2,2,4,32,512]{4,3,2,1,0:T(8,128)(2,1)S(1)}, bf16[2,2,4,32,512]{4,3,2,1,0:T(8,128)(2,1)S(1)}, u32[]{:S(2)}, u32[]{:S(2)}) collective-permute-start(bf16[2,2,4,32,512]{4,3,2,1,0:T(8,128)(2,1)S(1)} %get-tuple-element.53), channel_id=1, source_target_pairs={{0,144},{16,128},{128,16},{144,0},{1,145},{17,129},{129,17},{145,1... | collective-permute-start | bytes 1572872 | tf_op jit(solution)/shard_map/ppermute | solution.py:188
  36.6 17.3 %collective-permute-start.4 = (bf16[2,2,4,32,512]{4,3,2,1,0:T(8,128)(2,1)S(1)}, bf16[2,2,4,32,512]{4,3,2,1,0:T(8,128)(2,1)S(1)}, u32[]{:S(2)}, u32[]{:S(2)}) collective-permute-start(bf16[2,2,4,32,512]{4,3,2,1,0:T(8,128)(2,1)S(1)} %get-tuple-element.48), channel_id=1, source_target_pairs={{0,64},{32,96},{64,0},{96,32},{1,65},{33,97},{65,1},{97,33},{2,66}... | collective-permute-start | bytes 1572872 | tf_op jit(solution)/shard_map/ppermute | solution.py:188
  41.7 17.5 %collective-permute-start.3 = (bf16[2,2,4,32,512]{4,3,2,1,0:T(8,128)(2,1)S(1)}, bf16[2,2,4,32,512]{4,3,2,1,0:T(8,128)(2,1)S(1)}, u32[]{:S(2)}, u32[]{:S(2)}) collective-permute-start(bf16[2,2,4,32,512]{4,3,2,1,0:T(8,128)(2,1)S(1)} %get-tuple-element.47), channel_id=1, source_target_pairs={{0,32},{32,0},{64,96},{96,64},{1,33},{33,1},{65,97},{97,65},{2,34}... | collective-permute-start | bytes 1572872 | tf_op jit(solution)/shard_map/ppermute | solution.py:188
  53.0 17.1 %collective-permute-start.5 = (bf16[2,2,4,32,512]{4,3,2,1,0:T(8,128)(2,1)S(1)}, bf16[2,2,4,32,512]{4,3,2,1,0:T(8,128)(2,1)S(1)}, u32[]{:S(2)}, u32[]{:S(2)}) collective-permute-start(bf16[2,2,4,32,512]{4,3,2,1,0:T(8,128)(2,1)S(1)} %get-tuple-element.49), channel_id=1, source_target_pairs={{0,96},{32,64},{64,32},{96,0},{1,97},{33,65},{65,33},{97,1},{2,98}... | collective-permute-start | bytes 1572872 | tf_op jit(solution)/shard_map/ppermute | solution.py:188
  53.5 19.2 %collective-permute-start.14 = (bf16[4,32,512]{2,1,0:T(8,128)(2,1)S(1)}, bf16[4,32,512]{2,1,0:T(8,128)(2,1)S(1)}, u32[]{:S(2)}, u32[]{:S(2)}) collective-permute-start(bf16[4,32,512]{2,1,0:T(8,128)(2,1)S(1)} %get-tuple-element.93), channel_id=1, source_target_pairs={{0,32},{32,0},{64,96},{96,64},{1,33},{33,1},{65,97},{97,65},{2,34}... | collective-permute-start | bytes 393224 | tf_op jit(solution)/shard_map/ppermute | solution.py:188
  53.9 20.6 %collective-permute-start.15 = (bf16[4,32,512]{2,1,0:T(8,128)(2,1)S(1)}, bf16[4,32,512]{2,1,0:T(8,128)(2,1)S(1)}, u32[]{:S(2)}, u32[]{:S(2)}) collective-permute-start(bf16[4,32,512]{2,1,0:T(8,128)(2,1)S(1)} %get-tuple-element.92), channel_id=1, source_target_pairs={{0,64},{32,96},{64,0},{96,32},{1,65},{33,97},{65,1},{97,33},{2,66}... | collective-permute-start | bytes 393224 | tf_op jit(solution)/shard_map/ppermute | solution.py:188
  59.2 15.3 %collective-permute-start.16 = (bf16[4,32,512]{2,1,0:T(8,128)(2,1)S(1)}, bf16[4,32,512]{2,1,0:T(8,128)(2,1)S(1)}, u32[]{:S(2)}, u32[]{:S(2)}) collective-permute-start(bf16[4,32,512]{2,1,0:T(8,128)(2,1)S(1)} %get-tuple-element.91), channel_id=1, source_target_pairs={{0,96},{32,64},{64,32},{96,0},{1,97},{33,65},{65,33},{97,1},{2,98}... | collective-permute-start | bytes 393224 | tf_op jit(solution)/shard_map/ppermute | solution.py:188
  72.6 8.0 %collective-permute-start.8 = (bf16[4,32,512]{2,1,0:T(8,128)(2,1)S(1)}, bf16[4,32,512]{2,1,0:T(8,128)(2,1)S(1)}, u32[]{:S(2)}, u32[]{:S(2)}) collective-permute-start(bf16[4,32,512]{2,1,0:T(8,128)(2,1)S(1)} %get-tuple-element.94), channel_id=1, source_target_pairs={{0,144},{16,128},{128,16},{144,0},{1,145},{17,129},{129,17},{145,1... | collective-permute-start | bytes 393224 | tf_op jit(solution)/shard_map/ppermute | solution.py:188
  93.0 15.9 %collective-permute-start.35 = (f32[32,1024]{1,0:T(8,128)S(1)}, f32[32,1024]{1,0:T(8,128)S(1)}, u32[]{:S(2)}, u32[]{:S(2)}) collective-permute-start(f32[32,1024]{1,0:T(8,128)S(1)} %get-tuple-element.68.refs_0_), channel_id=1, source_target_pairs={{0,8},{2,10},{4,12},{6,14},{8,0},{10,2},{12,4},{14,6},{1,9},{3,11}... | collective-permute-start | bytes 393224 | tf_op jit(solution)/shard_map/ppermute | solution.py:306
  97.7 12.1 %collective-permute-start.36 = (f32[32,1024]{1,0:T(8,128)S(1)}, f32[32,1024]{1,0:T(8,128)S(1)}, u32[]{:S(2)}, u32[]{:S(2)}) collective-permute-start(f32[32,1024]{1,0:T(8,128)S(1)} %get-tuple-element.68.refs_0_), channel_id=1, source_target_pairs={{0,4},{2,6},{4,0},{6,2},{8,12},{10,14},{12,8},{14,10},{1,5},{3,7},... | collective-permute-start | bytes 393224 | tf_op jit(solution)/shard_map/ppermute | solution.py:306
  99.1 11.5 %collective-permute-start.37 = (f32[32,1024]{1,0:T(8,128)S(1)}, f32[32,1024]{1,0:T(8,128)S(1)}, u32[]{:S(2)}, u32[]{:S(2)}) collective-permute-start(f32[32,1024]{1,0:T(8,128)S(1)} %get-tuple-element.68.refs_0_), channel_id=1, source_target_pairs={{0,12},{2,14},{4,8},{6,10},{8,4},{10,6},{12,0},{14,2},{1,13},{3,15... | collective-permute-start | bytes 393224 | tf_op jit(solution)/shard_map/ppermute | solution.py:306
  111.2 34.6 %collective-permute-start.38 = (f32[4,32,1024]{2,1,0:T(8,128)S(1)}, f32[4,32,1024]{2,1,0:T(8,128)S(1)}, u32[]{:S(2)}, u32[]{:S(2)}) collective-permute-start(f32[4,32,1024]{2,1,0:T(8,128)S(1)} %shard_map.104.near_half), channel_id=1, source_target_pairs={{0,2},{2,0},{4,6},{6,4},{8,10},{10,8},{12,14},{14,12},{1,3},{3,1},... | collective-permute-start | bytes 1572872 | tf_op jit(solution)/shard_map/ppermute | solution.py:313
  118.9 14.4 %collective-permute-start.29 = (f32[8,512]{1,0:T(8,128)S(1)}, f32[8,512]{1,0:T(8,128)S(1)}, u32[]{:S(2)}, u32[]{:S(2)}) collective-permute-start(f32[8,512]{1,0:T(8,128)S(1)} %add_add_fusion.4), channel_id=1, source_target_pairs={{0,4},{2,6},{4,0},{6,2},{8,12},{10,14},{12,8},{14,10},{1,5},{3,7},... | collective-permute-start | bytes 49160 | tf_op jit(solution)/shard_map/ppermute | solution.py:317
  120.9 12.8 %collective-permute-start.30 = (f32[8,512]{1,0:T(8,128)S(1)}, f32[8,512]{1,0:T(8,128)S(1)}, u32[]{:S(2)}, u32[]{:S(2)}) collective-permute-start(f32[8,512]{1,0:T(8,128)S(1)} %add_add_fusion.4), channel_id=1, source_target_pairs={{0,2},{2,0},{4,6},{6,4},{8,10},{10,8},{12,14},{14,12},{1,3},{3,1},... | collective-permute-start | bytes 49160 | tf_op jit(solution)/shard_map/ppermute | solution.py:317
  122.0 11.8 %collective-permute-start.31 = (f32[8,512]{1,0:T(8,128)S(1)}, f32[8,512]{1,0:T(8,128)S(1)}, u32[]{:S(2)}, u32[]{:S(2)}) collective-permute-start(f32[8,512]{1,0:T(8,128)S(1)} %add_add_fusion.4), channel_id=1, source_target_pairs={{0,6},{2,4},{4,2},{6,0},{8,14},{10,12},{12,10},{14,8},{1,7},{3,5},... | collective-permute-start | bytes 49160 | tf_op jit(solution)/shard_map/ppermute | solution.py:317
  122.0 18.7 %collective-permute-start.33 = (f32[32,512]{1,0:T(8,128)S(1)}, f32[32,512]{1,0:T(8,128)S(1)}, u32[]{:S(2)}, u32[]{:S(2)}) collective-permute-start(f32[32,512]{1,0:T(8,128)S(1)} %add_add_fusion.2.g32), channel_id=1, source_target_pairs={{0,0},{1,64},{2,8},{3,72},{4,4},{5,68},{6,12},{7,76},{8,2},{9,66},... | collective-permute-start | bytes 196616 | tf_op jit(solution)/shard_map/ppermute | solution.py:295
  133.3 12.5 %collective-permute-start.34 = (f32[32,512]{1,0:T(8,128)S(1)}, f32[32,512]{1,0:T(8,128)S(1)}, u32[]{:S(2)}, u32[]{:S(2)}) collective-permute-start(f32[32,512]{1,0:T(8,128)S(1)} %add_add_fusion.2.g32), channel_id=1, source_target_pairs={{0,128},{1,192},{2,136},{3,200},{4,132},{5,196},{6,140},{7,204},{8... | collective-permute-start | bytes 196616 | tf_op jit(solution)/shard_map/ppermute | solution.py:296
  147.0 9.7 %collective-permute-start.43 = (bf16[4,32,512]{2,1,0:T(8,128)(2,1)S(1)}, bf16[4,32,512]{2,1,0:T(8,128)(2,1)S(1)}, u32[]{:S(2)}, u32[]{:S(2)}) collective-permute-start(bf16[4,32,512]{2,1,0:T(8,128)(2,1)S(1)} %get-tuple-element.73), channel_id=1, source_target_pairs={{0,32},{32,0},{64,96},{96,64},{1,33},{33,1},{65,97},{97,65},{2,34}... | collective-permute-start | bytes 393224 | tf_op jit(solution)/shard_map/ppermute | solution.py:188
  160.1 15.3 %collective-permute-start.50 = (bf16[2,2,4,32,512]{4,3,2,1,0:T(8,128)(2,1)S(1)}, bf16[2,2,4,32,512]{4,3,2,1,0:T(8,128)(2,1)S(1)}, u32[]{:S(2)}, u32[]{:S(2)}) collective-permute-start(bf16[2,2,4,32,512]{4,3,2,1,0:T(8,128)(2,1)S(1)} %bitcast.39), channel_id=1, source_target_pairs={{0,64},{32,96},{64,0},{96,32},{1,65},{33,97},{65,1},{97,33},{2,66}... | collective-permute-start | bytes 1572872 | tf_op jit(solution)/shard_map/ppermute | solution.py:343
  161.4 24.0 %collective-permute-start.47 = (bf16[2,2,4,32,512]{4,3,2,1,0:T(8,128)(2,1)S(1)}, bf16[2,2,4,32,512]{4,3,2,1,0:T(8,128)(2,1)S(1)}, u32[]{:S(2)}, u32[]{:S(2)}) collective-permute-start(bf16[2,2,4,32,512]{4,3,2,1,0:T(8,128)(2,1)S(1)} %bitcast.40), channel_id=1, source_target_pairs={{0,32},{32,0},{64,96},{96,64},{1,33},{33,1},{65,97},{97,65},{2,34}... | collective-permute-start | bytes 1572872 | tf_op jit(solution)/shard_map/ppermute | solution.py:343
  162.1 24.7 %collective-permute-start.48 = (bf16[2,2,4,32,512]{4,3,2,1,0:T(8,128)(2,1)S(1)}, bf16[2,2,4,32,512]{4,3,2,1,0:T(8,128)(2,1)S(1)}, u32[]{:S(2)}, u32[]{:S(2)}) collective-permute-start(bf16[2,2,4,32,512]{4,3,2,1,0:T(8,128)(2,1)S(1)} %bitcast.41), channel_id=1, source_target_pairs={{0,96},{32,64},{64,32},{96,0},{1,97},{33,65},{65,33},{97,1},{2,98}... | collective-permute-start | bytes 1572872 | tf_op jit(solution)/shard_map/ppermute | solution.py:343
  163.4 15.0 %collective-permute-start.49 = (bf16[2,2,4,32,512]{4,3,2,1,0:T(8,128)(2,1)S(1)}, bf16[2,2,4,32,512]{4,3,2,1,0:T(8,128)(2,1)S(1)}, u32[]{:S(2)}, u32[]{:S(2)}) collective-permute-start(bf16[2,2,4,32,512]{4,3,2,1,0:T(8,128)(2,1)S(1)} %bitcast.35), channel_id=1, source_target_pairs={{0,128},{16,144},{128,0},{144,16},{1,129},{17,145},{129,1},{145,17... | collective-permute-start | bytes 1572872 | tf_op jit(solution)/shard_map/ppermute | solution.py:344
  164.5 24.3 %collective-permute-start.45 = (bf16[2,2,4,32,512]{4,3,2,1,0:T(8,128)(2,1)S(1)}, bf16[2,2,4,32,512]{4,3,2,1,0:T(8,128)(2,1)S(1)}, u32[]{:S(2)}, u32[]{:S(2)}) collective-permute-start(bf16[2,2,4,32,512]{4,3,2,1,0:T(8,128)(2,1)S(1)} %bitcast.36), channel_id=1, source_target_pairs={{0,16},{16,0},{128,144},{144,128},{1,17},{17,1},{129,145},{145,129... | collective-permute-start | bytes 1572872 | tf_op jit(solution)/shard_map/ppermute | solution.py:344
  175.4 14.4 %collective-permute-start.46 = (bf16[2,2,4,32,512]{4,3,2,1,0:T(8,128)(2,1)S(1)}, bf16[2,2,4,32,512]{4,3,2,1,0:T(8,128)(2,1)S(1)}, u32[]{:S(2)}, u32[]{:S(2)}) collective-permute-start(bf16[2,2,4,32,512]{4,3,2,1,0:T(8,128)(2,1)S(1)} %bitcast.37), channel_id=1, source_target_pairs={{0,144},{16,128},{128,16},{144,0},{1,145},{17,129},{129,17},{145,1... | collective-permute-start | bytes 1572872 | tf_op jit(solution)/shard_map/ppermute | solution.py:344
  (26 other events, 216.5 us)

commit v8 on v7

--- a/solution.py
+++ b/solution.py
@@ -198,8 +198,8 @@
     seg = width // 16
     cuts, y1, y0, xlo, z, core = [lax.axis_index(a) for a in AXES]
     pos = jnp.stack([core, y1, y0, xlo, cuts, reverse_bits(z)]).astype(jnp.int32)
-    params = pltpu.CompilerParams(vmem_limit_bytes=16 * 2**20)
-    small = pltpu.CompilerParams(vmem_limit_bytes=6 * 2**20)
+    params = pltpu.CompilerParams(vmem_limit_bytes=32 * 2**20)
+    small = pltpu.CompilerParams(vmem_limit_bytes=32 * 2**20)
     cost = pl.CostEstimate(
         flops=64 * tok_rows * seg * hidden, bytes_accessed=16 * 2**20, transcendentals=0
     )

time: 197 us -> 196 us (level)
  waiting for transfers between devices: 73.1 us -> 65.5 us
  starting transfers between devices: 83.5 us -> 90.5 us
    ppermute x1, starting transfers between devices: 4.9 us -> 11.2 us  [on_device(): stats = stats + lax.ppermute(stats, 'core', SWAP)]
    ppermute x24, waiting for transfers between devices: 36.2 us -> 32.1 us  [exchange(): return [lax.ppermute(pieces[k], axes, xor_perm(4, k)) for k in (1, 2, 3)]]
    ppermute x1, starting transfers between devices: 0.09 us -> 2.34 us  [on_device(): far_half = lax.ppermute(near_half, 'z', xor_perm(ZN, 1))]
    unnamed x12 -> x14, local copies, waits for them, and re-layouts: 6.05 us -> 5.59 us
  transfers between devices with their start and end apart: 52 -> 52, of which waited for: 26 -> 23; matrix products, arithmetic and copies ran while one was open for 1% -> 1% of each run, Pallas kernels for 12% -> 12%
where the time goes in v8:
time: 196 us; the launch traced here: 195 us
  starting transfers between devices  90.5 us (46%)
  waiting for transfers between devices  65.5 us (33%)
  Pallas kernels  30 us (15%)
  local copies, waits for them, and re-layouts  5.86 us (3%)
  other arithmetic  2.41 us (1%)
    ppermute x24, waiting for transfers between devices, exchange(): return [lax.ppermute(pieces[k], axes, xor_perm(4, k)) for k in (1, 2, 3)]  32.1 us
    ppermute x24, starting transfers between devices, exchange(): return [lax.ppermute(pieces[k], axes, xor_perm(4, k)) for k in (1, 2, 3)]  29.6 us
    ppermute x3, waiting for transfers between devices, on_device(): got[0, k] = lax.ppermute(a_half, Y, xor_perm(4, k))  15.8 us
    pallas_call x4, Pallas kernels, on_device(): pl.pallas_call(functools.partial(grad_kernel, part), out_shape=[kept, jax...  13.1 us
    ppermute x1, starting transfers between devices, on_device(): stats = stats + lax.ppermute(stats, 'core', SWAP)  11.2 us
    ppermute x1, starting transfers between devices, on_device(): near = lax.ppermute(g32, TURNED, TURN)  10.5 us
    ppermute x1, starting transfers between devices, on_device(): packed = lax.ppermute(packed, TURNED, TURN)  10.1 us
    pallas_call x4, Pallas kernels, on_device(): pl.pallas_call(functools.partial(apply_kernel, part), out_shape=[result,...  8.28 us
  transfers between devices with their start and end apart: 52, of which 23 were waited for; matrix products, arithmetic and copies ran while one was open for 1% of the time, Pallas kernels for 12%

profile of v8, /device:TPU:33, one launch (start us, length us, event | category | flops | bytes accessed | tf_op | source)
XLA Modules:
  0.0 195.2 jit_solution(7290384365942703029)
XLA Ops:
  0.7 2.8 %copy-done = bf16[384,8192]{1,0:T(8,128)(2,1)S(1)} copy-done((bf16[384,8192]{1,0:T(8,128)(2,1)S(1)}, bf16[384,8192]{1,0:T(8,128)(2,1)}, u32[]{:S(2)}) %copy-start) | copy-done | bytes 6291480
  7.2 10.1 %collective-permute-start.17 = (f32[32,640]{1,0:T(8,128)S(1)}, f32[32,640]{1,0:T(8,128)S(1)}, u32[]{:S(2)}, u32[]{:S(2)}) collective-permute-start(f32[32,640]{1,0:T(8,128)S(1)} %shard_map.100), channel_id=1, source_target_pairs={{0,0},{1,64},{2,8},{3,72},{4,4},{5,68},{6,12},{7,76},{8,2},{9,66},... | collective-permute-start | bytes 245768 | tf_op jit(solution)/shard_map/ppermute | solution.py:250
  17.3 2.8 %copy-done.1 = bf16[384,8192]{1,0:T(8,128)(2,1)S(1)} copy-done((bf16[384,8192]{1,0:T(8,128)(2,1)S(1)}, bf16[384,8192]{1,0:T(8,128)(2,1)}, u32[]{:S(2)}) %copy-start.1) | copy-done | bytes 6291480
  22.4 3.3 %shard_map.97 = (f32[2,2,4,32,512]{4,3,2,1,0:T(8,128)S(1)}, bf16[2,2,4,32,512]{4,3,2,1,0:T(8,128)(2,1)S(1)}) custom-call(s32[6]{0:T(128)S(1)} %stack.57.pos, bf16[384,8192]{1,0:T(8,128)(2,1)S(1)} %copy-done.1, bf16[384,1024]{1,0:T(8,128)(2,1)S(1)} %collective-permute-done.9.tok2, bf16[384,512]{1,0:T(8,128)(2,1)} %cot.7, ...), custom_call_target="tpu_custom_call" | custom-call | flops 6442450944 | bytes 16777216 | tf_op jit(solution)/shard_map/pallas_call | solution.py:255
  25.7 2.8 %collective-permute-start.12 = (bf16[2,2,4,32,512]{4,3,2,1,0:T(8,128)(2,1)S(1)}, bf16[2,2,4,32,512]{4,3,2,1,0:T(8,128)(2,1)S(1)}, u32[]{:S(2)}, u32[]{:S(2)}) collective-permute-start(bf16[2,2,4,32,512]{4,3,2,1,0:T(8,128)(2,1)S(1)} %get-tuple-element.52), channel_id=1, source_target_pairs={{0,128},{16,144},{128,0},{144,16},{1,129},{17,145},{129,1},{145,17... | collective-permute-start | bytes 1572872 | tf_op jit(solution)/shard_map/ppermute | solution.py:188
  28.5 3.3 %shard_map.99 = (bf16[2,2,4,32,512]{4,3,2,1,0:T(8,128)(2,1)S(1)}, bf16[2,2,4,32,512]{4,3,2,1,0:T(8,128)(2,1)S(1)}) custom-call(s32[6]{0:T(128)S(1)} %stack.57.pos, bf16[384,8192]{1,0:T(8,128)(2,1)S(1)} %copy-done.1, bf16[384,1024]{1,0:T(8,128)(2,1)S(1)} %collective-permute-done.10.tok2, bf16[384,512]{1,0:T(8,128)(2,1)} %cot.7, ...), custom_call_target="tpu_custom_call" | custom-call | flops 6442450944 | bytes 16777216 | tf_op jit(solution)/shard_map/pallas_call | solution.py:255
  32.8 3.3 %shard_map.93 = (f32[2,2,4,32,512]{4,3,2,1,0:T(8,128)S(1)}, bf16[2,2,4,32,512]{4,3,2,1,0:T(8,128)(2,1)S(1)}) custom-call(s32[6]{0:T(128)S(1)} %stack.57.pos, bf16[384,8192]{1,0:T(8,128)(2,1)S(1)} %copy-done.1, bf16[384,1024]{1,0:T(8,128)(2,1)S(1)} %collective-permute-done.tok2, bf16[384,512]{1,0:T(8,128)(2,1)} %cot.7, ...), custom_call_target="tpu_custom_call" | custom-call | flops 6442450944 | bytes 16777216 | tf_op jit(solution)/shard_map/pallas_call | solution.py:255
  36.5 3.3 %shard_map.95 = (bf16[2,2,4,32,512]{4,3,2,1,0:T(8,128)(2,1)S(1)}, bf16[2,2,4,32,512]{4,3,2,1,0:T(8,128)(2,1)S(1)}) custom-call(s32[6]{0:T(128)S(1)} %stack.57.pos, bf16[384,8192]{1,0:T(8,128)(2,1)S(1)} %copy-done.1, bf16[384,1024]{1,0:T(8,128)(2,1)S(1)} %collective-permute-done.2.tok2, bf16[384,512]{1,0:T(8,128)(2,1)} %cot.7, ...), custom_call_target="tpu_custom_call" | custom-call | flops 6442450944 | bytes 16777216 | tf_op jit(solution)/shard_map/pallas_call | solution.py:255
  41.2 10.9 %collective-permute-done.11 = bf16[2,2,4,32,512]{4,3,2,1,0:T(8,128)(2,1)S(1)} collective-permute-done((bf16[2,2,4,32,512]{4,3,2,1,0:T(8,128)(2,1)S(1)}, bf16[2,2,4,32,512]{4,3,2,1,0:T(8,128)(2,1)S(1)}, u32[]{:S(2)}, u32[]{:S(2)}) %collective-permute-start.11) | collective-permute-done | bytes 524320 | tf_op jit(solution)/shard_map/ppermute | solution.py:188
  53.2 3.3 %collective-permute-start.15 = (bf16[4,32,512]{2,1,0:T(8,128)(2,1)S(1)}, bf16[4,32,512]{2,1,0:T(8,128)(2,1)S(1)}, u32[]{:S(2)}, u32[]{:S(2)}) collective-permute-start(bf16[4,32,512]{2,1,0:T(8,128)(2,1)S(1)} %get-tuple-element.92), channel_id=1, source_target_pairs={{0,64},{32,96},{64,0},{96,32},{1,65},{33,97},{65,1},{97,33},{2,66}... | collective-permute-start | bytes 393224 | tf_op jit(solution)/shard_map/ppermute | solution.py:188
  56.5 3.2 %collective-permute-done.3 = bf16[2,2,4,32,512]{4,3,2,1,0:T(8,128)(2,1)S(1)} collective-permute-done((bf16[2,2,4,32,512]{4,3,2,1,0:T(8,128)(2,1)S(1)}, bf16[2,2,4,32,512]{4,3,2,1,0:T(8,128)(2,1)S(1)}, u32[]{:S(2)}, u32[]{:S(2)}) %collective-permute-start.3) | collective-permute-done | bytes 524320 | tf_op jit(solution)/shard_map/ppermute | solution.py:188
  59.7 2.5 %collective-permute-start.16 = (bf16[4,32,512]{2,1,0:T(8,128)(2,1)S(1)}, bf16[4,32,512]{2,1,0:T(8,128)(2,1)S(1)}, u32[]{:S(2)}, u32[]{:S(2)}) collective-permute-start(bf16[4,32,512]{2,1,0:T(8,128)(2,1)S(1)} %get-tuple-element.91), channel_id=1, source_target_pairs={{0,96},{32,64},{64,32},{96,0},{1,97},{33,65},{65,33},{97,1},{2,98}... | collective-permute-start | bytes 393224 | tf_op jit(solution)/shard_map/ppermute | solution.py:188
  62.2 6.7 %collective-permute-done.5 = bf16[2,2,4,32,512]{4,3,2,1,0:T(8,128)(2,1)S(1)} collective-permute-done((bf16[2,2,4,32,512]{4,3,2,1,0:T(8,128)(2,1)S(1)}, bf16[2,2,4,32,512]{4,3,2,1,0:T(8,128)(2,1)S(1)}, u32[]{:S(2)}, u32[]{:S(2)}) %collective-permute-start.5) | collective-permute-done | bytes 524320 | tf_op jit(solution)/shard_map/ppermute | solution.py:188
  70.5 2.7 %collective-permute-start.8 = (bf16[4,32,512]{2,1,0:T(8,128)(2,1)S(1)}, bf16[4,32,512]{2,1,0:T(8,128)(2,1)S(1)}, u32[]{:S(2)}, u32[]{:S(2)}) collective-permute-start(bf16[4,32,512]{2,1,0:T(8,128)(2,1)S(1)} %get-tuple-element.94), channel_id=1, source_target_pairs={{0,144},{16,128},{128,16},{144,0},{1,145},{17,129},{129,17},{145,1... | collective-permute-start | bytes 393224 | tf_op jit(solution)/shard_map/ppermute | solution.py:188
  73.2 3.2 %collective-permute-done.7.refs_2_ = bf16[4,32,512]{2,1,0:T(8,128)(2,1)S(1)} collective-permute-done((bf16[4,32,512]{2,1,0:T(8,128)(2,1)S(1)}, bf16[4,32,512]{2,1,0:T(8,128)(2,1)S(1)}, u32[]{:S(2)}, u32[]{:S(2)}) %collective-permute-start.7) | collective-permute-done | bytes 131104 | tf_op jit(solution)/shard_map/ppermute | solution.py:188
  77.8 3.8 %collective-permute-done.18.got = bf16[4,32,512]{2,1,0:T(8,128)(2,1)S(1)} collective-permute-done((bf16[4,32,512]{2,1,0:T(8,128)(2,1)S(1)}, bf16[4,32,512]{2,1,0:T(8,128)(2,1)S(1)}, u32[]{:S(2)}, u32[]{:S(2)}) %collective-permute-start.18) | collective-permute-done | bytes 131104 | tf_op jit(solution)/shard_map/ppermute | solution.py:285
  84.2 3.7 %collective-permute-start.21 = (bf16[32,512]{1,0:T(8,128)(2,1)S(1)}, bf16[32,512]{1,0:T(8,128)(2,1)S(1)}, u32[]{:S(2)}, u32[]{:S(2)}) collective-permute-start(bf16[32,512]{1,0:T(8,128)(2,1)S(1)} %get-tuple-element.62), channel_id=1, source_target_pairs={{0,12},{2,14},{4,8},{6,10},{8,4},{10,6},{12,0},{14,2},{1,13},{3,15... | collective-permute-start | bytes 98312 | tf_op jit(solution)/shard_map/ppermute | solution.py:292
  89.5 4.6 %collective-permute-start.35 = (f32[32,1024]{1,0:T(8,128)S(1)}, f32[32,1024]{1,0:T(8,128)S(1)}, u32[]{:S(2)}, u32[]{:S(2)}) collective-permute-start(f32[32,1024]{1,0:T(8,128)S(1)} %get-tuple-element.68.refs_0_), channel_id=1, source_target_pairs={{0,8},{2,10},{4,12},{6,14},{8,0},{10,2},{12,4},{14,6},{1,9},{3,11}... | collective-permute-start | bytes 393224 | tf_op jit(solution)/shard_map/ppermute | solution.py:306
  95.2 11.2 %collective-permute-start.22 = (f32[8,512]{1,0:T(8,128)S(1)}, f32[8,512]{1,0:T(8,128)S(1)}, u32[]{:S(2)}, u32[]{:S(2)}) collective-permute-start(f32[8,512]{1,0:T(8,128)S(1)} %get-tuple-element.64), channel_id=1, source_target_pairs={{0,1},{1,0},{2,3},{3,2},{4,5},{5,4},{6,7},{7,6},{8,9},{9,8},{10,11... | collective-permute-start | bytes 49160 | tf_op jit(solution)/shard_map/ppermute | solution.py:314
  107.2 2.5 %collective-permute-start.24 = (f32[8,512]{1,0:T(8,128)S(1)}, f32[8,512]{1,0:T(8,128)S(1)}, u32[]{:S(2)}, u32[]{:S(2)}) collective-permute-start(f32[8,512]{1,0:T(8,128)S(1)} %add.80), channel_id=1, source_target_pairs={{0,32},{32,0},{64,96},{96,64},{1,33},{33,1},{65,97},{97,65},{2,34}... | collective-permute-start | bytes 49160 | tf_op jit(solution)/shard_map/ppermute | solution.py:188
  111.1 2.3 %collective-permute-start.38 = (f32[4,32,1024]{2,1,0:T(8,128)S(1)}, f32[4,32,1024]{2,1,0:T(8,128)S(1)}, u32[]{:S(2)}, u32[]{:S(2)}) collective-permute-start(f32[4,32,1024]{2,1,0:T(8,128)S(1)} %shard_map.104.near_half), channel_id=1, source_target_pairs={{0,2},{2,0},{4,6},{6,4},{8,10},{10,8},{12,14},{14,12},{1,3},{3,1},... | collective-permute-start | bytes 1572872 | tf_op jit(solution)/shard_map/ppermute | solution.py:313
  122.0 10.5 %collective-permute-start.33 = (f32[32,512]{1,0:T(8,128)S(1)}, f32[32,512]{1,0:T(8,128)S(1)}, u32[]{:S(2)}, u32[]{:S(2)}) collective-permute-start(f32[32,512]{1,0:T(8,128)S(1)} %add_add_fusion.2.g32), channel_id=1, source_target_pairs={{0,0},{1,64},{2,8},{3,72},{4,4},{5,68},{6,12},{7,76},{8,2},{9,66},... | collective-permute-start | bytes 196616 | tf_op jit(solution)/shard_map/ppermute | solution.py:295
  133.7 6.1 %collective-permute-done.32 = f32[8,512]{1,0:T(8,128)S(1)} collective-permute-done((f32[8,512]{1,0:T(8,128)S(1)}, f32[8,512]{1,0:T(8,128)S(1)}, u32[]{:S(2)}, u32[]{:S(2)}) %collective-permute-start.32) | collective-permute-done | bytes 16416 | tf_op jit(solution)/shard_map/ppermute | solution.py:318
  139.8 4.3 %collective-permute-done.34.far = f32[32,512]{1,0:T(8,128)S(1)} collective-permute-done((f32[32,512]{1,0:T(8,128)S(1)}, f32[32,512]{1,0:T(8,128)S(1)}, u32[]{:S(2)}, u32[]{:S(2)}) %collective-permute-start.34) | collective-permute-done | bytes 65568 | tf_op jit(solution)/shard_map/ppermute | solution.py:296
  145.4 2.3 %collective-permute-start.43 = (bf16[4,32,512]{2,1,0:T(8,128)(2,1)S(1)}, bf16[4,32,512]{2,1,0:T(8,128)(2,1)S(1)}, u32[]{:S(2)}, u32[]{:S(2)}) collective-permute-start(bf16[4,32,512]{2,1,0:T(8,128)(2,1)S(1)} %get-tuple-element.73), channel_id=1, source_target_pairs={{0,32},{32,0},{64,96},{96,64},{1,33},{33,1},{65,97},{97,65},{2,34}... | collective-permute-start | bytes 393224 | tf_op jit(solution)/shard_map/ppermute | solution.py:188
  147.7 2.4 %collective-permute-start.44 = (bf16[4,32,512]{2,1,0:T(8,128)(2,1)S(1)}, bf16[4,32,512]{2,1,0:T(8,128)(2,1)S(1)}, u32[]{:S(2)}, u32[]{:S(2)}) collective-permute-start(bf16[4,32,512]{2,1,0:T(8,128)(2,1)S(1)} %get-tuple-element.73), channel_id=1, source_target_pairs={{0,96},{32,64},{64,32},{96,0},{1,97},{33,65},{65,33},{97,1},{2,98}... | collective-permute-start | bytes 393224 | tf_op jit(solution)/shard_map/ppermute | solution.py:188
  164.4 8.9 %collective-permute-done.50.piece1 = bf16[2,2,4,32,512]{4,3,2,1,0:T(8,128)(2,1)S(1)} collective-permute-done((bf16[2,2,4,32,512]{4,3,2,1,0:T(8,128)(2,1)S(1)}, bf16[2,2,4,32,512]{4,3,2,1,0:T(8,128)(2,1)S(1)}, u32[]{:S(2)}, u32[]{:S(2)}) %collective-permute-start.50) | collective-permute-done | bytes 524320 | tf_op jit(solution)/shard_map/ppermute | solution.py:343
  176.7 2.1 %shard_map.108 = (f32[384,512]{1,0:T(8,128)S(1)}, f32[384,512]{1,0:T(8,128)S(1)}) custom-call(s32[6]{0:T(128)S(1)} %stack.57.pos, bf16[384,8192]{1,0:T(8,128)(2,1)S(1)} %bitcast.36, bf16[384,1024]{1,0:T(8,128)(2,1)S(1)} %collective-permute-done.9.tok2, bf16[2,2,4,32,512]{4,3,2,1,0:T(8,128)(2,1)S(1)} %bitcast.40, ...), custom_call_target="tpu_custom_call" | custom-call | flops 6442450944 | bytes 16777216 | tf_op jit(solution)/shard_map/pallas_call | solution.py:352
  178.8 3.8 %collective-permute-done.47.piece0 = bf16[2,2,4,32,512]{4,3,2,1,0:T(8,128)(2,1)S(1)} collective-permute-done((bf16[2,2,4,32,512]{4,3,2,1,0:T(8,128)(2,1)S(1)}, bf16[2,2,4,32,512]{4,3,2,1,0:T(8,128)(2,1)S(1)}, u32[]{:S(2)}, u32[]{:S(2)}) %collective-permute-start.47) | collective-permute-done | bytes 524320 | tf_op jit(solution)/shard_map/ppermute | solution.py:343
  182.6 3.1 %collective-permute-done.48.piece1 = bf16[2,2,4,32,512]{4,3,2,1,0:T(8,128)(2,1)S(1)} collective-permute-done((bf16[2,2,4,32,512]{4,3,2,1,0:T(8,128)(2,1)S(1)}, bf16[2,2,4,32,512]{4,3,2,1,0:T(8,128)(2,1)S(1)}, u32[]{:S(2)}, u32[]{:S(2)}) %collective-permute-start.48) | collective-permute-done | bytes 524320 | tf_op jit(solution)/shard_map/ppermute | solution.py:343
  185.7 2.1 %shard_map.109 = (f32[384,512]{1,0:T(8,128)S(1)}, f32[384,512]{1,0:T(8,128)S(1)}) custom-call(s32[6]{0:T(128)S(1)} %stack.57.pos, bf16[384,8192]{1,0:T(8,128)(2,1)S(1)} %bitcast.36, bf16[384,1024]{1,0:T(8,128)(2,1)S(1)} %collective-permute-done.2.tok2, bf16[2,2,4,32,512]{4,3,2,1,0:T(8,128)(2,1)S(1)} %collective-permute-done.47.piece0, ...), custom_call_target="tpu_custom_call" | custom-call | flops 6442450944 | bytes 16777216 | tf_op jit(solution)/shard_map/pallas_call | solution.py:352
  189.9 2.5 %collective-permute-start.51 = (f32[384,512]{1,0:T(8,128)S(1)}, f32[384,512]{1,0:T(8,128)S(1)}, u32[]{:S(2)}, u32[]{:S(2)}) collective-permute-start(f32[384,512]{1,0:T(8,128)S(1)} %get-tuple-element.86), channel_id=1, source_target_pairs={{0,1},{1,0},{2,3},{3,2},{4,5},{5,4},{6,7},{7,6},{8,9},{9,8},{10,11... | collective-permute-start | bytes 2359304 | tf_op jit(solution)/shard_map/ppermute | solution.py:368
  (124 shorter events, 53.8 us)
Async XLA Ops:
  4.3 18.1 %collective-permute-start.9 = (bf16[384,1024]{1,0:T(8,128)(2,1)S(1)}, bf16[384,1024]{1,0:T(8,128)(2,1)S(1)}, u32[]{:S(2)}, u32[]{:S(2)}) collective-permute-start(bf16[384,1024]{1,0:T(8,128)(2,1)S(1)} %shard_map.96), channel_id=1, source_target_pairs={{0,1},{1,0},{2,3},{3,2},{4,5},{5,4},{6,7},{7,6},{8,9},{9,8},{10,11... | collective-permute-start | bytes 2359304 | tf_op jit(solution)/shard_map/ppermute | solution.py:238
  5.1 16.7 %collective-permute-start.1 = (bf16[384,512]{1,0:T(8,128)(2,1)}, bf16[384,512]{1,0:T(8,128)(2,1)}, u32[]{:S(2)}, u32[]{:S(2)}) collective-permute-start(bf16[384,512]{1,0:T(8,128)(2,1)} %cot.7), channel_id=1, source_target_pairs={{0,1},{1,0},{2,3},{3,2},{4,5},{5,4},{6,7},{7,6},{8,9},{9,8},{10,11... | collective-permute-start | bytes 1179656 | tf_op jit(solution)/shard_map/ppermute | solution.py:218
  6.0 22.5 %collective-permute-start.10 = (bf16[384,1024]{1,0:T(8,128)(2,1)S(1)}, bf16[384,1024]{1,0:T(8,128)(2,1)S(1)}, u32[]{:S(2)}, u32[]{:S(2)}) collective-permute-start(bf16[384,1024]{1,0:T(8,128)(2,1)S(1)} %shard_map.98), channel_id=1, source_target_pairs={{0,1},{1,0},{2,3},{3,2},{4,5},{5,4},{6,7},{7,6},{8,9},{9,8},{10,11... | collective-permute-start | bytes 2359304 | tf_op jit(solution)/shard_map/ppermute | solution.py:238
  7.2 63.3 %collective-permute-start.17 = (f32[32,640]{1,0:T(8,128)S(1)}, f32[32,640]{1,0:T(8,128)S(1)}, u32[]{:S(2)}, u32[]{:S(2)}) collective-permute-start(f32[32,640]{1,0:T(8,128)S(1)} %shard_map.100), channel_id=1, source_target_pairs={{0,0},{1,64},{2,8},{3,72},{4,4},{5,68},{6,12},{7,76},{8,2},{9,66},... | collective-permute-start | bytes 245768 | tf_op jit(solution)/shard_map/ppermute | solution.py:250
  20.9 11.3 %collective-permute-start = (bf16[384,1024]{1,0:T(8,128)(2,1)S(1)}, bf16[384,1024]{1,0:T(8,128)(2,1)S(1)}, u32[]{:S(2)}, u32[]{:S(2)}) collective-permute-start(bf16[384,1024]{1,0:T(8,128)(2,1)S(1)} %shard_map.92), channel_id=1, source_target_pairs={{0,1},{1,0},{2,3},{3,2},{4,5},{5,4},{6,7},{7,6},{8,9},{9,8},{10,11... | collective-permute-start | bytes 2359304 | tf_op jit(solution)/shard_map/ppermute | solution.py:238
  21.8 14.4 %collective-permute-start.2 = (bf16[384,1024]{1,0:T(8,128)(2,1)S(1)}, bf16[384,1024]{1,0:T(8,128)(2,1)S(1)}, u32[]{:S(2)}, u32[]{:S(2)}) collective-permute-start(bf16[384,1024]{1,0:T(8,128)(2,1)S(1)} %shard_map.94), channel_id=1, source_target_pairs={{0,1},{1,0},{2,3},{3,2},{4,5},{5,4},{6,7},{7,6},{8,9},{9,8},{10,11... | collective-permute-start | bytes 2359304 | tf_op jit(solution)/shard_map/ppermute | solution.py:238
  25.7 15.2 %collective-permute-start.12 = (bf16[2,2,4,32,512]{4,3,2,1,0:T(8,128)(2,1)S(1)}, bf16[2,2,4,32,512]{4,3,2,1,0:T(8,128)(2,1)S(1)}, u32[]{:S(2)}, u32[]{:S(2)}) collective-permute-start(bf16[2,2,4,32,512]{4,3,2,1,0:T(8,128)(2,1)S(1)} %get-tuple-element.52), channel_id=1, source_target_pairs={{0,128},{16,144},{128,0},{144,16},{1,129},{17,145},{129,1},{145,17... | collective-permute-start | bytes 1572872 | tf_op jit(solution)/shard_map/ppermute | solution.py:188
  31.8 20.4 %collective-permute-start.11 = (bf16[2,2,4,32,512]{4,3,2,1,0:T(8,128)(2,1)S(1)}, bf16[2,2,4,32,512]{4,3,2,1,0:T(8,128)(2,1)S(1)}, u32[]{:S(2)}, u32[]{:S(2)}) collective-permute-start(bf16[2,2,4,32,512]{4,3,2,1,0:T(8,128)(2,1)S(1)} %get-tuple-element.51), channel_id=1, source_target_pairs={{0,16},{16,0},{128,144},{144,128},{1,17},{17,1},{129,145},{145,129... | collective-permute-start | bytes 1572872 | tf_op jit(solution)/shard_map/ppermute | solution.py:188
  32.2 20.2 %collective-permute-start.13 = (bf16[2,2,4,32,512]{4,3,2,1,0:T(8,128)(2,1)S(1)}, bf16[2,2,4,32,512]{4,3,2,1,0:T(8,128)(2,1)S(1)}, u32[]{:S(2)}, u32[]{:S(2)}) collective-permute-start(bf16[2,2,4,32,512]{4,3,2,1,0:T(8,128)(2,1)S(1)} %get-tuple-element.53), channel_id=1, source_target_pairs={{0,144},{16,128},{128,16},{144,0},{1,145},{17,129},{129,17},{145,1... | collective-permute-start | bytes 1572872 | tf_op jit(solution)/shard_map/ppermute | solution.py:188
  36.2 17.1 %collective-permute-start.4 = (bf16[2,2,4,32,512]{4,3,2,1,0:T(8,128)(2,1)S(1)}, bf16[2,2,4,32,512]{4,3,2,1,0:T(8,128)(2,1)S(1)}, u32[]{:S(2)}, u32[]{:S(2)}) collective-permute-start(bf16[2,2,4,32,512]{4,3,2,1,0:T(8,128)(2,1)S(1)} %get-tuple-element.48), channel_id=1, source_target_pairs={{0,64},{32,96},{64,0},{96,32},{1,65},{33,97},{65,1},{97,33},{2,66}... | collective-permute-start | bytes 1572872 | tf_op jit(solution)/shard_map/ppermute | solution.py:188
  40.8 18.8 %collective-permute-start.3 = (bf16[2,2,4,32,512]{4,3,2,1,0:T(8,128)(2,1)S(1)}, bf16[2,2,4,32,512]{4,3,2,1,0:T(8,128)(2,1)S(1)}, u32[]{:S(2)}, u32[]{:S(2)}) collective-permute-start(bf16[2,2,4,32,512]{4,3,2,1,0:T(8,128)(2,1)S(1)} %get-tuple-element.47), channel_id=1, source_target_pairs={{0,32},{32,0},{64,96},{96,64},{1,33},{33,1},{65,97},{97,65},{2,34}... | collective-permute-start | bytes 1572872 | tf_op jit(solution)/shard_map/ppermute | solution.py:188
  52.2 16.7 %collective-permute-start.5 = (bf16[2,2,4,32,512]{4,3,2,1,0:T(8,128)(2,1)S(1)}, bf16[2,2,4,32,512]{4,3,2,1,0:T(8,128)(2,1)S(1)}, u32[]{:S(2)}, u32[]{:S(2)}) collective-permute-start(bf16[2,2,4,32,512]{4,3,2,1,0:T(8,128)(2,1)S(1)} %get-tuple-element.49), channel_id=1, source_target_pairs={{0,96},{32,64},{64,32},{96,0},{1,97},{33,65},{65,33},{97,1},{2,98}... | collective-permute-start | bytes 1572872 | tf_op jit(solution)/shard_map/ppermute | solution.py:188
  52.7 17.7 %collective-permute-start.14 = (bf16[4,32,512]{2,1,0:T(8,128)(2,1)S(1)}, bf16[4,32,512]{2,1,0:T(8,128)(2,1)S(1)}, u32[]{:S(2)}, u32[]{:S(2)}) collective-permute-start(bf16[4,32,512]{2,1,0:T(8,128)(2,1)S(1)} %get-tuple-element.93), channel_id=1, source_target_pairs={{0,32},{32,0},{64,96},{96,64},{1,33},{33,1},{65,97},{97,65},{2,34}... | collective-permute-start | bytes 393224 | tf_op jit(solution)/shard_map/ppermute | solution.py:188
  53.2 20.0 %collective-permute-start.15 = (bf16[4,32,512]{2,1,0:T(8,128)(2,1)S(1)}, bf16[4,32,512]{2,1,0:T(8,128)(2,1)S(1)}, u32[]{:S(2)}, u32[]{:S(2)}) collective-permute-start(bf16[4,32,512]{2,1,0:T(8,128)(2,1)S(1)} %get-tuple-element.92), channel_id=1, source_target_pairs={{0,64},{32,96},{64,0},{96,32},{1,65},{33,97},{65,1},{97,33},{2,66}... | collective-permute-start | bytes 393224 | tf_op jit(solution)/shard_map/ppermute | solution.py:188
  59.7 13.6 %collective-permute-start.16 = (bf16[4,32,512]{2,1,0:T(8,128)(2,1)S(1)}, bf16[4,32,512]{2,1,0:T(8,128)(2,1)S(1)}, u32[]{:S(2)}, u32[]{:S(2)}) collective-permute-start(bf16[4,32,512]{2,1,0:T(8,128)(2,1)S(1)} %get-tuple-element.91), channel_id=1, source_target_pairs={{0,96},{32,64},{64,32},{96,0},{1,97},{33,65},{65,33},{97,1},{2,98}... | collective-permute-start | bytes 393224 | tf_op jit(solution)/shard_map/ppermute | solution.py:188
  89.5 20.3 %collective-permute-start.35 = (f32[32,1024]{1,0:T(8,128)S(1)}, f32[32,1024]{1,0:T(8,128)S(1)}, u32[]{:S(2)}, u32[]{:S(2)}) collective-permute-start(f32[32,1024]{1,0:T(8,128)S(1)} %get-tuple-element.68.refs_0_), channel_id=1, source_target_pairs={{0,8},{2,10},{4,12},{6,14},{8,0},{10,2},{12,4},{14,6},{1,9},{3,11}... | collective-permute-start | bytes 393224 | tf_op jit(solution)/shard_map/ppermute | solution.py:306
  94.1 16.4 %collective-permute-start.36 = (f32[32,1024]{1,0:T(8,128)S(1)}, f32[32,1024]{1,0:T(8,128)S(1)}, u32[]{:S(2)}, u32[]{:S(2)}) collective-permute-start(f32[32,1024]{1,0:T(8,128)S(1)} %get-tuple-element.68.refs_0_), channel_id=1, source_target_pairs={{0,4},{2,6},{4,0},{6,2},{8,12},{10,14},{12,8},{14,10},{1,5},{3,7},... | collective-permute-start | bytes 393224 | tf_op jit(solution)/shard_map/ppermute | solution.py:306
  95.2 15.3 %collective-permute-start.37 = (f32[32,1024]{1,0:T(8,128)S(1)}, f32[32,1024]{1,0:T(8,128)S(1)}, u32[]{:S(2)}, u32[]{:S(2)}) collective-permute-start(f32[32,1024]{1,0:T(8,128)S(1)} %get-tuple-element.68.refs_0_), channel_id=1, source_target_pairs={{0,12},{2,14},{4,8},{6,10},{8,4},{10,6},{12,0},{14,2},{1,13},{3,15... | collective-permute-start | bytes 393224 | tf_op jit(solution)/shard_map/ppermute | solution.py:306
  95.2 12.0 %collective-permute-start.22 = (f32[8,512]{1,0:T(8,128)S(1)}, f32[8,512]{1,0:T(8,128)S(1)}, u32[]{:S(2)}, u32[]{:S(2)}) collective-permute-start(f32[8,512]{1,0:T(8,128)S(1)} %get-tuple-element.64), channel_id=1, source_target_pairs={{0,1},{1,0},{2,3},{3,2},{4,5},{5,4},{6,7},{7,6},{8,9},{9,8},{10,11... | collective-permute-start | bytes 49160 | tf_op jit(solution)/shard_map/ppermute | solution.py:314
  111.1 33.0 %collective-permute-start.38 = (f32[4,32,1024]{2,1,0:T(8,128)S(1)}, f32[4,32,1024]{2,1,0:T(8,128)S(1)}, u32[]{:S(2)}, u32[]{:S(2)}) collective-permute-start(f32[4,32,1024]{2,1,0:T(8,128)S(1)} %shard_map.104.near_half), channel_id=1, source_target_pairs={{0,2},{2,0},{4,6},{6,4},{8,10},{10,8},{12,14},{14,12},{1,3},{3,1},... | collective-permute-start | bytes 1572872 | tf_op jit(solution)/shard_map/ppermute | solution.py:313
  119.3 13.3 %collective-permute-start.29 = (f32[8,512]{1,0:T(8,128)S(1)}, f32[8,512]{1,0:T(8,128)S(1)}, u32[]{:S(2)}, u32[]{:S(2)}) collective-permute-start(f32[8,512]{1,0:T(8,128)S(1)} %add_add_fusion.4), channel_id=1, source_target_pairs={{0,4},{2,6},{4,0},{6,2},{8,12},{10,14},{12,8},{14,10},{1,5},{3,7},... | collective-permute-start | bytes 49160 | tf_op jit(solution)/shard_map/ppermute | solution.py:317
  119.7 13.3 %collective-permute-start.30 = (f32[8,512]{1,0:T(8,128)S(1)}, f32[8,512]{1,0:T(8,128)S(1)}, u32[]{:S(2)}, u32[]{:S(2)}) collective-permute-start(f32[8,512]{1,0:T(8,128)S(1)} %add_add_fusion.4), channel_id=1, source_target_pairs={{0,2},{2,0},{4,6},{6,4},{8,10},{10,8},{12,14},{14,12},{1,3},{3,1},... | collective-permute-start | bytes 49160 | tf_op jit(solution)/shard_map/ppermute | solution.py:317
  120.5 12.5 %collective-permute-start.31 = (f32[8,512]{1,0:T(8,128)S(1)}, f32[8,512]{1,0:T(8,128)S(1)}, u32[]{:S(2)}, u32[]{:S(2)}) collective-permute-start(f32[8,512]{1,0:T(8,128)S(1)} %add_add_fusion.4), channel_id=1, source_target_pairs={{0,6},{2,4},{4,2},{6,0},{8,14},{10,12},{12,10},{14,8},{1,7},{3,5},... | collective-permute-start | bytes 49160 | tf_op jit(solution)/shard_map/ppermute | solution.py:317
  122.0 17.8 %collective-permute-start.33 = (f32[32,512]{1,0:T(8,128)S(1)}, f32[32,512]{1,0:T(8,128)S(1)}, u32[]{:S(2)}, u32[]{:S(2)}) collective-permute-start(f32[32,512]{1,0:T(8,128)S(1)} %add_add_fusion.2.g32), channel_id=1, source_target_pairs={{0,0},{1,64},{2,8},{3,72},{4,4},{5,68},{6,12},{7,76},{8,2},{9,66},... | collective-permute-start | bytes 196616 | tf_op jit(solution)/shard_map/ppermute | solution.py:295
  132.5 11.6 %collective-permute-start.34 = (f32[32,512]{1,0:T(8,128)S(1)}, f32[32,512]{1,0:T(8,128)S(1)}, u32[]{:S(2)}, u32[]{:S(2)}) collective-permute-start(f32[32,512]{1,0:T(8,128)S(1)} %add_add_fusion.2.g32), channel_id=1, source_target_pairs={{0,128},{1,192},{2,136},{3,200},{4,132},{5,196},{6,140},{7,204},{8... | collective-permute-start | bytes 196616 | tf_op jit(solution)/shard_map/ppermute | solution.py:296
  145.4 9.6 %collective-permute-start.43 = (bf16[4,32,512]{2,1,0:T(8,128)(2,1)S(1)}, bf16[4,32,512]{2,1,0:T(8,128)(2,1)S(1)}, u32[]{:S(2)}, u32[]{:S(2)}) collective-permute-start(bf16[4,32,512]{2,1,0:T(8,128)(2,1)S(1)} %get-tuple-element.73), channel_id=1, source_target_pairs={{0,32},{32,0},{64,96},{96,64},{1,33},{33,1},{65,97},{97,65},{2,34}... | collective-permute-start | bytes 393224 | tf_op jit(solution)/shard_map/ppermute | solution.py:188
  159.0 14.2 %collective-permute-start.50 = (bf16[2,2,4,32,512]{4,3,2,1,0:T(8,128)(2,1)S(1)}, bf16[2,2,4,32,512]{4,3,2,1,0:T(8,128)(2,1)S(1)}, u32[]{:S(2)}, u32[]{:S(2)}) collective-permute-start(bf16[2,2,4,32,512]{4,3,2,1,0:T(8,128)(2,1)S(1)} %bitcast.41), channel_id=1, source_target_pairs={{0,64},{32,96},{64,0},{96,32},{1,65},{33,97},{65,1},{97,33},{2,66}... | collective-permute-start | bytes 1572872 | tf_op jit(solution)/shard_map/ppermute | solution.py:343
  160.0 22.6 %collective-permute-start.47 = (bf16[2,2,4,32,512]{4,3,2,1,0:T(8,128)(2,1)S(1)}, bf16[2,2,4,32,512]{4,3,2,1,0:T(8,128)(2,1)S(1)}, u32[]{:S(2)}, u32[]{:S(2)}) collective-permute-start(bf16[2,2,4,32,512]{4,3,2,1,0:T(8,128)(2,1)S(1)} %bitcast.42), channel_id=1, source_target_pairs={{0,32},{32,0},{64,96},{96,64},{1,33},{33,1},{65,97},{97,65},{2,34}... | collective-permute-start | bytes 1572872 | tf_op jit(solution)/shard_map/ppermute | solution.py:343
  160.7 25.0 %collective-permute-start.48 = (bf16[2,2,4,32,512]{4,3,2,1,0:T(8,128)(2,1)S(1)}, bf16[2,2,4,32,512]{4,3,2,1,0:T(8,128)(2,1)S(1)}, u32[]{:S(2)}, u32[]{:S(2)}) collective-permute-start(bf16[2,2,4,32,512]{4,3,2,1,0:T(8,128)(2,1)S(1)} %bitcast.43), channel_id=1, source_target_pairs={{0,96},{32,64},{64,32},{96,0},{1,97},{33,65},{65,33},{97,1},{2,98}... | collective-permute-start | bytes 1572872 | tf_op jit(solution)/shard_map/ppermute | solution.py:343
  162.4 14.3 %collective-permute-start.49 = (bf16[2,2,4,32,512]{4,3,2,1,0:T(8,128)(2,1)S(1)}, bf16[2,2,4,32,512]{4,3,2,1,0:T(8,128)(2,1)S(1)}, u32[]{:S(2)}, u32[]{:S(2)}) collective-permute-start(bf16[2,2,4,32,512]{4,3,2,1,0:T(8,128)(2,1)S(1)} %bitcast.37), channel_id=1, source_target_pairs={{0,128},{16,144},{128,0},{144,16},{1,129},{17,145},{129,1},{145,17... | collective-permute-start | bytes 1572872 | tf_op jit(solution)/shard_map/ppermute | solution.py:344
  164.4 23.4 %collective-permute-start.45 = (bf16[2,2,4,32,512]{4,3,2,1,0:T(8,128)(2,1)S(1)}, bf16[2,2,4,32,512]{4,3,2,1,0:T(8,128)(2,1)S(1)}, u32[]{:S(2)}, u32[]{:S(2)}) collective-permute-start(bf16[2,2,4,32,512]{4,3,2,1,0:T(8,128)(2,1)S(1)} %bitcast.38), channel_id=1, source_target_pairs={{0,16},{16,0},{128,144},{144,128},{1,17},{17,1},{129,145},{145,129... | collective-permute-start | bytes 1572872 | tf_op jit(solution)/shard_map/ppermute | solution.py:344
  173.3 14.5 %collective-permute-start.46 = (bf16[2,2,4,32,512]{4,3,2,1,0:T(8,128)(2,1)S(1)}, bf16[2,2,4,32,512]{4,3,2,1,0:T(8,128)(2,1)S(1)}, u32[]{:S(2)}, u32[]{:S(2)}) collective-permute-start(bf16[2,2,4,32,512]{4,3,2,1,0:T(8,128)(2,1)S(1)} %bitcast.39), channel_id=1, source_target_pairs={{0,144},{16,128},{128,16},{144,0},{1,145},{17,129},{129,17},{145,1... | collective-permute-start | bytes 1572872 | tf_op jit(solution)/shard_map/ppermute | solution.py:344
  (27 other events, 444.1 us)
